TPU v7x, 32 devices: a whole 2x2x4 slice. The times are simulated.
32 devices in a mesh: wide: 8 (over z, y), narrow: 4 (over x, core).
Axes of the slice: x: 2, y: 2, z: 4, core: 2. Of those that a mesh axis runs over, the one named last changes fastest.
Arguments:
- inputs: bfloat16 [8192, 2048], P(('wide', 'narrow')), may hold values from -6 to 6
- out_grad: bfloat16 [8192, 2048], P(('wide', 'narrow')), may hold values from -6 to 6
- seq_lengths: int32 [10], replicated, may hold values from 1 to 2048, 8192 in all
- decay_rate: float32 [16], replicated, may hold values from 0.00012207031 to 0.05
- attn_in: float32 [2048, 8192], P(('wide', 'narrow')), may hold values from -0.125 to 0.125
- attn_out: float32 [2048, 2048], P(('wide', 'narrow')), may hold values from -0.125 to 0.125
- sglu_in: float32 [2, 2048, 5632], P(None, 'wide', 'narrow'), may hold values from -0.125 to 0.125
- sglu_out: float32 [5632, 2048], P('narrow', 'wide'), may hold values from -0.078125 to 0.078125
- mom_attn_in: float32 [2048, 8192], P(('wide', 'narrow')), may hold values from -512 to 512
- mom_attn_out: float32 [2048, 2048], P(('wide', 'narrow')), may hold values from -512 to 512
- mom_sglu_in: float32 [2, 2048, 5632], P(None, 'wide', 'narrow'), may hold values from -512 to 512
- mom_sglu_out: float32 [5632, 2048], P('narrow', 'wide'), may hold values from -512 to 512
- avg_attn_in: float32 [2048, 8192], P(('wide', 'narrow')), may hold values from -0.125 to 0.125
- avg_attn_out: float32 [2048, 2048], P(('wide', 'narrow')), may hold values from -0.125 to 0.125
- avg_sglu_in: float32 [2, 2048, 5632], P(None, 'wide', 'narrow'), may hold values from -0.125 to 0.125
- avg_sglu_out: float32 [5632, 2048], P('narrow', 'wide'), may hold values from -0.078125 to 0.078125
Outputs:
- output: float32 [8192, 2048], P(('wide', 'narrow'))
- input_grad: float32 [8192, 2048], P(('wide', 'narrow'))
- new_mom_attn_in: float32 [2048, 8192], P(('wide', 'narrow'))
- new_mom_attn_out: float32 [2048, 2048], P(('wide', 'narrow'))
- new_mom_sglu_in: float32 [2, 2048, 5632], P(None, 'wide', 'narrow')
- new_mom_sglu_out: float32 [5632, 2048], P('narrow', 'wide')
- new_attn_in: float32 [2048, 8192], P(('wide', 'narrow'))
- new_attn_out: float32 [2048, 2048], P(('wide', 'narrow'))
- new_sglu_in: float32 [2, 2048, 5632], P(None, 'wide', 'narrow')
- new_sglu_out: float32 [5632, 2048], P('narrow', 'wide')
- new_avg_attn_in: float32 [2048, 8192], P(('wide', 'narrow'))
- new_avg_attn_out: float32 [2048, 2048], P(('wide', 'narrow'))
- new_avg_sglu_in: float32 [2, 2048, 5632], P(None, 'wide', 'narrow')
- new_avg_sglu_out: float32 [5632, 2048], P('narrow', 'wide')
Inputs may be any that keep to these rules, and one draw needn't show every extreme that they name: `seq_lengths`: the lengths sum to 8192; the largest is exactly 2048.
All inputs are finite; a program needn't handle non-finite values.
Results may differ from a plain program's by a relative error of at most 0.012.
Values may be sent and summed in bfloat16 or wider, within the bound.
No kernel may reach another device: no remote copies, remote signals or barrier semaphores. Data moves between devices by JAX's collectives and lax.ppermute only.
A program may use at most 384 MiB of HBM per device.

v0:
```python
import math

import jax
import jax.numpy as jnp
from jax import lax
from jax.sharding import PartitionSpec as P

FF = 5632
BLOCK = 256


EPS = 1e-06
MU = 0.9
BETA = 0.8
HIGH = lax.Precision.HIGHEST


def prefix(part, axis, combine, identity):
    place = lax.axis_index(axis)
    gathered = jax.tree.map(lambda a: lax.all_gather(a, axis), part)
    state = jax.tree.map(lambda a, e: jnp.zeros_like(a) + jnp.asarray(e, a.dtype), part, identity)

    def one(lap, state):
        return combine(
            state, jax.tree.map(lambda a: lax.dynamic_index_in_dim(a, lap, 0, False), gathered)
        )

    return lax.fori_loop(0, place, one, state)


def prefix_2(x, axis, combine, identity):
    count, position = (lax.axis_size(axis), lax.axis_index(axis))
    everything = jax.tree.map(
        lambda part, kind: lax.all_gather(part.astype(kind), axis), x, (jnp.bfloat16, jnp.bfloat16)
    )
    start = jax.tree.map(
        lambda part, zero: jnp.broadcast_to(jnp.asarray(zero, part.dtype), part.shape), x, identity
    )

    def lap(k, before):
        at = count - 1 - k
        reached = at > position
        new = combine(
            before, jax.tree.map(lambda part, own: part[at].astype(own.dtype), everything, x)
        )
        return jax.tree.map(lambda a, b: jnp.where(reached, a, b), new, before)

    return lax.fori_loop(0, count, lap, start)


def srms(v):
    return v * lax.rsqrt(jnp.mean(v * v, axis=-1, keepdims=True) + EPS)


def srms_back(v, grad):
    _, pull = jax.vjp(srms, v)
    return pull(grad)[0]


def block_parts(seg_block, prev_seg, rate):
    length = seg_block.shape[0]
    index = jnp.arange(length).astype(jnp.float32)
    spread = index[:, None] - index[None, :]
    allowed = (spread >= 0) & (seg_block[:, None] == seg_block[None, :])
    mask = jnp.where(
        allowed[None], jnp.exp(-rate[:, None, None] * jnp.maximum(spread, 0.0)[None]), 0.0
    )
    enter = (
        jnp.exp(-rate[None, :] * index[:, None])
        * (seg_block == prev_seg).astype(jnp.float32)[:, None]
    )
    last = seg_block[length - 1]
    leave = (
        jnp.exp(-rate[None, :] * (length - index)[:, None])
        * (seg_block == last).astype(jnp.float32)[:, None]
    )
    carry = jnp.exp(-rate * length) * (prev_seg == last).astype(jnp.float32)
    return (mask, enter, leave, carry)


def chain(earlier, later):
    return (earlier[0] * later[0], later[0][:, None, None] * earlier[1] + later[1])


def renew(weight, moment, average, grad, fan, tokens):
    step = 0.4 / math.sqrt(fan * tokens)
    moment_new = MU * moment + grad
    weight_new = weight - step * (grad + MU * moment_new)
    average_new = BETA * average + (1.0 - BETA) * weight_new
    return (moment_new, weight_new, average_new)


def per_device(
    inputs,
    out_grad,
    seq_lengths,
    decay_rate,
    attn_in,
    attn_out,
    sglu_in,
    sglu_out,
    mom_attn_in,
    mom_attn_out,
    mom_sglu_in,
    mom_sglu_out,
    avg_attn_in,
    avg_attn_out,
    avg_sglu_in,
    avg_sglu_out,
):
    rows, width = inputs.shape
    heads = decay_rate.shape[0]
    head_dim = width // heads
    count = rows // BLOCK
    tokens = rows * lax.axis_size(("wide", "narrow"))
    start = lax.axis_index(("wide", "narrow")) * rows
    ends = jnp.cumsum(seq_lengths)
    places = start - 1 + jnp.arange(rows + 1, dtype=jnp.int32)
    marks = jnp.sum((places[:, None] >= ends[None, :]).astype(jnp.int32), axis=1)
    marks = jnp.where(places < 0, -1, marks)
    seg_ids = marks[1:]
    prev_ids = marks[:-1].reshape(count, BLOCK)[:, 0]
    w_in, w_out = (
        lax.all_gather(attn_in.astype(jnp.bfloat16), ("wide", "narrow"), axis=0, tiled=True),
        lax.all_gather(attn_out.astype(jnp.bfloat16), ("wide", "narrow"), axis=0, tiled=True),
    )
    w_pair, w_third = (
        lax.all_gather(sglu_in.astype(jnp.bfloat16), "wide", axis=1, tiled=True),
        lax.all_gather(sglu_out.astype(jnp.bfloat16), "wide", axis=1, tiled=True),
    )
    xf = inputs.astype(jnp.float32)
    norm1 = srms(xf).astype(jnp.bfloat16)
    pre = jnp.dot(norm1, w_in, preferred_element_type=jnp.float32)
    pre_query = pre[:, :width]
    pre_key = pre[:, width : 2 * width]
    gate = pre[:, 3 * width :]
    query = jax.nn.silu(pre_query).astype(jnp.bfloat16).reshape(rows, heads, head_dim)
    key = jax.nn.silu(pre_key).astype(jnp.bfloat16).reshape(rows, heads, head_dim)
    value = pre[:, 2 * width : 3 * width].astype(jnp.bfloat16).reshape(rows, heads, head_dim)
    parts = [block_parts(seg_ids, prev_ids[0], decay_rate)]
    q_blocks = [query]
    k_blocks = [key]
    v_blocks = [value]
    total_carry = jnp.ones((heads,), jnp.float32)
    total_state = jnp.zeros((heads, head_dim, head_dim), jnp.float32)
    b = 0
    leave = parts[b][2]
    term = jnp.einsum(
        "thd,the->hde",
        k_blocks[b].astype(jnp.float32) * leave[:, :, None],
        v_blocks[b].astype(jnp.float32),
        precision=HIGH,
    )
    total_carry = total_carry * parts[b][3]
    total_state = parts[b][3][:, None, None] * total_state + term
    identity = (
        jnp.ones((heads,), jnp.float32),
        jnp.zeros((heads, head_dim, head_dim), jnp.float32),
    )
    state = prefix((total_carry, total_state), ("wide", "narrow"), chain, identity)[1]
    b = 0
    mask, enter, leave, carry = parts[b]
    states = [state]
    scores = jnp.einsum(
        "thd,shd->hts", q_blocks[b], k_blocks[b], preferred_element_type=jnp.float32
    )
    weights = (scores * mask).astype(jnp.bfloat16)
    kept_weights = [weights]
    intra = jnp.einsum("hts,shd->thd", weights, v_blocks[b], preferred_element_type=jnp.float32)
    inter = jnp.einsum(
        "thd,hde->the", q_blocks[b].astype(jnp.float32) * enter[:, :, None], state, precision=HIGH
    )
    outs = intra + inter
    attn = outs.reshape(rows, width)
    normed = srms(attn)
    mixed = (normed * gate).astype(jnp.bfloat16)
    mid = xf + jnp.dot(mixed, w_out, preferred_element_type=jnp.float32)
    norm2 = srms(mid).astype(jnp.bfloat16)
    gathered = lax.all_gather(norm2, "narrow", axis=0, tiled=True)
    first = jnp.dot(gathered, w_pair[0], preferred_element_type=jnp.float32)
    second = jnp.dot(gathered, w_pair[1], preferred_element_type=jnp.float32)
    product = (first * second).astype(jnp.bfloat16)
    output = mid + lax.psum_scatter(
        jnp.dot(product, w_third, preferred_element_type=jnp.float32).astype(jnp.bfloat16),
        "narrow",
        scatter_dimension=0,
        tiled=True,
    ).astype(jnp.float32)
    grad_rows = lax.all_gather(out_grad, "narrow", axis=0, tiled=True)
    grad_prod = jnp.dot(grad_rows, w_third.T, preferred_element_type=jnp.float32)
    grad_third = jnp.dot(product.T, grad_rows, preferred_element_type=jnp.float32)
    grad_first = (grad_prod * second).astype(jnp.bfloat16)
    grad_second = (grad_prod * first).astype(jnp.bfloat16)
    grad_pair = jnp.stack(
        [
            jnp.dot(gathered.T, grad_first, preferred_element_type=jnp.float32),
            jnp.dot(gathered.T, grad_second, preferred_element_type=jnp.float32),
        ]
    )
    partial_value = jnp.dot(grad_first, w_pair[0].T, preferred_element_type=jnp.float32) + jnp.dot(
        grad_second, w_pair[1].T, preferred_element_type=jnp.float32
    )
    grad_norm2 = lax.psum_scatter(partial_value, "narrow", scatter_dimension=0, tiled=True)
    grad_mid = out_grad.astype(jnp.float32) + srms_back(mid, grad_norm2)
    grad_branch = grad_mid.astype(jnp.bfloat16)
    grad_mixed = jnp.dot(grad_branch, w_out.T, preferred_element_type=jnp.float32)
    grad_gate = grad_mixed * normed
    grad_attn = (
        srms_back(attn, grad_mixed * gate).astype(jnp.bfloat16).reshape(rows, heads, head_dim)
    )
    g_blocks = [grad_attn]
    b = 0
    enter = parts[b][1]
    local_terms = [
        jnp.einsum(
            "thd,the->hde",
            q_blocks[b].astype(jnp.float32) * enter[:, :, None],
            g_blocks[b].astype(jnp.float32),
            precision=HIGH,
        )
    ]
    back_state = jnp.zeros((heads, head_dim, head_dim), jnp.float32)
    b = 0
    back_state = local_terms[b] + parts[b][3][:, None, None] * back_state
    later = prefix_2((total_carry, back_state), ("wide", "narrow"), chain, identity)[1]
    grads_q = [None] * count
    grads_k = [None] * count
    grads_v = [None] * count
    b = 0
    mask, enter, leave, carry = parts[b]
    qb = q_blocks[b]
    kb = k_blocks[b]
    vb = v_blocks[b]
    gb = g_blocks[b]
    grad_w = jnp.einsum("the,she->hts", gb, vb, preferred_element_type=jnp.float32)
    grad_s = (grad_w * mask).astype(jnp.bfloat16)
    grads_q[b] = jnp.einsum("hts,shd->thd", grad_s, kb, preferred_element_type=jnp.float32) + enter[
        :, :, None
    ] * jnp.einsum("the,hde->thd", gb.astype(jnp.float32), states[b], precision=HIGH)
    grads_k[b] = jnp.einsum("hts,thd->shd", grad_s, qb, preferred_element_type=jnp.float32) + leave[
        :, :, None
    ] * jnp.einsum("she,hde->shd", vb.astype(jnp.float32), later, precision=HIGH)
    grads_v[b] = jnp.einsum(
        "hts,the->she", kept_weights[b], gb, preferred_element_type=jnp.float32
    ) + leave[:, :, None] * jnp.einsum(
        "shd,hde->she", kb.astype(jnp.float32), later, precision=HIGH
    )
    grad_query = grads_q[0].reshape(rows, width)
    grad_key = grads_k[0].reshape(rows, width)
    grad_value = grads_v[0].reshape(rows, width)
    sig_query = jax.nn.sigmoid(pre_query)
    sig_key = jax.nn.sigmoid(pre_key)
    slope_query = sig_query * (1.0 + pre_query * (1.0 - sig_query))
    slope_key = sig_key * (1.0 + pre_key * (1.0 - sig_key))
    grad_pre = jnp.concatenate(
        [grad_query * slope_query, grad_key * slope_key, grad_value, grad_gate], axis=1
    ).astype(jnp.bfloat16)
    grad_norm1 = jnp.dot(grad_pre, w_in.T, preferred_element_type=jnp.float32)
    input_grad = grad_mid + srms_back(xf, grad_norm1)
    grad_win = jnp.dot(norm1.T, grad_pre, preferred_element_type=jnp.float32)
    grad_wout = jnp.dot(mixed.T, grad_branch, preferred_element_type=jnp.float32)
    sum_in, sum_out = (
        lax.psum_scatter(grad_win, ("wide", "narrow"), scatter_dimension=0, tiled=True),
        lax.psum_scatter(grad_wout, ("wide", "narrow"), scatter_dimension=0, tiled=True),
    )
    sum_pair, sum_third = (
        lax.psum_scatter(
            grad_pair.astype(jnp.bfloat16), "wide", scatter_dimension=1, tiled=True
        ).astype(jnp.float32),
        lax.psum_scatter(
            grad_third.astype(jnp.bfloat16), "wide", scatter_dimension=1, tiled=True
        ).astype(jnp.float32),
    )
    m_in, w_in_new, a_in = renew(attn_in, mom_attn_in, avg_attn_in, sum_in, width, tokens)
    m_out, w_out_new, a_out = renew(attn_out, mom_attn_out, avg_attn_out, sum_out, width, tokens)
    m_pair, w_pair_new, a_pair = renew(sglu_in, mom_sglu_in, avg_sglu_in, sum_pair, width, tokens)
    m_third, w_third_new, a_third = renew(
        sglu_out, mom_sglu_out, avg_sglu_out, sum_third, FF, tokens
    )
    return (
        output,
        input_grad,
        m_in,
        m_out,
        m_pair,
        m_third,
        w_in_new,
        w_out_new,
        w_pair_new,
        w_third_new,
        a_in,
        a_out,
        a_pair,
        a_third,
    )


def solution(mesh):
    placed = (
        P(("wide", "narrow"), None),
        P(("wide", "narrow"), None),
        P(),
        P(),
        P(("wide", "narrow"), None),
        P(("wide", "narrow"), None),
        P(None, "wide", "narrow"),
        P("narrow", "wide"),
        P(("wide", "narrow"), None),
        P(("wide", "narrow"), None),
        P(None, "wide", "narrow"),
        P("narrow", "wide"),
        P(("wide", "narrow"), None),
        P(("wide", "narrow"), None),
        P(None, "wide", "narrow"),
        P("narrow", "wide"),
    )
    return jax.shard_map(
        per_device,
        mesh=mesh,
        in_specs=placed,
        out_specs=(
            P(("wide", "narrow"), None),
            P(("wide", "narrow"), None),
            P(("wide", "narrow"), None),
            P(("wide", "narrow"), None),
            P(None, "wide", "narrow"),
            P("narrow", "wide"),
            P(("wide", "narrow"), None),
            P(("wide", "narrow"), None),
            P(None, "wide", "narrow"),
            P("narrow", "wide"),
            P(("wide", "narrow"), None),
            P(("wide", "narrow"), None),
            P(None, "wide", "narrow"),
            P("narrow", "wide"),
        ),
        check_vma=False,
    )
```

profile of v0, /device:TPU:0, one launch (start us, length us, event | category | flops | bytes accessed | tf_op | source)
XLA Modules:
  0.0 2342.3 jit_solution(16107673629416900517)
XLA Ops:
  15.2 193.8 %all-gather.13.cloned.1.call-done = bf16[2048,8192]{1,0:T(8,128)(2,1)} async-done(((bf16[64,8192]{1,0:T(8,128)(2,1)}), bf16[2048,8192]{1,0:T(8,128)(2,1)}) %all-gather.13.cloned.1.call-update) | async-done | bytes 33554448 | tf_op jit(solution)/shard_map/all_gather | solution.py:124
  209.0 17.1 fusion.58
  240.0 40.2 %all-reduce = f32[512]{0:T(512)S(1)} all-reduce(f32[512]{0:T(512)S(1)} %dynamic-update-slice), channel_id=2, replica_groups=mesh['wide'=8,'narrow'=4] {'wide','narrow'}, use_global_device_ids=true, to_apply=%add | all-reduce | flops 512 | bytes 4096
  288.5 143.4 %all-gather.25.cloned.1.call-done = f32[512,128,128]{2,1,0:T(8,128)} async-done(((f32[16,128,128]{2,1,0:T(8,128)}), f32[512,128,128]{2,1,0:T(8,128)}) %all-gather.25.cloned.1.call-update) | async-done | bytes 33554448 | tf_op jit(solution)/shard_map/all_gather | solution.py:20
  442.7 68.2 %all-gather.15.cloned.1.call-done = bf16[2048,2048]{1,0:T(8,128)(2,1)} async-done(((bf16[64,2048]{1,0:T(8,128)(2,1)}), bf16[2048,2048]{1,0:T(8,128)(2,1)}) %all-gather.15.cloned.1.call-update) | async-done | bytes 8388624 | tf_op jit(solution)/shard_map/all_gather | solution.py:125
  522.9 152.8 %all-gather.19.cloned.1.call-done = bf16[2,2048,1408]{2,1,0:T(8,128)(2,1)} async-done(((bf16[2,256,1408]{2,1,0:T(8,128)(2,1)}), bf16[2,2048,1408]{2,1,0:T(8,128)(2,1)}) %all-gather.19.cloned.1.call-update) | async-done | bytes 11534352 | tf_op jit(solution)/shard_map/all_gather | solution.py:128
  675.8 34.7 %all-gather.17.cloned.1.call-done = bf16[1024,2048]{1,0:T(8,128)(2,1)} async-done(((bf16[256,2048]{1,0:T(8,128)(2,1)}), bf16[1024,2048]{1,0:T(8,128)(2,1)}) %all-gather.17.cloned.1.call-update) | async-done | bytes 4194320 | tf_op jit(solution)/shard_map/all_gather | solution.py:179
  710.5 12.1 fusion.4
  731.0 15.4 all-gather.23.cloned.1.call-done
  746.4 96.2 %all-gather.21.cloned.1.call-done = bf16[1408,2048]{1,0:T(8,128)(2,1)} async-done(((bf16[1408,256]{1,0:T(8,128)(2,1)}), bf16[1408,2048]{1,0:T(8,128)(2,1)}) %all-gather.21.cloned.1.call-update) | async-done | bytes 5767184 | tf_op jit(solution)/shard_map/all_gather | solution.py:129
  842.6 15.0 multiply_convert_fusion
  878.1 10.9 convolution_convert_fusion.3
  889.1 58.8 %reduce-scatter.9.cloned.1.call-done = f32[256,2048]{1,0:T(8,128)} async-done(((f32[1024,2048]{1,0:T(8,128)}), f32[256,2048]{1,0:T(8,128)}) %reduce-scatter.9.cloned.1.call-update) | async-done | bytes 2097168 | tf_op jit(solution)/shard_map/reduce_scatter | solution.py:203
  950.5 44.7 %reduce-scatter.7.cloned.1.call-done = bf16[256,2048]{1,0:T(8,128)(2,1)} async-done(((bf16[1024,2048]{1,0:T(8,128)(2,1)}), bf16[256,2048]{1,0:T(8,128)(2,1)}) %reduce-scatter.7.cloned.1.call-update) | async-done | bytes 1048592 | tf_op jit(solution)/shard_map/reduce_scatter | solution.py:183
  1014.9 10.5 convolution_convert_fusion
  1058.3 43.5 %all-reduce.1 = bf16[512]{0:T(512)(128)(2,1)S(1)} all-reduce(bf16[512]{0:T(512)(128)(2,1)S(1)} %dynamic-update-slice.1), channel_id=4, replica_groups=mesh['wide'=8,'narrow'=4] {'wide','narrow'}, use_global_device_ids=true, to_apply=%add.1 | all-reduce | flops 512 | bytes 2048
  1118.9 11.7 all-gather.27.cloned.1.call-done
  1130.5 43.2 %while.29 = (s32[]{:T(128)}, f32[16,128,128]{2,1,0:T(8,128)S(1)}, s32[]{:T(128)}, bf16[32,16]{1,0:T(8,128)(2,1)S(1)}, bf16[32,16,128,128]{3,2,1,0:T(8,128)(2,1)}...) while((s32[]{:T(128)}, f32[16,128,128]{2,1,0:T(8,128)S(1)}, s32[]{:T(128)}, ...), condition=%wide.region_12.13_spmd.clone, body=%wide.region_11.12_spmd.clone.sunk | while | flops 1310744 | bytes 2621775 | solution.py:48
  1194.1 26.3 %fusion.47 = f32[2048,8192]{1,0:T(8,128)} fusion(bf16[256,2048]{1,0:T(8,128)(2,1)} %get-tuple-element.252, bf16[256,2048]{1,0:T(8,128)(2,1)} %copy.124, bf16[256,2048]{1,0:T(8,128)(2,1)} %get-tuple-element.245, bf16[256,2048]{1,0:T(8,128)(2,1)} %get-tuple-element.244, bf16[256,2048]{1,0:T(8,128)(2,1)S(1)} %copy-done.11, f32[256]{0:T(256)S(1)} %copy-done.22), kind=kOutput, calls=%fused_computation.100 | convolution fusion | flops 8608284672 | bytes 72352768 | tf_op jit(solution)/shard_map/dot_general | solution.py:260
  1220.4 22.3 reduce-scatter.17.cloned.1.call-done
  1247.7 191.1 %reduce-scatter.15.cloned.1.call-done = bf16[2,256,1408]{2,1,0:T(8,128)(2,1)} async-done(((bf16[2,2048,1408]{2,1,0:T(8,128)(2,1)}), bf16[2,256,1408]{2,1,0:T(8,128)(2,1)}) %reduce-scatter.15.cloned.1.call-update) | async-done | bytes 1441808 | tf_op jit(solution)/shard_map/reduce_scatter | solution.py:267
  1446.9 17.9 fusion.15
  1468.3 154.8 %reduce-scatter.13.cloned.1.call-done = f32[64,2048]{1,0:T(8,128)} async-done(((f32[2048,2048]{1,0:T(8,128)}), f32[64,2048]{1,0:T(8,128)}) %reduce-scatter.13.cloned.1.call-update) | async-done | bytes 524304 | tf_op jit(solution)/shard_map/reduce_scatter | solution.py:264
  1625.9 703.5 %reduce-scatter.11.cloned.1.call-done = f32[64,8192]{1,0:T(8,128)} async-done(((f32[2048,8192]{1,0:T(8,128)}), f32[64,8192]{1,0:T(8,128)}) %reduce-scatter.11.cloned.1.call-update) | async-done | bytes 2097168 | tf_op jit(solution)/shard_map/reduce_scatter | solution.py:263
  (254 shorter events, 240.1 us)
Async XLA Ops:
  7.2 201.8 %all-gather.13.cloned.1.call-start = ((), (), s32[]{:S(2)}) async-start(), calls=%async_computation.6 | async-start | bytes 34603008 | tf_op jit(solution)/shard_map/all_gather | solution.py:124
  10.0 421.8 %all-gather.25.cloned.1.call-start = ((), (), s32[]{:S(2)}) async-start(), calls=%async_computation.18 | async-start | bytes 34603008 | tf_op jit(solution)/shard_map/all_gather | solution.py:20
  13.1 213.0 %copy-start.29 = (f32[256]{0:T(256)}, f32[256]{0:T(256)S(1)}, u32[]{:S(2)}) copy-start(f32[256]{0:T(256)S(1)} %fusion.13) | copy-start | bytes 3076
  13.7 268.4 %copy-start.31 = (f32[16]{0:T(128)}, f32[16]{0:T(128)S(1)}, u32[]{:S(2)}) copy-start(f32[16]{0:T(128)S(1)} %get-tuple-element.261) | copy-start | bytes 196
  13.7 212.4 %copy-start.21 = (f32[256]{0:T(256)}, f32[256]{0:T(256)S(1)}, u32[]{:S(2)}) copy-start(f32[256]{0:T(256)S(1)} %fusion.61) | copy-start | bytes 3076
  15.2 218.0 %copy-start.23 = (f32[256,16]{0,1:T(8,128)}, f32[256,16]{0,1:T(8,128)S(1)}, u32[]{:S(2)}) copy-start(f32[256,16]{0,1:T(8,128)S(1)} %get-tuple-element.260) | copy-start | bytes 49156
  237.5 273.4 %all-gather.15.cloned.1.call-start = ((), (), s32[]{:S(2)}) async-start(), calls=%async_computation.7 | async-start | bytes 8650752 | tf_op jit(solution)/shard_map/all_gather | solution.py:125
  238.3 437.5 %all-gather.19.cloned.1.call-start = ((), (), s32[]{:S(2)}) async-start(), calls=%async_computation.9 | async-start | bytes 12976128 | tf_op jit(solution)/shard_map/all_gather | solution.py:128
  239.7 470.8 %all-gather.17.cloned.1.call-start = ((), (), s32[]{:S(2)}) async-start(), calls=%async_computation.8 | async-start | bytes 5242880 | tf_op jit(solution)/shard_map/all_gather | solution.py:179
  282.1 730.7 %copy-start.5 = (bf16[256,2048]{0,1:T(8,128)(2,1)}, bf16[256,2048]{0,1:T(8,128)(2,1)S(1)}, u32[]{:S(2)}) copy-start(bf16[256,2048]{0,1:T(8,128)(2,1)S(1)} %copy.125) | copy-start | bytes 3145732
  519.8 226.6 %all-gather.23.cloned.1.call-start = ((), (), s32[]{:S(2)}) async-start(), calls=%async_computation.12 | async-start | bytes 5242880 | tf_op jit(solution)/shard_map/all_gather | solution.py:189
  520.3 322.3 %all-gather.21.cloned.1.call-start = ((), (), s32[]{:S(2)}) async-start(), calls=%async_computation.10 | async-start | bytes 6488064 | tf_op jit(solution)/shard_map/all_gather | solution.py:129
  522.9 425.1 %reduce-scatter.9.cloned.1.call-start = ((), (), s32[]{:S(2)}) async-start(), calls=%async_computation.13 | async-start | bytes 10485760 | tf_op jit(solution)/shard_map/reduce_scatter | solution.py:203
  877.9 117.3 %reduce-scatter.7.cloned.1.call-start = ((), (), s32[]{:S(2)}) async-start(), calls=%async_computation.11 | async-start | bytes 5242880 | tf_op jit(solution)/shard_map/reduce_scatter | solution.py:183
  889.1 241.5 %all-gather.27.cloned.1.call-start = ((), (), s32[]{:S(2)}) async-start(), calls=%async_computation.19 | async-start | bytes 17301504 | tf_op jit(solution)/shard_map/all_gather | solution.py:34
  1014.8 228.0 %reduce-scatter.17.cloned.1.call-start = ((), (), s32[]{:S(2)}) async-start(), calls=%async_computation.17 | async-start | bytes 6488064 | tf_op jit(solution)/shard_map/reduce_scatter | solution.py:270
  1025.4 413.4 %reduce-scatter.15.cloned.1.call-start = ((), (), s32[]{:S(2)}) async-start(), calls=%async_computation.16 | async-start | bytes 12976128 | tf_op jit(solution)/shard_map/reduce_scatter | solution.py:267
  1047.5 575.6 %reduce-scatter.13.cloned.1.call-start = ((), (), s32[]{:S(2)}) async-start(), calls=%async_computation.15 | async-start | bytes 17301504 | tf_op jit(solution)/shard_map/reduce_scatter | solution.py:264
  1057.5 44.4 %copy-start.26 = (f32[256,256]{1,0:T(8,128)S(1)}, f32[256,256]{1,0:T(8,128)}, u32[]{:S(2)}) copy-start(f32[256,256]{1,0:T(8,128)} %copy-done.25) | copy-start | bytes 786436
  1057.5 44.4 %copy-start.28 = (pred[256,256]{1,0:T(8,128)(4,1)S(1)}, pred[256,256]{1,0:T(8,128)(4,1)}, u32[]{:S(2)}) copy-start(pred[256,256]{1,0:T(8,128)(4,1)} %copy-done.27) | copy-start | bytes 196612
  1057.5 44.4 %copy-start.32 = (f32[16]{0:T(128)S(1)}, f32[16]{0:T(128)}, u32[]{:S(2)}) copy-start(f32[16]{0:T(128)} %copy-done.31) | copy-start | bytes 196
  1057.5 1271.9 %reduce-scatter.11.cloned.1.call-start = ((), (), s32[]{:S(2)}) async-start(), calls=%async_computation.14 | async-start | bytes 69206016 | tf_op jit(solution)/shard_map/reduce_scatter | solution.py:263
  1130.5 43.2 %copy-start.24 = (f32[256,16]{0,1:T(8,128)S(1)}, f32[256,16]{0,1:T(8,128)}, u32[]{:S(2)}) copy-start(f32[256,16]{0,1:T(8,128)} %copy-done.23) | copy-start | bytes 49156
  1468.3 861.1 %copy-start.15 = (f32[64,8192]{1,0:T(8,128)S(1)}, f32[64,8192]{1,0:T(8,128)}, u32[]{:S(2)}) copy-start(f32[64,8192]{1,0:T(8,128)} %param.24) | copy-start | bytes 6291460
  (33 other events, 256.0 us)
Sparse Core Ops, SparseCore 0:
  11.5 197.4 all-gather.12
  237.6 194.1 all-gather.24
  435.3 75.5 all-gather.14
  513.5 162.2 all-gather.18
  677.8 32.6 all-gather.16
  711.9 34.4 all-gather.22
  749.0 93.5 all-gather.20
  878.0 69.8 reduce-scatter.8
  950.6 44.5 reduce-scatter.6
  1015.0 115.5 all-gather.26
  1134.2 108.5 reduce-scatter.16
  1246.2 192.4 reduce-scatter.14
  1441.0 182.0 reduce-scatter.12
  1625.3 704.0 reduce-scatter.10
where the time goes:
time: 2360 us; the launch traced here: 2340 us
  waiting for transfers between devices  1890 us (80%)
  matrix products  215 us (9%)
  other arithmetic  109 us (5%)
  blocking collectives  83.6 us (4%)
  local copies, waits for them, and re-layouts  24.3 us (1%)
    reduce_scatter x1, waiting for transfers between devices, per_device(): lax.psum_scatter(grad_win, ('wide', 'narrow'), scatter_dimension=0, tiled...  704 us
    all_gather x1, waiting for transfers between devices, per_device(): lax.all_gather(attn_in.astype(jnp.bfloat16), ('wide', 'narrow'), axis=0,...  194 us
    reduce_scatter x1, waiting for transfers between devices, per_device(): lax.psum_scatter(grad_pair.astype(jnp.bfloat16), 'wide', scatter_dimensio...  191 us
    reduce_scatter x1, waiting for transfers between devices, per_device(): lax.psum_scatter(grad_wout, ('wide', 'narrow'), scatter_dimension=0, tile...  155 us
    all_gather x1, waiting for transfers between devices, per_device(): lax.all_gather(sglu_in.astype(jnp.bfloat16), 'wide', axis=1, tiled=True)  153 us
    all_gather x1, waiting for transfers between devices, prefix(): gathered = jax.tree.map(lambda a: lax.all_gather(a, axis), part)  143 us
    all_gather x1, waiting for transfers between devices, per_device(): lax.all_gather(sglu_out.astype(jnp.bfloat16), 'wide', axis=1, tiled=True)  96.2 us
    unnamed x2, blocking collectives  83.6 us
  transfers between devices with their start and end apart: 14, of which 14 were waited for; matrix products, arithmetic and copies ran while one was open for 11% of the time, Pallas kernels for 0%

commit v1 on v0

v1 whole, which is shorter than its diff:
```python
import math

import jax
import jax.numpy as jnp
from jax import lax
from jax.sharding import Mesh
from jax.sharding import PartitionSpec as P

BLOCK = 256
EPS = 1e-06
MU = 0.9
BETA = 0.8
HIGH = lax.Precision.HIGHEST
BF = jnp.bfloat16
F32 = jnp.float32
SWAP = [(0, 1), (1, 0)]
XORS = (0, 2, 4, 6, 1, 3, 5, 7)


def dot(a, b, dims=((1,), (0,))):
    return lax.dot_general(a, b, (dims, ((), ())), preferred_element_type=F32)


def inverse_rms(v):
    return lax.rsqrt(jnp.mean(v * v, axis=-1, keepdims=True) + EPS)


def srms_back(v, grad):
    r = inverse_rms(v)
    return r * grad - v * (r * r * r) * jnp.mean(grad * v, axis=-1, keepdims=True)


def renew(weight, moment, average, grad, fan, tokens):
    step = 0.4 / math.sqrt(fan * tokens)
    moment_new = MU * moment + grad
    weight_new = weight - step * (grad + MU * moment_new)
    average_new = BETA * average + (1.0 - BETA) * weight_new
    return (moment_new, weight_new, average_new)


class Square:
    def __init__(self):
        self.tp = ("y", "x", "c")
        self.fs = ("z",)
        self.size = 8
        self.groups = 4

    def begin(self):
        self.z = lax.axis_index("z")
        self.y = lax.axis_index("y")
        self.c = lax.axis_index("c")
        self.p = lax.axis_index(self.tp)
        self.q = self.p // 2
        self.group = self.z
        self.slot_ids = self.p ^ jnp.array(XORS, jnp.int32)
        self.head_ids = 8 * self.c + 4 * jnp.arange(2) + self.q

    def turn(self, v):
        wide = v.shape[1] // 4
        return jnp.concatenate(
            [
                lax.dynamic_slice_in_dim(v, ((self.z - k) % 4) * wide, wide, axis=1)
                for k in range(4)
            ],
            axis=1,
        )

    def rows_all(self, a):
        half = a.shape[0] // 2
        ax = lax.ppermute(a, "x", SWAP)
        ay = lax.ppermute(a, "y", SWAP)
        d0 = lax.ppermute(ay[:half], "x", SWAP)
        d1 = lax.ppermute(ax[half:], "y", SWAP)
        chip = [a, ax, ay, jnp.concatenate([d0, d1])]
        other = [lax.ppermute(v, "c", SWAP) for v in chip]
        return jnp.concatenate(chip + other)

    def rows_sum(self, part, kind=BF):
        rows = part.shape[0] // 8
        half = rows // 2
        keep, give = part[: 4 * rows], part[4 * rows :]
        got = lax.ppermute(give.astype(kind), "c", SWAP)
        total = keep.astype(F32) + got.astype(F32)
        s0, s2, s4, s6 = [total[i * rows : (i + 1) * rows] for i in range(4)]
        s6 = s6.astype(kind)
        u = lax.ppermute(s6[:half], "x", SWAP)
        v = lax.ppermute(s6[half:], "y", SWAP)
        s4 = jnp.concatenate([s4[:half] + u.astype(F32), s4[half:]]).astype(kind)
        s2 = jnp.concatenate([s2[:half], s2[half:] + v.astype(F32)]).astype(kind)
        return (
            s0
            + lax.ppermute(s2, "x", SWAP).astype(F32)
            + lax.ppermute(s4, "y", SWAP).astype(F32)
        )

    def planes_all(self, a):
        up = lambda v, s: lax.ppermute(v, "z", [(i, i + 1) for i in range(s, 3)])
        down = lambda v, s: lax.ppermute(v, "z", [(3 - i, 2 - i) for i in range(s, 3)])
        up1, down1 = up(a, 0), down(a, 0)
        up2, down2 = up(up1, 1), down(down1, 1)
        up3, down3 = up(up2, 2), down(down2, 2)
        return [
            a,
            jnp.where(self.z >= 1, up1, down3),
            jnp.where(self.z >= 2, up2, down2),
            jnp.where(self.z >= 3, up3, down1),
        ]

    def planes_sum(self, g):
        up = lambda v, s: lax.ppermute(v.astype(BF), "z", [(i, i + 1) for i in range(s)])
        down = lambda v, s: lax.ppermute(v.astype(BF), "z", [(3 - i, 2 - i) for i in range(s)])
        f = lambda v: v.astype(F32)
        u, d = up(g[1], 1), down(g[3], 1)
        u, d = up(f(g[2]) + f(u), 2), down(f(g[2]) + f(d), 2)
        u, d = up(f(g[3]) + f(u), 3), down(f(g[1]) + f(d), 3)
        return f(g[0]) + f(u) + f(d)

    def by_plane(self, slots):
        stack = jnp.stack(slots)
        return jnp.take(stack, (self.z - jnp.arange(4)) % 4, axis=0)

    def attn_in(self, w):
        rows = w.shape[0]
        view = w.reshape(rows, 4, 2, 2, 4, 128).transpose(4, 2, 0, 1, 3, 5)
        mine = lax.all_to_all(view.reshape(8, rows, 1024), self.tp, 0, 0, tiled=True)
        return jnp.concatenate(self.planes_all(mine.reshape(8 * rows, 1024)))

    def attn_in_back(self, g):
        rows = g.shape[0] // 4
        total = self.planes_sum([g[k * rows : (k + 1) * rows] for k in range(4)])
        view = total.astype(BF).reshape(8, rows // 8, 1024)
        mine = lax.all_to_all(view, self.tp, 0, 0, tiled=True)
        mine = mine.reshape(4, 2, rows // 8, 4, 2, 128).transpose(2, 3, 1, 4, 0, 5)
        return mine.reshape(rows // 8, 8192).astype(F32)

    def attn_out(self, w):
        planes = self.by_plane(self.planes_all(w))
        mine = lax.dynamic_slice_in_dim(planes, 2 * self.c, 2)
        give = lax.dynamic_slice_in_dim(planes, 2 * (1 - self.c), 2)
        got = lax.ppermute(give, "c", SWAP)
        first = self.c == 0
        pair = jnp.stack([jnp.where(first, mine, got), jnp.where(first, got, mine)], axis=1)
        return pair.reshape(4 * w.shape[0], w.shape[1])

    def attn_out_back(self, g):
        rows = g.shape[0] // 4
        halves = g.astype(BF).reshape(2, 2, rows, g.shape[1])
        first = self.c == 0
        keep = jnp.where(first, halves[:, 0], halves[:, 1])
        give = jnp.where(first, halves[:, 1], halves[:, 0])
        got = lax.ppermute(give, "c", SWAP)
        planes = jnp.concatenate([jnp.where(first, keep, got), jnp.where(first, got, keep)])
        slots = self.by_plane([planes[k] for k in range(4)])
        return self.planes_sum([slots[k] for k in range(4)])

    def sglu(self, pair, third):
        n = pair.shape[2] // 2
        first = self.y == 0

        def join(a, axis, cut):
            mine = jnp.where(first, cut(a, 0), cut(a, 1))
            give = jnp.where(first, cut(a, 1), cut(a, 0))
            got = lax.ppermute(give, "y", SWAP)
            return jnp.concatenate(
                [jnp.where(first, mine, got), jnp.where(first, got, mine)], axis=axis
            )

        both = join(pair, 1, lambda a, i: a[:, :, i * n : (i + 1) * n])
        back = join(third, 1, lambda a, i: a[i * n : (i + 1) * n])
        return both, back

    def sglu_all(self, both, back):
        return (
            jnp.concatenate(self.planes_all(both), axis=1),
            jnp.concatenate(self.planes_all(back), axis=1),
        )

    def pair_back(self, g):
        n = g.shape[1] // 4
        total = self.planes_sum([g[:, k * n : (k + 1) * n] for k in range(4)]).astype(BF)
        first = self.y == 0
        a, b = total[:, : n // 2], total[:, n // 2 :]
        mine, give = jnp.where(first, a, b), jnp.where(first, b, a)
        got = lax.ppermute(give, "y", SWAP)
        return jnp.concatenate(
            [jnp.where(first, mine, got), jnp.where(first, got, mine)], axis=2
        ).astype(F32)

    def third_back(self, g):
        n = g.shape[1] // 4
        total = self.planes_sum([g[:, k * n : (k + 1) * n] for k in range(4)]).astype(BF)
        first = self.y == 0
        a, b = total[:, : n // 2], total[:, n // 2 :]
        mine, give = jnp.where(first, a, b), jnp.where(first, b, a)
        got = lax.ppermute(give, "y", SWAP)
        return jnp.concatenate(
            [jnp.where(first, mine, got), jnp.where(first, got, mine)], axis=0
        ).astype(F32)


class Plain:
    def __init__(self, wide, narrow):
        self.tp = ("narrow",)
        self.fs = ("wide",)
        self.size = narrow
        self.groups = wide

    def begin(self):
        self.p = lax.axis_index("narrow")
        self.group = lax.axis_index("wide")
        self.slot_ids = jnp.arange(self.size, dtype=jnp.int32)

    def turn(self, v):
        return v

    def rows_all(self, a):
        return lax.all_gather(a, "narrow", axis=0, tiled=True)

    def rows_sum(self, part, kind=BF):
        return lax.psum_scatter(
            part.astype(kind), "narrow", scatter_dimension=0, tiled=True
        ).astype(F32)

    def attn_in(self, w):
        rows, cols = w.shape
        each = cols // 4 // self.size
        view = w.reshape(rows, 4, self.size, each).transpose(2, 0, 1, 3)
        view = view.reshape(self.size, rows, 4 * each)
        mine = lax.all_to_all(view, "narrow", 0, 0, tiled=True)
        mine = mine.reshape(self.size * rows, 4 * each)
        return lax.all_gather(mine, "wide", axis=0, tiled=True)

    def attn_in_back(self, g):
        cols = g.shape[1]
        total = lax.psum_scatter(g.astype(BF), "wide", scatter_dimension=0, tiled=True)
        rows = total.shape[0] // self.size
        view = total.reshape(self.size, rows, cols)
        mine = lax.all_to_all(view, "narrow", 0, 0, tiled=True)
        mine = mine.reshape(self.size, rows, 4, cols // 4).transpose(1, 2, 0, 3)
        return mine.reshape(rows, cols * self.size).astype(F32)

    def attn_out(self, w):
        whole = lax.all_gather(w, ("wide", "narrow"), axis=0, tiled=True)
        each = whole.shape[0] // self.size
        return lax.dynamic_slice_in_dim(whole, self.p * each, each)

    def attn_out_back(self, g):
        each = g.shape[0]
        whole = jnp.zeros((each * self.size, g.shape[1]), BF)
        whole = lax.dynamic_update_slice_in_dim(whole, g.astype(BF), self.p * each, 0)
        return lax.psum_scatter(
            whole, ("wide", "narrow"), scatter_dimension=0, tiled=True
        ).astype(F32)

    def sglu(self, pair, third):
        return pair, third

    def sglu_all(self, both, back):
        return (
            lax.all_gather(both, "wide", axis=1, tiled=True),
            lax.all_gather(back, "wide", axis=1, tiled=True),
        )

    def pair_back(self, g):
        return lax.psum_scatter(g.astype(BF), "wide", scatter_dimension=1, tiled=True).astype(F32)

    third_back = pair_back


def per_device(
    plan,
    inputs,
    out_grad,
    seq_lengths,
    decay_rate,
    attn_in,
    attn_out,
    sglu_in,
    sglu_out,
    mom_attn_in,
    mom_attn_out,
    mom_sglu_in,
    mom_sglu_out,
    avg_attn_in,
    avg_attn_out,
    avg_sglu_in,
    avg_sglu_out,
):
    plan.begin()
    rows, width = inputs.shape
    heads = decay_rate.shape[0]
    hd = width // heads
    size = plan.size
    own = heads // size
    cols = own * hd
    group_rows = size * rows
    tokens = group_rows * plan.groups
    fan_third = sglu_out.shape[0] * lax.axis_size(plan.narrow)

    ends = jnp.cumsum(seq_lengths)

    def seg_at(place):
        mark = jnp.sum((place[..., None] >= ends).astype(jnp.int32), axis=-1)
        return jnp.where(place < 0, -1, mark)

    first_block = plan.group * size
    blocks = first_block + plan.slot_ids
    seg = seg_at(blocks[:, None] * rows + jnp.arange(rows, dtype=jnp.int32)[None, :])
    prev = seg_at(blocks * rows - 1)
    last = seg[:, rows - 1]
    head_ids = plan.head_ids if hasattr(plan, "head_ids") else own * plan.p + jnp.arange(own)
    rate = jnp.take(decay_rate, head_ids)

    w_out = plan.attn_out(attn_out.astype(BF))
    w_in = plan.attn_in(attn_in.astype(BF))
    both, back = plan.sglu(sglu_in.astype(BF), sglu_out.astype(BF))
    w_in, both, back = lax.optimization_barrier((w_in, both, back))
    w_pair, w_third = plan.sglu_all(both, back)

    xf = inputs.astype(F32)
    norm1 = plan.rows_all(plan.turn((xf * inverse_rms(xf)).astype(BF)))
    pre = dot(norm1, w_in)
    pre_query, pre_key = pre[:, :cols], pre[:, cols : 2 * cols]
    gate = pre[:, 3 * cols :]

    def split(v):
        return v.astype(BF).reshape(size, rows, own, hd).transpose(0, 2, 1, 3)

    query = split(jax.nn.silu(pre_query))
    key = split(jax.nn.silu(pre_key))
    value = split(pre[:, 2 * cols : 3 * cols])

    index = jnp.arange(rows).astype(F32)
    spread = index[:, None] - index[None, :]
    fade = jnp.exp(-rate[:, None, None] * jnp.maximum(spread, 0.0)[None])
    allowed = (spread >= 0)[None] & (seg[:, :, None] == seg[:, None, :])
    mask = jnp.where(allowed[:, None], fade[None], 0.0)
    enter = jnp.where(
        (seg == prev[:, None])[:, None], jnp.exp(-rate[:, None] * index[None])[None], 0.0
    )[..., None]
    leave = jnp.where(
        (seg == last[:, None])[:, None], jnp.exp(-rate[:, None] * (rows - index)[None])[None], 0.0
    )[..., None]

    def reach(gap, same):
        return jnp.where(
            same & (gap >= 0), jnp.exp(-rate[:, None, None] * (rows * jnp.maximum(gap, 0))), 0.0
        )

    inner = reach(
        (blocks[:, None] - blocks[None, :] - 1).astype(F32)[None],
        (prev[:, None] == last[None, :])[None],
    )
    border = seg_at((first_block + size) * rows - 1)
    out_reach = reach(
        (first_block + size - 1 - blocks).astype(F32)[None, None], (last == border)[None, None]
    )[:, 0]
    entry = seg_at(first_block * rows - 1)
    in_reach = reach((blocks - first_block).astype(F32)[None, None], (prev == entry)[None, None])[
        :, 0
    ]
    longest = tokens // 4
    hops = min(-(-longest // group_rows), plan.groups - 1)

    def hop_factor(j, ahead):
        if ahead:
            here, there = border, seg_at((first_block + j * size) * rows - 1)
        else:
            here, there = entry, seg_at((first_block - (j - 1) * size) * rows - 1)
        return jnp.where(here == there, jnp.exp(-rate * ((j - 1) * group_rows)), 0.0)

    def bring(total, ahead):
        n = plan.groups
        got = jnp.zeros_like(total)
        for j in range(1, hops + 1):
            pairs = [(i + j, i) if ahead else (i, i + j) for i in range(n - j)]
            part = lax.ppermute(total, plan.fs, pairs)
            got = got + hop_factor(j, ahead)[:, None, None] * part
        return got

    term = jnp.einsum(
        "bhtd,bhte->bhde", key.astype(F32) * leave, value.astype(F32), precision=HIGH
    )
    leaving = jnp.einsum("hb,bhde->hde", out_reach, term, precision=HIGH)
    entering = bring(leaving, False)
    state = jnp.einsum("hbc,chde->bhde", inner, term, precision=HIGH) + (
        in_reach.T[:, :, None, None] * entering[None]
    )
    scores = jnp.einsum("bhtd,bhsd->bhts", query, key, preferred_element_type=F32)
    weights = (scores * mask).astype(BF)
    attn = jnp.einsum("bhts,bhsd->bhtd", weights, value, preferred_element_type=F32) + jnp.einsum(
        "bhtd,bhde->bhte", query.astype(F32) * enter, state, precision=HIGH
    )
    attn = attn.transpose(0, 2, 1, 3).reshape(group_rows, cols)
    branch = plan.rows_sum(dot((attn * gate).astype(BF), w_out))
    square = plan.rows_sum(jnp.sum(attn * attn, axis=1), F32)
    r_attn = lax.rsqrt(square / width + EPS)[:, None]
    mid = xf + r_attn * branch
    r_mid = inverse_rms(mid)
    norm2 = plan.rows_all(plan.turn((mid * r_mid).astype(BF)))
    grad_rows = plan.rows_all(plan.turn(out_grad))

    first = dot(norm2, w_pair[0])
    second = dot(norm2, w_pair[1])
    product = (first * second).astype(BF)
    grad_prod = dot(grad_rows, w_third, ((1,), (1,)))
    grad_first = (grad_prod * second).astype(BF)
    grad_second = (grad_prod * first).astype(BF)
    grad_norm2 = plan.rows_sum(
        dot(grad_first, w_pair[0], ((1,), (1,))) + dot(grad_second, w_pair[1], ((1,), (1,)))
    )
    grad_third = dot(product, grad_rows, ((0,), (0,))).astype(BF)
    grad_pair = jnp.stack(
        [dot(norm2, grad_first, ((0,), (0,))), dot(norm2, grad_second, ((0,), (0,)))]
    ).astype(BF)
    sum_third = plan.third_back(grad_third)
    sum_pair = plan.pair_back(grad_pair)
    output = mid + plan.turn(plan.rows_sum(dot(product, w_third)))

    grad_mid = out_grad.astype(F32) + srms_back(mid, plan.turn(grad_norm2))
    grad_branch = grad_mid.astype(BF)
    inward = jnp.mean(grad_branch.astype(F32) * branch, axis=1, keepdims=True)
    grad_branch = plan.rows_all(grad_branch)
    scales = plan.rows_all(jnp.concatenate([r_attn, r_attn * r_attn * r_attn * inward], axis=1))
    r_rows, pull_rows = scales[:, :1], scales[:, 1:]
    grad_mixed = dot(grad_branch, w_out, ((1,), (1,)))
    normed = r_rows * attn
    mixed = (normed * gate).astype(BF)
    grad_wout = dot(mixed, grad_branch, ((0,), (0,)))
    grad_gate = grad_mixed * normed
    grad_attn = split(r_rows * (grad_mixed * gate) - attn * pull_rows)
    d_term = jnp.einsum(
        "bhtd,bhte->bhde", query.astype(F32) * enter, grad_attn.astype(F32), precision=HIGH
    )
    d_leaving = jnp.einsum("hb,bhde->hde", in_reach, d_term, precision=HIGH)
    d_entering = bring(d_leaving, True)
    later = jnp.einsum("hcb,chde->bhde", inner, d_term, precision=HIGH) + (
        out_reach.T[:, :, None, None] * d_entering[None]
    )
    grad_w = jnp.einsum("bhte,bhse->bhts", grad_attn, value, preferred_element_type=F32)
    grad_s = (grad_w * mask).astype(BF)
    grad_query = jnp.einsum(
        "bhts,bhsd->bhtd", grad_s, key, preferred_element_type=F32
    ) + enter * jnp.einsum("bhte,bhde->bhtd", grad_attn.astype(F32), state, precision=HIGH)
    grad_key = jnp.einsum(
        "bhts,bhtd->bhsd", grad_s, query, preferred_element_type=F32
    ) + leave * jnp.einsum("bhse,bhde->bhsd", value.astype(F32), later, precision=HIGH)
    grad_value = jnp.einsum(
        "bhts,bhte->bhse", weights, grad_attn, preferred_element_type=F32
    ) + leave * jnp.einsum("bhsd,bhde->bhse", key.astype(F32), later, precision=HIGH)

    def merge(v):
        return v.transpose(0, 2, 1, 3).reshape(group_rows, cols)

    sig_query = jax.nn.sigmoid(pre_query)
    sig_key = jax.nn.sigmoid(pre_key)
    slope_query = sig_query * (1.0 + pre_query * (1.0 - sig_query))
    slope_key = sig_key * (1.0 + pre_key * (1.0 - sig_key))
    grad_pre = jnp.concatenate(
        [
            merge(grad_query) * slope_query,
            merge(grad_key) * slope_key,
            merge(grad_value),
            grad_gate,
        ],
        axis=1,
    ).astype(BF)
    grad_win = dot(norm1, grad_pre, ((0,), (0,))).astype(BF)
    grad_norm1 = plan.turn(plan.rows_sum(dot(grad_pre, w_in, ((1,), (1,)))))
    sum_out = plan.attn_out_back(grad_wout)
    sum_in = plan.attn_in_back(grad_win)
    input_grad = grad_mid + srms_back(xf, grad_norm1)

    m_in, w_in_new, a_in = renew(attn_in, mom_attn_in, avg_attn_in, sum_in, width, tokens)
    m_out, w_out_new, a_out = renew(attn_out, mom_attn_out, avg_attn_out, sum_out, width, tokens)
    m_pair, w_pair_new, a_pair = renew(sglu_in, mom_sglu_in, avg_sglu_in, sum_pair, width, tokens)
    m_third, w_third_new, a_third = renew(
        sglu_out, mom_sglu_out, avg_sglu_out, sum_third, fan_third, tokens
    )
    return (
        output,
        input_grad,
        m_in,
        m_out,
        m_pair,
        m_third,
        w_in_new,
        w_out_new,
        w_pair_new,
        w_third_new,
        a_in,
        a_out,
        a_pair,
        a_third,
    )


def solution(mesh):
    wide, narrow = mesh.shape["wide"], mesh.shape["narrow"]
    if (wide, narrow) == (8, 4):
        mesh = Mesh(mesh.devices.reshape(4, 2, 2, 2), ("z", "y", "x", "c"))
        plan, w, n = Square(), ("z", "y"), ("x", "c")
    else:
        plan, w, n = Plain(wide, narrow), ("wide",), ("narrow",)
    plan.narrow = n
    by_rows = P(w + n, None)
    pair, third = P(None, w, n), P(n, w)
    weights = (by_rows, by_rows, pair, third)

    def run(*args):
        return per_device(plan, *args)

    return jax.shard_map(
        run,
        mesh=mesh,
        in_specs=(by_rows, by_rows, P(), P()) + weights * 3,
        out_specs=(by_rows, by_rows) + weights * 3,
        check_vma=False,
    )
```

time: 2360 us -> 1090 us (0.46)
  waiting for transfers between devices: 1890 us -> 420 us
  starting transfers between devices: 0.96 us -> 164 us
  local copies, waits for them, and re-layouts: 24.3 us -> 166 us
  blocking collectives: 83.6 us -> 0 us
  matrix products: 215 us -> 181 us
  other arithmetic: 109 us -> 141 us
    reduce_scatter x6 -> x0, waiting for transfers between devices: 1180 us -> none  [the longest x1 704 us: per_device(): lax.psum_scatter(grad_win, ('wide', 'narrow'), scatter_dimension=0, tiled...]
    all_gather x8 -> x0, waiting for transfers between devices: 716 us -> none  [the longest x1 194 us: per_device(): lax.all_gather(attn_in.astype(jnp.bfloat16), ('wide', 'narrow'), axis=0,...]
    ppermute x0 -> x121, waiting for transfers between devices: none -> 420 us  [the longest x12 122 us: planes_all(): lax.ppermute(v, 'z', [(3 - i, 2 - i) for i in range(s, 3)])]
    ppermute x0 -> x121, starting transfers between devices: none -> 156 us  [the longest x12 45.1 us: planes_sum(): lax.ppermute(v.astype(BF), 'z', [(i, i + 1) for i in range(s)])]
    unnamed x91 -> x341, local copies, waits for them, and re-layouts: 8.21 us -> 97.5 us
    unnamed x2 -> x0, blocking collectives: 83.6 us -> none
    another operation x3 -> x19, other arithmetic: 11.9 us -> 57.5 us
    slice x2 -> x24, local copies, waits for them, and re-layouts: 1.02 us -> 36.6 us  [the longest x4 17.5 us: rows_sum(): keep, give = (part[:4 * rows], part[4 * rows:])]
  transfers between devices with their start and end apart: 14 -> 123, of which waited for: 14 -> 40; matrix products, arithmetic and copies ran while one was open for 11% -> 35% of each run, Pallas kernels for 0% -> 0%
where the time goes in v1:
time: 1090 us; the launch traced here: 1080 us
  waiting for transfers between devices  420 us (39%)
  matrix products  181 us (17%)
  local copies, waits for them, and re-layouts  166 us (15%)
  starting transfers between devices  164 us (15%)
  other arithmetic  141 us (13%)
    dot_general x15, matrix products, dot(): return lax.dot_general(a, b, (dims, ((), ())), preferred_element_type=F32)  151 us
    ppermute x12, waiting for transfers between devices, planes_all(): lax.ppermute(v, 'z', [(3 - i, 2 - i) for i in range(s, 3)])  122 us
    unnamed x341, local copies, waits for them, and re-layouts  97.5 us
    ppermute x12, waiting for transfers between devices, planes_sum(): lax.ppermute(v.astype(BF), 'z', [(i, i + 1) for i in range(s)])  79.6 us
    another operation x10, other arithmetic  53.8 us
    ppermute x5, waiting for transfers between devices, rows_sum(): lax.ppermute(s2, 'x', SWAP).astype(F32)  52.1 us
    ppermute x12, starting transfers between devices, planes_sum(): lax.ppermute(v.astype(BF), 'z', [(i, i + 1) for i in range(s)])  45.1 us
    ppermute x12, waiting for transfers between devices, planes_all(): up = lambda v, s: lax.ppermute(v, 'z', [(i, i + 1) for i in range(s, 3)])  35.6 us
  transfers between devices with their start and end apart: 123, of which 40 were waited for; matrix products, arithmetic and copies ran while one was open for 35% of the time, Pallas kernels for 0%

profile of v1, /device:TPU:0, one launch (start us, length us, event | category | flops | bytes accessed | tf_op | source)
XLA Modules:
  0.0 1077.2 jit_solution(10463318958103521928)
XLA Ops:
  118.9 20.0 %collective-permute-done.10 = bf16[512,1024]{1,0:T(8,128)(2,1)S(1)} collective-permute-done((bf16[512,1024]{1,0:T(8,128)(2,1)S(1)}, bf16[512,1024]{1,0:T(8,128)(2,1)S(1)}, u32[]{:S(2)}, u32[]{:S(2)}) %collective-permute-start.10) | collective-permute-done | bytes 1048608 | tf_op jit(solution)/shard_map/ppermute | solution.py:98
  142.8 22.7 %collective-permute-done.11 = bf16[512,1024]{1,0:T(8,128)(2,1)S(1)} collective-permute-done((bf16[512,1024]{1,0:T(8,128)(2,1)S(1)}, bf16[512,1024]{1,0:T(8,128)(2,1)S(1)}, u32[]{:S(2)}, u32[]{:S(2)}) %collective-permute-start.11) | collective-permute-done | bytes 1048608 | tf_op jit(solution)/shard_map/ppermute | solution.py:98
  167.3 13.3 %fusion.142 = f32[2048,1024]{0,1:T(8,128)S(1)} fusion(bf16[2048,2048]{0,1:T(8,128)(2,1)} %constant_dynamic-update-slice_fusion, bf16[2048,1024]{1,0:T(8,128)(2,1)S(1)} %pad_maximum_fusion.1), kind=kOutput, calls=%fused_computation.446 | convolution fusion | flops 8589934592 | bytes 20971520 | tf_op jit(solution)/shard_map/dot_general | solution.py:21
  220.2 21.9 %collective-permute-done.60 = bf16[256,2048]{1,0:T(8,128)(2,1)S(1)} collective-permute-done((bf16[256,2048]{1,0:T(8,128)(2,1)}, bf16[256,2048]{1,0:T(8,128)(2,1)S(1)}, u32[]{:S(2)}, u32[]{:S(2)}) %collective-permute-start.60) | collective-permute-done | bytes 1048608 | tf_op jit(solution)/shard_map/ppermute | solution.py:71
  271.3 11.7 %fusion.132 = (bf16[1024,2048]{0,1:T(8,128)(2,1)}, f32[1024,2048]{0,1:T(8,128)}) fusion(bf16[1024,2048]{0,1:T(8,128)(2,1)} %collective-permute-done.29, f32[2048,2048]{0,1:T(8,128)} %copy-done.7), kind=kLoop, calls=%fused_computation.437 | loop fusion | flops 6291456 | bytes 25165824 | tf_op jit(solution)/shard_map/convert.43
  312.6 30.2 %collective-permute-done.48 = bf16[704,512]{1,0:T(8,128)(2,1)S(1)} collective-permute-done((bf16[704,512]{1,0:T(8,128)(2,1)}, bf16[704,512]{1,0:T(8,128)(2,1)S(1)}, u32[]{:S(2)}, u32[]{:S(2)}) %collective-permute-start.48) | collective-permute-done | bytes 720928 | tf_op jit(solution)/shard_map/ppermute | solution.py:97
  352.9 45.7 %collective-permute-done.51 = bf16[704,512]{1,0:T(8,128)(2,1)S(1)} collective-permute-done((bf16[704,512]{1,0:T(8,128)(2,1)S(1)}, bf16[704,512]{1,0:T(8,128)(2,1)S(1)}, u32[]{:S(2)}, u32[]{:S(2)}) %collective-permute-start.51) | collective-permute-done | bytes 720928 | tf_op jit(solution)/shard_map/ppermute | solution.py:98
  408.3 25.4 %collective-permute-done.45 = bf16[2,512,704]{1,2,0:T(8,128)(2,1)S(1)} collective-permute-done((bf16[2,512,704]{1,2,0:T(8,128)(2,1)S(1)}, bf16[2,512,704]{1,2,0:T(8,128)(2,1)S(1)}, u32[]{:S(2)}, u32[]{:S(2)}) %collective-permute-start.45) | collective-permute-done | bytes 1441824 | tf_op jit(solution)/shard_map/ppermute | solution.py:98
  468.6 13.2 %multiply_convert_fusion = (bf16[2048,704]{0,1:T(8,128)(2,1)}, bf16[2048,704]{0,1:T(8,128)(2,1)S(1)}, bf16[2048,704]{0,1:T(8,128)(2,1)}) fusion(f32[2048,704]{0,1:T(8,128)} %fusion.9, f32[2048,704]{0,1:T(8,128)S(1)} %fusion.10, bf16[2048,2048]{1,0:T(8,128)(2,1)} %constant_dynamic-update-slice_fusion.18, bf16[704,512]{1,0:T(8,128)(2,1)S(1)} %broadcast_select_fusion.8, ...), kind=kOutput, calls=%fused_computation.21 | convolution fusion | flops 5925765120 | bytes 31457280 | tf_op jit(solution)/shard_map/dot_general | solution.py:21
  526.8 11.6 %fusion.90 = f32[2048,2048]{0,1:T(8,128)} fusion(bf16[2048,704]{0,1:T(8,128)(2,1)S(1)} %copy-done.136, bf16[704,512]{1,0:T(8,128)(2,1)S(1)} %copy-done.87, bf16[704,512]{1,0:T(8,128)(2,1)S(1)} %copy-done.83, bf16[704,512]{1,0:T(8,128)(2,1)S(1)} %copy-done.85, bf16[704,512]{1,0:T(8,128)(2,1)} %pad_maximum_fusion.27), kind=kOutput, calls=%fused_computation.256 | convolution fusion | flops 5917114368 | bytes 22544384 | tf_op jit(solution)/shard_map/dot_general | solution.py:21
  544.6 26.5 %collective-permute-done.115 = bf16[704,512]{1,0:T(8,128)(2,1)S(1)} collective-permute-done((bf16[704,512]{1,0:T(8,128)(2,1)S(1)}, bf16[704,512]{1,0:T(8,128)(2,1)S(1)}, u32[]{:S(2)}, u32[]{:S(2)}) %collective-permute-start.115) | collective-permute-done | bytes 720928 | tf_op jit(solution)/shard_map/ppermute | solution.py:110
  579.3 15.0 %convolution_add_fusion = f32[2048,2048]{0,1:T(8,128)} fusion(f32[2048,2048]{0,1:T(8,128)} %fusion.8, bf16[2048,704]{0,1:T(8,128)(2,1)} %get-tuple-element.124, bf16[2,2048,704]{1,2,0:T(8,128)(2,1)} %copy-done.53), kind=kOutput, calls=%fused_computation.17 | convolution fusion | flops 5909774336 | bytes 39321600 | tf_op jit(solution)/shard_map/dot_general | solution.py:21
  620.8 16.3 %collective-permute-done.108 = bf16[2,512,704]{1,2,0:T(8,128)(2,1)S(1)} collective-permute-done((bf16[2,512,704]{1,2,0:T(8,128)(2,1)S(1)}, bf16[2,512,704]{1,2,0:T(8,128)(2,1)S(1)}, u32[]{:S(2)}, u32[]{:S(2)}) %collective-permute-start.108) | collective-permute-done | bytes 1441824 | tf_op jit(solution)/shard_map/ppermute | solution.py:110
  646.7 11.5 %fusion.131 = (bf16[1024,2048]{0,1:T(8,128)(2,1)}, f32[1024,2048]{0,1:T(8,128)}) fusion(bf16[1024,2048]{0,1:T(8,128)(2,1)} %collective-permute-done.54, f32[2048,2048]{0,1:T(8,128)} %fusion.90), kind=kLoop, calls=%fused_computation.436 | loop fusion | flops 6291456 | bytes 25165824 | tf_op jit(solution)/shard_map/convert.35
  663.0 11.5 %fusion.130 = (bf16[1024,2048]{0,1:T(8,128)(2,1)}, f32[1024,2048]{0,1:T(8,128)}) fusion(bf16[1024,2048]{0,1:T(8,128)(2,1)} %collective-permute-done.67, f32[2048,2048]{0,1:T(8,128)} %convolution_add_fusion), kind=kLoop, calls=%fused_computation.435 | loop fusion | flops 6291456 | bytes 25165824 | tf_op jit(solution)/shard_map/convert.27
  697.8 17.3 %collective-permute-done.56 = bf16[256,2048]{0,1:T(8,128)(2,1)S(1)} collective-permute-done((bf16[256,2048]{0,1:T(8,128)(2,1)S(1)}, bf16[256,2048]{0,1:T(8,128)(2,1)S(1)}, u32[]{:S(2)}, u32[]{:S(2)}) %collective-permute-start.56) | collective-permute-done | bytes 1048608 | tf_op jit(solution)/shard_map/ppermute | solution.py:92
  719.0 16.2 %collective-permute-done.69 = bf16[256,2048]{0,1:T(8,128)(2,1)S(1)} collective-permute-done((bf16[256,2048]{0,1:T(8,128)(2,1)S(1)}, bf16[256,2048]{0,1:T(8,128)(2,1)S(1)}, u32[]{:S(2)}, u32[]{:S(2)}) %collective-permute-start.69) | collective-permute-done | bytes 1048608 | tf_op jit(solution)/shard_map/ppermute | solution.py:92
  753.7 12.6 %collective-permute-done.73 = f32[256,2]{0,1:T(2,128)S(1)} collective-permute-done((f32[256,2]{0,1:T(2,128)S(1)}, f32[256,2]{0,1:T(2,128)S(1)}, u32[]{:S(2)}, u32[]{:S(2)}) %collective-permute-start.73) | collective-permute-done | bytes 2080 | tf_op jit(solution)/shard_map/ppermute | solution.py:71
  783.2 22.6 %collective-permute-done.112 = bf16[2,512,704]{1,2,0:T(8,128)(2,1)S(1)} collective-permute-done((bf16[2,512,704]{1,2,0:T(8,128)(2,1)S(1)}, bf16[2,512,704]{1,2,0:T(8,128)(2,1)S(1)}, u32[]{:S(2)}, u32[]{:S(2)}) %collective-permute-start.112) | collective-permute-done | bytes 1441824 | tf_op jit(solution)/shard_map/ppermute | solution.py:111
  875.1 10.9 %fusion.85 = f32[2048,2048]{0,1:T(8,128)S(1)} fusion(bf16[2048,1024]{1,0:T(8,128)(2,1)} %copy-done.60, bf16[2048,256]{0,1:T(8,128)(2,1)S(1)} %copy-done.132, bf16[2048,256]{0,1:T(8,128)(2,1)S(1)} %bitcast.294, bf16[2048,256]{0,1:T(8,128)(2,1)S(1)} %get-tuple-element.115, bf16[2048,256]{0,1:T(8,128)(2,1)S(1)} %get-tuple-element.114), kind=kOutput, calls=%fused_computation.234 | convolution fusion | flops 8606711808 | bytes 25165824 | tf_op jit(solution)/shard_map/dot_general | solution.py:21
  886.0 18.0 %convolution_convert_fusion = bf16[2048,1024]{1,0:T(8,128)(2,1)} fusion(bf16[2048,2048]{0,1:T(8,128)(2,1)} %constant_dynamic-update-slice_fusion, bf16[2048,256]{0,1:T(8,128)(2,1)S(1)} %copy-done.133, bf16[2048,256]{0,1:T(8,128)(2,1)} %bitcast.295, bf16[2048,256]{0,1:T(8,128)(2,1)} %copy-done.79, bf16[2048,256]{0,1:T(8,128)(2,1)S(1)} %get-tuple-element.114), kind=kOutput, calls=%fused_computation.33 | convolution fusion | flops 8608808960 | bytes 16777216 | tf_op jit(solution)/shard_map/dot_general | solution.py:21
  919.7 15.7 %collective-permute-done.94 = bf16[512,1024]{1,0:T(8,128)(2,1)S(1)} collective-permute-done((bf16[512,1024]{1,0:T(8,128)(2,1)}, bf16[512,1024]{1,0:T(8,128)(2,1)S(1)}, u32[]{:S(2)}, u32[]{:S(2)}) %collective-permute-start.94) | collective-permute-done | bytes 1048608 | tf_op jit(solution)/shard_map/ppermute | solution.py:110
  948.7 20.7 %collective-permute-done.102 = bf16[64,2048]{1,0:T(8,128)(2,1)S(1)} collective-permute-done((bf16[64,2048]{1,0:T(8,128)(2,1)S(1)}, bf16[64,2048]{1,0:T(8,128)(2,1)S(1)}, u32[]{:S(2)}, u32[]{:S(2)}) %collective-permute-start.102) | collective-permute-done | bytes 262176 | tf_op jit(solution)/shard_map/ppermute | solution.py:110
  1049.3 18.5 %collective-permute-done.91 = bf16[256,2048]{0,1:T(8,128)(2,1)S(1)} collective-permute-done((bf16[256,2048]{0,1:T(8,128)(2,1)S(1)}, bf16[256,2048]{0,1:T(8,128)(2,1)S(1)}, u32[]{:S(2)}, u32[]{:S(2)}) %collective-permute-start.91) | collective-permute-done | bytes 1048608 | tf_op jit(solution)/shard_map/ppermute | solution.py:92
  (787 shorter events, 622.5 us)
Async XLA Ops:
  5.5 76.2 %collective-permute-start = (bf16[256,2048]{0,1:T(8,128)(2,1)}, bf16[256,2048]{0,1:T(8,128)(2,1)}, u32[]{:S(2)}, u32[]{:S(2)}) collective-permute-start(bf16[256,2048]{0,1:T(8,128)(2,1)} %get-tuple-element.199), channel_id=1, source_target_pairs={{0,2},{2,0},{1,3},{3,1},{4,6},{6,4},{5,7},{7,5},{8,10},{10,8},{9,1... | collective-permute-start | bytes 3145736 | tf_op jit(solution)/shard_map/ppermute | solution.py:70
  8.5 70.9 %collective-permute-start.1 = (bf16[256,2048]{0,1:T(8,128)(2,1)}, bf16[256,2048]{0,1:T(8,128)(2,1)}, u32[]{:S(2)}, u32[]{:S(2)}) collective-permute-start(bf16[256,2048]{0,1:T(8,128)(2,1)} %get-tuple-element.199), channel_id=1, source_target_pairs={{0,4},{4,0},{1,5},{5,1},{2,6},{6,2},{3,7},{7,3},{8,12},{12,8},{9,1... | collective-permute-start | bytes 3145736 | tf_op jit(solution)/shard_map/ppermute | solution.py:71
  22.6 50.8 %all-to-all-start = ((bf16[8,64,1024]{2,1,0:T(8,128)(2,1)}), bf16[8,64,1024]{2,1,0:T(8,128)(2,1)}, u32[]{:S(2)}, u32[]{:S(2)}) async-start(bf16[8,64,1024]{2,1,0:T(8,128)(2,1)} %reshape.621), calls=%async_computation | async-start | bytes 2097152 | tf_op jit(solution)/shard_map/all_to_all | solution.py:125
  56.5 56.4 %collective-permute-start.4 = (bf16[256,2048]{0,1:T(8,128)(2,1)}, bf16[256,2048]{0,1:T(8,128)(2,1)}, u32[]{:S(2)}, u32[]{:S(2)}) collective-permute-start(bf16[256,2048]{0,1:T(8,128)(2,1)} %get-tuple-element.199), channel_id=1, source_target_pairs={{0,1},{1,0},{2,3},{3,2},{4,5},{5,4},{6,7},{7,6},{8,9},{9,8},{10,11... | collective-permute-start | bytes 3145736 | tf_op jit(solution)/shard_map/ppermute | solution.py:75
  213.1 56.7 %collective-permute-start.29 = (bf16[1024,2048]{0,1:T(8,128)(2,1)}, bf16[1024,2048]{0,1:T(8,128)(2,1)}, u32[]{:S(2)}, u32[]{:S(2)}) collective-permute-start(bf16[1024,2048]{0,1:T(8,128)(2,1)} %slice.728), channel_id=1, source_target_pairs={{0,1},{1,0},{2,3},{3,2},{4,5},{5,4},{6,7},{7,6},{8,9},{9,8},{10,11... | collective-permute-start | bytes 12582920 | tf_op jit(solution)/shard_map/ppermute | solution.py:82
  220.2 64.7 %collective-permute-start.63 = (bf16[256,2048]{1,0:T(8,128)(2,1)}, bf16[256,2048]{1,0:T(8,128)(2,1)}, u32[]{:S(2)}, u32[]{:S(2)}) collective-permute-start(bf16[256,2048]{1,0:T(8,128)(2,1)} %get-tuple-element.187), channel_id=1, source_target_pairs={{0,1},{1,0},{2,3},{3,2},{4,5},{5,4},{6,7},{7,6},{8,9},{9,8},{10,11... | collective-permute-start | bytes 3145736 | tf_op jit(solution)/shard_map/ppermute | solution.py:75
  289.3 56.0 %collective-permute-start.43 = (bf16[2,512,704]{1,2,0:T(8,128)(2,1)S(1)}, bf16[2,512,704]{1,2,0:T(8,128)(2,1)S(1)}, u32[]{:S(2)}, u32[]{:S(2)}) collective-permute-start(bf16[2,512,704]{1,2,0:T(8,128)(2,1)S(1)} %pad_maximum_fusion.7), channel_id=1, source_target_pairs={{24,16},{16,8},{8,0},{25,17},{17,9},{9,1},{26,18},{18,10},{10,2},{... | collective-permute-start | bytes 4325384 | tf_op jit(solution)/shard_map/ppermute | solution.py:98
  290.6 55.9 %collective-permute-start.42 = (bf16[2,512,704]{1,2,0:T(8,128)(2,1)S(1)}, bf16[2,512,704]{1,2,0:T(8,128)(2,1)S(1)}, u32[]{:S(2)}, u32[]{:S(2)}) collective-permute-start(bf16[2,512,704]{1,2,0:T(8,128)(2,1)S(1)} %pad_maximum_fusion.7), channel_id=1, source_target_pairs={{0,8},{8,16},{16,24},{1,9},{9,17},{17,25},{2,10},{10,18},{18,26},{... | collective-permute-start | bytes 4325384 | tf_op jit(solution)/shard_map/ppermute | solution.py:97
  300.0 42.9 %collective-permute-start.48 = (bf16[704,512]{1,0:T(8,128)(2,1)}, bf16[704,512]{1,0:T(8,128)(2,1)S(1)}, u32[]{:S(2)}, u32[]{:S(2)}) collective-permute-start(bf16[704,512]{1,0:T(8,128)(2,1)} %pad_maximum_fusion.27), channel_id=1, source_target_pairs={{0,8},{8,16},{16,24},{1,9},{9,17},{17,25},{2,10},{10,18},{18,26},{... | collective-permute-start | bytes 2162696 | tf_op jit(solution)/shard_map/ppermute | solution.py:97
  345.3 54.8 %collective-permute-start.44 = (bf16[2,512,704]{1,2,0:T(8,128)(2,1)S(1)}, bf16[2,512,704]{1,2,0:T(8,128)(2,1)S(1)}, u32[]{:S(2)}, u32[]{:S(2)}) collective-permute-start(bf16[2,512,704]{1,2,0:T(8,128)(2,1)S(1)} %collective-permute-done.43), channel_id=1, source_target_pairs={{16,8},{8,0},{17,9},{9,1},{18,10},{10,2},{19,11},{11,3},{20,12},{1... | collective-permute-start | bytes 4325384 | tf_op jit(solution)/shard_map/ppermute | solution.py:98
  346.6 52.8 %collective-permute-start.46 = (bf16[2,512,704]{1,2,0:T(8,128)(2,1)S(1)}, bf16[2,512,704]{1,2,0:T(8,128)(2,1)S(1)}, u32[]{:S(2)}, u32[]{:S(2)}) collective-permute-start(bf16[2,512,704]{1,2,0:T(8,128)(2,1)S(1)} %collective-permute-done.42), channel_id=1, source_target_pairs={{8,16},{16,24},{9,17},{17,25},{10,18},{18,26},{11,19},{19,27},{12,... | collective-permute-start | bytes 4325384 | tf_op jit(solution)/shard_map/ppermute | solution.py:97
  347.5 54.0 %collective-permute-start.31 = (bf16[256,2048]{0,1:T(8,128)(2,1)S(1)}, bf16[256,2048]{0,1:T(8,128)(2,1)S(1)}, u32[]{:S(2)}, u32[]{:S(2)}) collective-permute-start(bf16[256,2048]{0,1:T(8,128)(2,1)S(1)} %pad_maximum_fusion.13), channel_id=1, source_target_pairs={{0,2},{2,0},{1,3},{3,1},{4,6},{6,4},{5,7},{7,5},{8,10},{10,8},{9,1... | collective-permute-start | bytes 3145736 | tf_op jit(solution)/shard_map/ppermute | solution.py:92
  348.4 53.1 %collective-permute-start.33 = (bf16[256,2048]{0,1:T(8,128)(2,1)S(1)}, bf16[256,2048]{0,1:T(8,128)(2,1)S(1)}, u32[]{:S(2)}, u32[]{:S(2)}) collective-permute-start(bf16[256,2048]{0,1:T(8,128)(2,1)S(1)} %pad_maximum_fusion.14), channel_id=1, source_target_pairs={{0,4},{4,0},{1,5},{5,1},{2,6},{6,2},{3,7},{7,3},{8,12},{12,8},{9,1... | collective-permute-start | bytes 3145736 | tf_op jit(solution)/shard_map/ppermute | solution.py:93
  350.4 48.1 %collective-permute-start.51 = (bf16[704,512]{1,0:T(8,128)(2,1)S(1)}, bf16[704,512]{1,0:T(8,128)(2,1)S(1)}, u32[]{:S(2)}, u32[]{:S(2)}) collective-permute-start(bf16[704,512]{1,0:T(8,128)(2,1)S(1)} %collective-permute-done.50), channel_id=1, source_target_pairs={{8,0},{9,1},{10,2},{11,3},{12,4},{13,5},{14,6},{15,7}} | collective-permute-start | bytes 2162696 | tf_op jit(solution)/shard_map/ppermute | solution.py:98
  522.5 77.9 %collective-permute-start.107 = (bf16[2,512,704]{1,2,0:T(8,128)(2,1)S(1)}, bf16[2,512,704]{1,2,0:T(8,128)(2,1)S(1)}, u32[]{:S(2)}, u32[]{:S(2)}) collective-permute-start(bf16[2,512,704]{1,2,0:T(8,128)(2,1)S(1)} %pad_maximum_fusion.6), channel_id=1, source_target_pairs={{0,8},{1,9},{2,10},{3,11},{4,12},{5,13},{6,14},{7,15}} | collective-permute-start | bytes 4325384 | tf_op jit(solution)/shard_map/ppermute | solution.py:110
  524.7 46.5 %collective-permute-start.115 = (bf16[704,512]{1,0:T(8,128)(2,1)S(1)}, bf16[704,512]{1,0:T(8,128)(2,1)S(1)}, u32[]{:S(2)}, u32[]{:S(2)}) collective-permute-start(bf16[704,512]{1,0:T(8,128)(2,1)S(1)} %get-tuple-element.154), channel_id=1, source_target_pairs={{0,8},{8,16},{1,9},{9,17},{2,10},{10,18},{3,11},{11,19},{4,12},{12... | collective-permute-start | bytes 2162696 | tf_op jit(solution)/shard_map/ppermute | solution.py:110
  526.0 45.1 %collective-permute-start.118 = (bf16[704,512]{1,0:T(8,128)(2,1)S(1)}, bf16[704,512]{1,0:T(8,128)(2,1)S(1)}, u32[]{:S(2)}, u32[]{:S(2)}) collective-permute-start(bf16[704,512]{1,0:T(8,128)(2,1)S(1)} %get-tuple-element.155), channel_id=1, source_target_pairs={{24,16},{16,8},{25,17},{17,9},{26,18},{18,10},{27,19},{19,11},{28,... | collective-permute-start | bytes 2162696 | tf_op jit(solution)/shard_map/ppermute | solution.py:111
  544.4 102.3 %collective-permute-start.54 = (bf16[1024,2048]{0,1:T(8,128)(2,1)}, bf16[1024,2048]{0,1:T(8,128)(2,1)}, u32[]{:S(2)}, u32[]{:S(2)}) collective-permute-start(bf16[1024,2048]{0,1:T(8,128)(2,1)} %slice.727), channel_id=1, source_target_pairs={{0,1},{1,0},{2,3},{3,2},{4,5},{5,4},{6,7},{7,6},{8,9},{9,8},{10,11... | collective-permute-start | bytes 12582920 | tf_op jit(solution)/shard_map/ppermute | solution.py:82
  600.4 62.6 %collective-permute-start.67 = (bf16[1024,2048]{0,1:T(8,128)(2,1)}, bf16[1024,2048]{0,1:T(8,128)(2,1)}, u32[]{:S(2)}, u32[]{:S(2)}) collective-permute-start(bf16[1024,2048]{0,1:T(8,128)(2,1)} %slice.726), channel_id=1, source_target_pairs={{0,1},{1,0},{2,3},{3,2},{4,5},{5,4},{6,7},{7,6},{8,9},{9,8},{10,11... | collective-permute-start | bytes 12582920 | tf_op jit(solution)/shard_map/ppermute | solution.py:82
  639.3 54.4 %collective-permute-start.110 = (bf16[2,512,704]{1,2,0:T(8,128)(2,1)}, bf16[2,512,704]{1,2,0:T(8,128)(2,1)}, u32[]{:S(2)}, u32[]{:S(2)}) collective-permute-start(bf16[2,512,704]{1,2,0:T(8,128)(2,1)} %get-tuple-element.91), channel_id=1, source_target_pairs={{24,16},{25,17},{26,18},{27,19},{28,20},{29,21},{30,22},{31,23}} | collective-permute-start | bytes 4325384 | tf_op jit(solution)/shard_map/ppermute | solution.py:111
  641.0 142.1 %collective-permute-start.109 = (bf16[2,512,704]{1,2,0:T(8,128)(2,1)}, bf16[2,512,704]{1,2,0:T(8,128)(2,1)}, u32[]{:S(2)}, u32[]{:S(2)}) collective-permute-start(bf16[2,512,704]{1,2,0:T(8,128)(2,1)} %get-tuple-element.90), channel_id=1, source_target_pairs={{0,8},{8,16},{16,24},{1,9},{9,17},{17,25},{2,10},{10,18},{18,26},{... | collective-permute-start | bytes 4325384 | tf_op jit(solution)/shard_map/ppermute | solution.py:110
  810.0 133.9 %collective-permute-start.113 = (bf16[2,256,704]{1,2,0:T(8,128)(2,1)}, bf16[2,256,704]{1,2,0:T(8,128)(2,1)}, u32[]{:S(2)}, u32[]{:S(2)}) collective-permute-start(bf16[2,256,704]{1,2,0:T(8,128)(2,1)} %broadcast_select_fusion.13), channel_id=1, source_target_pairs={{0,4},{4,0},{1,5},{5,1},{2,6},{6,2},{3,7},{7,3},{8,12},{12,8},{9,1... | collective-permute-start | bytes 2162696 | tf_op jit(solution)/shard_map/ppermute | solution.py:184
  839.7 76.5 %collective-permute-start.100 = (bf16[2,64,2048]{2,1,0:T(8,128)(2,1)}, bf16[2,64,2048]{2,1,0:T(8,128)(2,1)}, u32[]{:S(2)}, u32[]{:S(2)}) collective-permute-start(bf16[2,64,2048]{2,1,0:T(8,128)(2,1)} %select_bitcast_fusion), channel_id=1, source_target_pairs={{0,1},{1,0},{2,3},{3,2},{4,5},{5,4},{6,7},{7,6},{8,9},{9,8},{10,11... | collective-permute-start | bytes 1572872 | tf_op jit(solution)/shard_map/ppermute | solution.py:151
  916.2 97.4 %collective-permute-start.89 = (bf16[1024,2048]{0,1:T(8,128)(2,1)}, bf16[1024,2048]{0,1:T(8,128)(2,1)}, u32[]{:S(2)}, u32[]{:S(2)}) collective-permute-start(bf16[1024,2048]{0,1:T(8,128)(2,1)} %slice.725), channel_id=1, source_target_pairs={{0,1},{1,0},{2,3},{3,2},{4,5},{5,4},{6,7},{7,6},{8,9},{9,8},{10,11... | collective-permute-start | bytes 12582920 | tf_op jit(solution)/shard_map/ppermute | solution.py:82
  (241 other events, 4404.6 us)

commit v2 on v1

v2 whole, which is shorter than its diff:
```python
import math

import jax
import jax.numpy as jnp
from jax import lax
from jax.experimental import pallas as pl
from jax.experimental.layout import Layout, with_layout_constraint
from jax.experimental.pallas import tpu as pltpu
from jax.sharding import Mesh
from jax.sharding import PartitionSpec as P

BLOCK = 256
EPS = 1e-06
MU = 0.9
BETA = 0.8
HIGH = lax.Precision.HIGHEST
BF = jnp.bfloat16
F32 = jnp.float32
SWAP = [(0, 1), (1, 0)]
XORS = (0, 2, 4, 6, 1, 3, 5, 7)


def dot(a, b, dims=((1,), (0,))):
    return lax.dot_general(a, b, (dims, ((), ())), preferred_element_type=F32)


def inverse_rms(v):
    return lax.rsqrt(jnp.mean(v * v, axis=-1, keepdims=True) + EPS)


def srms_back(v, grad):
    r = inverse_rms(v)
    return r * grad - v * (r * r * r) * jnp.mean(grad * v, axis=-1, keepdims=True)


def renew(weight, moment, average, grad, fan, tokens):
    step = 0.4 / math.sqrt(fan * tokens)
    moment_new = MU * moment + grad
    weight_new = weight - step * (grad + MU * moment_new)
    average_new = BETA * average + (1.0 - BETA) * weight_new
    return (moment_new, weight_new, average_new)


ROWS = 256
HALF = 4
HD = 128
VMEM = 56 * 1024 * 1024
EXTRA = 128


def pin(v):
    return with_layout_constraint(v, Layout(major_to_minor=tuple(range(v.ndim))))


class Clock:
    def __init__(self):
        self.token = jnp.zeros((8, 128), F32)

    def now(self, *values):
        out = [lax.optimization_barrier((v, self.token))[0] for v in values]
        return out if len(out) > 1 else out[0]

    def end(self, *done):
        self.token = lax.optimization_barrier((self.token,) + done)[0]


def block_spec(shape):
    return pl.BlockSpec(shape, lambda i: (i,) + (0,) * (len(shape) - 1))


def whole_spec(a):
    return pl.BlockSpec(a.shape, lambda i: (0,) * a.ndim)


def scalar_spec():
    return pl.BlockSpec(memory_space=pltpu.SMEM)


def call(kernel, steps, ins, outs, flops):
    moved = sum(a.size * a.dtype.itemsize for a, _ in ins)
    moved += sum(math.prod(s) * jnp.dtype(d).itemsize for s, d, _ in outs)
    return pl.pallas_call(
        kernel,
        grid=(steps,),
        in_specs=[s for _, s in ins],
        out_specs=[b if isinstance(b, pl.BlockSpec) else block_spec(b) for _, _, b in outs],
        out_shape=[jax.ShapeDtypeStruct(s, d) for s, d, _ in outs],
        compiler_params=pltpu.CompilerParams(
            vmem_limit_bytes=VMEM, dimension_semantics=("arbitrary",)
        ),
        cost_estimate=pl.CostEstimate(
            flops=int(flops), bytes_accessed=int(moved), transcendentals=0
        ),
    )(*[a for a, _ in ins])


NT = ((1,), (1,))
TN = ((0,), (0,))


def fades(rate, seg_c, prev, last):
    t = lax.broadcasted_iota(jnp.int32, (ROWS, 1), 0).astype(F32)
    enter = jnp.where(seg_c == prev, jnp.exp(-rate * t), 0.0)
    leave = jnp.where(seg_c == last, jnp.exp(-rate * (ROWS - t)), 0.0)
    return enter, leave


def mask_of(rate, seg_c, seg_r):
    t = lax.broadcasted_iota(jnp.int32, (ROWS, ROWS), 0)
    s = lax.broadcasted_iota(jnp.int32, (ROWS, ROWS), 1)
    spread = (t - s).astype(F32)
    allowed = (t >= s) & (seg_c == seg_r)
    return jnp.where(allowed, jnp.exp(-rate * jnp.maximum(spread, 0.0)), 0.0)


def project(n1, w_in, seg_c, prev, last, rate):
    own = rate.shape[0]
    cols = own * HD
    parts = len(w_in)
    deep = n1.shape[1] // parts

    def kernel(*refs):
        x_ref, w_refs = refs[0], refs[1 : 1 + parts]
        seg_ref, prev_ref, last_ref, rate_ref = refs[1 + parts : 5 + parts]
        raw_ref, gate_ref, qkv_ref, term_ref = refs[5 + parts :]
        i = pl.program_id(0)
        pre = dot(x_ref[:, :deep], w_refs[0][...])
        for k in range(1, parts):
            pre = pre + dot(x_ref[:, k * deep : (k + 1) * deep], w_refs[k][...])
        pq, pk, pv = pre[:, :cols], pre[:, cols : 2 * cols], pre[:, 2 * cols : 3 * cols]
        raw_ref[...] = pre[:, : 2 * cols]
        gate_ref[...] = pre[:, 3 * cols :]
        key = (pk * jax.nn.sigmoid(pk)).astype(BF)
        value = pv.astype(BF)
        qkv_ref[:, :cols] = (pq * jax.nn.sigmoid(pq)).astype(BF)
        qkv_ref[:, cols : 2 * cols] = key
        qkv_ref[:, 2 * cols :] = value
        for j in range(own):
            _, leave = fades(rate_ref[j], seg_ref[0], prev_ref[i], last_ref[i])
            at = slice(j * HD, (j + 1) * HD)
            scaled = (key[:, at].astype(F32) * leave).astype(BF)
            term_ref[0, j] = dot(scaled, value[:, at], TN)

    n = n1.shape[0] // ROWS
    some = pl.BlockSpec((deep, 4 * cols), lambda i: (0, 0))
    ins = [(n1, block_spec((ROWS, n1.shape[1])))] + [(w, some) for w in w_in]
    ins += [(seg_c, block_spec((1, ROWS, 1)))] + [(a, scalar_spec()) for a in (prev, last, rate)]
    outs = [
        ((n * ROWS, 2 * cols), F32, (ROWS, 2 * cols)),
        ((n * ROWS, cols), F32, (ROWS, cols)),
        ((n * ROWS, 3 * cols), BF, (ROWS, 3 * cols)),
        ((n, own, HD, HD), F32, (1, own, HD, HD)),
    ]
    return call(kernel, n, ins, outs, 2 * n1.size * 4 * cols)


def attend(qkv, gate, state, w_out, seg_c, seg_r, prev, last, rate):
    own = rate.shape[0]
    cols = own * HD

    def kernel(
        qkv_ref, gate_ref, state_ref, w_ref, sc_ref, sr_ref, prev_ref, last_ref, rate_ref,
        attn_ref, branch_ref,
    ):
        i = pl.program_id(0)
        for j in range(own):
            at = slice(j * HD, (j + 1) * HD)
            q = qkv_ref[:, j * HD : (j + 1) * HD]
            k = qkv_ref[:, cols + j * HD : cols + (j + 1) * HD]
            v = qkv_ref[:, 2 * cols + j * HD : 2 * cols + (j + 1) * HD]
            enter, _ = fades(rate_ref[j], sc_ref[0], prev_ref[i], last_ref[i])
            weights = (dot(q, k, NT) * mask_of(rate_ref[j], sc_ref[0], sr_ref[0])).astype(BF)
            attn_ref[:, at] = dot(weights, v) + enter * dot(q, state_ref[0, j].astype(BF))
        attn = attn_ref[...]
        branch_ref[:, :width] = dot((attn * gate_ref[...]).astype(BF), w_ref[...]).astype(BF)
        rest = jnp.sum(attn * attn, axis=1, keepdims=True)
        lane = lax.broadcasted_iota(jnp.int32, (ROWS, EXTRA), 1)
        strip = jnp.zeros((ROWS, EXTRA), F32)
        for n in range(3):
            top = rest.astype(BF).astype(F32)
            strip = jnp.where(lane == n, top, strip)
            rest = rest - top
        branch_ref[:, width:] = strip.astype(BF)

    n = qkv.shape[0] // ROWS
    width = w_out.shape[1]
    ins = [
        (qkv, block_spec((ROWS, 3 * cols))),
        (gate, block_spec((ROWS, cols))),
        (state, block_spec((1, own, HD, HD))),
        (w_out, whole_spec(w_out)),
        (seg_c, block_spec((1, ROWS, 1))),
        (seg_r, block_spec((1, 1, ROWS))),
    ] + [(a, scalar_spec()) for a in (prev, last, rate)]
    outs = [
        ((n * ROWS, cols), F32, (ROWS, cols)),
        ((n * ROWS, width + EXTRA), BF, (ROWS, width + EXTRA)),
    ]
    return call(kernel, n, ins, outs, 2 * n * ROWS * cols * (width + 2 * ROWS))


def sglu_rows(n2, g, w_pair, w_third):
    parts = len(w_pair)
    _, hidden, deep = w_pair[0].shape
    block = 2 * ROWS

    def kernel(*refs):
        x_ref, g_ref = refs[:2]
        both, three = (refs[2 + k * parts : 2 + (k + 1) * parts] for k in range(2))
        prod_ref, prod_t, gf_t, gs_t, back_ref = refs[2 + 2 * parts :]
        first = second = grad = None
        for k in range(parts):
            at = slice(k * deep, (k + 1) * deep)
            x, gk = x_ref[:, at], g_ref[:, at]
            a, b, c = dot(x, both[k][0], NT), dot(x, both[k][1], NT), dot(gk, three[k][...], NT)
            first = a if first is None else first + a
            second = b if second is None else second + b
            grad = c if grad is None else grad + c
        prod = (first * second).astype(BF)
        gf = (grad * second).astype(BF)
        gs = (grad * first).astype(BF)
        prod_ref[...] = prod
        prod_t[...] = prod.T
        gf_t[...] = gf.T
        gs_t[...] = gs.T
        for k in range(parts):
            at = slice(k * deep, (k + 1) * deep)
            back_ref[:, at] = (dot(gf, both[k][0]) + dot(gs, both[k][1])).astype(BF)

    n = n2.shape[0] // block
    width = n2.shape[1]
    ins = [(n2, block_spec((block, width))), (g, block_spec((block, width)))]
    ins += [(w, whole_spec(w)) for w in w_pair + w_third]
    outs = [((n * block, hidden), BF, (block, hidden))]
    turned = pl.BlockSpec((hidden, block), lambda i: (0, i))
    outs += [((hidden, n * block), BF, turned)] * 3
    outs += [((n * block, width), BF, (block, width))]
    return call(kernel, n, ins, outs, 10 * n2.size * hidden)


def sglu_last(product, w_third):
    parts = len(w_third)
    deep = w_third[0].shape[1]
    block = 2 * ROWS

    def kernel(*refs):
        for k in range(parts):
            refs[-1][:, k * deep : (k + 1) * deep] = dot(refs[0][...], refs[1 + k][...]).astype(BF)

    n, width = product.shape[0] // block, parts * deep
    ins = [(product, block_spec((block, product.shape[1])))]
    ins += [(w, whole_spec(w)) for w in w_third]
    return call(
        kernel, n, ins, [((n * block, width), BF, (block, width))], 2 * product.size * width
    )[0]


def attend_back_rows(gb, w_out, attn, gate, qkv, seg_c, prev, last, rate):
    own = rate.shape[0]
    cols = own * HD
    width = w_out.shape[1]

    def kernel(
        gb_ref, w_ref, attn_ref, gate_ref, qkv_ref, sc_ref, prev_ref, last_ref, rate_ref,
        ga_ref, gg_ref, mixed_ref, term_ref,
    ):
        i = pl.program_id(0)
        extra = gb_ref[:, width : width + 8].astype(F32)
        r = extra[:, 0:1] + extra[:, 1:2] + extra[:, 2:3]
        pull = extra[:, 3:4] + extra[:, 4:5] + extra[:, 5:6]
        gm = dot(gb_ref[:, :width], w_ref[...], NT)
        attn, gate = attn_ref[...], gate_ref[...]
        normed = r * attn
        gg_ref[...] = (gm * normed).astype(BF)
        mixed_ref[...] = (normed * gate).astype(BF)
        ga = (r * (gm * gate) - attn * pull).astype(BF)
        ga_ref[...] = ga
        for j in range(own):
            enter, _ = fades(rate_ref[j], sc_ref[0], prev_ref[i], last_ref[i])
            q = qkv_ref[:, j * HD : (j + 1) * HD].astype(F32)
            term_ref[0, j] = dot((q * enter).astype(BF), ga[:, j * HD : (j + 1) * HD], TN)

    n = gb.shape[0] // ROWS
    ins = [
        (gb, block_spec((ROWS, gb.shape[1]))),
        (w_out, whole_spec(w_out)),
        (attn, block_spec((ROWS, cols))),
        (gate, block_spec((ROWS, cols))),
        (qkv, block_spec((ROWS, 3 * cols))),
        (seg_c, block_spec((1, ROWS, 1))),
    ] + [(a, scalar_spec()) for a in (prev, last, rate)]
    outs = [((n * ROWS, cols), BF, (ROWS, cols))] * 3
    outs += [((n, own, HD, HD), F32, (1, own, HD, HD))]
    return call(kernel, n, ins, outs, 2 * n * ROWS * cols * width)


def project_back(qkv, raw, ga, gg, state, later, w_in, width, seg_c, seg_r, prev, last, rate):
    own = rate.shape[0]
    cols = own * HD
    parts = len(w_in)
    deep = width // parts

    def kernel(*refs):
        qkv_ref, raw_ref, ga_ref, gg_ref, state_ref, later_ref = refs[:6]
        w_refs = refs[6 : 6 + parts]
        sc_ref, sr_ref, prev_ref, last_ref, rate_ref, gp_ref, back_ref = refs[6 + parts :]
        i = pl.program_id(0)
        for j in range(own):
            at = slice(j * HD, (j + 1) * HD)
            kt = slice(cols + j * HD, cols + (j + 1) * HD)
            vt = slice(2 * cols + j * HD, 2 * cols + (j + 1) * HD)
            q, k, v = qkv_ref[:, at], qkv_ref[:, kt], qkv_ref[:, vt]
            g = ga_ref[:, at]
            mask = mask_of(rate_ref[j], sc_ref[0], sr_ref[0])
            enter, leave = fades(rate_ref[j], sc_ref[0], prev_ref[i], last_ref[i])
            weights = (dot(q, k, NT) * mask).astype(BF)
            gs = (dot(g, v, NT) * mask).astype(BF)
            st, lt = state_ref[0, j].astype(BF), later_ref[0, j].astype(BF)
            gq = dot(gs, k) + enter * dot(g, st, NT)
            gk = dot(gs, q, TN) + leave * dot(v, lt, NT)
            gv = dot(weights, g, TN) + leave * dot(k, lt)
            rq, rk = raw_ref[:, at], raw_ref[:, kt]
            sq, sk = jax.nn.sigmoid(rq), jax.nn.sigmoid(rk)
            gp_ref[:, at] = (gq * (sq * (1.0 + rq * (1.0 - sq)))).astype(BF)
            gp_ref[:, kt] = (gk * (sk * (1.0 + rk * (1.0 - sk)))).astype(BF)
            gp_ref[:, vt] = gv.astype(BF)
        gp_ref[:, 3 * cols :] = gg_ref[...]
        for k in range(parts):
            at = slice(k * deep, (k + 1) * deep)
            back_ref[:, at] = dot(gp_ref[...], w_refs[k][...], NT).astype(BF)

    n = qkv.shape[0] // ROWS
    some = pl.BlockSpec((deep, 4 * cols), lambda i: (0, 0))
    ins = [
        (qkv, block_spec((ROWS, 3 * cols))),
        (raw, block_spec((ROWS, 2 * cols))),
        (ga, block_spec((ROWS, cols))),
        (gg, block_spec((ROWS, cols))),
        (state, block_spec((1, own, HD, HD))),
        (later, block_spec((1, own, HD, HD))),
    ] + [(w, some) for w in w_in]
    ins += [(seg_c, block_spec((1, ROWS, 1))), (seg_r, block_spec((1, 1, ROWS)))]
    ins += [(a, scalar_spec()) for a in (prev, last, rate)]
    outs = [
        ((n * ROWS, 4 * cols), BF, (ROWS, 4 * cols)),
        ((n * ROWS, width), BF, (ROWS, width)),
    ]
    return call(kernel, n, ins, outs, 2 * n * ROWS * 4 * cols * width)


def grads_by_left(left, right, cut):
    def kernel(l0, l1, r0, r1, out):
        out[0] = (dot(l0[...], r0[...], TN) + dot(l1[...], r1[...], TN)).astype(BF)

    n, cols = left[0].shape[1] // cut, right[0].shape[1]
    ins = [(a, pl.BlockSpec((a.shape[0], cut), lambda i: (0, i))) for a in left]
    ins += [(a, whole_spec(a)) for a in right]
    return call(
        kernel, n, ins, [((n, cut, cols), BF, (1, cut, cols))], 4 * left[0].size * cols
    )[0]


def grads_by_right(lefts, right, cut, width):
    count = len(lefts)

    def kernel(*refs):
        r0, r1, out = refs[2 * count :]
        for m in range(count):
            l0, l1 = refs[2 * m : 2 * m + 2]
            out[0, m] = (dot(l0[...], r0[...]) + dot(l1[...], r1[...])).astype(BF)

    n = width // cut
    tall = lefts[0][0].shape[0]
    ins = [(a, whole_spec(a)) for left in lefts for a in left]
    ins += [(a, pl.BlockSpec((a.shape[0], cut), lambda i: (0, i))) for a in right]
    outs = [((n, count, tall, cut), BF, (1, count, tall, cut))]
    return call(kernel, n, ins, outs, 4 * count * right[0].size * tall)[0]


def grads_out(left, right, width):
    def kernel(l0, l1, r0, r1, out):
        out[...] = (dot(l0[...], r0[...], TN) + dot(l1[...], r1[...], TN)).astype(BF)

    cut, tall = width // 4, left[0].shape[1]
    spec = lambda rows: pl.BlockSpec((rows, cut), lambda i: (0, i))
    ins = [(a, whole_spec(a)) for a in left] + [(a, spec(a.shape[0])) for a in right]
    return call(kernel, 4, ins, [((tall, width), BF, spec(tall))], 4 * left[0].size * width)[0]


def add_strips(width, *parts):
    total = parts[0][:, :width].astype(F32)
    for p in parts[1:]:
        total = total + p[:, :width].astype(F32)
    out = [total.astype(BF)]
    if parts[0].shape[1] > width:
        rest = 0.0
        for p in parts:
            for n in range(3):
                rest = rest + p[:, width + n : width + n + 1].astype(F32)
        lane = lax.broadcasted_iota(jnp.int32, (total.shape[0], EXTRA), 1)
        strip = jnp.zeros((total.shape[0], EXTRA), F32)
        for n in range(3):
            top = rest.astype(BF).astype(F32)
            strip = jnp.where(lane == n, top, strip)
            rest = rest - top
        out.append(strip.astype(BF))
    return out


def add_rows(a, b, width):
    n, wide = a.shape[0] // ROWS, a.shape[1]
    half = ROWS // 2

    block = pl.BlockSpec((ROWS, wide), lambda i: ((i + n - 1) % n, 0))
    one = pl.BlockSpec((half, wide), lambda i: (0, 0))

    def kernel(a_ref, b_ref, out_ref, low_ref, high_ref):
        parts = add_strips(width, a_ref[...], b_ref[...])
        for v, at in zip(parts, (slice(0, width), slice(width, wide))):
            out_ref[:, at] = v

            @pl.when(pl.program_id(0) == 0)
            def _():
                low_ref[:, at] = v[:half]
                high_ref[:, at] = v[half:]

    outs = [((n * ROWS, wide), BF, block)] + [((half, wide), BF, one)] * 2
    return call(kernel, n, [(a, block), (b, block)], outs, a.size)


def add_halves(sums, u, v, width):
    wide = sums.shape[1]
    half = ROWS // 2

    def kernel(s2_ref, s4_ref, u_ref, v_ref, to_2, to_4):
        to_2[:half] = s2_ref[:half]
        to_4[half:] = s4_ref[half:]
        two = add_strips(width, s2_ref[half:], v_ref[...])
        four = add_strips(width, s4_ref[:half], u_ref[...])
        for a, b, at in zip(two, four, (slice(0, width), slice(width, wide))):
            to_2[half:, at] = a
            to_4[:half, at] = b

    ins = [(sums, pl.BlockSpec((ROWS, wide), lambda i, k=k: (k, 0))) for k in (1, 2)]
    ins += [(u, whole_spec(u)), (v, whole_spec(v))]
    whole = pl.BlockSpec((ROWS, wide), lambda i: (0, 0))
    return call(kernel, 1, ins, [((ROWS, wide), BF, whole)] * 2, sums.size)


def cut4(v, axis):
    n = v.shape[axis] // 4
    return [lax.slice_in_dim(v, k * n, (k + 1) * n, axis=axis) for k in range(4)]


def strip_sum(v):
    strip = v[:, v.shape[1] - EXTRA :].astype(F32)
    return strip[:, 0:1] + strip[:, 1:2] + strip[:, 2:3]


def pieces(v):
    out = []
    for _ in range(3):
        top = lax.reduce_precision(v, 8, 7)
        out.append(top.astype(BF))
        v = v - top
    return out


class Places:
    def __init__(self, plan, seq_lengths, decay_rate, rows):
        size = plan.size
        group_rows = size * rows
        tokens = group_rows * plan.groups
        ends = jnp.cumsum(seq_lengths)

        def seg_at(place):
            mark = jnp.sum((place[..., None] >= ends).astype(jnp.int32), axis=-1)
            return jnp.where(place < 0, -1, mark)

        first_block = plan.group * size
        blocks = first_block + plan.slot_ids
        seg = seg_at(blocks[:, None] * rows + jnp.arange(rows, dtype=jnp.int32)[None, :])
        prev = seg_at(blocks * rows - 1)
        last = seg[:, rows - 1]
        head_ids = plan.head_ids if hasattr(plan, "head_ids") else plan.own * plan.p + jnp.arange(plan.own)
        rate = jnp.take(decay_rate, head_ids)

        def reach(gap, same):
            return jnp.where(
                same & (gap >= 0), jnp.exp(-rate[:, None, None] * (rows * jnp.maximum(gap, 0))), 0.0
            )

        inner = reach(
            (blocks[:, None] - blocks[None, :] - 1).astype(F32)[None],
            (prev[:, None] == last[None, :])[None],
        )
        border = seg_at((first_block + size) * rows - 1)
        out_reach = reach(
            (first_block + size - 1 - blocks).astype(F32)[None, None], (last == border)[None, None]
        )[:, 0]
        entry = seg_at(first_block * rows - 1)
        in_reach = reach((blocks - first_block).astype(F32)[None, None], (prev == entry)[None, None])[
            :, 0
        ]
        longest = tokens // 4
        hops = min(-(-longest // group_rows), plan.groups - 1)

        def hop_factor(j, ahead):
            if ahead:
                here, there = border, seg_at((first_block + j * size) * rows - 1)
            else:
                here, there = entry, seg_at((first_block - (j - 1) * size) * rows - 1)
            return jnp.where(here == there, jnp.exp(-rate * ((j - 1) * group_rows)), 0.0)

        def bring(total, ahead):
            n = plan.groups
            got = jnp.zeros_like(total)
            for j in range(1, hops + 1):
                pairs = [(i + j, i) if ahead else (i, i + j) for i in range(n - j)]
                part = lax.ppermute(total, plan.fs, pairs)
                got = got + hop_factor(j, ahead)[:, None, None] * part
            return got

        self.rate, self.bring = rate, bring
        self.inner, self.out_reach, self.in_reach = inner, out_reach, in_reach
        cut = lambda v: (v[:HALF], v[HALF:])
        self.cols, self.rows = cut(seg[:, :, None]), cut(seg[:, None, :])
        self.prev, self.last = cut(prev), cut(last)

    def states(self, term):
        leaving = jnp.einsum("hb,bhde->hde", self.out_reach, term, precision=HIGH)
        entering = self.bring(leaving, False)
        state = jnp.einsum("hbc,chde->bhde", self.inner, term, precision=HIGH)
        state = state + self.in_reach.T[:, :, None, None] * entering[None]
        return state[:HALF], state[HALF:]

    def states_back(self, term):
        leaving = jnp.einsum("hb,bhde->hde", self.in_reach, term, precision=HIGH)
        entering = self.bring(leaving, True)
        state = jnp.einsum("hcb,chde->bhde", self.inner, term, precision=HIGH)
        state = state + self.out_reach.T[:, :, None, None] * entering[None]
        return state[:HALF], state[HALF:]


class Square:
    def __init__(self):
        self.tp = ("y", "x", "c")
        self.fs = ("z",)
        self.size = 8
        self.groups = 4

    def begin(self):
        self.z = lax.axis_index("z")
        self.y = lax.axis_index("y")
        self.c = lax.axis_index("c")
        self.p = lax.axis_index(self.tp)
        self.q = self.p // 2
        self.group = self.z
        self.slot_ids = self.p ^ jnp.array(XORS, jnp.int32)
        self.head_ids = 8 * self.c + 4 * jnp.arange(2) + self.q

    def turn(self, v):
        wide = v.shape[1] // 4
        return jnp.concatenate(
            [
                lax.dynamic_slice_in_dim(v, ((self.z - k) % 4) * wide, wide, axis=1)
                for k in range(4)
            ],
            axis=1,
        )

    def slots(self, own, one, two, three):
        return [
            own,
            pin(jnp.where(self.z >= 1, one[0], three[1])),
            pin(jnp.where(self.z >= 2, two[0], two[1])),
            pin(jnp.where(self.z >= 3, three[0], one[1])),
        ]

    def by_y(self, mine, got, axis):
        first = self.y == 0
        parts = [jnp.where(first, mine, got), jnp.where(first, got, mine)]
        return pin(jnp.concatenate(parts, axis=axis))

    def of_y(self, one, two):
        first = self.y == 0
        return pin(jnp.where(first, one, two)), pin(jnp.where(first, two, one))


def over(axis, pairs=SWAP):
    return lambda v: pin(lax.ppermute(pin(v), axis, pairs))


to_x, to_y, to_core = over("x"), over("y"), over("c")


def spread(pair, step):
    up = over("z", [(i, i + 1) for i in range(step, 3)])
    down = over("z", [(3 - i, 2 - i) for i in range(step, 3)])
    return up(pair[0]), down(pair[1])


def gather(up, down, step):
    go_up = over("z", [(i, i + 1) for i in range(step)])
    go_down = over("z", [(3 - i, 2 - i) for i in range(step)])
    return go_up(up), go_down(down)


def plus(a, b):
    return (a.astype(F32) + b.astype(F32)).astype(BF)


def square_layer(plan, at, inputs, out_grad, attn_in, attn_out, sglu_in, sglu_out):
    rows, width = inputs.shape
    h2 = rows // 2
    cut = width // 4
    clock = Clock()
    now, end = clock.now, clock.end
    rate = at.rate

    def pick(slots, plane):
        return lax.dynamic_index_in_dim(slots, (plan.z - plane) % 4, 0, False)

    xf = inputs.astype(F32)
    n1 = pin(plan.turn((xf * inverse_rms(xf)).astype(BF)))
    og = pin(plan.turn(out_grad))
    few = attn_in.shape[0]
    view = attn_in.astype(BF).reshape(few, 4, 2, 2, 4, HD).transpose(4, 2, 0, 1, 3, 5)
    own_in = lax.all_to_all(view.reshape(8, few, -1), plan.tp, 0, 0, tiled=True)
    own_in = own_in.reshape(8 * few, -1)
    deep, across = own_in.shape
    own_out = attn_out.astype(BF)
    own_w = pin(jnp.concatenate([own_in, own_out[:, :across], own_out[:, across:]]))
    hid = sglu_in.shape[2] // 2
    three = jnp.concatenate([sglu_in.astype(BF).swapaxes(1, 2), sglu_out.astype(BF)[None]])
    my_three, to_three = plan.of_y(three[:, :hid], three[:, hid:])
    end(own_w, n1, og, to_three)

    a_w, a_n1 = now(own_w, n1)
    w1 = spread((a_w, a_w), 0)
    nx, ny, nc = to_x(a_n1), to_y(a_n1), to_core(a_n1)
    end(*w1, nx, ny, nc)

    w2 = spread(now(*w1), 1)
    ax, ay = now(nx, ny)
    nd = to_x(ay[:h2]), to_y(ax[h2:])
    nxyc = to_core(jnp.concatenate([ax, ay]))
    end(*w2, *nd, nxyc)

    w3 = spread(now(*w2), 2)
    a_og, a_three = now(og, to_three)
    gx = to_x(a_og)
    got = to_y(a_three)
    ndc = to_core(jnp.concatenate(now(*nd)))
    norm1 = pin(jnp.concatenate([n1, nx, ny, *nd])), pin(jnp.concatenate([nc, nxyc, ndc]))
    own_three = plan.by_y(my_three, got, 2)
    owns = [pin(own_three[m]) for m in range(3)]
    end(*w3, gx, *norm1, *owns)

    owns = now(*owns)
    third1 = spread((owns[2],) * 2, 0)
    w_in = plan.slots(own_w, *[now(*v) for v in (w1, w2, w3)])
    a_rate, a_og, a_gx = now(rate, og, gx)
    gy = to_y(a_og)
    crossed = to_core(jnp.concatenate([a_og, a_gx]))
    outs = jnp.stack([w[deep:] for w in w_in])
    w_mine = [pick(outs, 2 * plan.c + j) for j in (0, 1)]
    w_got = to_core(jnp.concatenate([pick(outs, 2 * (1 - plan.c) + j) for j in (0, 1)]))
    core0 = plan.c == 0
    raw, gate, qkv, term = zip(
        *[project(norm1[h], w_in, at.cols[h], at.prev[h], at.last[h], a_rate) for h in (0, 1)]
    )
    end(*third1, gy, crossed, w_got, *term)

    first1 = spread((now(owns[0]),) * 2, 0)
    a_gx, a_gy = now(gx, gy)
    gd = to_x(a_gy[:h2]), to_y(a_gx[h2:])
    w_rows = []
    for j in (0, 1):
        got = w_got[j * 2 * few : (j + 1) * 2 * few]
        for half in (jnp.where(core0, w_mine[j], got), jnp.where(core0, got, w_mine[j])):
            w_rows.append(jnp.concatenate([half[:few], half[few:]], axis=1))
    w_out = pin(jnp.concatenate(w_rows))
    state = at.states(jnp.concatenate(now(*term)))

    def attend_half(h, fade):
        return attend(
            qkv[h], gate[h], state[h], w_out, at.cols[h], at.rows[h], at.prev[h], at.last[h], fade
        )

    attn_b, give = attend_half(1, rate)
    end(*first1, *gd, give)

    second1 = spread((now(owns[1]),) * 2, 0)
    a_rate, give = now(rate, give)
    attn_a, keep = attend_half(0, a_rate)
    got = to_core(give)
    end(*second1, got, keep)

    def last_sum(own, x, y):
        return own.astype(F32) + x.astype(F32) + y.astype(F32)

    def first_step(keep, got):
        sums, low, high = add_rows(keep, got, width)
        return sums, to_x(low), to_y(high)

    def second_step(sums, u, v):
        to_2, to_4 = add_halves(sums, u, v, width)
        return to_x(to_2), to_y(to_4)

    sums, u, v = first_step(*now(keep, got))
    third2 = spread(now(*third1), 1)
    gydc = to_core(jnp.concatenate(now(gy, *gd)))
    end(u, v, *third2, gydc)

    sx, sy = second_step(sums, *now(u, v))
    first2 = spread(now(*first1), 1)
    second2 = spread(now(*second1), 1)
    g_a = pin(jnp.concatenate([og, gx, gy, *gd]))
    g_b = pin(jnp.concatenate([crossed, gydc]))
    end(sx, sy, *first2, *second2, g_a, g_b)

    third3 = spread(now(*third2), 2)
    first3 = spread(now(*first2), 2)
    sx, sy = now(sx, sy)
    branch = pin(last_sum(sums[:rows, :width], sx[:, :width], sy[:, :width]))
    square = strip_sum(sums[:rows]) + strip_sum(sx) + strip_sum(sy)
    r_attn = lax.rsqrt(square / width + EPS)
    mid = pin(xf + r_attn * branch)
    n2 = pin(plan.turn((mid * inverse_rms(mid)).astype(BF)))
    mx, my, mc = to_x(n2), to_y(n2), to_core(n2)
    w_third = plan.slots(owns[2], third1, third2, third3)
    end(mx, my, mc, *third3, *first3)

    second3 = spread(now(*second2), 2)
    ax, ay = now(mx, my)
    md = to_x(ay[:h2]), to_y(ax[h2:])
    mxyc = to_core(jnp.concatenate([ax, ay]))
    mdc = to_core(jnp.concatenate(md))
    n2_a = pin(jnp.concatenate([n2, mx, my, *md]))
    n2_b = pin(jnp.concatenate([mc, mxyc, mdc]))
    end(*second3, n2_a, n2_b)

    both = [[now(*v) for v in s] for s in ((first1, first2, first3), (second1, second2, second3))]
    w_pair = [
        pin(jnp.stack([a, b]))
        for a, b in zip(plan.slots(owns[0], *both[0]), plan.slots(owns[1], *both[1]))
    ]
    prod_b, turned_b, gf_b, gs_b, give = sglu_rows(n2_b, g_b, w_pair, w_third)
    end(give)

    give, a_n2 = now(give, n2_a)
    got = to_core(give)
    prod_a, turned_a, gf_a, gs_a, keep = sglu_rows(a_n2, g_a, w_pair, w_third)
    end(keep, got)

    sums, u, v = first_step(*now(keep, got))
    d_third = grads_by_right([(now(turned_a), turned_b)], (g_a, g_b), cut, width)[:, 0]
    end(u, v, d_third)

    sx, sy = second_step(sums, *now(u, v))
    d_third = now(d_third)
    third1 = gather(d_third[1], d_third[3], 1)
    d_pair = grads_by_right([(now(gf_a), gf_b), (gs_a, gs_b)], (n2_a, n2_b), cut, width)
    d_one = [[d_pair[k, m] for k in range(4)] for m in (0, 1)]
    ready = [v for m in (0, 1) for v in (pin(d_one[m][1]), pin(d_one[m][3]))]
    end(sx, sy, *third1, d_pair, *ready)

    ready = now(*ready)
    first1 = gather(ready[0], ready[1], 1)
    second1 = gather(ready[2], ready[3], 1)
    grad_norm2 = last_sum(sums[:rows], *now(sx, sy))
    grad_mid = pin(out_grad.astype(F32) + srms_back(mid, plan.turn(grad_norm2)))
    gb = grad_mid.astype(BF)
    inward = jnp.mean(gb.astype(F32) * branch, axis=1, keepdims=True)
    extra = pieces(r_attn) + pieces(r_attn * r_attn * r_attn * inward)
    extra.append(jnp.zeros((rows, EXTRA - len(extra)), BF))
    gb = pin(jnp.concatenate([gb] + extra, axis=1))
    bx, by, bc = to_x(gb), to_y(gb), to_core(gb)
    give = sglu_last(now(prod_b), w_third)
    keep = sglu_last(now(prod_a), w_third)

    def join(parts, up, down, k_up, k_down):
        a, b = now(up, down)
        return pin(plus(parts[k_up], a)), pin(plus(parts[k_down], b))

    ready = join(d_third, *third1, 2, 2)
    end(bx, by, bc, *first1, *second1, keep, give, *ready)

    third2 = gather(*now(*ready), 2)
    ax, ay = now(bx, by)
    bd = to_x(ay[:h2]), to_y(ax[h2:])
    bxyc = to_core(jnp.concatenate([ax, ay]))
    bdc = to_core(jnp.concatenate(bd))
    gb_a = pin(jnp.concatenate([gb, bx, by, *bd]))
    gb_b = pin(jnp.concatenate([bc, bxyc, bdc]))
    ready = join(d_one[0], *first1, 2, 2) + join(d_one[1], *second1, 2, 2)
    end(*third2, gb_a, gb_b, *ready)

    ready = now(*ready)
    first2 = gather(ready[0], ready[1], 2)
    second2 = gather(ready[2], ready[3], 2)
    o_got = to_core(now(give))
    a_rate = now(rate)
    ga, gg, mixed, d_term = zip(
        *[
            attend_back_rows(g, w_out, attn, gate[h], qkv[h], at.cols[h],
                             at.prev[h], at.last[h], a_rate)
            for h, g, attn in ((0, gb_a, attn_a), (1, gb_b, attn_b))
        ]
    )
    d_out = grads_out(mixed, (gb_a, gb_b), width)
    ready = join(d_third, *third2, 3, 1)
    end(*first2, *second2, *d_term, d_out, o_got, *ready)

    third3 = gather(*now(*ready), 3)
    o_sums, ou, ov = first_step(*now(keep, o_got))
    later = at.states_back(jnp.concatenate(now(*d_term)))

    def back_half(h, fade):
        return project_back(
            qkv[h], raw[h], ga[h], gg[h], state[h], later[h], w_in, width,
            at.cols[h], at.rows[h], at.prev[h], at.last[h], fade,
        )

    gp_b, give = back_half(1, rate)
    ready = join(d_one[0], *first2, 3, 1)
    end(*third3, ou, ov, give, *ready)

    first3 = gather(*now(*ready), 3)
    a_rate, give = now(rate, give)
    gp_a, keep = back_half(0, a_rate)
    got = to_core(give)
    parts = now(d_out).reshape(2, 2, few, width)
    o_keep = jnp.where(core0, parts[:, 0], parts[:, 1])
    o_got = to_core(jnp.where(core0, parts[:, 1], parts[:, 0]))
    ready = join(d_one[1], *second2, 3, 1)
    end(*first3, keep, got, o_got, *ready)

    second3 = gather(*now(*ready), 3)
    sums, u, v = first_step(*now(keep, got))
    d_in = grads_by_left(norm1, (now(gp_a), gp_b), cut)
    planes = jnp.concatenate([jnp.where(core0, o_keep, o_got), jnp.where(core0, o_got, o_keep)])
    planes = [pick(planes, k) for k in range(4)]
    d_w = [
        pin(jnp.concatenate([d_in[k], planes[k][:, :across], planes[k][:, across:]]))
        for k in range(4)
    ]
    end(u, v, *second3, *d_w)

    d_w = now(*d_w)
    w1 = gather(d_w[1], d_w[3], 1)
    sx, sy = second_step(sums, *now(u, v))
    sum_three = [last_sum(d_one[m][0], *now(*v)) for m, v in ((0, first3), (1, second3))]
    sum_three.append(last_sum(d_third[0], *now(*third3)))
    sum_three = jnp.stack([v.astype(BF) for v in sum_three])
    my_three, to_three = plan.of_y(sum_three[:, :, :rows], sum_three[:, :, rows:])
    end(sx, sy, *w1, my_three, to_three)

    w2 = gather(*join(d_w, *w1, 2, 2), 2)
    ox, oy = second_step(o_sums, *now(ou, ov))
    grad_norm1 = last_sum(sums[:rows], *now(sx, sy))
    input_grad = grad_mid + srms_back(xf, plan.turn(grad_norm1))
    end(*w2, ox, oy)

    w3 = gather(*join(d_w, *w2, 3, 1), 3)
    got = to_y(now(to_three))
    output = mid + plan.turn(last_sum(o_sums[:rows], *now(ox, oy)))
    end(*w3, got)

    sum_w = pin(last_sum(d_w[0], *now(*w3)))
    sum_in = sum_w[:deep].astype(BF).reshape(8, few, across)
    mine = lax.all_to_all(sum_in, plan.tp, 0, 0, tiled=True)
    mine = mine.reshape(4, 2, few, 4, 2, HD).transpose(2, 3, 1, 4, 0, 5)
    sum_in = mine.reshape(few, -1).astype(F32)
    sum_out = jnp.concatenate([sum_w[deep : deep + few], sum_w[deep + few :]], axis=1)
    sum_three = plan.by_y(my_three, got, 1)
    sum_pair = sum_three[:2].swapaxes(1, 2).astype(F32)
    sum_third = sum_three[2].astype(F32)
    return output, input_grad, sum_in, sum_out, sum_pair, sum_third


class Plain:
    def __init__(self, wide, narrow):
        self.tp = ("narrow",)
        self.fs = ("wide",)
        self.size = narrow
        self.groups = wide

    def begin(self):
        self.p = lax.axis_index("narrow")
        self.group = lax.axis_index("wide")
        self.slot_ids = jnp.arange(self.size, dtype=jnp.int32)

    def turn(self, v):
        return v

    def rows_all(self, a):
        whole = lax.all_gather(a, "narrow", axis=0, tiled=True)
        return whole[: whole.shape[0] // 2], whole[whole.shape[0] // 2 :]

    def rows_sum(self, keep, give, kind=BF):
        total = lax.psum_scatter(
            jnp.concatenate([keep, give]), "narrow", scatter_dimension=0, tiled=True
        )
        return total.astype(F32)

    def attn_in(self, w):
        rows, cols = w.shape
        each = cols // 4 // self.size
        view = w.reshape(rows, 4, self.size, each).transpose(2, 0, 1, 3)
        view = view.reshape(self.size, rows, 4 * each)
        mine = lax.all_to_all(view, "narrow", 0, 0, tiled=True)
        mine = mine.reshape(self.size * rows, 4 * each)
        return cut4(lax.all_gather(mine, "wide", axis=0, tiled=True), 0)

    def attn_in_back(self, g):
        cols = g.shape[2]
        g = g.reshape(-1, cols)
        total = lax.psum_scatter(g.astype(BF), "wide", scatter_dimension=0, tiled=True)
        rows = total.shape[0] // self.size
        view = total.reshape(self.size, rows, cols)
        mine = lax.all_to_all(view, "narrow", 0, 0, tiled=True)
        mine = mine.reshape(self.size, rows, 4, cols // 4).transpose(1, 2, 0, 3)
        return mine.reshape(rows, cols * self.size).astype(F32)

    def attn_out(self, w):
        whole = lax.all_gather(w, ("wide", "narrow"), axis=0, tiled=True)
        each = whole.shape[0] // self.size
        return lax.dynamic_slice_in_dim(whole, self.p * each, each)

    def attn_out_back(self, g):
        each = g.shape[0]
        whole = jnp.zeros((each * self.size, g.shape[1]), BF)
        whole = lax.dynamic_update_slice_in_dim(whole, g.astype(BF), self.p * each, 0)
        total = lax.psum_scatter(whole, ("wide", "narrow"), scatter_dimension=0, tiled=True)
        return total.astype(F32)

    def sglu(self, pair, third):
        return pair, third

    def sglu_all(self, both, back):
        pair = lax.all_gather(both.swapaxes(1, 2), "wide", axis=2, tiled=True)
        third = lax.all_gather(back, "wide", axis=1, tiled=True)
        return cut4(pair, 2), cut4(third, 1)

    def pair_back(self, g):
        g = jnp.concatenate([g[k] for k in range(4)], axis=2)
        total = lax.psum_scatter(g, "wide", scatter_dimension=2, tiled=True)
        return total.swapaxes(1, 2).astype(F32)

    def third_back(self, g):
        g = jnp.concatenate([g[k] for k in range(4)], axis=1)
        total = lax.psum_scatter(g, "wide", scatter_dimension=1, tiled=True)
        return total.astype(F32)


def plain_layer(
    plan, at, inputs, out_grad, attn_in, attn_out, sglu_in, sglu_out
):
    rows, width = inputs.shape
    w_out = plan.attn_out(attn_out.astype(BF))
    w_in = plan.attn_in(attn_in.astype(BF))
    w_pair, w_third = plan.sglu_all(sglu_in.astype(BF), sglu_out.astype(BF))
    xf = inputs.astype(F32)
    norm1 = plan.rows_all(plan.turn((xf * inverse_rms(xf)).astype(BF)))
    grad_rows = plan.rows_all(plan.turn(out_grad))
    raw, gate, qkv, term = zip(
        *[project(norm1[h], w_in, at.cols[h], at.prev[h], at.last[h], at.rate) for h in (0, 1)]
    )
    state = at.states(jnp.concatenate(term))
    attn, branch = [None] * 2, [None] * 2
    for h in (1, 0):
        attn[h], branch[h] = attend(
            qkv[h], gate[h], state[h], w_out, at.cols[h], at.rows[h], at.prev[h], at.last[h], at.rate
        )
    square = plan.rows_sum(*[strip_sum(v) for v in branch], F32)
    branch = plan.rows_sum(*[v[:, :width] for v in branch])
    r_attn = lax.rsqrt(square / width + EPS)
    mid = xf + r_attn * branch
    r_mid = inverse_rms(mid)
    norm2 = plan.rows_all(plan.turn((mid * r_mid).astype(BF)))

    product, turned, grad_first, grad_second, back = [[None] * 2 for _ in range(5)]
    for h in (1, 0):
        product[h], turned[h], grad_first[h], grad_second[h], back[h] = sglu_rows(
            norm2[h], grad_rows[h], w_pair, w_third
        )
    cut = width // 4
    sum_third = plan.third_back(grads_by_right([turned], grad_rows, cut, width)[:, 0])
    grad_norm2 = plan.rows_sum(*back)
    sum_pair = plan.pair_back(grads_by_right([grad_first, grad_second], norm2, cut, width))

    grad_mid = out_grad.astype(F32) + srms_back(mid, plan.turn(grad_norm2))
    grad_branch = grad_mid.astype(BF)
    inward = jnp.mean(grad_branch.astype(F32) * branch, axis=1, keepdims=True)
    extra = pieces(r_attn) + pieces(r_attn * r_attn * r_attn * inward)
    extra.append(jnp.zeros((rows, 128 - len(extra)), BF))
    grad_branch = jnp.concatenate([grad_branch] + extra, axis=1)
    grad_branch = plan.rows_all(grad_branch)
    branch_out = plan.rows_sum(*[sglu_last(v, w_third) for v in product])
    output = mid + plan.turn(branch_out)
    grad_attn, grad_gate, mixed, d_term = zip(
        *[
            attend_back_rows(
                grad_branch[h], w_out, attn[h], gate[h], qkv[h], at.cols[h],
                at.prev[h], at.last[h], at.rate,
            )
            for h in (0, 1)
        ]
    )
    later = at.states_back(jnp.concatenate(d_term))
    grad_pre, back = [None] * 2, [None] * 2
    for h in (1, 0):
        grad_pre[h], back[h] = project_back(
            qkv[h], raw[h], grad_attn[h], grad_gate[h], state[h], later[h], w_in, width,
            at.cols[h], at.rows[h], at.prev[h], at.last[h], at.rate,
        )
    grad_win = grads_by_left(norm1, grad_pre, cut)
    sum_in = plan.attn_in_back(grad_win)
    sum_out = plan.attn_out_back(grads_out(mixed, grad_branch, width))
    grad_norm1 = plan.rows_sum(*back)
    input_grad = grad_mid + srms_back(xf, plan.turn(grad_norm1))
    return output, input_grad, sum_in, sum_out, sum_pair, sum_third


def per_device(plan, layer, *args):
    inputs, out_grad, seq_lengths, decay_rate = args[:4]
    weights, moments, averages = args[4:8], args[8:12], args[12:16]
    plan.begin()
    rows, width = inputs.shape
    plan.own = decay_rate.shape[0] // plan.size
    at = Places(plan, seq_lengths, decay_rate, rows)
    output, input_grad, *grads = layer(plan, at, inputs, out_grad, *weights)
    tokens = plan.size * rows * plan.groups
    fans = (width, width, width, weights[3].shape[0] * lax.axis_size(plan.narrow))
    new = [renew(*v, tokens) for v in zip(weights, moments, averages, grads, fans)]
    return (output, input_grad) + tuple(n[i] for i in range(3) for n in new)


def solution(mesh):
    wide, narrow = mesh.shape["wide"], mesh.shape["narrow"]
    if (wide, narrow) == (8, 4):
        mesh = Mesh(mesh.devices.reshape(4, 2, 2, 2), ("z", "y", "x", "c"))
        plan, layer, w, n = Square(), square_layer, ("z", "y"), ("x", "c")
    else:
        plan, layer, w, n = Plain(wide, narrow), plain_layer, ("wide",), ("narrow",)
    plan.narrow = n
    by_rows = P(w + n, None)
    pair, third = P(None, w, n), P(n, w)
    weights = (by_rows, by_rows, pair, third)

    def run(*args):
        return per_device(plan, layer, *args)

    return jax.shard_map(
        run,
        mesh=mesh,
        in_specs=(by_rows, by_rows, P(), P()) + weights * 3,
        out_specs=(by_rows, by_rows) + weights * 3,
        check_vma=False,
    )
```

time: 1090 us -> 863 us (0.79)
  Pallas kernels: 0 us -> 222 us
  waiting for transfers between devices: 420 us -> 230 us
  matrix products: 181 us -> 6.24 us
  local copies, waits for them, and re-layouts: 166 us -> 101 us
  other arithmetic: 141 us -> 126 us
    pallas_call x0 -> x24, Pallas kernels: none -> 222 us  [call(): pl.pallas_call(kernel, grid=(steps,), in_specs=[s for _, s in ins], out_s...]
    ppermute x119 -> x99, waiting for transfers between devices: 420 us -> 225 us  [over(): return lambda v: pin(lax.ppermute(pin(v), axis, pairs))]
    dot_general x31 -> x4, matrix products: 181 us -> 6.24 us  [the longest x1 1.66 us: states(): state = jnp.einsum('hbc,chde->bhde', self.inner, term, precision=HIGH)]
    another operation x19 -> x16, other arithmetic: 57.5 us -> 13 us  [the longest x10 6.64 us: square_layer(): jnp.stack([a, b])]
    unnamed x341 -> x256, local copies, waits for them, and re-layouts: 97.5 us -> 54.1 us
    slice x24 -> x29, local copies, waits for them, and re-layouts: 36.6 us -> 17.1 us  [the longest x7 7.33 us: __init__(): cut = lambda v: (v[:HALF], v[HALF:])]
    ppermute x119 -> x99, starting transfers between devices: 153 us -> 148 us  [over(): return lambda v: pin(lax.ppermute(pin(v), axis, pairs))]
    convert_element_type x22 -> x17, other arithmetic: 29.9 us -> 27.8 us  [the longest x8 23.5 us: plus(): return (a.astype(F32) + b.astype(F32)).astype(BF)]
  transfers between devices with their start and end apart: 123 -> 103, of which waited for: 40 -> 37; matrix products, arithmetic and copies ran while one was open for 35% -> 19% of each run, Pallas kernels for 0% -> 21%
where the time goes in v2:
time: 863 us; the launch traced here: 853 us
  waiting for transfers between devices  230 us (27%)
  Pallas kernels  222 us (26%)
  starting transfers between devices  162 us (19%)
  other arithmetic  126 us (15%)
  local copies, waits for them, and re-layouts  101 us (12%)
    ppermute x99, waiting for transfers between devices, over(): return lambda v: pin(lax.ppermute(pin(v), axis, pairs))  225 us
    pallas_call x24, Pallas kernels, call(): pl.pallas_call(kernel, grid=(steps,), in_specs=[s for _, s in ins], out_s...  222 us
    ppermute x99, starting transfers between devices, over(): return lambda v: pin(lax.ppermute(pin(v), axis, pairs))  148 us
    unnamed x256, local copies, waits for them, and re-layouts  54.1 us
    convert_element_type x8, other arithmetic, plus(): return (a.astype(F32) + b.astype(F32)).astype(BF)  23.5 us
  transfers between devices with their start and end apart: 103, of which 37 were waited for; matrix products, arithmetic and copies ran while one was open for 19% of the time, Pallas kernels for 21%

profile of v2, /device:TPU:0, one launch (start us, length us, event | category | flops | bytes accessed | tf_op | source)
XLA Modules:
  0.0 852.7 jit_solution(17862634182363731069)
XLA Ops:
  42.5 17.1 %collective-permute-done = bf16[256,2048]{1,0:T(8,128)(2,1)} collective-permute-done((bf16[256,2048]{1,0:T(8,128)(2,1)}, bf16[256,2048]{1,0:T(8,128)(2,1)}, u32[]{:S(2)}, u32[]{:S(2)}) %collective-permute-start) | collective-permute-done | bytes 1048608 | tf_op jit(solution)/shard_map/ppermute | solution.py:591
  100.1 10.1 %collective-permute-done.8 = bf16[640,1024]{1,0:T(8,128)(2,1)} collective-permute-done((bf16[640,1024]{1,0:T(8,128)(2,1)}, bf16[640,1024]{1,0:T(8,128)(2,1)}, u32[]{:S(2)}, u32[]{:S(2)}) %collective-permute-start.8) | collective-permute-done | bytes 1310752 | tf_op jit(solution)/shard_map/ppermute | solution.py:591
  125.9 14.3 %collective-permute-done.14 = bf16[3,704,256]{2,1,0:T(8,128)(2,1)S(1)} collective-permute-done((bf16[3,704,256]{2,1,0:T(8,128)(2,1)S(1)}, bf16[3,704,256]{2,1,0:T(8,128)(2,1)S(1)}, u32[]{:S(2)}, u32[]{:S(2)}) %collective-permute-start.14) | collective-permute-done | bytes 1081376 | tf_op jit(solution)/shard_map/ppermute | solution.py:591
  167.1 9.1 %shard_map.272 = (f32[1024,512]{1,0:T(8,128)}, f32[1024,256]{1,0:T(8,128)}, bf16[1024,768]{1,0:T(8,128)(2,1)}, f32[4,2,128,128]{3,2,1,0:T(8,128)}) custom-call(bf16[1024,2048]{1,0:T(8,128)(2,1)} %constant_dynamic-update-slice_fusion.refs_0_.l0, bf16[640,1024]{1,0:T(8,128)(2,1)} %pad_maximum_fusion.12.refs_1_.refs_6_, bf16[640,1024]{1,0:T(8,128)(2,1)} %copy-done.44, ...), custom_call_target="tpu_custom_call" | custom-call | flops 4294967296 | bytes 14684200 | tf_op jit(solution)/shard_map/pallas_call | solution.py:82
  176.2 9.1 %shard_map.273 = (f32[1024,512]{1,0:T(8,128)}, f32[1024,256]{1,0:T(8,128)}, bf16[1024,768]{1,0:T(8,128)(2,1)}, f32[4,2,128,128]{3,2,1,0:T(8,128)}) custom-call(bf16[1024,2048]{1,0:T(8,128)(2,1)} %copy-done.94, bf16[640,1024]{1,0:T(8,128)(2,1)} %pad_maximum_fusion.12.refs_1_.refs_6_, bf16[640,1024]{1,0:T(8,128)(2,1)} %copy-done.44, ...), custom_call_target="tpu_custom_call" | custom-call | flops 4294967296 | bytes 14684200 | tf_op jit(solution)/shard_map/pallas_call | solution.py:82
  253.4 8.0 shard_map.276
  265.6 11.0 %collective-permute-done.28.u_ref = bf16[128,2176]{1,0:T(8,128)(2,1)S(1)} collective-permute-done((bf16[128,2176]{1,0:T(8,128)(2,1)}, bf16[128,2176]{1,0:T(8,128)(2,1)S(1)}, u32[]{:S(2)}, u32[]{:S(2)}) %collective-permute-start.28) | collective-permute-done | bytes 557088 | tf_op jit(solution)/shard_map/ppermute | solution.py:591
  294.2 17.3 %collective-permute-done.36 = bf16[704,512]{1,0:T(8,128)(2,1)S(1)} collective-permute-done((bf16[704,512]{1,0:T(8,128)(2,1)S(1)}, bf16[704,512]{1,0:T(8,128)(2,1)S(1)}, u32[]{:S(2)}, u32[]{:S(2)}) %collective-permute-start.36) | collective-permute-done | bytes 720928 | tf_op jit(solution)/shard_map/ppermute | solution.py:591
  311.5 12.9 %collective-permute-done.38 = bf16[704,512]{1,0:T(8,128)(2,1)S(1)} collective-permute-done((bf16[704,512]{1,0:T(8,128)(2,1)}, bf16[704,512]{1,0:T(8,128)(2,1)S(1)}, u32[]{:S(2)}, u32[]{:S(2)}) %collective-permute-start.38) | collective-permute-done | bytes 720928 | tf_op jit(solution)/shard_map/ppermute | solution.py:591
  334.3 13.7 %collective-permute-done.43 = bf16[704,512]{1,0:T(8,128)(2,1)S(1)} collective-permute-done((bf16[704,512]{1,0:T(8,128)(2,1)}, bf16[704,512]{1,0:T(8,128)(2,1)S(1)}, u32[]{:S(2)}, u32[]{:S(2)}) %collective-permute-start.43) | collective-permute-done | bytes 720928 | tf_op jit(solution)/shard_map/ppermute | solution.py:591
  350.5 14.0 %collective-permute-done.45 = bf16[704,512]{1,0:T(8,128)(2,1)S(1)} collective-permute-done((bf16[704,512]{1,0:T(8,128)(2,1)S(1)}, bf16[704,512]{1,0:T(8,128)(2,1)S(1)}, u32[]{:S(2)}, u32[]{:S(2)}) %collective-permute-start.45) | collective-permute-done | bytes 720928 | tf_op jit(solution)/shard_map/ppermute | solution.py:591
  373.2 9.3 %collective-permute-done.46 = bf16[128,2048]{1,0:T(8,128)(2,1)S(1)} collective-permute-done((bf16[128,2048]{1,0:T(8,128)(2,1)S(1)}, bf16[128,2048]{1,0:T(8,128)(2,1)S(1)}, u32[]{:S(2)}, u32[]{:S(2)}) %collective-permute-start.46) | collective-permute-done | bytes 524320 | tf_op jit(solution)/shard_map/ppermute | solution.py:591
  397.1 23.5 %shard_map.278 = (bf16[1024,704]{1,0:T(8,128)(2,1)}, bf16[704,1024]{1,0:T(8,128)(2,1)}, bf16[704,1024]{1,0:T(8,128)(2,1)}, bf16[704,1024]{1,0:T(8,128)(2,1)}, bf16[1024,2048]{1,0:T(8,128)(2,1)}) custom-call(bf16[1024,2048]{1,0:T(8,128)(2,1)} %copy-done.95, bf16[1024,2048]{1,0:T(8,128)(2,1)} %copy-done.54, bf16[2,704,512]{2,1,0:T(8,128)(2,1)} %pad_maximum_fusion.8.refs_2_, ...), custom_call_target="tpu_custom_call" | custom-call | flops 14763950080 | bytes 27000832 | tf_op jit(solution)/shard_map/pallas_call | solution.py:82
  420.7 24.1 %shard_map.279 = (bf16[1024,704]{1,0:T(8,128)(2,1)}, bf16[704,1024]{1,0:T(8,128)(2,1)}, bf16[704,1024]{1,0:T(8,128)(2,1)}, bf16[704,1024]{1,0:T(8,128)(2,1)}, bf16[1024,2048]{1,0:T(8,128)(2,1)}) custom-call(bf16[1024,2048]{1,0:T(8,128)(2,1)} %copy-done.93, bf16[1024,2048]{1,0:T(8,128)(2,1)} %constant_dynamic-update-slice_fusion.8.refs_1_.refs_2_, ...), custom_call_target="tpu_custom_call" | custom-call | flops 14763950080 | bytes 27000832 | tf_op jit(solution)/shard_map/pallas_call | solution.py:82
  456.3 10.2 %shard_map.281 = bf16[4,1,704,512]{3,2,1,0:T(8,128)(2,1)} custom-call(bf16[704,1024]{1,0:T(8,128)(2,1)} %get-tuple-element.342.refs_0_, bf16[704,1024]{1,0:T(8,128)(2,1)} %get-tuple-element.343.refs_1_, bf16[1024,2048]{1,0:T(8,128)(2,1)} %constant_dynamic-update-slice_fusion.8.refs_1_.refs_2_, bf16[1024,2048]{1,0:T(8,128)(2,1)} %copy-done.54), custom_call_target="tpu_custom_call" | custom-call | flops 5905580032 | bytes 14155776 | tf_op jit(solution)/shard_map/pallas_call | solution.py:82
  480.9 17.2 %shard_map.283 = bf16[4,2,704,512]{3,2,1,0:T(8,128)(2,1)} custom-call(bf16[704,1024]{1,0:T(8,128)(2,1)} %get-tuple-element.352.refs_0_, bf16[704,1024]{1,0:T(8,128)(2,1)} %get-tuple-element.353.refs_1_, bf16[704,1024]{1,0:T(8,128)(2,1)} %get-tuple-element.354.refs_2_, bf16[704,1024]{1,0:T(8,128)(2,1)} %get-tuple-element.355.refs_3_, ...), custom_call_target="tpu_custom_call" | custom-call | flops 11811160064 | bytes 19922944 | tf_op jit(solution)/shard_map/pallas_call | solution.py:82
  517.1 7.0 shard_map.284.a_ref
  564.7 7.2 collective-permute-start.72
  630.0 12.8 %shard_map.290 = (bf16[1024,1024]{1,0:T(8,128)(2,1)}, bf16[1024,2048]{1,0:T(8,128)(2,1)}) custom-call(bf16[1024,768]{1,0:T(8,128)(2,1)} %get-tuple-element.276.qkv_ref.refs_0_, f32[1024,512]{1,0:T(8,128)} %get-tuple-element.400.refs_1_, bf16[1024,256]{1,0:T(8,128)(2,1)} %get-tuple-element.401.refs_2_, bf16[1024,256]{1,0:T(8,128)(2,1)} %get-tuple-element.402.refs_3_, ...), custom_call_target="tpu_custom_call" | custom-call | flops 4294967296 | bytes 17309736 | tf_op jit(solution)/shard_map/pallas_call | solution.py:82
  652.4 12.7 %shard_map.291 = (bf16[1024,1024]{1,0:T(8,128)(2,1)}, bf16[1024,2048]{1,0:T(8,128)(2,1)}) custom-call(bf16[1024,768]{1,0:T(8,128)(2,1)} %get-tuple-element.262.qkv_ref.refs_0_, f32[1024,512]{1,0:T(8,128)} %get-tuple-element.411.refs_1_, bf16[1024,256]{1,0:T(8,128)(2,1)} %get-tuple-element.412.refs_2_, bf16[1024,256]{1,0:T(8,128)(2,1)} %get-tuple-element.413.refs_3_, ...), custom_call_target="tpu_custom_call" | custom-call | flops 4294967296 | bytes 17309736 | tf_op jit(solution)/shard_map/pallas_call | solution.py:82
  682.6 13.4 %shard_map.293 = bf16[4,512,1024]{2,1,0:T(8,128)(2,1)} custom-call(bf16[1024,2048]{1,0:T(8,128)(2,1)} %constant_dynamic-update-slice_fusion.refs_0_.l0, bf16[1024,2048]{1,0:T(8,128)(2,1)} %copy-done.94, bf16[1024,1024]{1,0:T(8,128)(2,1)} %get-tuple-element.428.r0, bf16[1024,1024]{1,0:T(8,128)(2,1)} %get-tuple-element.429.r1), custom_call_target="tpu_custom_call" | custom-call | flops 8589934592 | bytes 16777216 | tf_op jit(solution)/shard_map/pallas_call | solution.py:82
  720.1 16.4 %collective-permute-done.91 = bf16[256,2048]{1,0:T(8,128)(2,1)S(1)} collective-permute-done((bf16[256,2048]{1,0:T(8,128)(2,1)}, bf16[256,2048]{1,0:T(8,128)(2,1)S(1)}, u32[]{:S(2)}, u32[]{:S(2)}) %collective-permute-start.91) | collective-permute-done | bytes 1048608 | tf_op jit(solution)/shard_map/ppermute | solution.py:591
  760.6 11.8 %collective-permute-done.97 = bf16[256,2048]{1,0:T(8,128)(2,1)} collective-permute-done((bf16[256,2048]{1,0:T(8,128)(2,1)}, bf16[256,2048]{1,0:T(8,128)(2,1)}, u32[]{:S(2)}, u32[]{:S(2)}) %collective-permute-start.97) | collective-permute-done | bytes 1048608 | tf_op jit(solution)/shard_map/ppermute | solution.py:591
  792.3 17.2 %collective-permute-done.100 = bf16[3,704,256]{2,1,0:T(8,128)(2,1)S(1)} collective-permute-done((bf16[3,704,256]{2,1,0:T(8,128)(2,1)S(1)}, bf16[3,704,256]{2,1,0:T(8,128)(2,1)S(1)}, u32[]{:S(2)}, u32[]{:S(2)}) %collective-permute-start.100) | collective-permute-done | bytes 1081376 | tf_op jit(solution)/shard_map/ppermute | solution.py:591
  (636 shorter events, 528.8 us)
Async XLA Ops:
  28.6 32.3 %collective-permute-start.2 = (bf16[640,1024]{1,0:T(8,128)(2,1)}, bf16[640,1024]{1,0:T(8,128)(2,1)}, u32[]{:S(2)}, u32[]{:S(2)}) collective-permute-start(bf16[640,1024]{1,0:T(8,128)(2,1)} %pad_maximum_fusion.12.refs_1_.refs_6_), channel_id=1, source_target_pairs={{0,8},{8,16},{16,24},{1,9},{9,17},{17,25},{2,10},{10,18},{18,26},{... | collective-permute-start | bytes 3932168 | tf_op jit(solution)/shard_map/ppermute | solution.py:591
  33.7 31.6 %collective-permute-start.3 = (bf16[640,1024]{1,0:T(8,128)(2,1)}, bf16[640,1024]{1,0:T(8,128)(2,1)}, u32[]{:S(2)}, u32[]{:S(2)}) collective-permute-start(bf16[640,1024]{1,0:T(8,128)(2,1)} %pad_maximum_fusion.12.refs_1_.refs_6_), channel_id=1, source_target_pairs={{24,16},{16,8},{8,0},{25,17},{17,9},{9,1},{26,18},{18,10},{10,2},{... | collective-permute-start | bytes 3932168 | tf_op jit(solution)/shard_map/ppermute | solution.py:591
  68.2 42.0 %collective-permute-start.9 = (bf16[512,2048]{1,0:T(8,128)(2,1)}, bf16[512,2048]{1,0:T(8,128)(2,1)}, u32[]{:S(2)}, u32[]{:S(2)}) collective-permute-start(bf16[512,2048]{1,0:T(8,128)(2,1)} %pad_maximum_fusion.2), channel_id=1, source_target_pairs={{0,1},{1,0},{2,3},{3,2},{4,5},{5,4},{6,7},{7,6},{8,9},{9,8},{10,11... | collective-permute-start | bytes 6291464 | tf_op jit(solution)/shard_map/ppermute | solution.py:591
  75.6 34.6 %collective-permute-start.8 = (bf16[640,1024]{1,0:T(8,128)(2,1)}, bf16[640,1024]{1,0:T(8,128)(2,1)}, u32[]{:S(2)}, u32[]{:S(2)}) collective-permute-start(bf16[640,1024]{1,0:T(8,128)(2,1)} %collective-permute-done.3), channel_id=1, source_target_pairs={{16,8},{8,0},{17,9},{9,1},{18,10},{10,2},{19,11},{11,3},{20,12},{1... | collective-permute-start | bytes 3932168 | tf_op jit(solution)/shard_map/ppermute | solution.py:591
  119.3 33.0 %collective-permute-start.11 = (bf16[640,1024]{1,0:T(8,128)(2,1)}, bf16[640,1024]{1,0:T(8,128)(2,1)S(1)}, u32[]{:S(2)}, u32[]{:S(2)}) collective-permute-start(bf16[640,1024]{1,0:T(8,128)(2,1)} %collective-permute-done.8), channel_id=1, source_target_pairs={{8,0},{9,1},{10,2},{11,3},{12,4},{13,5},{14,6},{15,7}} | collective-permute-start | bytes 3932168 | tf_op jit(solution)/shard_map/ppermute | solution.py:591
  152.3 35.4 %collective-permute-start.15 = (bf16[704,512]{1,0:T(8,128)(2,1)}, bf16[704,512]{1,0:T(8,128)(2,1)}, u32[]{:S(2)}, u32[]{:S(2)}) collective-permute-start(bf16[704,512]{1,0:T(8,128)(2,1)} %get-tuple-element.265.refs_6_.refs_1_), channel_id=1, source_target_pairs={{0,8},{8,16},{16,24},{1,9},{9,17},{17,25},{2,10},{10,18},{18,26},{... | collective-permute-start | bytes 2162696 | tf_op jit(solution)/shard_map/ppermute | solution.py:591
  154.7 33.0 %collective-permute-start.16 = (bf16[704,512]{1,0:T(8,128)(2,1)}, bf16[704,512]{1,0:T(8,128)(2,1)}, u32[]{:S(2)}, u32[]{:S(2)}) collective-permute-start(bf16[704,512]{1,0:T(8,128)(2,1)} %get-tuple-element.265.refs_6_.refs_1_), channel_id=1, source_target_pairs={{24,16},{16,8},{8,0},{25,17},{17,9},{9,1},{26,18},{18,10},{10,2},{... | collective-permute-start | bytes 2162696 | tf_op jit(solution)/shard_map/ppermute | solution.py:591
  156.5 31.2 %collective-permute-start.17 = (bf16[256,2048]{1,0:T(8,128)(2,1)}, bf16[256,2048]{1,0:T(8,128)(2,1)S(1)}, u32[]{:S(2)}, u32[]{:S(2)}) collective-permute-start(bf16[256,2048]{1,0:T(8,128)(2,1)} %get-tuple-element.266), channel_id=1, source_target_pairs={{0,4},{4,0},{1,5},{5,1},{2,6},{6,2},{3,7},{7,3},{8,12},{12,8},{9,1... | collective-permute-start | bytes 3145736 | tf_op jit(solution)/shard_map/ppermute | solution.py:591
  187.7 32.4 %collective-permute-start.21 = (bf16[704,512]{1,0:T(8,128)(2,1)S(1)}, bf16[704,512]{1,0:T(8,128)(2,1)}, u32[]{:S(2)}, u32[]{:S(2)}) collective-permute-start(bf16[704,512]{1,0:T(8,128)(2,1)S(1)} %get-tuple-element.273), channel_id=1, source_target_pairs={{0,8},{8,16},{16,24},{1,9},{9,17},{17,25},{2,10},{10,18},{18,26},{... | collective-permute-start | bytes 2162696 | tf_op jit(solution)/shard_map/ppermute | solution.py:591
  284.0 40.4 %collective-permute-start.34 = (bf16[256,2176]{1,0:T(8,128)(2,1)}, bf16[256,2176]{1,0:T(8,128)(2,1)S(1)}, u32[]{:S(2)}, u32[]{:S(2)}) collective-permute-start(bf16[256,2176]{1,0:T(8,128)(2,1)} %get-tuple-element.300), channel_id=1, source_target_pairs={{0,4},{4,0},{1,5},{5,1},{2,6},{6,2},{3,7},{7,3},{8,12},{12,8},{9,1... | collective-permute-start | bytes 3342344 | tf_op jit(solution)/shard_map/ppermute | solution.py:591
  285.5 38.9 %collective-permute-start.33 = (bf16[256,2176]{1,0:T(8,128)(2,1)}, bf16[256,2176]{1,0:T(8,128)(2,1)S(1)}, u32[]{:S(2)}, u32[]{:S(2)}) collective-permute-start(bf16[256,2176]{1,0:T(8,128)(2,1)} %get-tuple-element.299), channel_id=1, source_target_pairs={{0,2},{2,0},{1,3},{3,1},{4,6},{6,4},{5,7},{7,5},{8,10},{10,8},{9,1... | collective-permute-start | bytes 3342344 | tf_op jit(solution)/shard_map/ppermute | solution.py:591
  289.4 35.0 %collective-permute-start.38 = (bf16[704,512]{1,0:T(8,128)(2,1)}, bf16[704,512]{1,0:T(8,128)(2,1)S(1)}, u32[]{:S(2)}, u32[]{:S(2)}) collective-permute-start(bf16[704,512]{1,0:T(8,128)(2,1)} %collective-permute-done.26), channel_id=1, source_target_pairs={{16,8},{8,0},{17,9},{9,1},{18,10},{10,2},{19,11},{11,3},{20,12},{1... | collective-permute-start | bytes 2162696 | tf_op jit(solution)/shard_map/ppermute | solution.py:591
  332.1 32.5 %collective-permute-start.39 = (bf16[256,2048]{1,0:T(8,128)(2,1)S(1)}, bf16[256,2048]{1,0:T(8,128)(2,1)S(1)}, u32[]{:S(2)}, u32[]{:S(2)}) collective-permute-start(bf16[256,2048]{1,0:T(8,128)(2,1)S(1)} %get-tuple-element.610), channel_id=1, source_target_pairs={{0,2},{2,0},{1,3},{3,1},{4,6},{6,4},{5,7},{7,5},{8,10},{10,8},{9,1... | collective-permute-start | bytes 3145736 | tf_op jit(solution)/shard_map/ppermute | solution.py:591
  333.0 31.6 %collective-permute-start.40 = (bf16[256,2048]{1,0:T(8,128)(2,1)S(1)}, bf16[256,2048]{1,0:T(8,128)(2,1)S(1)}, u32[]{:S(2)}, u32[]{:S(2)}) collective-permute-start(bf16[256,2048]{1,0:T(8,128)(2,1)S(1)} %get-tuple-element.610), channel_id=1, source_target_pairs={{0,4},{4,0},{1,5},{5,1},{2,6},{6,2},{3,7},{7,3},{8,12},{12,8},{9,1... | collective-permute-start | bytes 3145736 | tf_op jit(solution)/shard_map/ppermute | solution.py:591
  333.6 31.0 %collective-permute-start.41 = (bf16[256,2048]{1,0:T(8,128)(2,1)S(1)}, bf16[256,2048]{1,0:T(8,128)(2,1)S(1)}, u32[]{:S(2)}, u32[]{:S(2)}) collective-permute-start(bf16[256,2048]{1,0:T(8,128)(2,1)S(1)} %get-tuple-element.610), channel_id=1, source_target_pairs={{0,1},{1,0},{2,3},{3,2},{4,5},{5,4},{6,7},{7,6},{8,9},{9,8},{10,11... | collective-permute-start | bytes 3145736 | tf_op jit(solution)/shard_map/ppermute | solution.py:591
  564.6 38.1 %collective-permute-start.76 = (bf16[1024,2048]{1,0:T(8,128)(2,1)}, bf16[1024,2048]{1,0:T(8,128)(2,1)}, u32[]{:S(2)}, u32[]{:S(2)}) collective-permute-start(bf16[1024,2048]{1,0:T(8,128)(2,1)} %shard_map.285), channel_id=1, source_target_pairs={{0,1},{1,0},{2,3},{3,2},{4,5},{5,4},{6,7},{7,6},{8,9},{9,8},{10,11... | collective-permute-start | bytes 12582920 | tf_op jit(solution)/shard_map/ppermute | solution.py:591
  564.7 33.9 %collective-permute-start.72 = (bf16[704,512]{1,0:T(8,128)(2,1)}, bf16[704,512]{1,0:T(8,128)(2,1)}, u32[]{:S(2)}, u32[]{:S(2)}) collective-permute-start(bf16[704,512]{1,0:T(8,128)(2,1)} %get-tuple-element.378), channel_id=1, source_target_pairs={{0,8},{8,16},{1,9},{9,17},{2,10},{10,18},{3,11},{11,19},{4,12},{12... | collective-permute-start | bytes 2162696 | tf_op jit(solution)/shard_map/ppermute | solution.py:591
  606.5 36.3 %collective-permute-start.78 = (bf16[704,512]{1,0:T(8,128)(2,1)}, bf16[704,512]{1,0:T(8,128)(2,1)}, u32[]{:S(2)}, u32[]{:S(2)}) collective-permute-start(bf16[704,512]{1,0:T(8,128)(2,1)} %get-tuple-element.397), channel_id=1, source_target_pairs={{0,8},{8,16},{16,24},{1,9},{9,17},{17,25},{2,10},{10,18},{18,26},{... | collective-permute-start | bytes 2162696 | tf_op jit(solution)/shard_map/ppermute | solution.py:591
  701.2 35.5 %collective-permute-start.92 = (bf16[640,1024]{1,0:T(8,128)(2,1)S(1)}, bf16[640,1024]{1,0:T(8,128)(2,1)}, u32[]{:S(2)}, u32[]{:S(2)}) collective-permute-start(bf16[640,1024]{1,0:T(8,128)(2,1)S(1)} %pad_maximum_fusion.14), channel_id=1, source_target_pairs={{0,8},{1,9},{2,10},{3,11},{4,12},{5,13},{6,14},{7,15}} | collective-permute-start | bytes 3932168 | tf_op jit(solution)/shard_map/ppermute | solution.py:591
  706.7 30.0 %collective-permute-start.93 = (bf16[640,1024]{1,0:T(8,128)(2,1)S(1)}, bf16[640,1024]{1,0:T(8,128)(2,1)}, u32[]{:S(2)}, u32[]{:S(2)}) collective-permute-start(bf16[640,1024]{1,0:T(8,128)(2,1)S(1)} %pad_maximum_fusion.16), channel_id=1, source_target_pairs={{24,16},{25,17},{26,18},{27,19},{28,20},{29,21},{30,22},{31,23}} | collective-permute-start | bytes 3932168 | tf_op jit(solution)/shard_map/ppermute | solution.py:591
  741.5 31.8 %collective-permute-start.95 = (bf16[640,1024]{1,0:T(8,128)(2,1)}, bf16[640,1024]{1,0:T(8,128)(2,1)}, u32[]{:S(2)}, u32[]{:S(2)}) collective-permute-start(bf16[640,1024]{1,0:T(8,128)(2,1)} %get-tuple-element.603), channel_id=1, source_target_pairs={{0,8},{8,16},{1,9},{9,17},{2,10},{10,18},{3,11},{11,19},{4,12},{12... | collective-permute-start | bytes 3932168 | tf_op jit(solution)/shard_map/ppermute | solution.py:591
  743.8 29.5 %collective-permute-start.96 = (bf16[640,1024]{1,0:T(8,128)(2,1)}, bf16[640,1024]{1,0:T(8,128)(2,1)}, u32[]{:S(2)}, u32[]{:S(2)}) collective-permute-start(bf16[640,1024]{1,0:T(8,128)(2,1)} %get-tuple-element.602), channel_id=1, source_target_pairs={{24,16},{16,8},{25,17},{17,9},{26,18},{18,10},{27,19},{19,11},{28,... | collective-permute-start | bytes 3932168 | tf_op jit(solution)/shard_map/ppermute | solution.py:591
  779.3 34.3 %collective-permute-start.99 = (bf16[640,1024]{1,0:T(8,128)(2,1)S(1)}, bf16[640,1024]{1,0:T(8,128)(2,1)S(1)}, u32[]{:S(2)}, u32[]{:S(2)}) collective-permute-start(bf16[640,1024]{1,0:T(8,128)(2,1)S(1)} %add_convert_fusion), channel_id=1, source_target_pairs={{24,16},{16,8},{8,0},{25,17},{17,9},{9,1},{26,18},{18,10},{10,2},{... | collective-permute-start | bytes 3932168 | tf_op jit(solution)/shard_map/ppermute | solution.py:591
  782.4 31.1 %collective-permute-start.98 = (bf16[640,1024]{1,0:T(8,128)(2,1)S(1)}, bf16[640,1024]{1,0:T(8,128)(2,1)S(1)}, u32[]{:S(2)}, u32[]{:S(2)}) collective-permute-start(bf16[640,1024]{1,0:T(8,128)(2,1)S(1)} %add_convert_fusion.1), channel_id=1, source_target_pairs={{0,8},{8,16},{16,24},{1,9},{9,17},{17,25},{2,10},{10,18},{18,26},{... | collective-permute-start | bytes 3932168 | tf_op jit(solution)/shard_map/ppermute | solution.py:591
  (194 other events, 2531.0 us)

commit v3 on v2

v3 whole, which is shorter than its diff:
```python
import math

import jax
import jax.numpy as jnp
from jax import lax
from jax.experimental import pallas as pl
from jax.experimental.layout import Layout, with_layout_constraint
from jax.experimental.pallas import tpu as pltpu
from jax.sharding import Mesh
from jax.sharding import PartitionSpec as P

BLOCK = 256
EPS = 1e-06
MU = 0.9
BETA = 0.8
HIGH = lax.Precision.HIGHEST
BF = jnp.bfloat16
F32 = jnp.float32
SWAP = [(0, 1), (1, 0)]
XORS = (0, 2, 4, 6, 1, 3, 5, 7)


def dot(a, b, dims=((1,), (0,))):
    return lax.dot_general(a, b, (dims, ((), ())), preferred_element_type=F32)


def inverse_rms(v):
    return lax.rsqrt(jnp.mean(v * v, axis=-1, keepdims=True) + EPS)


def srms_back(v, grad):
    r = inverse_rms(v)
    return r * grad - v * (r * r * r) * jnp.mean(grad * v, axis=-1, keepdims=True)


def renew(weight, moment, average, grad, fan, tokens):
    step = 0.4 / math.sqrt(fan * tokens)
    moment_new = MU * moment + grad
    weight_new = weight - step * (grad + MU * moment_new)
    average_new = BETA * average + (1.0 - BETA) * weight_new
    return (moment_new, weight_new, average_new)


ROWS = 256
HALF = 4
HD = 128
VMEM = 56 * 1024 * 1024
EXTRA = 128


def pin(v):
    return with_layout_constraint(v, Layout(major_to_minor=tuple(range(v.ndim))))


def after(value, *done):
    return lax.optimization_barrier((value,) + done)[0]


class Clock:
    def __init__(self):
        self.token = jnp.zeros((8, 128), F32)

    def now(self, *values):
        out = [lax.optimization_barrier((v, self.token))[0] for v in values]
        return out if len(out) > 1 else out[0]

    def end(self, *done):
        self.token = lax.optimization_barrier((self.token,) + done)[0]


def block_spec(shape):
    return pl.BlockSpec(shape, lambda i: (i,) + (0,) * (len(shape) - 1))


def whole_spec(a):
    return pl.BlockSpec(a.shape, lambda i: (0,) * a.ndim, pipeline_mode=pl.Buffered(1))


def scalar_spec():
    return pl.BlockSpec(memory_space=pltpu.SMEM)


def call(kernel, steps, ins, outs, flops):
    moved = sum(a.size * a.dtype.itemsize for a, _ in ins)
    moved += sum(math.prod(s) * jnp.dtype(d).itemsize for s, d, _ in outs)
    return pl.pallas_call(
        kernel,
        grid=(steps,),
        in_specs=[s for _, s in ins],
        out_specs=[b if isinstance(b, pl.BlockSpec) else block_spec(b) for _, _, b in outs],
        out_shape=[jax.ShapeDtypeStruct(s, d) for s, d, _ in outs],
        compiler_params=pltpu.CompilerParams(
            vmem_limit_bytes=VMEM, dimension_semantics=("arbitrary",)
        ),
        cost_estimate=pl.CostEstimate(
            flops=int(flops), bytes_accessed=int(moved), transcendentals=0
        ),
    )(*[a for a, _ in ins])


NT = ((1,), (1,))
TN = ((0,), (0,))


def mask_of(fade, seg_c, seg_r):
    return jnp.where(seg_c == seg_r, fade, 0.0)


def pair_spec(shape, late):
    if late:
        return pl.BlockSpec(shape, lambda i: (jnp.maximum(i - HALF, 0),) + (0,) * (len(shape) - 1))
    return pl.BlockSpec(shape, lambda i: (jnp.minimum(i, HALF - 1),) + (0,) * (len(shape) - 1))


def half_spec(shape, h):
    return pl.BlockSpec(shape, lambda i: (i + h * HALF,) + (0,) * (len(shape) - 1))


def project(n1, w_in, at):
    own = at.own
    cols = own * HD
    parts = len(w_in)
    width = n1[0].shape[1]
    deep = width // parts

    def kernel(*refs):
        a_ref, b_ref, w_refs = refs[0], refs[1], refs[2 : 2 + parts]
        seg_ref, ramp_ref, last_ref, reach_ref = refs[2 + parts : 6 + parts]
        raw_ref, gate_ref, qkv_ref, term_ref, leaving_ref = refs[6 + parts :]
        i = pl.program_id(0)
        pre = None
        for k in range(parts):
            some = slice(k * deep, (k + 1) * deep)
            x = jnp.where(i < HALF, a_ref[:, some], b_ref[:, some])
            new = dot(x, w_refs[k][...])
            pre = new if pre is None else pre + new
        pq, pk, pv = pre[:, :cols], pre[:, cols : 2 * cols], pre[:, 2 * cols : 3 * cols]
        raw_ref[...] = pre[:, : 2 * cols]
        gate_ref[...] = pre[:, 3 * cols :]
        key = (pk * jax.nn.sigmoid(pk)).astype(BF)
        value = pv.astype(BF)
        qkv_ref[:, :cols] = (pq * jax.nn.sigmoid(pq)).astype(BF)
        qkv_ref[:, cols : 2 * cols] = key
        qkv_ref[:, 2 * cols :] = value

        @pl.when(i == 0)
        def _():
            leaving_ref[...] = jnp.zeros_like(leaving_ref)

        for j in range(own):
            leave = jnp.where(seg_ref[0] == last_ref[i], ramp_ref[:, own + j : own + j + 1], 0.0)
            head = slice(j * HD, (j + 1) * HD)
            scaled = (key[:, head].astype(F32) * leave).astype(BF)
            term = dot(scaled, value[:, head], TN)
            term_ref[0, j] = term
            leaving_ref[j] += reach_ref[j, i] * term

    some = pl.BlockSpec((deep, 4 * cols), lambda i: (0, 0), pipeline_mode=pl.Buffered(1))
    ins = [(v, pair_spec((ROWS, width), late)) for late, v in enumerate(n1)]
    ins += [(w, some) for w in w_in]
    ins += [(at.cols, block_spec((1, ROWS, 1))), (at.ramps, whole_spec(at.ramps))]
    ins += [(v, scalar_spec()) for v in (at.last, at.out_reach)]
    n = 2 * HALF
    outs = [
        ((n * ROWS, 2 * cols), F32, (ROWS, 2 * cols)),
        ((n * ROWS, cols), F32, (ROWS, cols)),
        ((n * ROWS, 3 * cols), BF, (ROWS, 3 * cols)),
        ((n, own, HD, HD), F32, (1, own, HD, HD)),
        ((own, HD, HD), F32, pl.BlockSpec((own, HD, HD), lambda i: (0, 0, 0))),
    ]
    return call(kernel, n, ins, outs, 4 * n1[0].size * 4 * cols)


def combine(weights, terms, more, reach):
    state = reach * more
    for c in range(2 * HALF):
        state = state + weights(c) * terms(c)
    return state


def attend(h, qkv, gate, term, entering, w_out, at):
    own = at.own
    cols = own * HD
    width = w_out.shape[1]

    def kernel(
        qkv_ref, gate_ref, term_ref, more_ref, w_ref, sc_ref, sr_ref, fade_ref, ramp_ref,
        prev_ref, inner_ref, reach_ref, attn_ref, branch_ref, state_ref,
    ):
        i = pl.program_id(0) + h * HALF
        for j in range(own):
            head = slice(j * HD, (j + 1) * HD)
            q = qkv_ref[:, j * HD : (j + 1) * HD]
            k = qkv_ref[:, cols + j * HD : cols + (j + 1) * HD]
            v = qkv_ref[:, 2 * cols + j * HD : 2 * cols + (j + 1) * HD]
            state = combine(
                lambda c: inner_ref[j, i * 2 * HALF + c],
                lambda c: term_ref[c, j],
                more_ref[j],
                reach_ref[j, i],
            ).astype(BF)
            state_ref[0, j] = state
            enter = jnp.where(sc_ref[0] == prev_ref[i], ramp_ref[:, j : j + 1], 0.0)
            weights = (dot(q, k, NT) * mask_of(fade_ref[j], sc_ref[0], sr_ref[0])).astype(BF)
            attn_ref[:, head] = dot(weights, v) + enter * dot(q, state)
        attn = attn_ref[...]
        branch_ref[:, :width] = dot((attn * gate_ref[...]).astype(BF), w_ref[...]).astype(BF)
        rest = jnp.sum(attn * attn, axis=1, keepdims=True)
        lane = lax.broadcasted_iota(jnp.int32, (ROWS, EXTRA), 1)
        strip = jnp.zeros((ROWS, EXTRA), F32)
        for n in range(3):
            top = rest.astype(BF).astype(F32)
            strip = jnp.where(lane == n, top, strip)
            rest = rest - top
        branch_ref[:, width:] = strip.astype(BF)

    n = HALF
    ins = [
        (qkv, half_spec((ROWS, 3 * cols), h)),
        (gate, half_spec((ROWS, cols), h)),
        (term, whole_spec(term)),
        (entering, whole_spec(entering)),
        (w_out, whole_spec(w_out)),
        (at.cols, half_spec((1, ROWS, 1), h)),
        (at.rows, half_spec((1, 1, ROWS), h)),
        (at.fade, whole_spec(at.fade)),
        (at.ramps, whole_spec(at.ramps)),
    ] + [(v, scalar_spec()) for v in (at.prev, at.inner, at.in_reach)]
    outs = [
        ((n * ROWS, cols), F32, (ROWS, cols)),
        ((n * ROWS, width + EXTRA), BF, (ROWS, width + EXTRA)),
        ((n, own, HD, HD), BF, (1, own, HD, HD)),
    ]
    return call(kernel, n, ins, outs, 2 * n * ROWS * cols * (width + 2 * ROWS))


def sglu_rows(n2, g, w_pair, w_third):
    parts = len(w_pair)
    _, hidden, deep = w_pair[0].shape
    block = 2 * ROWS

    def kernel(*refs):
        x_ref, g_ref = refs[:2]
        both, three = (refs[2 + k * parts : 2 + (k + 1) * parts] for k in range(2))
        prod_ref, prod_t, gf_t, gs_t, back_ref = refs[2 + 2 * parts :]
        first = second = grad = None
        for k in range(parts):
            at = slice(k * deep, (k + 1) * deep)
            x, gk = x_ref[:, at], g_ref[:, at]
            a, b, c = dot(x, both[k][0], NT), dot(x, both[k][1], NT), dot(gk, three[k][...], NT)
            first = a if first is None else first + a
            second = b if second is None else second + b
            grad = c if grad is None else grad + c
        prod = (first * second).astype(BF)
        gf = (grad * second).astype(BF)
        gs = (grad * first).astype(BF)
        prod_ref[...] = prod
        prod_t[...] = prod.T
        gf_t[...] = gf.T
        gs_t[...] = gs.T
        for k in range(parts):
            at = slice(k * deep, (k + 1) * deep)
            back_ref[:, at] = (dot(gf, both[k][0]) + dot(gs, both[k][1])).astype(BF)

    n = n2.shape[0] // block
    width = n2.shape[1]
    ins = [(n2, block_spec((block, width))), (g, block_spec((block, width)))]
    ins += [(w, whole_spec(w)) for w in w_pair + w_third]
    outs = [((n * block, hidden), BF, (block, hidden))]
    turned = pl.BlockSpec((hidden, block), lambda i: (0, i))
    outs += [((hidden, n * block), BF, turned)] * 3
    outs += [((n * block, width), BF, (block, width))]
    return call(kernel, n, ins, outs, 10 * n2.size * hidden)


def sglu_last(product, w_third):
    parts = len(w_third)
    deep = w_third[0].shape[1]
    block = 2 * ROWS

    def kernel(*refs):
        for k in range(parts):
            refs[-1][:, k * deep : (k + 1) * deep] = dot(refs[0][...], refs[1 + k][...]).astype(BF)

    n, width = product.shape[0] // block, parts * deep
    ins = [(product, block_spec((block, product.shape[1])))]
    ins += [(w, whole_spec(w)) for w in w_third]
    return call(
        kernel, n, ins, [((n * block, width), BF, (block, width))], 2 * product.size * width
    )[0]


def attend_back_rows(gb, w_out, attn, gate, qkv, at):
    own = at.own
    cols = own * HD
    width = w_out.shape[1]

    def kernel(
        gb_a, gb_b, w_ref, attn_a, attn_b, gate_ref, qkv_ref, sc_ref, ramp_ref, prev_ref, reach_ref,
        ga_ref, gg_ref, mixed_ref, term_ref, leaving_ref,
    ):
        i = pl.program_id(0)
        early = i < HALF
        extra = jnp.where(early, gb_a[:, width:], gb_b[:, width:]).astype(F32)
        r = extra[:, 0:1] + extra[:, 1:2] + extra[:, 2:3]
        pull = extra[:, 3:4] + extra[:, 4:5] + extra[:, 5:6]
        gm = dot(jnp.where(early, gb_a[:, :width], gb_b[:, :width]), w_ref[...], NT)
        attn, gate = jnp.where(early, attn_a[...], attn_b[...]), gate_ref[...]
        normed = r * attn
        gg_ref[...] = (gm * normed).astype(BF)
        mixed_ref[...] = (normed * gate).astype(BF)
        ga = (r * (gm * gate) - attn * pull).astype(BF)
        ga_ref[...] = ga

        @pl.when(i == 0)
        def _():
            leaving_ref[...] = jnp.zeros_like(leaving_ref)

        for j in range(own):
            enter = jnp.where(sc_ref[0] == prev_ref[i], ramp_ref[:, j : j + 1], 0.0)
            q = qkv_ref[:, j * HD : (j + 1) * HD].astype(F32)
            term = dot((q * enter).astype(BF), ga[:, j * HD : (j + 1) * HD], TN)
            term_ref[0, j] = term
            leaving_ref[j] += reach_ref[j, i] * term

    n = 2 * HALF
    ins = [(v, pair_spec((ROWS, v.shape[1]), late)) for late, v in enumerate(gb)]
    ins += [(w_out, whole_spec(w_out))]
    ins += [(v, pair_spec((ROWS, cols), late)) for late, v in enumerate(attn)]
    ins += [
        (gate, block_spec((ROWS, cols))),
        (qkv, block_spec((ROWS, 3 * cols))),
        (at.cols, block_spec((1, ROWS, 1))),
        (at.ramps, whole_spec(at.ramps)),
    ] + [(v, scalar_spec()) for v in (at.prev, at.in_reach)]
    outs = [((n * ROWS, cols), BF, (ROWS, cols))] * 3
    outs += [((n, own, HD, HD), F32, (1, own, HD, HD))]
    outs += [((own, HD, HD), F32, pl.BlockSpec((own, HD, HD), lambda i: (0, 0, 0)))]
    return call(kernel, n, ins, outs, 2 * n * ROWS * cols * width)


def project_back(h, qkv, raw, ga, gg, state, term, entering, w_in, width, at):
    own = at.own
    cols = own * HD
    parts = len(w_in)
    deep = width // parts

    def kernel(*refs):
        qkv_ref, raw_ref, ga_ref, gg_ref, state_ref, term_ref, more_ref = refs[:7]
        w_refs = refs[7 : 7 + parts]
        sc_ref, sr_ref, fade_ref, ramp_ref = refs[7 + parts : 11 + parts]
        prev_ref, last_ref, inner_ref, reach_ref, gp_ref, back_ref = refs[11 + parts :]
        i = pl.program_id(0) + h * HALF
        for j in range(own):
            head = slice(j * HD, (j + 1) * HD)
            kt = slice(cols + j * HD, cols + (j + 1) * HD)
            vt = slice(2 * cols + j * HD, 2 * cols + (j + 1) * HD)
            q, k, v = qkv_ref[:, head], qkv_ref[:, kt], qkv_ref[:, vt]
            g = ga_ref[:, head]
            mask = mask_of(fade_ref[j], sc_ref[0], sr_ref[0])
            enter = jnp.where(sc_ref[0] == prev_ref[i], ramp_ref[:, j : j + 1], 0.0)
            leave = jnp.where(sc_ref[0] == last_ref[i], ramp_ref[:, own + j : own + j + 1], 0.0)
            later = combine(
                lambda c: inner_ref[j, c * 2 * HALF + i],
                lambda c: term_ref[c, j],
                more_ref[j],
                reach_ref[j, i],
            ).astype(BF)
            weights = (dot(q, k, NT) * mask).astype(BF)
            gs = (dot(g, v, NT) * mask).astype(BF)
            gq = dot(gs, k) + enter * dot(g, state_ref[0, j], NT)
            gk = dot(gs, q, TN) + leave * dot(v, later, NT)
            gv = dot(weights, g, TN) + leave * dot(k, later)
            rq, rk = raw_ref[:, head], raw_ref[:, kt]
            sq, sk = jax.nn.sigmoid(rq), jax.nn.sigmoid(rk)
            gp_ref[:, head] = (gq * (sq * (1.0 + rq * (1.0 - sq)))).astype(BF)
            gp_ref[:, kt] = (gk * (sk * (1.0 + rk * (1.0 - sk)))).astype(BF)
            gp_ref[:, vt] = gv.astype(BF)
        gp_ref[:, 3 * cols :] = gg_ref[...]
        for k in range(parts):
            some = slice(k * deep, (k + 1) * deep)
            back_ref[:, some] = dot(gp_ref[...], w_refs[k][...], NT).astype(BF)

    n = HALF
    some = pl.BlockSpec((deep, 4 * cols), lambda i: (0, 0), pipeline_mode=pl.Buffered(1))
    ins = [
        (qkv, half_spec((ROWS, 3 * cols), h)),
        (raw, half_spec((ROWS, 2 * cols), h)),
        (ga, half_spec((ROWS, cols), h)),
        (gg, half_spec((ROWS, cols), h)),
        (state, block_spec((1, own, HD, HD))),
        (term, whole_spec(term)),
        (entering, whole_spec(entering)),
    ] + [(w, some) for w in w_in]
    ins += [
        (at.cols, half_spec((1, ROWS, 1), h)),
        (at.rows, half_spec((1, 1, ROWS), h)),
        (at.fade, whole_spec(at.fade)),
        (at.ramps, whole_spec(at.ramps)),
    ]
    ins += [(v, scalar_spec()) for v in (at.prev, at.last, at.inner, at.out_reach)]
    outs = [
        ((n * ROWS, 4 * cols), BF, (ROWS, 4 * cols)),
        ((n * ROWS, width), BF, (ROWS, width)),
    ]
    return call(kernel, n, ins, outs, 2 * n * ROWS * 4 * cols * width)


def one_by_one(count, shape):
    spec = pl.BlockSpec(shape, lambda i: (0,) * len(shape), pipeline_mode=pl.Buffered(1))
    return [(shape, BF, spec) for _ in range(count)]


def grads_by_left(left, right, more):
    n = len(more)
    cut, cols = left[0].shape[1] // n, right[0].shape[1]

    def kernel(*refs):
        l0, l1, r0, r1 = refs[:4]
        grad = (dot(l0[...], r0[...], TN) + dot(l1[...], r1[...], TN)).astype(BF)
        for k in range(n):

            @pl.when(pl.program_id(0) == k)
            def _():
                refs[4 + n + k][:cut] = grad
                refs[4 + n + k][cut:] = refs[4 + k][...]

    ins = [(a, pl.BlockSpec((a.shape[0], cut), lambda i: (0, i))) for a in left]
    ins += [(a, whole_spec(a)) for a in (*right, *more)]
    outs = one_by_one(n, (cut + more[0].shape[0], cols))
    return call(kernel, n, ins, outs, 4 * left[0].size * cols)


def grads_by_right(lefts, right, cut, width):
    count = len(lefts)
    n = width // cut
    tall = lefts[0][0].shape[0]

    def kernel(*refs):
        r0, r1 = refs[2 * count : 2 * count + 2]
        outs = refs[2 * count + 2 :]
        for m in range(count):
            l0, l1 = refs[2 * m : 2 * m + 2]
            grad = (dot(l0[...], r0[...]) + dot(l1[...], r1[...])).astype(BF)
            for k in range(n):

                @pl.when(pl.program_id(0) == k)
                def _():
                    outs[k][m] = grad

    ins = [(a, whole_spec(a)) for left in lefts for a in left]
    ins += [(a, pl.BlockSpec((a.shape[0], cut), lambda i: (0, i))) for a in right]
    outs = one_by_one(n, (count, tall, cut))
    return call(kernel, n, ins, outs, 4 * count * right[0].size * tall)


def grads_out(left, right, width):
    def kernel(l0, l1, r0, r1, out):
        out[...] = (dot(l0[...], r0[...], TN) + dot(l1[...], r1[...], TN)).astype(BF)

    cut, (rows, tall) = width // 4, left.shape
    spec = lambda rows: pl.BlockSpec((rows, cut), lambda i: (0, i))
    half = lambda k: pl.BlockSpec((rows // 2, tall), lambda i: (k, 0))
    ins = [(left, half(k)) for k in (0, 1)] + [(a, spec(a.shape[0])) for a in right]
    return call(kernel, 4, ins, [((tall, width), BF, spec(tall))], 2 * left.size * width)[0]


def add_strips(width, *parts):
    total = parts[0][:, :width].astype(F32)
    for p in parts[1:]:
        total = total + p[:, :width].astype(F32)
    out = [total.astype(BF)]
    if parts[0].shape[1] > width:
        rest = 0.0
        for p in parts:
            for n in range(3):
                rest = rest + p[:, width + n : width + n + 1].astype(F32)
        lane = lax.broadcasted_iota(jnp.int32, (total.shape[0], EXTRA), 1)
        strip = jnp.zeros((total.shape[0], EXTRA), F32)
        for n in range(3):
            top = rest.astype(BF).astype(F32)
            strip = jnp.where(lane == n, top, strip)
            rest = rest - top
        out.append(strip.astype(BF))
    return out


def add_last(a, b, width):
    n, wide = a.shape[0] // ROWS, a.shape[1]
    half = ROWS // 2

    def kernel(a_ref, b_ref, low_ref, high_ref):
        parts = add_strips(width, a_ref[...], b_ref[...])
        for v, at in zip(parts, (slice(0, width), slice(width, wide))):
            low_ref[:, at] = v[:half]
            high_ref[:, at] = v[half:]

    block = pl.BlockSpec((ROWS, wide), lambda i: (n - 1, 0))
    one = pl.BlockSpec((half, wide), lambda i: (0, 0))
    return call(kernel, 1, [(a, block), (b, block)], [((half, wide), BF, one)] * 2, ROWS * wide)


def add_halves(a, b, u, v, width):
    wide = a.shape[1]
    half = ROWS // 2

    def kernel(a2, a4, b2, b4, u_ref, v_ref, to_2, to_4):
        low, high = slice(0, half), slice(half, ROWS)
        for out, rows, terms in (
            (to_2, low, (a2[low], b2[low])),
            (to_2, high, (a2[high], b2[high], v_ref[...])),
            (to_4, low, (a4[low], b4[low], u_ref[...])),
            (to_4, high, (a4[high], b4[high])),
        ):
            parts = add_strips(width, *terms)
            for p, at in zip(parts, (slice(0, width), slice(width, wide))):
                out[rows, at] = p

    spec = lambda k: pl.BlockSpec((ROWS, wide), lambda i: (k, 0))
    ins = [(t, spec(k)) for t in (a, b) for k in (1, 2)] + [(u, whole_spec(u)), (v, whole_spec(v))]
    return call(kernel, 1, ins, [((ROWS, wide), BF, spec(0))] * 2, ROWS * wide)


def strip_of(column):
    lane = lax.broadcasted_iota(jnp.int32, (column[0].shape[0], EXTRA), 1)
    strip = jnp.zeros(lane.shape, F32)
    for m, rest in enumerate(column):
        for n in range(3):
            top = rest.astype(BF).astype(F32)
            strip = jnp.where(lane == 3 * m + n, top, strip)
            rest = rest - top
    return strip.astype(BF)


def mid_rows(sums, inputs, dest):
    width = inputs.shape[1]
    cut = width // 4
    block = ROWS // 2

    def kernel(a, b, c, d, x_ref, dest_ref, mid_ref, branch_ref, scale_ref, norm_ref):
        branch = square = None
        for ref in (a, b, c, d):
            part = ref[:, :width].astype(F32)
            extra = ref[:, width:].astype(F32)
            more = extra[:, 0:1] + extra[:, 1:2] + extra[:, 2:3]
            branch = part if branch is None else branch + part
            square = more if square is None else square + more
        r = lax.rsqrt(square / width + EPS)
        mid = x_ref[...].astype(F32) + r * branch
        branch_ref[...] = branch.astype(BF)
        scale_ref[...] = jnp.broadcast_to(r, (block, EXTRA))
        mid_ref[...] = mid
        norm = (mid * inverse_rms(mid)).astype(BF)
        for p in range(4):
            to = pl.ds(pl.multiple_of(dest_ref[p] * cut, cut), cut)
            norm_ref[:, to] = norm[:, p * cut : (p + 1) * cut]

    ins = [(v, block_spec((block, width + EXTRA))) for v in sums]
    ins += [(inputs, block_spec((block, width))), (dest, scalar_spec())]
    outs = [
        ((ROWS, width), F32, (block, width)),
        ((ROWS, width), BF, (block, width)),
        ((ROWS, EXTRA), F32, (block, EXTRA)),
        ((ROWS, width), BF, (block, width)),
    ]
    return call(kernel, 2, ins, outs, 20 * ROWS * width)


def mid_back_rows(sums, out_grad, mid, branch, scale, dest):
    width = mid.shape[1]
    cut = width // 4
    block = ROWS // 2

    def kernel(a, b, c, d, g_ref, mid_ref, branch_ref, scale_ref, dest_ref, grad_ref, out_ref):
        parts = []
        for p in range(4):
            at = pl.ds(pl.multiple_of(dest_ref[p] * cut, cut), cut)
            part = a[:, at].astype(F32)
            for ref in (b, c, d):
                part = part + ref[:, at].astype(F32)
            parts.append(part)
        grad = g_ref[...].astype(F32) + srms_back(mid_ref[...], jnp.concatenate(parts, axis=1))
        grad_ref[...] = grad
        low = grad.astype(BF)
        out_ref[:, :width] = low
        inward = low.astype(F32) * branch_ref[...].astype(F32)
        inward = jnp.mean(inward, axis=1, keepdims=True)
        r = scale_ref[:, 0:1]
        out_ref[:, width:] = strip_of([r, r * r * r * inward])

    ins = [(v, block_spec((block, width))) for v in (*sums, out_grad, mid, branch)]
    ins += [(scale, block_spec((block, EXTRA))), (dest, scalar_spec())]
    outs = [
        ((ROWS, width), F32, (block, width)),
        ((ROWS, width + EXTRA), BF, (block, width + EXTRA)),
    ]
    return call(kernel, 2, ins, outs, 20 * ROWS * width)


def renew_turned(grad, weight, moment, average, fan, tokens):
    few, total = weight.shape
    block = 16

    def kernel(g_ref, w_ref, m_ref, a_ref, m_new, w_new, a_new):
        for p in range(8):
            for t in range(4):
                for j in range(2):
                    col = t * (total // 4) + (8 * (p % 2) + 4 * j + p // 2) * HD
                    to = slice(col, col + HD)
                    at = slice((2 * t + j) * HD, (2 * t + j + 1) * HD)
                    new = renew(
                        w_ref[:, to], m_ref[:, to], a_ref[:, to], g_ref[p, :, at].astype(F32),
                        fan, tokens,
                    )
                    m_new[:, to], w_new[:, to], a_new[:, to] = new

    ins = [(grad, pl.BlockSpec((8, block, grad.shape[2]), lambda i: (0, i, 0)))]
    ins += [(v, block_spec((block, total))) for v in (weight, moment, average)]
    outs = [((few, total), F32, (block, total))] * 3
    return call(kernel, few // block, ins, outs, 10 * weight.size)


def cut4(v, axis):
    n = v.shape[axis] // 4
    return [lax.slice_in_dim(v, k * n, (k + 1) * n, axis=axis) for k in range(4)]


def strip_sum(v):
    strip = v[:, v.shape[1] - EXTRA :].astype(F32)
    return strip[:, 0:1] + strip[:, 1:2] + strip[:, 2:3]


def pieces(v):
    out = []
    for _ in range(3):
        top = lax.reduce_precision(v, 8, 7)
        out.append(top.astype(BF))
        v = v - top
    return out


class Places:
    def __init__(self, plan, seq_lengths, decay_rate, rows):
        size = plan.size
        group_rows = size * rows
        tokens = group_rows * plan.groups
        ends = jnp.cumsum(seq_lengths)

        def seg_at(place):
            mark = jnp.sum((place[..., None] >= ends).astype(jnp.int32), axis=-1)
            return jnp.where(place < 0, -1, mark)

        first_block = plan.group * size
        blocks = first_block + plan.slot_ids
        seg = seg_at(blocks[:, None] * rows + jnp.arange(rows, dtype=jnp.int32)[None, :])
        prev = seg_at(blocks * rows - 1)
        last = seg[:, rows - 1]
        head_ids = plan.head_ids if hasattr(plan, "head_ids") else plan.own * plan.p + jnp.arange(plan.own)
        rate = jnp.take(decay_rate, head_ids)

        def reach(gap, same):
            return jnp.where(
                same & (gap >= 0), jnp.exp(-rate[:, None, None] * (rows * jnp.maximum(gap, 0))), 0.0
            )

        inner = reach(
            (blocks[:, None] - blocks[None, :] - 1).astype(F32)[None],
            (prev[:, None] == last[None, :])[None],
        )
        border = seg_at((first_block + size) * rows - 1)
        out_reach = reach(
            (first_block + size - 1 - blocks).astype(F32)[None, None], (last == border)[None, None]
        )[:, 0]
        entry = seg_at(first_block * rows - 1)
        in_reach = reach((blocks - first_block).astype(F32)[None, None], (prev == entry)[None, None])[
            :, 0
        ]
        longest = tokens // 4
        hops = min(-(-longest // group_rows), plan.groups - 1)

        def hop_factor(j, ahead):
            if ahead:
                here, there = border, seg_at((first_block + j * size) * rows - 1)
            else:
                here, there = entry, seg_at((first_block - (j - 1) * size) * rows - 1)
            return jnp.where(here == there, jnp.exp(-rate * ((j - 1) * group_rows)), 0.0)

        def bring(total, ahead):
            n = plan.groups
            got = jnp.zeros_like(total)
            for j in range(1, hops + 1):
                pairs = [(i + j, i) if ahead else (i, i + j) for i in range(n - j)]
                part = lax.ppermute(total, plan.fs, pairs)
                got = got + hop_factor(j, ahead)[:, None, None] * part
            return got

        self.bring, self.hop = bring, hop_factor
        self.inner = inner.reshape(inner.shape[0], -1)
        self.out_reach, self.in_reach = out_reach, in_reach
        self.own = plan.own
        self.cols, self.rows = seg[:, :, None], seg[:, None, :]
        self.prev, self.last = prev, last
        step = jnp.arange(rows).astype(F32)
        spread = step[:, None] - step[None, :]
        fade = jnp.exp(-rate[:, None, None] * jnp.maximum(spread, 0.0)[None])
        self.fade = jnp.where((spread >= 0)[None], fade, 0.0)
        ramps = [jnp.exp(-rate[None] * step[:, None]), jnp.exp(-rate[None] * (rows - step)[:, None])]
        blank = jnp.zeros((rows, EXTRA - 2 * plan.own), F32)
        self.ramps = jnp.concatenate(ramps + [blank], axis=1)


class Square:
    def __init__(self):
        self.tp = ("y", "x", "c")
        self.fs = ("z",)
        self.size = 8
        self.groups = 4

    def begin(self):
        self.z = lax.axis_index("z")
        self.y = lax.axis_index("y")
        self.c = lax.axis_index("c")
        self.p = lax.axis_index(self.tp)
        self.q = self.p // 2
        self.group = self.z
        self.slot_ids = self.p ^ jnp.array(XORS, jnp.int32)
        self.head_ids = 8 * self.c + 4 * jnp.arange(2) + self.q

    def turn(self, v):
        wide = v.shape[1] // 4
        return jnp.concatenate(
            [
                lax.dynamic_slice_in_dim(v, ((self.z - k) % 4) * wide, wide, axis=1)
                for k in range(4)
            ],
            axis=1,
        )

    def places(self):
        return (self.z - jnp.arange(4, dtype=jnp.int32)) % 4

    def slots(self, own, one, two, three):
        return [
            own,
            pin(jnp.where(self.z >= 1, one[0], three[1])),
            pin(jnp.where(self.z >= 2, two[0], two[1])),
            pin(jnp.where(self.z >= 3, three[0], one[1])),
        ]

    def by_y(self, mine, got, axis):
        first = self.y == 0
        parts = [jnp.where(first, mine, got), jnp.where(first, got, mine)]
        return pin(jnp.concatenate(parts, axis=axis))

    def of_y(self, one, two):
        first = self.y == 0
        return pin(jnp.where(first, one, two)), pin(jnp.where(first, two, one))


def over(axis, pairs=SWAP):
    return lambda v: pin(lax.ppermute(pin(v), axis, pairs))


to_x, to_y, to_core = over("x"), over("y"), over("c")


def spread(pair, step):
    up = over("z", [(i, i + 1) for i in range(step, 3)])
    down = over("z", [(3 - i, 2 - i) for i in range(step, 3)])
    return up(pair[0]), down(pair[1])


def gather(up, down, step):
    go_up = over("z", [(i, i + 1) for i in range(step)])
    go_down = over("z", [(3 - i, 2 - i) for i in range(step)])
    return go_up(up), go_down(down)


def plus(a, b):
    return (a.astype(F32) + b.astype(F32)).astype(BF)


def square_layer(plan, places, lengths, inputs, out_grad, attn_in, attn_out, sglu_in, sglu_out):
    rows, width = inputs.shape
    h2 = rows // 2
    cut = width // 4
    clock = Clock()
    now, end = clock.now, clock.end

    def pick(slots, plane):
        return lax.dynamic_index_in_dim(slots, (plan.z - plane) % 4, 0, False)

    xf = inputs.astype(F32)
    n1 = pin(plan.turn((xf * inverse_rms(xf)).astype(BF)))
    og = pin(plan.turn(out_grad))
    few = attn_in.shape[0]
    view = attn_in.astype(BF).reshape(few, 4, 2, 2, 4, HD).transpose(4, 2, 0, 1, 3, 5)
    own_in = lax.all_to_all(view.reshape(8, few, -1), plan.tp, 0, 0, tiled=True)
    own_in = own_in.reshape(8 * few, -1)
    deep, across = own_in.shape
    own_out = attn_out.astype(BF)
    own_w = pin(jnp.concatenate([own_in, own_out[:, :across], own_out[:, across:]]))
    end(own_w, n1, og)

    a_w, a_n1 = now(own_w, n1)
    w1 = spread((a_w, a_w), 0)
    nx, ny = to_x(a_n1), to_y(a_n1)
    at = places(now(lengths))
    hid = sglu_in.shape[2] // 2
    three = pin(now(sglu_in).astype(BF)).swapaxes(1, 2)
    three = jnp.concatenate([three, sglu_out.astype(BF)[None]])
    my_three, to_three = plan.of_y(three[:, :hid], three[:, hid:])
    tables = [at.cols, at.rows, at.prev, at.last, at.fade, at.ramps]
    tables += [at.inner, at.out_reach, at.in_reach, at.hop(1, False), at.hop(1, True)]
    end(*w1, nx, ny, my_three, to_three, *tables)

    w2 = spread(now(*w1), 1)
    ax, ay = now(nx, ny)
    nd = to_x(ay[:h2]), to_y(ax[h2:])
    end(*w2, *nd)

    w3 = spread(now(*w2), 2)
    a_og, a_three = now(og, to_three)
    gx = to_x(a_og)
    got = to_y(a_three)
    n1_a = pin(jnp.concatenate([n1, nx, ny, *now(*nd)]))
    norm1 = n1_a, to_core(n1_a)
    own_three = plan.by_y(my_three, got, 2)
    own_pair, own_third = pin(own_three[:2]), pin(own_three[2])
    own_first, own_second = pin(own_three[0]), pin(own_three[1])
    end(*w3, gx, *norm1, own_pair, own_first, own_second, own_third)

    first1 = spread((now(own_first),) * 2, 0)
    w_in = plan.slots(own_w, *[now(*v) for v in (w1, w2, w3)])
    outs = jnp.stack([w[deep:] for w in w_in])
    w_mine = [pick(outs, 2 * plan.c + j) for j in (0, 1)]
    w_got = to_core(jnp.concatenate([pick(outs, 2 * (1 - plan.c) + j) for j in (0, 1)]))
    core0 = plan.c == 0
    raw, gate, qkv, term, leaving = project((now(norm1[0]), norm1[1]), w_in, at)
    end(*first1, w_got, leaving)

    gy = to_y(now(og))
    w_rows = []
    for j in (0, 1):
        got = w_got[j * 2 * few : (j + 1) * 2 * few]
        for half in (jnp.where(core0, w_mine[j], got), jnp.where(core0, got, w_mine[j])):
            w_rows.append(jnp.concatenate([half[:few], half[few:]], axis=1))
    w_out = pin(jnp.concatenate(w_rows))
    entering = at.bring(now(leaving), False)
    second1 = spread((after(now(own_second), entering),) * 2, 0)
    attn_b, give, state_b = attend(1, qkv, gate, term, entering, w_out, at)
    end(*second1, gy, give)

    third1 = spread((now(own_third),) * 2, 0)
    a_qkv, give = now(qkv, give)
    attn_a, keep, state_a = attend(0, a_qkv, gate, term, entering, w_out, at)
    got = to_core(give)
    a_gx, a_gy = now(gx, gy)
    gd = to_x(a_gy[:h2]), to_y(a_gx[h2:])
    f1, s1 = now(*first1), now(*second1)
    pair1 = pin(jnp.stack([f1[0], s1[0]])), pin(jnp.stack([f1[1], s1[1]]))
    end(*third1, got, keep, *pair1, *gd)

    def first_step(keep, got):
        low, high = add_last(keep, got, width)
        return to_x(low), to_y(high)

    def total(*parts):
        out = parts[0].astype(F32)
        for p in parts[1:]:
            out = out + p.astype(F32)
        return out

    keep, got = now(keep, got)
    u, v = first_step(keep, got)
    third2 = spread(now(*third1), 1)
    g_a = pin(jnp.concatenate([og, gx, gy, *now(*gd)]))
    end(u, v, *third2, g_a)

    to_2, to_4 = add_halves(keep, got, *now(u, v), width)
    sx, sy = to_x(to_2), to_y(to_4)
    pair2 = spread(now(*pair1), 1)
    g_b = to_core(now(g_a))
    end(sx, sy, *pair2, g_b)

    pair3 = spread(now(*pair2), 2)
    dest = plan.places()
    mid, branch, r_attn, n2 = mid_rows((keep, got, *now(sx, sy)), inputs, dest)
    mx, my, mc = to_x(n2), to_y(n2), to_core(n2)
    end(mx, my, mc, *pair3)

    third3 = spread(now(*third2), 2)
    ax, ay = now(mx, my)
    md = to_x(ay[:h2]), to_y(ax[h2:])
    mxyc = to_core(jnp.concatenate([ax, ay]))
    mdc = to_core(jnp.concatenate(md))
    n2_a = pin(jnp.concatenate([n2, mx, my, *md]))
    n2_b = pin(jnp.concatenate([mc, mxyc, mdc]))
    w_pair = plan.slots(own_pair, now(*pair1), now(*pair2), now(*pair3))
    end(*third3, n2_a, n2_b, *w_pair)

    w_third = plan.slots(own_third, *[now(*v) for v in (third1, third2, third3)])
    prod_b, turned_b, gf_b, gs_b, give = sglu_rows(n2_b, g_b, w_pair, w_third)
    end(give)

    give, a_n2 = now(give, n2_a)
    got = to_core(give)
    prod_a, turned_a, gf_a, gs_a, keep = sglu_rows(a_n2, g_a, w_pair, w_third)
    end(keep, got)

    keep, got = now(keep, got)
    u, v = first_step(keep, got)
    d_pair = grads_by_right([(now(gf_a), gf_b), (gs_a, gs_b)], (n2_a, n2_b), cut, width)
    end(u, v, *d_pair)

    d_pair = now(*d_pair)
    pair1 = gather(d_pair[1], d_pair[3], 1)
    to_2, to_4 = add_halves(keep, got, *now(u, v), width)
    sx, sy = to_x(to_2), to_y(to_4)
    d_third = grads_by_right([(now(turned_a), turned_b)], (g_a, g_b), cut, width)

    def join(to_up, to_down, up, down):
        a, b = now(up, down)
        return pin(plus(to_up, a)), pin(plus(to_down, b))

    def join_part(m, up, down, moved):
        a, b = now(*moved)
        return pin(plus(up[m], a[m])), pin(plus(down[m], b[m]))

    end(sx, sy, *pair1, *d_third)

    d_third = [d[0] for d in now(*d_third)]
    third1 = gather(d_third[1], d_third[3], 1)
    first2 = gather(*join_part(0, d_pair[2], d_pair[2], pair1), 2)
    ready = join_part(1, d_pair[2], d_pair[2], pair1)
    grad_mid, gb = mid_back_rows((keep, got, *now(sx, sy)), out_grad, mid, branch, r_attn, dest)
    bx, by, bc = to_x(gb), to_y(gb), to_core(gb)
    o_give = sglu_last(now(prod_b), w_third)
    o_keep = sglu_last(now(prod_a), w_third)

    end(bx, by, bc, *third1, *first2, o_keep, o_give, *ready)

    second2 = gather(*now(*ready), 2)
    ax, ay = now(bx, by)
    bd = to_x(ay[:h2]), to_y(ax[h2:])
    bxyc = to_core(jnp.concatenate([ax, ay]))
    bdc = to_core(jnp.concatenate(bd))
    gb_a = pin(jnp.concatenate([gb, bx, by, *bd]))
    gb_b = pin(jnp.concatenate([bc, bxyc, bdc]))
    ready = join(d_third[2], d_third[2], *third1)
    end(*second2, gb_a, gb_b, *ready)

    third2 = gather(*now(*ready), 2)
    o_got = to_core(now(o_give))
    ga, gg, mixed, d_term, d_leaving = attend_back_rows(
        (now(gb_a), gb_b), w_out, (attn_a, attn_b), gate, qkv, at
    )
    d_out = grads_out(mixed, (gb_a, gb_b), width).reshape(2, 2, few, width)
    ready = join(d_pair[3][0], d_pair[1][0], *first2)
    core0 = plan.c == 0
    w_keep = jnp.where(core0, d_out[:, 0], d_out[:, 1])
    w_got = to_core(jnp.where(core0, d_out[:, 1], d_out[:, 0]))
    end(*third2, d_leaving, o_got, w_keep, w_got, *ready)

    first3 = gather(*now(*ready), 3)
    w_got = now(w_got)
    planes = jnp.concatenate([jnp.where(core0, w_keep, w_got), jnp.where(core0, w_got, w_keep)])
    planes = [pick(planes, k) for k in range(4)]
    planes = [pin(jnp.concatenate([v[:, :across], v[:, across:]])) for v in planes]
    d_entering = at.bring(now(d_leaving), True)

    def back_half(h, first, state):
        return project_back(
            h, first, raw, ga, gg, state, d_term, d_entering, w_in, width, at
        )

    gp_b, give = back_half(1, qkv, state_b)
    ready = join(d_pair[3][1], d_pair[1][1], *second2)
    end(*first3, give, *planes, *ready)

    second3 = gather(*now(*ready), 3)
    a_qkv, give = now(qkv, give)
    gp_a, keep = back_half(0, a_qkv, state_a)
    got = to_core(give)
    ready = join(d_third[3], d_third[1], *third2)
    end(*second3, keep, got, *ready)

    third3 = gather(*now(*ready), 3)
    keep, got = now(keep, got)
    u, v = first_step(keep, got)
    d_w = grads_by_left(norm1, (now(gp_a), gp_b), planes)
    end(u, v, *third3, *d_w)

    d_w = now(*d_w)
    w1 = gather(d_w[1], d_w[3], 1)
    to_2, to_4 = add_halves(keep, got, *now(u, v), width)
    sx, sy = to_x(to_2), to_y(to_4)
    sum_three = [
        total(d_pair[0][0], *now(*first3)),
        total(d_pair[0][1], *now(*second3)),
        total(d_third[0], *now(*third3)),
    ]
    sum_three = jnp.stack([v.astype(BF) for v in sum_three])
    my_three, to_three = plan.of_y(sum_three[:, :, :rows], sum_three[:, :, rows:])
    end(sx, sy, *w1, my_three, to_three)

    ready = join(d_w[2], d_w[2], *w1)
    w2 = gather(*ready, 2)
    three_got = to_y(now(to_three))
    o_keep = after(o_keep, *ready)
    ou, ov = first_step(o_keep, o_got)
    grad_norm1 = total(keep[:rows], got[:rows], *now(sx, sy))
    input_grad = grad_mid + srms_back(xf, plan.turn(grad_norm1))
    end(*w2, three_got, ou, ov)

    ready = join(d_w[3], d_w[1], *w2)
    w3 = gather(*ready, 3)
    to_2, to_4 = add_halves(after(o_keep, *ready), o_got, *now(ou, ov), width)
    ox, oy = to_x(to_2), to_y(to_4)
    sum_three = plan.by_y(my_three, now(three_got), 1)
    sum_pair = pin(sum_three[:2].swapaxes(1, 2)).astype(F32)
    sum_third = sum_three[2].astype(F32)
    end(*w3, ox, oy)

    sum_w = pin(total(d_w[0], *now(*w3)))
    sum_in = pin(sum_w[:deep].astype(BF)).reshape(8, few, across)
    sum_in = lax.all_to_all(sum_in, plan.tp, 0, 0, tiled=True)
    sum_out = jnp.concatenate([sum_w[deep : deep + few], sum_w[deep + few :]], axis=1)
    output = mid + plan.turn(total(o_keep[:rows], o_got[:rows], *now(ox, oy)))
    return output, input_grad, sum_in, sum_out, sum_pair, sum_third


class Plain:
    def __init__(self, wide, narrow):
        self.tp = ("narrow",)
        self.fs = ("wide",)
        self.size = narrow
        self.groups = wide

    def begin(self):
        self.p = lax.axis_index("narrow")
        self.group = lax.axis_index("wide")
        self.slot_ids = jnp.arange(self.size, dtype=jnp.int32)

    def turn(self, v):
        return v

    def rows_all(self, a):
        whole = lax.all_gather(a, "narrow", axis=0, tiled=True)
        return whole[: whole.shape[0] // 2], whole[whole.shape[0] // 2 :]

    def rows_sum(self, keep, give, kind=BF):
        total = lax.psum_scatter(
            jnp.concatenate([keep, give]), "narrow", scatter_dimension=0, tiled=True
        )
        return total.astype(F32)

    def attn_in(self, w):
        rows, cols = w.shape
        each = cols // 4 // self.size
        view = w.reshape(rows, 4, self.size, each).transpose(2, 0, 1, 3)
        view = view.reshape(self.size, rows, 4 * each)
        mine = lax.all_to_all(view, "narrow", 0, 0, tiled=True)
        mine = mine.reshape(self.size * rows, 4 * each)
        return cut4(lax.all_gather(mine, "wide", axis=0, tiled=True), 0)

    def attn_in_back(self, g):
        cols = g.shape[1]
        total = lax.psum_scatter(g.astype(BF), "wide", scatter_dimension=0, tiled=True)
        rows = total.shape[0] // self.size
        view = total.reshape(self.size, rows, cols)
        mine = lax.all_to_all(view, "narrow", 0, 0, tiled=True)
        mine = mine.reshape(self.size, rows, 4, cols // 4).transpose(1, 2, 0, 3)
        return mine.reshape(rows, cols * self.size).astype(F32)

    def attn_out(self, w):
        whole = lax.all_gather(w, ("wide", "narrow"), axis=0, tiled=True)
        each = whole.shape[0] // self.size
        return lax.dynamic_slice_in_dim(whole, self.p * each, each)

    def attn_out_back(self, g):
        each = g.shape[0]
        whole = jnp.zeros((each * self.size, g.shape[1]), BF)
        whole = lax.dynamic_update_slice_in_dim(whole, g.astype(BF), self.p * each, 0)
        total = lax.psum_scatter(whole, ("wide", "narrow"), scatter_dimension=0, tiled=True)
        return total.astype(F32)

    def sglu(self, pair, third):
        return pair, third

    def sglu_all(self, both, back):
        pair = lax.all_gather(both.swapaxes(1, 2), "wide", axis=2, tiled=True)
        third = lax.all_gather(back, "wide", axis=1, tiled=True)
        return cut4(pair, 2), cut4(third, 1)

    def pair_back(self, g):
        g = jnp.concatenate([g[k] for k in range(4)], axis=2)
        total = lax.psum_scatter(g, "wide", scatter_dimension=2, tiled=True)
        return total.swapaxes(1, 2).astype(F32)

    def third_back(self, g):
        g = jnp.concatenate([g[k] for k in range(4)], axis=1)
        total = lax.psum_scatter(g, "wide", scatter_dimension=1, tiled=True)
        return total.astype(F32)


def plain_layer(plan, places, lengths, inputs, out_grad, attn_in, attn_out, sglu_in, sglu_out):
    rows, width = inputs.shape
    at = places(lengths)
    w_out = plan.attn_out(attn_out.astype(BF))
    w_in = plan.attn_in(attn_in.astype(BF))
    w_pair, w_third = plan.sglu_all(sglu_in.astype(BF), sglu_out.astype(BF))
    xf = inputs.astype(F32)
    norm1 = plan.rows_all(plan.turn((xf * inverse_rms(xf)).astype(BF)))
    grad_rows = plan.rows_all(plan.turn(out_grad))
    raw, gate, qkv, term, leaving = project(norm1, w_in, at)
    entering = at.bring(leaving, False)
    attn, branch, state = [None] * 2, [None] * 2, [None] * 2
    for h in (1, 0):
        attn[h], branch[h], state[h] = attend(h, qkv, gate, term, entering, w_out, at)
    square = plan.rows_sum(*[strip_sum(v) for v in branch], F32)
    branch = plan.rows_sum(*[v[:, :width] for v in branch])
    r_attn = lax.rsqrt(square / width + EPS)
    mid = xf + r_attn * branch
    r_mid = inverse_rms(mid)
    norm2 = plan.rows_all(plan.turn((mid * r_mid).astype(BF)))

    product, turned, grad_first, grad_second, back = [[None] * 2 for _ in range(5)]
    for h in (1, 0):
        product[h], turned[h], grad_first[h], grad_second[h], back[h] = sglu_rows(
            norm2[h], grad_rows[h], w_pair, w_third
        )
    cut = width // 4
    sum_third = plan.third_back([g[0] for g in grads_by_right([turned], grad_rows, cut, width)])
    grad_norm2 = plan.rows_sum(*back)
    sum_pair = plan.pair_back(grads_by_right([grad_first, grad_second], norm2, cut, width))

    grad_mid = out_grad.astype(F32) + srms_back(mid, plan.turn(grad_norm2))
    grad_branch = grad_mid.astype(BF)
    inward = jnp.mean(grad_branch.astype(F32) * branch, axis=1, keepdims=True)
    extra = pieces(r_attn) + pieces(r_attn * r_attn * r_attn * inward)
    extra.append(jnp.zeros((rows, 128 - len(extra)), BF))
    grad_branch = jnp.concatenate([grad_branch] + extra, axis=1)
    grad_branch = plan.rows_all(grad_branch)
    branch_out = plan.rows_sum(*[sglu_last(v, w_third) for v in product])
    output = mid + plan.turn(branch_out)
    grad_attn, grad_gate, mixed, d_term, d_leaving = attend_back_rows(
        grad_branch, w_out, attn, gate, qkv, at
    )
    d_entering = at.bring(d_leaving, True)
    grad_pre, back = [None] * 2, [None] * 2
    for h in (1, 0):
        grad_pre[h], back[h] = project_back(
            h, qkv, raw, grad_attn, grad_gate, state[h], d_term, d_entering, w_in, width, at
        )
    none = [jnp.zeros((16, grad_pre[0].shape[1]), BF)] * 4
    grad_win = jnp.concatenate([g[:cut] for g in grads_by_left(norm1, grad_pre, none)])
    sum_in = plan.attn_in_back(grad_win)
    sum_out = plan.attn_out_back(grads_out(mixed, grad_branch, width))
    grad_norm1 = plan.rows_sum(*back)
    input_grad = grad_mid + srms_back(xf, plan.turn(grad_norm1))
    return output, input_grad, sum_in, sum_out, sum_pair, sum_third


def per_device(plan, layer, *args):
    inputs, out_grad, seq_lengths, decay_rate = args[:4]
    weights, moments, averages = args[4:8], args[8:12], args[12:16]
    plan.begin()
    rows, width = inputs.shape
    plan.own = decay_rate.shape[0] // plan.size

    def places(lengths):
        return Places(plan, lengths, decay_rate, rows)

    output, input_grad, *grads = layer(plan, places, seq_lengths, inputs, out_grad, *weights)
    tokens = plan.size * rows * plan.groups
    fans = (width, width, width, weights[3].shape[0] * lax.axis_size(plan.narrow))
    new = []
    for w, m, a, grad, fan in zip(weights, moments, averages, grads, fans):
        if grad.shape == w.shape:
            new.append(renew(w, m, a, grad, fan, tokens))
        else:
            new.append(renew_turned(grad, w, m, a, fan, tokens))
    return (output, input_grad) + tuple(n[i] for i in range(3) for n in new)


def solution(mesh):
    wide, narrow = mesh.shape["wide"], mesh.shape["narrow"]
    if (wide, narrow) == (8, 4):
        mesh = Mesh(mesh.devices.reshape(4, 2, 2, 2), ("z", "y", "x", "c"))
        plan, layer, w, n = Square(), square_layer, ("z", "y"), ("x", "c")
    else:
        plan, layer, w, n = Plain(wide, narrow), plain_layer, ("wide",), ("narrow",)
    plan.narrow = n
    by_rows = P(w + n, None)
    pair, third = P(None, w, n), P(n, w)
    weights = (by_rows, by_rows, pair, third)

    def run(*args):
        return per_device(plan, layer, *args)

    return jax.shard_map(
        run,
        mesh=mesh,
        in_specs=(by_rows, by_rows, P(), P()) + weights * 3,
        out_specs=(by_rows, by_rows) + weights * 3,
        check_vma=False,
    )
```

time: 863 us -> 774 us (0.90)
  local copies, waits for them, and re-layouts: 101 us -> 52.7 us
  other arithmetic: 126 us -> 92.2 us
  starting transfers between devices: 162 us -> 136 us
  waiting for transfers between devices: 230 us -> 248 us
    ppermute x99 -> x90, starting transfers between devices: 148 us -> 121 us  [over(): return lambda v: pin(lax.ppermute(pin(v), axis, pairs))]
    unnamed x256 -> x213, local copies, waits for them, and re-layouts: 54.1 us -> 35 us
    convert_element_type x8 -> x11, other arithmetic: 23.5 us -> 11.1 us  [plus(): return (a.astype(F32) + b.astype(F32)).astype(BF)]
    ppermute x99 -> x90, waiting for transfers between devices: 225 us -> 237 us  [over(): return lambda v: pin(lax.ppermute(pin(v), axis, pairs))]
    slice x15 -> x5, local copies, waits for them, and re-layouts: 12.2 us -> 1.23 us  [the longest x1 1.15 us: square_layer(): sum_in = pin(sum_w[:deep].astype(BF)).reshape(8, few, across)]
    pallas_call x24 -> x25, Pallas kernels: 222 us -> 230 us  [call(): pl.pallas_call(kernel, grid=(steps,), in_specs=[s for _, s in ins], out_s...]
  transfers between devices with their start and end apart: 103 -> 94, of which waited for: 37 -> 43; matrix products, arithmetic and copies ran while one was open for 19% -> 14% of each run, Pallas kernels for 21% -> 26%
where the time goes in v3:
time: 774 us; the launch traced here: 763 us
  waiting for transfers between devices  248 us (32%)
  Pallas kernels  230 us (30%)
  starting transfers between devices  136 us (18%)
  other arithmetic  92.2 us (12%)
  local copies, waits for them, and re-layouts  52.7 us (7%)
    ppermute x90, waiting for transfers between devices, over(): return lambda v: pin(lax.ppermute(pin(v), axis, pairs))  237 us
    pallas_call x25, Pallas kernels, call(): pl.pallas_call(kernel, grid=(steps,), in_specs=[s for _, s in ins], out_s...  230 us
    ppermute x90, starting transfers between devices, over(): return lambda v: pin(lax.ppermute(pin(v), axis, pairs))  121 us
    unnamed x213, local copies, waits for them, and re-layouts  35 us
  transfers between devices with their start and end apart: 94, of which 43 were waited for; matrix products, arithmetic and copies ran while one was open for 14% of the time, Pallas kernels for 26%

profile of v3, /device:TPU:0, one launch (start us, length us, event | category | flops | bytes accessed | tf_op | source)
XLA Modules:
  0.0 763.1 jit_solution(2767618738383443455)
XLA Ops:
  80.1 16.6 %collective-permute-done.6 = bf16[640,1024]{1,0:T(8,128)(2,1)} collective-permute-done((bf16[640,1024]{1,0:T(8,128)(2,1)}, bf16[640,1024]{1,0:T(8,128)(2,1)}, u32[]{:S(2)}, u32[]{:S(2)}) %collective-permute-start.6) | collective-permute-done | bytes 1310752 | tf_op jit(solution)/shard_map/ppermute | solution.py:761
  104.6 20.6 %collective-permute-done.12 = bf16[3,704,256]{2,1,0:T(8,128)(2,1)} collective-permute-done((bf16[3,704,256]{2,1,0:T(8,128)(2,1)}, bf16[3,704,256]{2,1,0:T(8,128)(2,1)}, u32[]{:S(2)}, u32[]{:S(2)}) %collective-permute-start.12) | collective-permute-done | bytes 1081376 | tf_op jit(solution)/shard_map/ppermute | solution.py:761
  144.5 17.6 %shard_map.272 = (f32[2048,512]{1,0:T(8,128)}, f32[2048,256]{1,0:T(8,128)}, bf16[2048,768]{1,0:T(8,128)(2,1)}, f32[8,2,128,128]{3,2,1,0:T(8,128)}, f32[2,128,128]{2,1,0:T(8,128)}) custom-call(bf16[1024,2048]{1,0:T(8,128)(2,1)} %constant_dynamic-update-slice_fusion.refs_0_, bf16[1024,2048]{1,0:T(8,128)(2,1)} %collective-permute-done.11.refs_1_, ...), custom_call_target="tpu_custom_call" | custom-call | flops 8589934592 | bytes 24387680 | tf_op jit(solution)/shard_map/pallas_call | solution.py:86
  178.5 7.4 shard_map.273
  203.3 7.4 shard_map.274
  232.1 7.7 %collective-permute-done.25.u_ref = bf16[128,2176]{1,0:T(8,128)(2,1)S(1)} collective-permute-done((bf16[128,2176]{1,0:T(8,128)(2,1)}, bf16[128,2176]{1,0:T(8,128)(2,1)S(1)}, u32[]{:S(2)}, u32[]{:S(2)}) %collective-permute-start.25) | collective-permute-done | bytes 557088 | tf_op jit(solution)/shard_map/ppermute | solution.py:761
  249.4 26.2 %collective-permute-done.29.c = bf16[256,2176]{1,0:T(8,128)(2,1)S(1)} collective-permute-done((bf16[256,2176]{1,0:T(8,128)(2,1)}, bf16[256,2176]{1,0:T(8,128)(2,1)S(1)}, u32[]{:S(2)}, u32[]{:S(2)}) %collective-permute-start.29) | collective-permute-done | bytes 1114144 | tf_op jit(solution)/shard_map/ppermute | solution.py:761
  292.0 22.2 %collective-permute-done.35 = bf16[256,2048]{1,0:T(8,128)(2,1)S(1)} collective-permute-done((bf16[256,2048]{1,0:T(8,128)(2,1)}, bf16[256,2048]{1,0:T(8,128)(2,1)S(1)}, u32[]{:S(2)}, u32[]{:S(2)}) %collective-permute-start.35) | collective-permute-done | bytes 1048608 | tf_op jit(solution)/shard_map/ppermute | solution.py:761
  324.8 7.5 collective-permute-done.40
  345.9 23.5 %shard_map.278 = (bf16[1024,704]{1,0:T(8,128)(2,1)}, bf16[704,1024]{1,0:T(8,128)(2,1)}, bf16[704,1024]{1,0:T(8,128)(2,1)}, bf16[704,1024]{1,0:T(8,128)(2,1)}, bf16[1024,2048]{1,0:T(8,128)(2,1)}) custom-call(bf16[1024,2048]{1,0:T(8,128)(2,1)} %copy-done.86, bf16[1024,2048]{1,0:T(8,128)(2,1)} %collective-permute-done.33.refs_1_.refs_3_, ...), custom_call_target="tpu_custom_call" | custom-call | flops 14763950080 | bytes 27000832 | tf_op jit(solution)/shard_map/pallas_call | solution.py:86
  369.4 24.0 %shard_map.279 = (bf16[1024,704]{1,0:T(8,128)(2,1)}, bf16[704,1024]{1,0:T(8,128)(2,1)}, bf16[704,1024]{1,0:T(8,128)(2,1)}, bf16[704,1024]{1,0:T(8,128)(2,1)}, bf16[1024,2048]{1,0:T(8,128)(2,1)}) custom-call(bf16[1024,2048]{1,0:T(8,128)(2,1)} %copy-done.87, bf16[1024,2048]{1,0:T(8,128)(2,1)} %constant_dynamic-update-slice_fusion.5.refs_1_.refs_2_, ...), custom_call_target="tpu_custom_call" | custom-call | flops 14763950080 | bytes 27000832 | tf_op jit(solution)/shard_map/pallas_call | solution.py:86
  400.0 19.7 %shard_map.281 = (bf16[2,704,512]{2,1,0:T(8,128)(2,1)}, bf16[2,704,512]{2,1,0:T(8,128)(2,1)}, bf16[2,704,512]{2,1,0:T(8,128)(2,1)}, bf16[2,704,512]{2,1,0:T(8,128)(2,1)}) custom-call(bf16[704,1024]{1,0:T(8,128)(2,1)} %get-tuple-element.351.refs_0_, bf16[704,1024]{1,0:T(8,128)(2,1)} %get-tuple-element.352.refs_1_, ...), custom_call_target="tpu_custom_call" | custom-call | flops 11811160064 | bytes 19922944 | tf_op jit(solution)/shard_map/pallas_call | solution.py:86
  428.4 11.0 %shard_map.283 = (bf16[1,704,512]{2,1,0:T(8,128)(2,1)}, bf16[1,704,512]{2,1,0:T(8,128)(2,1)}, bf16[1,704,512]{2,1,0:T(8,128)(2,1)}, bf16[1,704,512]{2,1,0:T(8,128)(2,1)}) custom-call(bf16[704,1024]{1,0:T(8,128)(2,1)} %get-tuple-element.367.refs_0_, bf16[704,1024]{1,0:T(8,128)(2,1)} %get-tuple-element.368.refs_1_, ...), custom_call_target="tpu_custom_call" | custom-call | flops 5905580032 | bytes 14155776 | tf_op jit(solution)/shard_map/pallas_call | solution.py:86
  439.4 11.8 %collective-permute-done.48.c = bf16[256,2048]{1,0:T(8,128)(2,1)S(1)} collective-permute-done((bf16[256,2048]{1,0:T(8,128)(2,1)}, bf16[256,2048]{1,0:T(8,128)(2,1)S(1)}, u32[]{:S(2)}, u32[]{:S(2)}) %collective-permute-start.48) | collective-permute-done | bytes 1048608 | tf_op jit(solution)/shard_map/ppermute | solution.py:761
  477.5 7.0 shard_map.284.a_ref.a2.a4
  484.5 7.0 shard_map.286
  521.0 13.0 %shard_map.287 = (bf16[2048,256]{1,0:T(8,128)(2,1)}, bf16[2048,256]{1,0:T(8,128)(2,1)}, bf16[2048,256]{1,0:T(8,128)(2,1)}, f32[8,2,128,128]{3,2,1,0:T(8,128)}, f32[2,128,128]{2,1,0:T(8,128)}) custom-call(bf16[1024,2176]{1,0:T(8,128)(2,1)} %copy-done.7, bf16[1024,2176]{1,0:T(8,128)(2,1)} %constant_dynamic-update-slice_fusion.23.gb_b.r1, ...), custom_call_target="tpu_custom_call" | custom-call | flops 2147483648 | bytes 21766240 | tf_op jit(solution)/shard_map/pallas_call | solution.py:86
  534.0 6.7 shard_map.288
  557.4 12.7 %shard_map.289 = (bf16[1024,1024]{1,0:T(8,128)(2,1)}, bf16[1024,2048]{1,0:T(8,128)(2,1)}) custom-call(bf16[2048,768]{1,0:T(8,128)(2,1)} %get-tuple-element.420.qkv_ref.refs_0_, f32[2048,512]{1,0:T(8,128)} %get-tuple-element.409.refs_1_, bf16[2048,256]{1,0:T(8,128)(2,1)} %get-tuple-element.410.refs_2_, bf16[2048,256]{1,0:T(8,128)(2,1)} %get-tuple-element.411.refs_3_, ...), custom_call_target="tpu_custom_call" | custom-call | flops 4294967296 | bytes 23085696 | tf_op jit(solution)/shard_map/pallas_call | solution.py:86
  579.9 12.8 %shard_map.290 = (bf16[1024,1024]{1,0:T(8,128)(2,1)}, bf16[1024,2048]{1,0:T(8,128)(2,1)}) custom-call(bf16[2048,768]{1,0:T(8,128)(2,1)} %get-tuple-element.420.qkv_ref.refs_0_, f32[2048,512]{1,0:T(8,128)} %get-tuple-element.409.refs_1_, bf16[2048,256]{1,0:T(8,128)(2,1)} %get-tuple-element.410.refs_2_, bf16[2048,256]{1,0:T(8,128)(2,1)} %get-tuple-element.411.refs_3_, ...), custom_call_target="tpu_custom_call" | custom-call | flops 4294967296 | bytes 23085696 | tf_op jit(solution)/shard_map/pallas_call | solution.py:86
  606.0 15.6 %shard_map.291 = (bf16[640,1024]{1,0:T(8,128)(2,1)}, bf16[640,1024]{1,0:T(8,128)(2,1)}, bf16[640,1024]{1,0:T(8,128)(2,1)}, bf16[640,1024]{1,0:T(8,128)(2,1)}) custom-call(bf16[1024,2048]{1,0:T(8,128)(2,1)} %constant_dynamic-update-slice_fusion.refs_0_, bf16[1024,2048]{1,0:T(8,128)(2,1)} %collective-permute-done.11.refs_1_, ...), custom_call_target="tpu_custom_call" | custom-call | flops 8589934592 | bytes 18874368 | tf_op jit(solution)/shard_map/pallas_call | solution.py:86
  637.5 17.2 %collective-permute-done.80 = bf16[256,2048]{1,0:T(8,128)(2,1)S(1)} collective-permute-done((bf16[256,2048]{1,0:T(8,128)(2,1)}, bf16[256,2048]{1,0:T(8,128)(2,1)S(1)}, u32[]{:S(2)}, u32[]{:S(2)}) %collective-permute-start.80) | collective-permute-done | bytes 1048608 | tf_op jit(solution)/shard_map/ppermute | solution.py:761
  674.9 20.3 %collective-permute-done.87.v_ref = bf16[128,2048]{1,0:T(8,128)(2,1)S(1)} collective-permute-done((bf16[128,2048]{1,0:T(8,128)(2,1)}, bf16[128,2048]{1,0:T(8,128)(2,1)S(1)}, u32[]{:S(2)}, u32[]{:S(2)}) %collective-permute-start.87) | collective-permute-done | bytes 524320 | tf_op jit(solution)/shard_map/ppermute | solution.py:761
  718.8 7.5 multiply_add_fusion
  (546 shorter events, 415.7 us)
Async XLA Ops:
  27.6 30.9 %collective-permute-start.2 = (bf16[640,1024]{1,0:T(8,128)(2,1)S(1)}, bf16[640,1024]{1,0:T(8,128)(2,1)}, u32[]{:S(2)}, u32[]{:S(2)}) collective-permute-start(bf16[640,1024]{1,0:T(8,128)(2,1)S(1)} %pad_maximum_fusion.6.refs_2_.refs_7_), channel_id=1, source_target_pairs={{0,8},{8,16},{16,24},{1,9},{9,17},{17,25},{2,10},{10,18},{18,26},{... | collective-permute-start | bytes 3932168 | tf_op jit(solution)/shard_map/ppermute | solution.py:761
  32.1 31.6 %collective-permute-start.3 = (bf16[640,1024]{1,0:T(8,128)(2,1)S(1)}, bf16[640,1024]{1,0:T(8,128)(2,1)}, u32[]{:S(2)}, u32[]{:S(2)}) collective-permute-start(bf16[640,1024]{1,0:T(8,128)(2,1)S(1)} %pad_maximum_fusion.6.refs_2_.refs_7_), channel_id=1, source_target_pairs={{24,16},{16,8},{8,0},{25,17},{17,9},{9,1},{26,18},{18,10},{10,2},{... | collective-permute-start | bytes 3932168 | tf_op jit(solution)/shard_map/ppermute | solution.py:761
  64.5 32.2 %collective-permute-start.6 = (bf16[640,1024]{1,0:T(8,128)(2,1)}, bf16[640,1024]{1,0:T(8,128)(2,1)}, u32[]{:S(2)}, u32[]{:S(2)}) collective-permute-start(bf16[640,1024]{1,0:T(8,128)(2,1)} %collective-permute-done.3), channel_id=1, source_target_pairs={{16,8},{8,0},{17,9},{9,1},{18,10},{10,2},{19,11},{11,3},{20,12},{1... | collective-permute-start | bytes 3932168 | tf_op jit(solution)/shard_map/ppermute | solution.py:761
  98.4 36.8 %collective-permute-start.11 = (bf16[1024,2048]{1,0:T(8,128)(2,1)}, bf16[1024,2048]{1,0:T(8,128)(2,1)}, u32[]{:S(2)}, u32[]{:S(2)}) collective-permute-start(bf16[1024,2048]{1,0:T(8,128)(2,1)} %constant_dynamic-update-slice_fusion.refs_0_), channel_id=1, source_target_pairs={{0,1},{1,0},{2,3},{3,2},{4,5},{5,4},{6,7},{7,6},{8,9},{9,8},{10,11... | collective-permute-start | bytes 12582920 | tf_op jit(solution)/shard_map/ppermute | solution.py:761
  100.4 28.6 %collective-permute-start.8 = (bf16[640,1024]{1,0:T(8,128)(2,1)S(1)}, bf16[640,1024]{1,0:T(8,128)(2,1)}, u32[]{:S(2)}, u32[]{:S(2)}) collective-permute-start(bf16[640,1024]{1,0:T(8,128)(2,1)S(1)} %collective-permute-done.5), channel_id=1, source_target_pairs={{16,24},{17,25},{18,26},{19,27},{20,28},{21,29},{22,30},{23,31}} | collective-permute-start | bytes 3932168 | tf_op jit(solution)/shard_map/ppermute | solution.py:761
  102.1 33.1 %collective-permute-start.9 = (bf16[640,1024]{1,0:T(8,128)(2,1)}, bf16[640,1024]{1,0:T(8,128)(2,1)}, u32[]{:S(2)}, u32[]{:S(2)}) collective-permute-start(bf16[640,1024]{1,0:T(8,128)(2,1)} %collective-permute-done.6), channel_id=1, source_target_pairs={{8,0},{9,1},{10,2},{11,3},{12,4},{13,5},{14,6},{15,7}} | collective-permute-start | bytes 3932168 | tf_op jit(solution)/shard_map/ppermute | solution.py:761
  167.6 27.9 %collective-permute-start.19 = (bf16[256,2048]{1,0:T(8,128)(2,1)}, bf16[256,2048]{1,0:T(8,128)(2,1)S(1)}, u32[]{:S(2)}, u32[]{:S(2)}) collective-permute-start(bf16[256,2048]{1,0:T(8,128)(2,1)} %get-tuple-element.282), channel_id=1, source_target_pairs={{0,4},{4,0},{1,5},{5,1},{2,6},{6,2},{3,7},{7,3},{8,12},{12,8},{9,1... | collective-permute-start | bytes 3145736 | tf_op jit(solution)/shard_map/ppermute | solution.py:761
  240.9 39.4 %collective-permute-start.33 = (bf16[1024,2048]{1,0:T(8,128)(2,1)}, bf16[1024,2048]{1,0:T(8,128)(2,1)}, u32[]{:S(2)}, u32[]{:S(2)}) collective-permute-start(bf16[1024,2048]{1,0:T(8,128)(2,1)} %constant_dynamic-update-slice_fusion.5.refs_1_.refs_2_), channel_id=1, source_target_pairs={{0,1},{1,0},{2,3},{3,2},{4,5},{5,4},{6,7},{7,6},{8,9},{9,8},{10,11... | collective-permute-start | bytes 12582920 | tf_op jit(solution)/shard_map/ppermute | solution.py:761
  240.9 35.0 %collective-permute-start.31 = (bf16[2,704,512]{2,1,0:T(8,128)(2,1)S(1)}, bf16[2,704,512]{2,1,0:T(8,128)(2,1)S(1)}, u32[]{:S(2)}, u32[]{:S(2)}) collective-permute-start(bf16[2,704,512]{2,1,0:T(8,128)(2,1)S(1)} %pad_maximum_fusion.4), channel_id=1, source_target_pairs={{8,16},{16,24},{9,17},{17,25},{10,18},{18,26},{11,19},{19,27},{12,... | collective-permute-start | bytes 4325384 | tf_op jit(solution)/shard_map/ppermute | solution.py:761
  241.7 38.7 %collective-permute-start.32 = (bf16[2,704,512]{2,1,0:T(8,128)(2,1)S(1)}, bf16[2,704,512]{2,1,0:T(8,128)(2,1)S(1)}, u32[]{:S(2)}, u32[]{:S(2)}) collective-permute-start(bf16[2,704,512]{2,1,0:T(8,128)(2,1)S(1)} %pad_maximum_fusion.5), channel_id=1, source_target_pairs={{16,8},{8,0},{17,9},{9,1},{18,10},{10,2},{19,11},{11,3},{20,12},{1... | collective-permute-start | bytes 4325384 | tf_op jit(solution)/shard_map/ppermute | solution.py:761
  280.3 33.9 %collective-permute-start.37 = (bf16[2,704,512]{2,1,0:T(8,128)(2,1)S(1)}, bf16[2,704,512]{2,1,0:T(8,128)(2,1)}, u32[]{:S(2)}, u32[]{:S(2)}) collective-permute-start(bf16[2,704,512]{2,1,0:T(8,128)(2,1)S(1)} %collective-permute-done.31), channel_id=1, source_target_pairs={{16,24},{17,25},{18,26},{19,27},{20,28},{21,29},{22,30},{23,31}} | collective-permute-start | bytes 4325384 | tf_op jit(solution)/shard_map/ppermute | solution.py:761
  282.1 35.1 %collective-permute-start.38 = (bf16[2,704,512]{2,1,0:T(8,128)(2,1)S(1)}, bf16[2,704,512]{2,1,0:T(8,128)(2,1)S(1)}, u32[]{:S(2)}, u32[]{:S(2)}) collective-permute-start(bf16[2,704,512]{2,1,0:T(8,128)(2,1)S(1)} %collective-permute-done.32), channel_id=1, source_target_pairs={{8,0},{9,1},{10,2},{11,3},{12,4},{13,5},{14,6},{15,7}} | collective-permute-start | bytes 4325384 | tf_op jit(solution)/shard_map/ppermute | solution.py:761
  419.8 32.9 %collective-permute-start.50 = (bf16[2,704,512]{2,1,0:T(8,128)(2,1)}, bf16[2,704,512]{2,1,0:T(8,128)(2,1)S(1)}, u32[]{:S(2)}, u32[]{:S(2)}) collective-permute-start(bf16[2,704,512]{2,1,0:T(8,128)(2,1)} %get-tuple-element.364), channel_id=1, source_target_pairs={{0,8},{1,9},{2,10},{3,11},{4,12},{5,13},{6,14},{7,15}} | collective-permute-start | bytes 4325384 | tf_op jit(solution)/shard_map/ppermute | solution.py:761
  421.4 31.3 %collective-permute-start.51 = (bf16[2,704,512]{2,1,0:T(8,128)(2,1)}, bf16[2,704,512]{2,1,0:T(8,128)(2,1)S(1)}, u32[]{:S(2)}, u32[]{:S(2)}) collective-permute-start(bf16[2,704,512]{2,1,0:T(8,128)(2,1)} %get-tuple-element.365), channel_id=1, source_target_pairs={{24,16},{25,17},{26,18},{27,19},{28,20},{29,21},{30,22},{31,23}} | collective-permute-start | bytes 4325384 | tf_op jit(solution)/shard_map/ppermute | solution.py:761
  513.9 30.2 %collective-permute-start.67 = (bf16[1024,2048]{1,0:T(8,128)(2,1)}, bf16[1024,2048]{1,0:T(8,128)(2,1)}, u32[]{:S(2)}, u32[]{:S(2)}) collective-permute-start(bf16[1024,2048]{1,0:T(8,128)(2,1)} %shard_map.286), channel_id=1, source_target_pairs={{0,1},{1,0},{2,3},{3,2},{4,5},{5,4},{6,7},{7,6},{8,9},{9,8},{10,11... | collective-permute-start | bytes 12582920 | tf_op jit(solution)/shard_map/ppermute | solution.py:761
  513.9 30.2 %collective-permute-start.65 = (bf16[704,512]{1,0:T(8,128)(2,1)S(1)}, bf16[704,512]{1,0:T(8,128)(2,1)S(1)}, u32[]{:S(2)}, u32[]{:S(2)}) collective-permute-start(bf16[704,512]{1,0:T(8,128)(2,1)S(1)} %get-tuple-element.396), channel_id=1, source_target_pairs={{0,8},{8,16},{1,9},{9,17},{2,10},{10,18},{3,11},{11,19},{4,12},{12... | collective-permute-start | bytes 2162696 | tf_op jit(solution)/shard_map/ppermute | solution.py:761
  621.6 34.5 %collective-permute-start.79 = (bf16[640,1024]{1,0:T(8,128)(2,1)}, bf16[640,1024]{1,0:T(8,128)(2,1)S(1)}, u32[]{:S(2)}, u32[]{:S(2)}) collective-permute-start(bf16[640,1024]{1,0:T(8,128)(2,1)} %get-tuple-element.444), channel_id=1, source_target_pairs={{0,8},{1,9},{2,10},{3,11},{4,12},{5,13},{6,14},{7,15}} | collective-permute-start | bytes 3932168 | tf_op jit(solution)/shard_map/ppermute | solution.py:761
  626.4 29.8 %collective-permute-start.82 = (bf16[640,1024]{1,0:T(8,128)(2,1)}, bf16[640,1024]{1,0:T(8,128)(2,1)S(1)}, u32[]{:S(2)}, u32[]{:S(2)}) collective-permute-start(bf16[640,1024]{1,0:T(8,128)(2,1)} %get-tuple-element.449), channel_id=1, source_target_pairs={{24,16},{25,17},{26,18},{27,19},{28,20},{29,21},{30,22},{31,23}} | collective-permute-start | bytes 3932168 | tf_op jit(solution)/shard_map/ppermute | solution.py:761
  658.1 37.1 %collective-permute-start.84 = (bf16[640,1024]{1,0:T(8,128)(2,1)S(1)}, bf16[640,1024]{1,0:T(8,128)(2,1)S(1)}, u32[]{:S(2)}, u32[]{:S(2)}) collective-permute-start(bf16[640,1024]{1,0:T(8,128)(2,1)S(1)} %get-tuple-element.536), channel_id=1, source_target_pairs={{24,16},{16,8},{25,17},{17,9},{26,18},{18,10},{27,19},{19,11},{28,... | collective-permute-start | bytes 3932168 | tf_op jit(solution)/shard_map/ppermute | solution.py:761
  658.9 36.3 %collective-permute-start.83 = (bf16[640,1024]{1,0:T(8,128)(2,1)S(1)}, bf16[640,1024]{1,0:T(8,128)(2,1)S(1)}, u32[]{:S(2)}, u32[]{:S(2)}) collective-permute-start(bf16[640,1024]{1,0:T(8,128)(2,1)S(1)} %get-tuple-element.537), channel_id=1, source_target_pairs={{0,8},{8,16},{1,9},{9,17},{2,10},{10,18},{3,11},{11,19},{4,12},{12... | collective-permute-start | bytes 3932168 | tf_op jit(solution)/shard_map/ppermute | solution.py:761
  661.3 33.9 %collective-permute-start.85 = (bf16[3,704,256]{2,1,0:T(8,128)(2,1)S(1)}, bf16[3,704,256]{2,1,0:T(8,128)(2,1)}, u32[]{:S(2)}, u32[]{:S(2)}) collective-permute-start(bf16[3,704,256]{2,1,0:T(8,128)(2,1)S(1)} %get-tuple-element.462), channel_id=1, source_target_pairs={{0,4},{4,0},{1,5},{5,1},{2,6},{6,2},{3,7},{7,3},{8,12},{12,8},{9,1... | collective-permute-start | bytes 3244040 | tf_op jit(solution)/shard_map/ppermute | solution.py:761
  665.4 29.8 %collective-permute-start.87 = (bf16[128,2048]{1,0:T(8,128)(2,1)}, bf16[128,2048]{1,0:T(8,128)(2,1)S(1)}, u32[]{:S(2)}, u32[]{:S(2)}) collective-permute-start(bf16[128,2048]{1,0:T(8,128)(2,1)} %get-tuple-element.464), channel_id=1, source_target_pairs={{0,4},{4,0},{1,5},{5,1},{2,6},{6,2},{3,7},{7,3},{8,12},{12,8},{9,1... | collective-permute-start | bytes 1572872 | tf_op jit(solution)/shard_map/ppermute | solution.py:761
  698.5 34.7 %collective-permute-start.89 = (bf16[640,1024]{1,0:T(8,128)(2,1)}, bf16[640,1024]{1,0:T(8,128)(2,1)}, u32[]{:S(2)}, u32[]{:S(2)}) collective-permute-start(bf16[640,1024]{1,0:T(8,128)(2,1)} %add_convert_fusion.1), channel_id=1, source_target_pairs={{0,8},{8,16},{16,24},{1,9},{9,17},{17,25},{2,10},{10,18},{18,26},{... | collective-permute-start | bytes 3932168 | tf_op jit(solution)/shard_map/ppermute | solution.py:761
  703.7 29.4 %collective-permute-start.90 = (bf16[640,1024]{1,0:T(8,128)(2,1)}, bf16[640,1024]{1,0:T(8,128)(2,1)}, u32[]{:S(2)}, u32[]{:S(2)}) collective-permute-start(bf16[640,1024]{1,0:T(8,128)(2,1)} %add_convert_fusion), channel_id=1, source_target_pairs={{24,16},{16,8},{8,0},{25,17},{17,9},{9,1},{26,18},{18,10},{10,2},{... | collective-permute-start | bytes 3932168 | tf_op jit(solution)/shard_map/ppermute | solution.py:761
  (167 other events, 1952.9 us)

commit v4 on v3

--- a/solution.py
+++ b/solution.py
@@ -18,6 +18,8 @@
 F32 = jnp.float32
 SWAP = [(0, 1), (1, 0)]
 XORS = (0, 2, 4, 6, 1, 3, 5, 7)
+MEETS = ((0, 1, 2, 3), (1, 0, 2, 3), (2, 3, 1, 0), (3, 2, 1, 0))
+PLACES = ((0, 1, 2, 3), (1, 0, 2, 3), (3, 2, 0, 1), (3, 2, 1, 0))
 
 
 def dot(a, b, dims=((1,), (0,))):
@@ -411,29 +413,35 @@
     return [(shape, BF, spec) for _ in range(count)]
 
 
-def grads_by_left(left, right, more):
-    n = len(more)
+def grads_by_left(left, right, n, below=None):
     cut, cols = left[0].shape[1] // n, right[0].shape[1]
+    more = 0 if below is None else 2 * below[0].shape[1]
 
     def kernel(*refs):
         l0, l1, r0, r1 = refs[:4]
+        outs = refs[len(refs) - n :]
         grad = (dot(l0[...], r0[...], TN) + dot(l1[...], r1[...], TN)).astype(BF)
         for k in range(n):
 
             @pl.when(pl.program_id(0) == k)
             def _():
-                refs[4 + n + k][:cut] = grad
-                refs[4 + n + k][cut:] = refs[4 + k][...]
+                outs[k][:cut] = grad
+                if more:
+                    a_ref, b_ref, from_a, row = refs[4:8]
+                    part = jnp.where(from_a[k] == 1, a_ref[row[k]], b_ref[row[k]])
+                    outs[k][cut : cut + more // 2] = part[:, :cols]
+                    outs[k][cut + more // 2 :] = part[:, cols:]
 
     ins = [(a, pl.BlockSpec((a.shape[0], cut), lambda i: (0, i))) for a in left]
-    ins += [(a, whole_spec(a)) for a in (*right, *more)]
-    outs = one_by_one(n, (cut + more[0].shape[0], cols))
+    ins += [(a, whole_spec(a)) for a in right]
+    if more:
+        ins += [(a, whole_spec(a)) for a in below[:2]] + [(a, scalar_spec()) for a in below[2:]]
+    outs = one_by_one(n, (cut + more, cols))
     return call(kernel, n, ins, outs, 4 * left[0].size * cols)
 
 
-def grads_by_right(lefts, right, cut, width):
+def grads_by_right(lefts, right, cut, first, n, step=1):
     count = len(lefts)
-    n = width // cut
     tall = lefts[0][0].shape[0]
 
     def kernel(*refs):
@@ -449,7 +457,7 @@
                     outs[k][m] = grad
 
     ins = [(a, whole_spec(a)) for left in lefts for a in left]
-    ins += [(a, pl.BlockSpec((a.shape[0], cut), lambda i: (0, i))) for a in right]
+    ins += [(a, pl.BlockSpec((a.shape[0], cut), lambda i: (0, first + step * i))) for a in right]
     outs = one_by_one(n, (count, tall, cut))
     return call(kernel, n, ins, outs, 4 * count * right[0].size * tall)
 
@@ -725,26 +733,22 @@
         self.group = self.z
         self.slot_ids = self.p ^ jnp.array(XORS, jnp.int32)
         self.head_ids = 8 * self.c + 4 * jnp.arange(2) + self.q
-
-    def turn(self, v):
+        self.order = jnp.array(MEETS, jnp.int32)[self.z]
+        self.dest = jnp.array(PLACES, jnp.int32)[self.z]
+
+    def turn(self, v, places):
         wide = v.shape[1] // 4
         return jnp.concatenate(
-            [
-                lax.dynamic_slice_in_dim(v, ((self.z - k) % 4) * wide, wide, axis=1)
-                for k in range(4)
-            ],
-            axis=1,
+            [lax.dynamic_slice_in_dim(v, places[k] * wide, wide, axis=1) for k in range(4)], axis=1
         )
 
-    def places(self):
-        return (self.z - jnp.arange(4, dtype=jnp.int32)) % 4
-
     def slots(self, own, one, two, three):
+        outer = (self.z == 0) | (self.z == 3)
         return [
             own,
-            pin(jnp.where(self.z >= 1, one[0], three[1])),
-            pin(jnp.where(self.z >= 2, two[0], two[1])),
-            pin(jnp.where(self.z >= 3, three[0], one[1])),
+            one[0],
+            pin(jnp.where(outer, two[0], one[1])),
+            pin(jnp.where(outer, three, two[1])),
         ]
 
     def by_y(self, mine, got, axis):
@@ -764,16 +768,34 @@
 to_x, to_y, to_core = over("x"), over("y"), over("c")
 
 
-def spread(pair, step):
-    up = over("z", [(i, i + 1) for i in range(step, 3)])
-    down = over("z", [(3 - i, 2 - i) for i in range(step, 3)])
-    return up(pair[0]), down(pair[1])
-
-
-def gather(up, down, step):
-    go_up = over("z", [(i, i + 1) for i in range(step)])
-    go_down = over("z", [(3 - i, 2 - i) for i in range(step)])
-    return go_up(up), go_down(down)
+to_pair = over("z", [(0, 1), (1, 0), (2, 3), (3, 2)])
+to_middle = over("z", [(1, 2), (2, 1)])
+outward = over("z", [(1, 0), (2, 3)])
+inward_z = over("z", [(0, 1), (3, 2)])
+
+
+def spread0(own):
+    return to_pair(own), to_middle(own)
+
+
+def spread1(one):
+    return outward(one[1]), to_middle(one[0])
+
+
+def spread2(two):
+    return outward(two[1])
+
+
+def gather1(g):
+    return inward_z(g[3])
+
+
+def gather2(g2, third):
+    return inward_z(g2), to_middle(third)
+
+
+def gather3(first, second):
+    return to_pair(first), to_middle(second)
 
 
 def plus(a, b):
@@ -787,12 +809,14 @@
     clock = Clock()
     now, end = clock.now, clock.end
 
-    def pick(slots, plane):
-        return lax.dynamic_index_in_dim(slots, (plan.z - plane) % 4, 0, False)
+    order, dest = plan.order, plan.dest
+
+    def pick(stack, place):
+        return lax.dynamic_index_in_dim(stack, place, 0, False)
 
     xf = inputs.astype(F32)
-    n1 = pin(plan.turn((xf * inverse_rms(xf)).astype(BF)))
-    og = pin(plan.turn(out_grad))
+    n1 = pin(plan.turn((xf * inverse_rms(xf)).astype(BF), order))
+    og = pin(plan.turn(out_grad, order))
     few = attn_in.shape[0]
     view = attn_in.astype(BF).reshape(few, 4, 2, 2, 4, HD).transpose(4, 2, 0, 1, 3, 5)
     own_in = lax.all_to_all(view.reshape(8, few, -1), plan.tp, 0, 0, tiled=True)
@@ -803,7 +827,7 @@
     end(own_w, n1, og)
 
     a_w, a_n1 = now(own_w, n1)
-    w1 = spread((a_w, a_w), 0)
+    w1 = spread0(a_w)
     nx, ny = to_x(a_n1), to_y(a_n1)
     at = places(now(lengths))
     hid = sglu_in.shape[2] // 2
@@ -814,12 +838,12 @@
     tables += [at.inner, at.out_reach, at.in_reach, at.hop(1, False), at.hop(1, True)]
     end(*w1, nx, ny, my_three, to_three, *tables)
 
-    w2 = spread(now(*w1), 1)
+    w2 = spread1(now(*w1))
     ax, ay = now(nx, ny)
     nd = to_x(ay[:h2]), to_y(ax[h2:])
     end(*w2, *nd)
 
-    w3 = spread(now(*w2), 2)
+    w3 = spread2(now(*w2))
     a_og, a_three = now(og, to_three)
     gx = to_x(a_og)
     got = to_y(a_three)
@@ -827,19 +851,18 @@
     norm1 = n1_a, to_core(n1_a)
     own_three = plan.by_y(my_three, got, 2)
     own_pair, own_third = pin(own_three[:2]), pin(own_three[2])
-    own_first, own_second = pin(own_three[0]), pin(own_three[1])
-    end(*w3, gx, *norm1, own_pair, own_first, own_second, own_third)
-
-    first1 = spread((now(own_first),) * 2, 0)
-    w_in = plan.slots(own_w, *[now(*v) for v in (w1, w2, w3)])
+    end(w3, gx, *norm1, own_pair, own_third)
+
+    pair1 = spread0(now(own_pair))
+    gy = to_y(now(og))
+    w_in = plan.slots(own_w, now(*w1), now(*w2), now(w3))
     outs = jnp.stack([w[deep:] for w in w_in])
-    w_mine = [pick(outs, 2 * plan.c + j) for j in (0, 1)]
-    w_got = to_core(jnp.concatenate([pick(outs, 2 * (1 - plan.c) + j) for j in (0, 1)]))
+    w_mine = [pick(outs, dest[2 * plan.c + j]) for j in (0, 1)]
+    w_got = to_core(jnp.concatenate([pick(outs, dest[2 * (1 - plan.c) + j]) for j in (0, 1)]))
     core0 = plan.c == 0
     raw, gate, qkv, term, leaving = project((now(norm1[0]), norm1[1]), w_in, at)
-    end(*first1, w_got, leaving)
-
-    gy = to_y(now(og))
+    end(*pair1, gy, w_got, leaving)
+
     w_rows = []
     for j in (0, 1):
         got = w_got[j * 2 * few : (j + 1) * 2 * few]
@@ -847,19 +870,16 @@
             w_rows.append(jnp.concatenate([half[:few], half[few:]], axis=1))
     w_out = pin(jnp.concatenate(w_rows))
     entering = at.bring(now(leaving), False)
-    second1 = spread((after(now(own_second), entering),) * 2, 0)
     attn_b, give, state_b = attend(1, qkv, gate, term, entering, w_out, at)
-    end(*second1, gy, give)
-
-    third1 = spread((now(own_third),) * 2, 0)
+    end(give)
+
+    third1 = spread0(now(own_third))
     a_qkv, give = now(qkv, give)
     attn_a, keep, state_a = attend(0, a_qkv, gate, term, entering, w_out, at)
     got = to_core(give)
     a_gx, a_gy = now(gx, gy)
     gd = to_x(a_gy[:h2]), to_y(a_gx[h2:])
-    f1, s1 = now(*first1), now(*second1)
-    pair1 = pin(jnp.stack([f1[0], s1[0]])), pin(jnp.stack([f1[1], s1[1]]))
-    end(*third1, got, keep, *pair1, *gd)
+    end(*third1, got, keep, *gd)
 
     def first_step(keep, got):
         low, high = add_last(keep, got, width)
@@ -873,33 +893,32 @@
 
     keep, got = now(keep, got)
     u, v = first_step(keep, got)
-    third2 = spread(now(*third1), 1)
+    third2 = spread1(now(*third1))
     g_a = pin(jnp.concatenate([og, gx, gy, *now(*gd)]))
     end(u, v, *third2, g_a)
 
     to_2, to_4 = add_halves(keep, got, *now(u, v), width)
     sx, sy = to_x(to_2), to_y(to_4)
-    pair2 = spread(now(*pair1), 1)
+    pair2 = spread1(now(*pair1))
     g_b = to_core(now(g_a))
     end(sx, sy, *pair2, g_b)
 
-    pair3 = spread(now(*pair2), 2)
-    dest = plan.places()
+    pair3 = spread2(now(*pair2))
     mid, branch, r_attn, n2 = mid_rows((keep, got, *now(sx, sy)), inputs, dest)
     mx, my, mc = to_x(n2), to_y(n2), to_core(n2)
-    end(mx, my, mc, *pair3)
-
-    third3 = spread(now(*third2), 2)
+    end(mx, my, mc, pair3)
+
+    third3 = spread2(now(*third2))
     ax, ay = now(mx, my)
     md = to_x(ay[:h2]), to_y(ax[h2:])
     mxyc = to_core(jnp.concatenate([ax, ay]))
     mdc = to_core(jnp.concatenate(md))
     n2_a = pin(jnp.concatenate([n2, mx, my, *md]))
     n2_b = pin(jnp.concatenate([mc, mxyc, mdc]))
-    w_pair = plan.slots(own_pair, now(*pair1), now(*pair2), now(*pair3))
-    end(*third3, n2_a, n2_b, *w_pair)
-
-    w_third = plan.slots(own_third, *[now(*v) for v in (third1, third2, third3)])
+    w_pair = plan.slots(own_pair, now(*pair1), now(*pair2), now(pair3))
+    end(third3, n2_a, n2_b, *w_pair)
+
+    w_third = plan.slots(own_third, now(*third1), now(*third2), now(third3))
     prod_b, turned_b, gf_b, gs_b, give = sglu_rows(n2_b, g_b, w_pair, w_third)
     end(give)
 
@@ -910,63 +929,57 @@
 
     keep, got = now(keep, got)
     u, v = first_step(keep, got)
-    d_pair = grads_by_right([(now(gf_a), gf_b), (gs_a, gs_b)], (n2_a, n2_b), cut, width)
-    end(u, v, *d_pair)
-
-    d_pair = now(*d_pair)
-    pair1 = gather(d_pair[1], d_pair[3], 1)
+    lefts = [(now(gf_a), gf_b), (gs_a, gs_b)]
+    d_late = grads_by_right(lefts, (n2_a, n2_b), cut, 2, 2)
+    end(u, v, *d_late)
+
+    d_late = now(*d_late)
+    pair1 = inward_z(d_late[1])
+    lefts = [(now(gf_a), gf_b), (gs_a, gs_b)]
+    d_pair = [*grads_by_right(lefts, (n2_a, n2_b), cut, 0, 2), *d_late]
     to_2, to_4 = add_halves(keep, got, *now(u, v), width)
     sx, sy = to_x(to_2), to_y(to_4)
-    d_third = grads_by_right([(now(turned_a), turned_b)], (g_a, g_b), cut, width)
-
-    def join(to_up, to_down, up, down):
-        a, b = now(up, down)
-        return pin(plus(to_up, a)), pin(plus(to_down, b))
-
-    def join_part(m, up, down, moved):
-        a, b = now(*moved)
-        return pin(plus(up[m], a[m])), pin(plus(down[m], b[m]))
-
-    end(sx, sy, *pair1, *d_third)
+    d_third = grads_by_right([(now(turned_a), turned_b)], (g_a, g_b), cut, 0, 4)
+
+    def join(part, more):
+        return pin(plus(part, now(more)))
+
+    end(sx, sy, pair1, *d_third, *d_pair)
 
     d_third = [d[0] for d in now(*d_third)]
-    third1 = gather(d_third[1], d_third[3], 1)
-    first2 = gather(*join_part(0, d_pair[2], d_pair[2], pair1), 2)
-    ready = join_part(1, d_pair[2], d_pair[2], pair1)
+    d_pair = now(*d_pair)
+    pair2 = gather2(d_pair[2], pin(plus(d_pair[3], now(pair1))))
     grad_mid, gb = mid_back_rows((keep, got, *now(sx, sy)), out_grad, mid, branch, r_attn, dest)
     bx, by, bc = to_x(gb), to_y(gb), to_core(gb)
     o_give = sglu_last(now(prod_b), w_third)
     o_keep = sglu_last(now(prod_a), w_third)
 
-    end(bx, by, bc, *third1, *first2, o_keep, o_give, *ready)
-
-    second2 = gather(*now(*ready), 2)
+    end(bx, by, bc, *pair2, o_keep, o_give)
+
+    third1 = gather1(now(*d_third))
+    o_got = to_core(now(o_give))
     ax, ay = now(bx, by)
     bd = to_x(ay[:h2]), to_y(ax[h2:])
     bxyc = to_core(jnp.concatenate([ax, ay]))
     bdc = to_core(jnp.concatenate(bd))
     gb_a = pin(jnp.concatenate([gb, bx, by, *bd]))
     gb_b = pin(jnp.concatenate([bc, bxyc, bdc]))
-    ready = join(d_third[2], d_third[2], *third1)
-    end(*second2, gb_a, gb_b, *ready)
-
-    third2 = gather(*now(*ready), 2)
-    o_got = to_core(now(o_give))
+    end(third1, gb_a, gb_b, o_got)
+
+    third2 = gather2(now(d_third[2]), join(d_third[3], third1))
+    ou, ov = first_step(*now(o_keep, o_got))
     ga, gg, mixed, d_term, d_leaving = attend_back_rows(
         (now(gb_a), gb_b), w_out, (attn_a, attn_b), gate, qkv, at
     )
-    d_out = grads_out(mixed, (gb_a, gb_b), width).reshape(2, 2, few, width)
-    ready = join(d_pair[3][0], d_pair[1][0], *first2)
-    core0 = plan.c == 0
-    w_keep = jnp.where(core0, d_out[:, 0], d_out[:, 1])
-    w_got = to_core(jnp.where(core0, d_out[:, 1], d_out[:, 0]))
-    end(*third2, d_leaving, o_got, w_keep, w_got, *ready)
-
-    first3 = gather(*now(*ready), 3)
-    w_got = now(w_got)
-    planes = jnp.concatenate([jnp.where(core0, w_keep, w_got), jnp.where(core0, w_got, w_keep)])
-    planes = [pick(planes, k) for k in range(4)]
-    planes = [pin(jnp.concatenate([v[:, :across], v[:, across:]])) for v in planes]
+    a_pair = now(*pair2)
+    ready = [
+        (pin(plus(d_pair[1][m], a_pair[1][m])), pin(plus(d_pair[2][m], a_pair[0][m])))
+        for m in (0, 1)
+    ]
+    end(*third2, d_leaving, ou, ov, *ready[0], *ready[1])
+
+    first3 = gather3(*now(*ready[0]))
+    d_out = grads_out(now(mixed), (gb_a, gb_b), width)
     d_entering = at.bring(now(d_leaving), True)
 
     def back_half(h, first, state):
@@ -974,25 +987,28 @@
             h, first, raw, ga, gg, state, d_term, d_entering, w_in, width, at
         )
 
-    gp_b, give = back_half(1, qkv, state_b)
-    ready = join(d_pair[3][1], d_pair[1][1], *second2)
-    end(*first3, give, *planes, *ready)
-
-    second3 = gather(*now(*ready), 3)
+    gp_b, give = back_half(1, after(qkv, d_out), state_b)
+    end(*first3, give, d_out)
+
+    second3 = gather3(*now(*ready[1]))
+    parts = now(d_out).reshape(2, 2, few, width)
+    w_keep = jnp.where(core0, parts[:, 0], parts[:, 1])
+    w_got = to_core(jnp.where(core0, parts[:, 1], parts[:, 0]))
     a_qkv, give = now(qkv, give)
     gp_a, keep = back_half(0, a_qkv, state_a)
     got = to_core(give)
-    ready = join(d_third[3], d_third[1], *third2)
-    end(*second3, keep, got, *ready)
-
-    third3 = gather(*now(*ready), 3)
+    ready = join(d_third[1], third2[1]), join(d_third[2], third2[0])
+    end(*second3, keep, got, w_keep, w_got, *ready)
+
+    third3 = gather3(*now(*ready))
     keep, got = now(keep, got)
     u, v = first_step(keep, got)
-    d_w = grads_by_left(norm1, (now(gp_a), gp_b), planes)
+    mine = (order // 2 == plan.c).astype(jnp.int32)
+    d_w = grads_by_left(norm1, (now(gp_a), gp_b), 4, (*now(w_keep, w_got), mine, order % 2))
     end(u, v, *third3, *d_w)
 
     d_w = now(*d_w)
-    w1 = gather(d_w[1], d_w[3], 1)
+    w1 = gather1(d_w)
     to_2, to_4 = add_halves(keep, got, *now(u, v), width)
     sx, sy = to_x(to_2), to_y(to_4)
     sum_three = [
@@ -1002,19 +1018,16 @@
     ]
     sum_three = jnp.stack([v.astype(BF) for v in sum_three])
     my_three, to_three = plan.of_y(sum_three[:, :, :rows], sum_three[:, :, rows:])
-    end(sx, sy, *w1, my_three, to_three)
-
-    ready = join(d_w[2], d_w[2], *w1)
-    w2 = gather(*ready, 2)
+    end(sx, sy, w1, my_three, to_three)
+
+    w2 = gather2(d_w[2], join(d_w[3], w1))
     three_got = to_y(now(to_three))
-    o_keep = after(o_keep, *ready)
-    ou, ov = first_step(o_keep, o_got)
     grad_norm1 = total(keep[:rows], got[:rows], *now(sx, sy))
-    input_grad = grad_mid + srms_back(xf, plan.turn(grad_norm1))
-    end(*w2, three_got, ou, ov)
-
-    ready = join(d_w[3], d_w[1], *w2)
-    w3 = gather(*ready, 3)
+    input_grad = grad_mid + srms_back(xf, plan.turn(grad_norm1, dest))
+    end(*w2, three_got)
+
+    ready = join(d_w[1], w2[1]), join(d_w[2], w2[0])
+    w3 = gather3(*ready)
     to_2, to_4 = add_halves(after(o_keep, *ready), o_got, *now(ou, ov), width)
     ox, oy = to_x(to_2), to_y(to_4)
     sum_three = plan.by_y(my_three, now(three_got), 1)
@@ -1026,7 +1039,7 @@
     sum_in = pin(sum_w[:deep].astype(BF)).reshape(8, few, across)
     sum_in = lax.all_to_all(sum_in, plan.tp, 0, 0, tiled=True)
     sum_out = jnp.concatenate([sum_w[deep : deep + few], sum_w[deep + few :]], axis=1)
-    output = mid + plan.turn(total(o_keep[:rows], o_got[:rows], *now(ox, oy)))
+    output = mid + plan.turn(total(o_keep[:rows], o_got[:rows], *now(ox, oy)), dest)
     return output, input_grad, sum_in, sum_out, sum_pair, sum_third
 
 
@@ -1131,9 +1144,9 @@
             norm2[h], grad_rows[h], w_pair, w_third
         )
     cut = width // 4
-    sum_third = plan.third_back([g[0] for g in grads_by_right([turned], grad_rows, cut, width)])
+    sum_third = plan.third_back([g[0] for g in grads_by_right([turned], grad_rows, cut, 0, 4)])
     grad_norm2 = plan.rows_sum(*back)
-    sum_pair = plan.pair_back(grads_by_right([grad_first, grad_second], norm2, cut, width))
+    sum_pair = plan.pair_back(grads_by_right([grad_first, grad_second], norm2, cut, 0, 4))
 
     grad_mid = out_grad.astype(F32) + srms_back(mid, plan.turn(grad_norm2))
     grad_branch = grad_mid.astype(BF)
@@ -1153,8 +1166,7 @@
         grad_pre[h], back[h] = project_back(
             h, qkv, raw, grad_attn, grad_gate, state[h], d_term, d_entering, w_in, width, at
         )
-    none = [jnp.zeros((16, grad_pre[0].shape[1]), BF)] * 4
-    grad_win = jnp.concatenate([g[:cut] for g in grads_by_left(norm1, grad_pre, none)])
+    grad_win = jnp.concatenate(grads_by_left(norm1, grad_pre, 4))
     sum_in = plan.attn_in_back(grad_win)
     sum_out = plan.attn_out_back(grads_out(mixed, grad_branch, width))
     grad_norm1 = plan.rows_sum(*back)

time: 774 us -> 732 us (0.946)
  waiting for transfers between devices: 248 us -> 217 us
  starting transfers between devices: 136 us -> 118 us
  other arithmetic: 92.2 us -> 76.8 us
  between operations: 4.35 us -> 16.7 us
    ppermute x90 -> x80, waiting for transfers between devices: 237 us -> 208 us  [over(): return lambda v: pin(lax.ppermute(pin(v), axis, pairs))]
    ppermute x90 -> x80, starting transfers between devices: 121 us -> 103 us  [over(): return lambda v: pin(lax.ppermute(pin(v), axis, pairs))]
    select_n x12 -> x8, other arithmetic: 16.3 us -> 7.58 us  [the longest x3 3.65 us: slots(): jnp.where(outer, three, two[1])]
    pallas_call x25 -> x26, Pallas kernels: 230 us -> 235 us  [call(): pl.pallas_call(kernel, grid=(steps,), in_specs=[s for _, s in ins], out_s...]
    unnamed x213 -> x199, local copies, waits for them, and re-layouts: 35 us -> 36.5 us
  transfers between devices with their start and end apart: 94 -> 84, of which waited for: 43 -> 40; matrix products, arithmetic and copies ran while one was open for 14% -> 13% of each run, Pallas kernels for 26% -> 27%
where the time goes in v4:
time: 732 us; the launch traced here: 721 us
  Pallas kernels  235 us (32%)
  waiting for transfers between devices  217 us (30%)
  starting transfers between devices  118 us (16%)
  other arithmetic  76.8 us (10%)
  local copies, waits for them, and re-layouts  57.4 us (8%)
  between operations  16.7 us (2%)
    pallas_call x26, Pallas kernels, call(): pl.pallas_call(kernel, grid=(steps,), in_specs=[s for _, s in ins], out_s...  235 us
    ppermute x80, waiting for transfers between devices, over(): return lambda v: pin(lax.ppermute(pin(v), axis, pairs))  208 us
    ppermute x80, starting transfers between devices, over(): return lambda v: pin(lax.ppermute(pin(v), axis, pairs))  103 us
    unnamed x199, local copies, waits for them, and re-layouts  36.5 us
  transfers between devices with their start and end apart: 84, of which 40 were waited for; matrix products, arithmetic and copies ran while one was open for 13% of the time, Pallas kernels for 27%

profile of v4, /device:TPU:0, one launch (start us, length us, event | category | flops | bytes accessed | tf_op | source)
XLA Modules:
  0.0 721.1 jit_solution(16129732384764473017)
XLA Ops:
  79.5 18.0 %collective-permute-done.5 = bf16[640,1024]{1,0:T(8,128)(2,1)S(1)} collective-permute-done((bf16[640,1024]{1,0:T(8,128)(2,1)}, bf16[640,1024]{1,0:T(8,128)(2,1)S(1)}, u32[]{:S(2)}, u32[]{:S(2)}) %collective-permute-start.5) | collective-permute-done | bytes 1310752 | tf_op jit(solution)/shard_map/ppermute | solution.py:765
  112.7 13.1 %collective-permute-done.11 = bf16[3,704,256]{2,1,0:T(8,128)(2,1)} collective-permute-done((bf16[3,704,256]{2,1,0:T(8,128)(2,1)}, bf16[3,704,256]{2,1,0:T(8,128)(2,1)}, u32[]{:S(2)}, u32[]{:S(2)}) %collective-permute-start.11) | collective-permute-done | bytes 1081376 | tf_op jit(solution)/shard_map/ppermute | solution.py:765
  138.9 17.6 %shard_map.290 = (f32[2048,512]{1,0:T(8,128)}, f32[2048,256]{1,0:T(8,128)}, bf16[2048,768]{1,0:T(8,128)(2,1)}, f32[8,2,128,128]{3,2,1,0:T(8,128)}, f32[2,128,128]{2,1,0:T(8,128)}) custom-call(bf16[1024,2048]{1,0:T(8,128)(2,1)} %constant_dynamic-update-slice_fusion.refs_0_, bf16[1024,2048]{1,0:T(8,128)(2,1)} %collective-permute-done.10.refs_1_, ...), custom_call_target="tpu_custom_call" | custom-call | flops 8589934592 | bytes 24387680 | tf_op jit(solution)/shard_map/pallas_call | solution.py:88
  175.3 7.3 %shard_map.291 = (f32[1024,256]{1,0:T(8,128)}, bf16[1024,2176]{1,0:T(8,128)(2,1)}, bf16[4,2,128,128]{3,2,1,0:T(8,128)(2,1)}) custom-call(bf16[2048,768]{1,0:T(8,128)(2,1)} %get-tuple-element.398.qkv_ref.refs_0_, f32[2048,256]{1,0:T(8,128)} %get-tuple-element.267.gate_ref, f32[8,2,128,128]{3,2,1,0:T(8,128)} %get-tuple-element.268.term_ref, ...), custom_call_target="tpu_custom_call" | custom-call | flops 1342177280 | bytes 13910624 | tf_op jit(solution)/shard_map/pallas_call | solution.py:88
  191.0 7.3 %shard_map.292 = (f32[1024,256]{1,0:T(8,128)}, bf16[1024,2176]{1,0:T(8,128)(2,1)}, bf16[4,2,128,128]{3,2,1,0:T(8,128)(2,1)}) custom-call(bf16[2048,768]{1,0:T(8,128)(2,1)} %get-tuple-element.398.qkv_ref.refs_0_, f32[2048,256]{1,0:T(8,128)} %get-tuple-element.267.gate_ref, f32[8,2,128,128]{3,2,1,0:T(8,128)} %get-tuple-element.268.term_ref, ...), custom_call_target="tpu_custom_call" | custom-call | flops 1342177280 | bytes 13910624 | tf_op jit(solution)/shard_map/pallas_call | solution.py:88
  234.7 25.1 %collective-permute-done.26.c = bf16[256,2176]{1,0:T(8,128)(2,1)S(1)} collective-permute-done((bf16[256,2176]{1,0:T(8,128)(2,1)}, bf16[256,2176]{1,0:T(8,128)(2,1)S(1)}, u32[]{:S(2)}, u32[]{:S(2)}) %collective-permute-start.26) | collective-permute-done | bytes 1114144 | tf_op jit(solution)/shard_map/ppermute | solution.py:765
  273.5 21.5 %collective-permute-done.31 = bf16[256,2048]{1,0:T(8,128)(2,1)S(1)} collective-permute-done((bf16[256,2048]{1,0:T(8,128)(2,1)}, bf16[256,2048]{1,0:T(8,128)(2,1)S(1)}, u32[]{:S(2)}, u32[]{:S(2)}) %collective-permute-start.31) | collective-permute-done | bytes 1048608 | tf_op jit(solution)/shard_map/ppermute | solution.py:765
  304.1 9.8 %collective-permute-done.36 = bf16[128,2048]{1,0:T(8,128)(2,1)S(1)} collective-permute-done((bf16[128,2048]{1,0:T(8,128)(2,1)S(1)}, bf16[128,2048]{1,0:T(8,128)(2,1)S(1)}, u32[]{:S(2)}, u32[]{:S(2)}) %collective-permute-start.36) | collective-permute-done | bytes 524320 | tf_op jit(solution)/shard_map/ppermute | solution.py:765
  322.9 23.7 %shard_map.296 = (bf16[1024,704]{1,0:T(8,128)(2,1)}, bf16[704,1024]{1,0:T(8,128)(2,1)}, bf16[704,1024]{1,0:T(8,128)(2,1)}, bf16[704,1024]{1,0:T(8,128)(2,1)}, bf16[1024,2048]{1,0:T(8,128)(2,1)}) custom-call(bf16[1024,2048]{1,0:T(8,128)(2,1)} %copy-done.77, bf16[1024,2048]{1,0:T(8,128)(2,1)} %collective-permute-done.30.refs_1_.refs_3_, ...), custom_call_target="tpu_custom_call" | custom-call | flops 14763950080 | bytes 27000832 | tf_op jit(solution)/shard_map/pallas_call | solution.py:88
  346.6 24.1 %shard_map.297 = (bf16[1024,704]{1,0:T(8,128)(2,1)}, bf16[704,1024]{1,0:T(8,128)(2,1)}, bf16[704,1024]{1,0:T(8,128)(2,1)}, bf16[704,1024]{1,0:T(8,128)(2,1)}, bf16[1024,2048]{1,0:T(8,128)(2,1)}) custom-call(bf16[1024,2048]{1,0:T(8,128)(2,1)} %copy-done.78, bf16[1024,2048]{1,0:T(8,128)(2,1)} %constant_dynamic-update-slice_fusion.5.refs_1_.refs_2_, ...), custom_call_target="tpu_custom_call" | custom-call | flops 14763950080 | bytes 27000832 | tf_op jit(solution)/shard_map/pallas_call | solution.py:88
  378.0 11.8 %shard_map.299 = (bf16[2,704,512]{2,1,0:T(8,128)(2,1)}, bf16[2,704,512]{2,1,0:T(8,128)(2,1)}) custom-call(bf16[704,1024]{1,0:T(8,128)(2,1)} %get-tuple-element.347.refs_0_, bf16[704,1024]{1,0:T(8,128)(2,1)} %get-tuple-element.329.refs_1_, bf16[704,1024]{1,0:T(8,128)(2,1)} %get-tuple-element.330.refs_2_, bf16[704,1024]{1,0:T(8,128)(2,1)} %get-tuple-element.331.refs_3_, ...), custom_call_target="tpu_custom_call" | custom-call | flops 11811160064 | bytes 17039360 | tf_op jit(solution)/shard_map/pallas_call | solution.py:88
  398.5 11.2 %shard_map.301 = (bf16[1,704,512]{2,1,0:T(8,128)(2,1)}, bf16[1,704,512]{2,1,0:T(8,128)(2,1)}, bf16[1,704,512]{2,1,0:T(8,128)(2,1)}, bf16[1,704,512]{2,1,0:T(8,128)(2,1)}) custom-call(bf16[704,1024]{1,0:T(8,128)(2,1)} %get-tuple-element.341.refs_0_, bf16[704,1024]{1,0:T(8,128)(2,1)} %get-tuple-element.342.refs_1_, ...), custom_call_target="tpu_custom_call" | custom-call | flops 5905580032 | bytes 14155776 | tf_op jit(solution)/shard_map/pallas_call | solution.py:88
  409.7 11.9 %shard_map.302 = (bf16[2,704,512]{2,1,0:T(8,128)(2,1)}, bf16[2,704,512]{2,1,0:T(8,128)(2,1)}) custom-call(bf16[704,1024]{1,0:T(8,128)(2,1)} %get-tuple-element.347.refs_0_, bf16[704,1024]{1,0:T(8,128)(2,1)} %get-tuple-element.329.refs_1_, bf16[704,1024]{1,0:T(8,128)(2,1)} %get-tuple-element.330.refs_2_, bf16[704,1024]{1,0:T(8,128)(2,1)} %get-tuple-element.331.refs_3_, ...), custom_call_target="tpu_custom_call" | custom-call | flops 11811160064 | bytes 17039360 | tf_op jit(solution)/shard_map/pallas_call | solution.py:88
  453.0 8.8 %collective-permute-done.46 = bf16[256,2176]{1,0:T(8,128)(2,1)S(1)} collective-permute-done((bf16[256,2176]{1,0:T(8,128)(2,1)}, bf16[256,2176]{1,0:T(8,128)(2,1)S(1)}, u32[]{:S(2)}, u32[]{:S(2)}) %collective-permute-start.46) | collective-permute-done | bytes 1114144 | tf_op jit(solution)/shard_map/ppermute | solution.py:765
  470.4 10.7 %collective-permute-done.54 = bf16[128,2176]{1,0:T(8,128)(2,1)S(1)} collective-permute-done((bf16[128,2176]{1,0:T(8,128)(2,1)S(1)}, bf16[128,2176]{1,0:T(8,128)(2,1)S(1)}, u32[]{:S(2)}, u32[]{:S(2)}) %collective-permute-start.54) | collective-permute-done | bytes 557088 | tf_op jit(solution)/shard_map/ppermute | solution.py:765
  505.8 13.1 %shard_map.306 = (bf16[2048,256]{1,0:T(8,128)(2,1)}, bf16[2048,256]{1,0:T(8,128)(2,1)}, bf16[2048,256]{1,0:T(8,128)(2,1)}, f32[8,2,128,128]{3,2,1,0:T(8,128)}, f32[2,128,128]{2,1,0:T(8,128)}) custom-call(bf16[1024,2176]{1,0:T(8,128)(2,1)} %copy-done.9, bf16[1024,2176]{1,0:T(8,128)(2,1)} %copy-done.8, bf16[256,2048]{1,0:T(8,128)(2,1)} %maximum_maximum_fusion.w_ref, ...), custom_call_target="tpu_custom_call" | custom-call | flops 2147483648 | bytes 21766240 | tf_op jit(solution)/shard_map/pallas_call | solution.py:88
  534.1 12.7 %shard_map.309 = (bf16[1024,1024]{1,0:T(8,128)(2,1)}, bf16[1024,2048]{1,0:T(8,128)(2,1)}) custom-call(bf16[2048,768]{1,0:T(8,128)(2,1)} %get-tuple-element.398.qkv_ref.refs_0_, f32[2048,512]{1,0:T(8,128)} %get-tuple-element.390.refs_1_, bf16[2048,256]{1,0:T(8,128)(2,1)} %get-tuple-element.391.refs_2_, bf16[2048,256]{1,0:T(8,128)(2,1)} %get-tuple-element.392.refs_3_, ...), custom_call_target="tpu_custom_call" | custom-call | flops 4294967296 | bytes 23085696 | tf_op jit(solution)/shard_map/pallas_call | solution.py:88
  553.6 12.7 %shard_map.310 = (bf16[1024,1024]{1,0:T(8,128)(2,1)}, bf16[1024,2048]{1,0:T(8,128)(2,1)}) custom-call(bf16[2048,768]{1,0:T(8,128)(2,1)} %get-tuple-element.398.qkv_ref.refs_0_, f32[2048,512]{1,0:T(8,128)} %get-tuple-element.390.refs_1_, bf16[2048,256]{1,0:T(8,128)(2,1)} %get-tuple-element.391.refs_2_, bf16[2048,256]{1,0:T(8,128)(2,1)} %get-tuple-element.392.refs_3_, ...), custom_call_target="tpu_custom_call" | custom-call | flops 4294967296 | bytes 23085696 | tf_op jit(solution)/shard_map/pallas_call | solution.py:88
  577.9 15.5 %shard_map.311 = (bf16[640,1024]{1,0:T(8,128)(2,1)}, bf16[640,1024]{1,0:T(8,128)(2,1)}, bf16[640,1024]{1,0:T(8,128)(2,1)}, bf16[640,1024]{1,0:T(8,128)(2,1)}) custom-call(bf16[1024,2048]{1,0:T(8,128)(2,1)} %constant_dynamic-update-slice_fusion.refs_0_, bf16[1024,2048]{1,0:T(8,128)(2,1)} %collective-permute-done.10.refs_1_, ...), custom_call_target="tpu_custom_call" | custom-call | flops 8589934592 | bytes 18874400 | tf_op jit(solution)/shard_map/pallas_call | solution.py:88
  610.5 17.1 %collective-permute-done.73 = bf16[256,2048]{1,0:T(8,128)(2,1)S(1)} collective-permute-done((bf16[256,2048]{1,0:T(8,128)(2,1)}, bf16[256,2048]{1,0:T(8,128)(2,1)S(1)}, u32[]{:S(2)}, u32[]{:S(2)}) %collective-permute-start.73) | collective-permute-done | bytes 1048608 | tf_op jit(solution)/shard_map/ppermute | solution.py:765
  636.2 15.3 %collective-permute-done.76 = bf16[640,1024]{1,0:T(8,128)(2,1)S(1)} collective-permute-done((bf16[640,1024]{1,0:T(8,128)(2,1)S(1)}, bf16[640,1024]{1,0:T(8,128)(2,1)S(1)}, u32[]{:S(2)}, u32[]{:S(2)}) %collective-permute-start.76) | collective-permute-done | bytes 1310752 | tf_op jit(solution)/shard_map/ppermute | solution.py:765
  656.6 8.6 %collective-permute-start.79 = (bf16[640,1024]{1,0:T(8,128)(2,1)}, bf16[640,1024]{1,0:T(8,128)(2,1)}, u32[]{:S(2)}, u32[]{:S(2)}) collective-permute-start(bf16[640,1024]{1,0:T(8,128)(2,1)} %add_convert_fusion.2), channel_id=1, source_target_pairs={{0,8},{8,0},{16,24},{24,16},{1,9},{9,1},{17,25},{25,17},{2,10},{10... | collective-permute-start | bytes 3932168 | tf_op jit(solution)/shard_map/ppermute | solution.py:765
  678.7 7.5 %multiply_add_fusion = (f32[2,256,1408]{2,1,0:T(8,128)}, f32[2,256,1408]{2,1,0:T(8,128)}, f32[2,256,1408]{2,1,0:T(8,128)}) fusion(f32[2,256,1408]{2,1,0:T(8,128)} %param.33, f32[2,256,1408]{2,1,0:T(8,128)S(1)} %copy-done.13, bf16[2,1408,256]{1,2,0:T(8,128)(2,1)} %copy.74, f32[2,256,1408]{2,1,0:T(8,128)} %param.29), kind=kLoop, calls=%fused_computation.9 | loop fusion | flops 7208960 | bytes 18743296 | tf_op jit(solution)/shard_map/add | solution.py:42
  705.6 8.2 %all-to-all-done.1.g_ref = bf16[8,64,1024]{2,1,0:T(8,128)(2,1)S(1)} async-done(((bf16[8,64,1024]{2,1,0:T(8,128)(2,1)}), bf16[8,64,1024]{2,1,0:T(8,128)(2,1)S(1)}, u32[]{:S(2)}, u32[]{:S(2)}) %all-to-all-start.1) | async-done | bytes 1048608 | tf_op jit(solution)/shard_map/all_to_all | solution.py:1040
  (502 shorter events, 371.6 us)
Async XLA Ops:
  28.4 31.2 %collective-permute-start.2 = (bf16[640,1024]{1,0:T(8,128)(2,1)S(1)}, bf16[640,1024]{1,0:T(8,128)(2,1)S(1)}, u32[]{:S(2)}, u32[]{:S(2)}) collective-permute-start(bf16[640,1024]{1,0:T(8,128)(2,1)S(1)} %pad_maximum_fusion.4.refs_2_.refs_7_), channel_id=1, source_target_pairs={{0,8},{8,0},{16,24},{24,16},{1,9},{9,1},{17,25},{25,17},{2,10},{10... | collective-permute-start | bytes 3932168 | tf_op jit(solution)/shard_map/ppermute | solution.py:765
  30.1 29.6 %collective-permute-start.3 = (bf16[640,1024]{1,0:T(8,128)(2,1)S(1)}, bf16[640,1024]{1,0:T(8,128)(2,1)}, u32[]{:S(2)}, u32[]{:S(2)}) collective-permute-start(bf16[640,1024]{1,0:T(8,128)(2,1)S(1)} %pad_maximum_fusion.4.refs_2_.refs_7_), channel_id=1, source_target_pairs={{8,16},{16,8},{9,17},{17,9},{10,18},{18,10},{11,19},{19,11},{12,20... | collective-permute-start | bytes 3932168 | tf_op jit(solution)/shard_map/ppermute | solution.py:765
  61.4 36.1 %collective-permute-start.5 = (bf16[640,1024]{1,0:T(8,128)(2,1)}, bf16[640,1024]{1,0:T(8,128)(2,1)S(1)}, u32[]{:S(2)}, u32[]{:S(2)}) collective-permute-start(bf16[640,1024]{1,0:T(8,128)(2,1)} %collective-permute-done.3), channel_id=1, source_target_pairs={{8,0},{16,24},{9,1},{17,25},{10,2},{18,26},{11,3},{19,27},{12,4},{... | collective-permute-start | bytes 3932168 | tf_op jit(solution)/shard_map/ppermute | solution.py:765
  99.2 34.4 %collective-permute-start.10 = (bf16[1024,2048]{1,0:T(8,128)(2,1)}, bf16[1024,2048]{1,0:T(8,128)(2,1)}, u32[]{:S(2)}, u32[]{:S(2)}) collective-permute-start(bf16[1024,2048]{1,0:T(8,128)(2,1)} %constant_dynamic-update-slice_fusion.refs_0_), channel_id=1, source_target_pairs={{0,1},{1,0},{2,3},{3,2},{4,5},{5,4},{6,7},{7,6},{8,9},{9,8},{10,11... | collective-permute-start | bytes 12582920 | tf_op jit(solution)/shard_map/ppermute | solution.py:765
  99.3 26.6 %collective-permute-start.11 = (bf16[3,704,256]{2,1,0:T(8,128)(2,1)}, bf16[3,704,256]{2,1,0:T(8,128)(2,1)}, u32[]{:S(2)}, u32[]{:S(2)}) collective-permute-start(bf16[3,704,256]{2,1,0:T(8,128)(2,1)} %get-tuple-element.254), channel_id=1, source_target_pairs={{0,4},{4,0},{1,5},{5,1},{2,6},{6,2},{3,7},{7,3},{8,12},{12,8},{9,1... | collective-permute-start | bytes 3244040 | tf_op jit(solution)/shard_map/ppermute | solution.py:765
  100.5 33.1 %collective-permute-start.8 = (bf16[640,1024]{1,0:T(8,128)(2,1)}, bf16[640,1024]{1,0:T(8,128)(2,1)}, u32[]{:S(2)}, u32[]{:S(2)}) collective-permute-start(bf16[640,1024]{1,0:T(8,128)(2,1)} %collective-permute-done.6), channel_id=1, source_target_pairs={{8,0},{16,24},{9,1},{17,25},{10,2},{18,26},{11,3},{19,27},{12,4},{... | collective-permute-start | bytes 3932168 | tf_op jit(solution)/shard_map/ppermute | solution.py:765
  133.7 33.0 %collective-permute-start.12 = (bf16[2,704,512]{2,1,0:T(8,128)(2,1)S(1)}, bf16[2,704,512]{2,1,0:T(8,128)(2,1)}, u32[]{:S(2)}, u32[]{:S(2)}) collective-permute-start(bf16[2,704,512]{2,1,0:T(8,128)(2,1)S(1)} %fusion.11.refs_2_), channel_id=1, source_target_pairs={{0,8},{8,0},{16,24},{24,16},{1,9},{9,1},{17,25},{25,17},{2,10},{10... | collective-permute-start | bytes 4325384 | tf_op jit(solution)/shard_map/ppermute | solution.py:765
  133.7 33.0 %collective-permute-start.13 = (bf16[2,704,512]{2,1,0:T(8,128)(2,1)S(1)}, bf16[2,704,512]{2,1,0:T(8,128)(2,1)S(1)}, u32[]{:S(2)}, u32[]{:S(2)}) collective-permute-start(bf16[2,704,512]{2,1,0:T(8,128)(2,1)S(1)} %fusion.11.refs_2_), channel_id=1, source_target_pairs={{8,16},{16,8},{9,17},{17,9},{10,18},{18,10},{11,19},{19,11},{12,20... | collective-permute-start | bytes 4325384 | tf_op jit(solution)/shard_map/ppermute | solution.py:765
  138.1 25.8 %collective-permute-start.14 = (bf16[256,2048]{1,0:T(8,128)(2,1)}, bf16[256,2048]{1,0:T(8,128)(2,1)S(1)}, u32[]{:S(2)}, u32[]{:S(2)}) collective-permute-start(bf16[256,2048]{1,0:T(8,128)(2,1)} %get-tuple-element.264), channel_id=1, source_target_pairs={{0,4},{4,0},{1,5},{5,1},{2,6},{6,2},{3,7},{7,3},{8,12},{12,8},{9,1... | collective-permute-start | bytes 3145736 | tf_op jit(solution)/shard_map/ppermute | solution.py:765
  225.2 39.4 %collective-permute-start.30 = (bf16[1024,2048]{1,0:T(8,128)(2,1)}, bf16[1024,2048]{1,0:T(8,128)(2,1)}, u32[]{:S(2)}, u32[]{:S(2)}) collective-permute-start(bf16[1024,2048]{1,0:T(8,128)(2,1)} %constant_dynamic-update-slice_fusion.5.refs_1_.refs_2_), channel_id=1, source_target_pairs={{0,1},{1,0},{2,3},{3,2},{4,5},{5,4},{6,7},{7,6},{8,9},{9,8},{10,11... | collective-permute-start | bytes 12582920 | tf_op jit(solution)/shard_map/ppermute | solution.py:765
  225.2 35.7 %collective-permute-start.29 = (bf16[2,704,512]{2,1,0:T(8,128)(2,1)}, bf16[2,704,512]{2,1,0:T(8,128)(2,1)S(1)}, u32[]{:S(2)}, u32[]{:S(2)}) collective-permute-start(bf16[2,704,512]{2,1,0:T(8,128)(2,1)} %collective-permute-done.12.refs_3_), channel_id=1, source_target_pairs={{8,16},{16,8},{9,17},{17,9},{10,18},{18,10},{11,19},{19,11},{12,20... | collective-permute-start | bytes 4325384 | tf_op jit(solution)/shard_map/ppermute | solution.py:765
  226.0 38.6 %collective-permute-start.28 = (bf16[2,704,512]{2,1,0:T(8,128)(2,1)S(1)}, bf16[2,704,512]{2,1,0:T(8,128)(2,1)S(1)}, u32[]{:S(2)}, u32[]{:S(2)}) collective-permute-start(bf16[2,704,512]{2,1,0:T(8,128)(2,1)S(1)} %copy-done.28), channel_id=1, source_target_pairs={{8,0},{16,24},{9,1},{17,25},{10,2},{18,26},{11,3},{19,27},{12,4},{... | collective-permute-start | bytes 4325384 | tf_op jit(solution)/shard_map/ppermute | solution.py:765
  232.6 27.2 %collective-permute-start.26 = (bf16[256,2176]{1,0:T(8,128)(2,1)}, bf16[256,2176]{1,0:T(8,128)(2,1)S(1)}, u32[]{:S(2)}, u32[]{:S(2)}) collective-permute-start(bf16[256,2176]{1,0:T(8,128)(2,1)} %get-tuple-element.290), channel_id=1, source_target_pairs={{0,2},{2,0},{1,3},{3,1},{4,6},{6,4},{5,7},{7,5},{8,10},{10,8},{9,1... | collective-permute-start | bytes 3342344 | tf_op jit(solution)/shard_map/ppermute | solution.py:765
  234.1 26.9 %collective-permute-start.27 = (bf16[256,2176]{1,0:T(8,128)(2,1)}, bf16[256,2176]{1,0:T(8,128)(2,1)S(1)}, u32[]{:S(2)}, u32[]{:S(2)}) collective-permute-start(bf16[256,2176]{1,0:T(8,128)(2,1)} %get-tuple-element.291), channel_id=1, source_target_pairs={{0,4},{4,0},{1,5},{5,1},{2,6},{6,2},{3,7},{7,3},{8,12},{12,8},{9,1... | collective-permute-start | bytes 3342344 | tf_op jit(solution)/shard_map/ppermute | solution.py:765
  264.6 34.3 %collective-permute-start.34 = (bf16[2,704,512]{2,1,0:T(8,128)(2,1)S(1)}, bf16[2,704,512]{2,1,0:T(8,128)(2,1)S(1)}, u32[]{:S(2)}, u32[]{:S(2)}) collective-permute-start(bf16[2,704,512]{2,1,0:T(8,128)(2,1)S(1)} %collective-permute-done.29), channel_id=1, source_target_pairs={{8,0},{16,24},{9,1},{17,25},{10,2},{18,26},{11,3},{19,27},{12,4},{... | collective-permute-start | bytes 4325384 | tf_op jit(solution)/shard_map/ppermute | solution.py:765
  390.9 32.3 %collective-permute-start.45 = (bf16[2,704,512]{2,1,0:T(8,128)(2,1)}, bf16[2,704,512]{2,1,0:T(8,128)(2,1)S(1)}, u32[]{:S(2)}, u32[]{:S(2)}) collective-permute-start(bf16[2,704,512]{2,1,0:T(8,128)(2,1)} %get-tuple-element.361), channel_id=1, source_target_pairs={{0,8},{24,16},{1,9},{25,17},{2,10},{26,18},{3,11},{27,19},{4,12},{... | collective-permute-start | bytes 4325384 | tf_op jit(solution)/shard_map/ppermute | solution.py:765
  423.6 38.7 %collective-permute-start.50 = (bf16[2,704,512]{2,1,0:T(8,128)(2,1)S(1)}, bf16[2,704,512]{2,1,0:T(8,128)(2,1)S(1)}, u32[]{:S(2)}, u32[]{:S(2)}) collective-permute-start(bf16[2,704,512]{2,1,0:T(8,128)(2,1)S(1)} %add_convert_fusion), channel_id=1, source_target_pairs={{8,16},{16,8},{9,17},{17,9},{10,18},{18,10},{11,19},{19,11},{12,20... | collective-permute-start | bytes 4325384 | tf_op jit(solution)/shard_map/ppermute | solution.py:765
  424.5 39.9 %collective-permute-start.49 = (bf16[2,704,512]{2,1,0:T(8,128)(2,1)S(1)}, bf16[2,704,512]{2,1,0:T(8,128)(2,1)}, u32[]{:S(2)}, u32[]{:S(2)}) collective-permute-start(bf16[2,704,512]{2,1,0:T(8,128)(2,1)S(1)} %copy-done.29), channel_id=1, source_target_pairs={{0,8},{24,16},{1,9},{25,17},{2,10},{26,18},{3,11},{27,19},{4,12},{... | collective-permute-start | bytes 4325384 | tf_op jit(solution)/shard_map/ppermute | solution.py:765
  492.7 27.6 %collective-permute-start.59 = (bf16[128,2048]{1,0:T(8,128)(2,1)}, bf16[128,2048]{1,0:T(8,128)(2,1)}, u32[]{:S(2)}, u32[]{:S(2)}) collective-permute-start(bf16[128,2048]{1,0:T(8,128)(2,1)} %get-tuple-element.379), channel_id=1, source_target_pairs={{0,2},{2,0},{1,3},{3,1},{4,6},{6,4},{5,7},{7,5},{8,10},{10,8},{9,1... | collective-permute-start | bytes 1572872 | tf_op jit(solution)/shard_map/ppermute | solution.py:765
  494.1 26.2 %collective-permute-start.60 = (bf16[128,2048]{1,0:T(8,128)(2,1)}, bf16[128,2048]{1,0:T(8,128)(2,1)}, u32[]{:S(2)}, u32[]{:S(2)}) collective-permute-start(bf16[128,2048]{1,0:T(8,128)(2,1)} %get-tuple-element.380), channel_id=1, source_target_pairs={{0,4},{4,0},{1,5},{5,1},{2,6},{6,2},{3,7},{7,3},{8,12},{12,8},{9,1... | collective-permute-start | bytes 1572872 | tf_op jit(solution)/shard_map/ppermute | solution.py:765
  594.5 33.7 %collective-permute-start.72 = (bf16[640,1024]{1,0:T(8,128)(2,1)}, bf16[640,1024]{1,0:T(8,128)(2,1)S(1)}, u32[]{:S(2)}, u32[]{:S(2)}) collective-permute-start(bf16[640,1024]{1,0:T(8,128)(2,1)} %get-tuple-element.426), channel_id=1, source_target_pairs={{0,8},{24,16},{1,9},{25,17},{2,10},{26,18},{3,11},{27,19},{4,12},{... | collective-permute-start | bytes 3932168 | tf_op jit(solution)/shard_map/ppermute | solution.py:765
  605.3 46.2 %collective-permute-start.76 = (bf16[640,1024]{1,0:T(8,128)(2,1)S(1)}, bf16[640,1024]{1,0:T(8,128)(2,1)S(1)}, u32[]{:S(2)}, u32[]{:S(2)}) collective-permute-start(bf16[640,1024]{1,0:T(8,128)(2,1)S(1)} %copy-done.41), channel_id=1, source_target_pairs={{0,8},{24,16},{1,9},{25,17},{2,10},{26,18},{3,11},{27,19},{4,12},{... | collective-permute-start | bytes 3932168 | tf_op jit(solution)/shard_map/ppermute | solution.py:765
  653.2 38.2 %collective-permute-start.80 = (bf16[640,1024]{1,0:T(8,128)(2,1)}, bf16[640,1024]{1,0:T(8,128)(2,1)}, u32[]{:S(2)}, u32[]{:S(2)}) collective-permute-start(bf16[640,1024]{1,0:T(8,128)(2,1)} %add_convert_fusion.1), channel_id=1, source_target_pairs={{8,16},{16,8},{9,17},{17,9},{10,18},{18,10},{11,19},{19,11},{12,20... | collective-permute-start | bytes 3932168 | tf_op jit(solution)/shard_map/ppermute | solution.py:765
  656.6 34.8 %collective-permute-start.79 = (bf16[640,1024]{1,0:T(8,128)(2,1)}, bf16[640,1024]{1,0:T(8,128)(2,1)}, u32[]{:S(2)}, u32[]{:S(2)}) collective-permute-start(bf16[640,1024]{1,0:T(8,128)(2,1)} %add_convert_fusion.2), channel_id=1, source_target_pairs={{0,8},{8,0},{16,24},{24,16},{1,9},{9,1},{17,25},{25,17},{2,10},{10... | collective-permute-start | bytes 3932168 | tf_op jit(solution)/shard_map/ppermute | solution.py:765
  (150 other events, 1881.0 us)

commit v5 on v4

--- a/solution.py
+++ b/solution.py
@@ -45,6 +45,9 @@
 
 ROWS = 256
 HALF = 4
+SUB = 2
+STEPS = HALF // SUB
+TALL = SUB * ROWS
 HD = 128
 VMEM = 56 * 1024 * 1024
 EXTRA = 128
@@ -110,12 +113,12 @@
 
 def pair_spec(shape, late):
     if late:
-        return pl.BlockSpec(shape, lambda i: (jnp.maximum(i - HALF, 0),) + (0,) * (len(shape) - 1))
-    return pl.BlockSpec(shape, lambda i: (jnp.minimum(i, HALF - 1),) + (0,) * (len(shape) - 1))
+        return pl.BlockSpec(shape, lambda i: (jnp.maximum(i - STEPS, 0),) + (0,) * (len(shape) - 1))
+    return pl.BlockSpec(shape, lambda i: (jnp.minimum(i, STEPS - 1),) + (0,) * (len(shape) - 1))
 
 
 def half_spec(shape, h):
-    return pl.BlockSpec(shape, lambda i: (i + h * HALF,) + (0,) * (len(shape) - 1))
+    return pl.BlockSpec(shape, lambda i: (i + h * STEPS,) + (0,) * (len(shape) - 1))
 
 
 def project(n1, w_in, at):
@@ -133,7 +136,7 @@
         pre = None
         for k in range(parts):
             some = slice(k * deep, (k + 1) * deep)
-            x = jnp.where(i < HALF, a_ref[:, some], b_ref[:, some])
+            x = jnp.where(i < STEPS, a_ref[:, some], b_ref[:, some])
             new = dot(x, w_refs[k][...])
             pre = new if pre is None else pre + new
         pq, pk, pv = pre[:, :cols], pre[:, cols : 2 * cols], pre[:, 2 * cols : 3 * cols]
@@ -149,28 +152,32 @@
         def _():
             leaving_ref[...] = jnp.zeros_like(leaving_ref)
 
-        for j in range(own):
-            leave = jnp.where(seg_ref[0] == last_ref[i], ramp_ref[:, own + j : own + j + 1], 0.0)
-            head = slice(j * HD, (j + 1) * HD)
-            scaled = (key[:, head].astype(F32) * leave).astype(BF)
-            term = dot(scaled, value[:, head], TN)
-            term_ref[0, j] = term
-            leaving_ref[j] += reach_ref[j, i] * term
+        for s in range(SUB):
+            b = i * SUB + s
+            block = slice(s * ROWS, (s + 1) * ROWS)
+            for j in range(own):
+                ramp = ramp_ref[:, own + j : own + j + 1]
+                leave = jnp.where(seg_ref[s] == last_ref[b], ramp, 0.0)
+                head = slice(j * HD, (j + 1) * HD)
+                scaled = (key[block, head].astype(F32) * leave).astype(BF)
+                term = dot(scaled, value[block, head], TN)
+                term_ref[s, j] = term
+                leaving_ref[j] += reach_ref[j, b] * term
 
     some = pl.BlockSpec((deep, 4 * cols), lambda i: (0, 0), pipeline_mode=pl.Buffered(1))
-    ins = [(v, pair_spec((ROWS, width), late)) for late, v in enumerate(n1)]
+    ins = [(v, pair_spec((TALL, width), late)) for late, v in enumerate(n1)]
     ins += [(w, some) for w in w_in]
-    ins += [(at.cols, block_spec((1, ROWS, 1))), (at.ramps, whole_spec(at.ramps))]
+    ins += [(at.cols, block_spec((SUB, ROWS, 1))), (at.ramps, whole_spec(at.ramps))]
     ins += [(v, scalar_spec()) for v in (at.last, at.out_reach)]
     n = 2 * HALF
     outs = [
-        ((n * ROWS, 2 * cols), F32, (ROWS, 2 * cols)),
-        ((n * ROWS, cols), F32, (ROWS, cols)),
-        ((n * ROWS, 3 * cols), BF, (ROWS, 3 * cols)),
-        ((n, own, HD, HD), F32, (1, own, HD, HD)),
+        ((n * ROWS, 2 * cols), F32, (TALL, 2 * cols)),
+        ((n * ROWS, cols), F32, (TALL, cols)),
+        ((n * ROWS, 3 * cols), BF, (TALL, 3 * cols)),
+        ((n, own, HD, HD), F32, (SUB, own, HD, HD)),
         ((own, HD, HD), F32, pl.BlockSpec((own, HD, HD), lambda i: (0, 0, 0))),
     ]
-    return call(kernel, n, ins, outs, 4 * n1[0].size * 4 * cols)
+    return call(kernel, 2 * STEPS, ins, outs, 4 * n1[0].size * 4 * cols)
 
 
 def combine(weights, terms, more, reach):
@@ -189,51 +196,46 @@
         qkv_ref, gate_ref, term_ref, more_ref, w_ref, sc_ref, sr_ref, fade_ref, ramp_ref,
         prev_ref, inner_ref, reach_ref, attn_ref, branch_ref, state_ref,
     ):
-        i = pl.program_id(0) + h * HALF
-        for j in range(own):
+        for s, j in ((s, j) for s in range(SUB) for j in range(own)):
+            i = (pl.program_id(0) + h * STEPS) * SUB + s
+            block = slice(s * ROWS, (s + 1) * ROWS)
             head = slice(j * HD, (j + 1) * HD)
-            q = qkv_ref[:, j * HD : (j + 1) * HD]
-            k = qkv_ref[:, cols + j * HD : cols + (j + 1) * HD]
-            v = qkv_ref[:, 2 * cols + j * HD : 2 * cols + (j + 1) * HD]
+            q = qkv_ref[block, j * HD : (j + 1) * HD]
+            k = qkv_ref[block, cols + j * HD : cols + (j + 1) * HD]
+            v = qkv_ref[block, 2 * cols + j * HD : 2 * cols + (j + 1) * HD]
             state = combine(
                 lambda c: inner_ref[j, i * 2 * HALF + c],
                 lambda c: term_ref[c, j],
                 more_ref[j],
                 reach_ref[j, i],
             ).astype(BF)
-            state_ref[0, j] = state
-            enter = jnp.where(sc_ref[0] == prev_ref[i], ramp_ref[:, j : j + 1], 0.0)
-            weights = (dot(q, k, NT) * mask_of(fade_ref[j], sc_ref[0], sr_ref[0])).astype(BF)
-            attn_ref[:, head] = dot(weights, v) + enter * dot(q, state)
+            state_ref[s, j] = state
+            enter = jnp.where(sc_ref[s] == prev_ref[i], ramp_ref[:, j : j + 1], 0.0)
+            weights = (dot(q, k, NT) * mask_of(fade_ref[j], sc_ref[s], sr_ref[s])).astype(BF)
+            attn_ref[block, head] = dot(weights, v) + enter * dot(q, state)
         attn = attn_ref[...]
         branch_ref[:, :width] = dot((attn * gate_ref[...]).astype(BF), w_ref[...]).astype(BF)
         rest = jnp.sum(attn * attn, axis=1, keepdims=True)
-        lane = lax.broadcasted_iota(jnp.int32, (ROWS, EXTRA), 1)
-        strip = jnp.zeros((ROWS, EXTRA), F32)
-        for n in range(3):
-            top = rest.astype(BF).astype(F32)
-            strip = jnp.where(lane == n, top, strip)
-            rest = rest - top
-        branch_ref[:, width:] = strip.astype(BF)
+        branch_ref[:, width:] = strip_of([rest])
 
     n = HALF
     ins = [
-        (qkv, half_spec((ROWS, 3 * cols), h)),
-        (gate, half_spec((ROWS, cols), h)),
+        (qkv, half_spec((TALL, 3 * cols), h)),
+        (gate, half_spec((TALL, cols), h)),
         (term, whole_spec(term)),
         (entering, whole_spec(entering)),
         (w_out, whole_spec(w_out)),
-        (at.cols, half_spec((1, ROWS, 1), h)),
-        (at.rows, half_spec((1, 1, ROWS), h)),
+        (at.cols, half_spec((SUB, ROWS, 1), h)),
+        (at.rows, half_spec((SUB, 1, ROWS), h)),
         (at.fade, whole_spec(at.fade)),
         (at.ramps, whole_spec(at.ramps)),
     ] + [(v, scalar_spec()) for v in (at.prev, at.inner, at.in_reach)]
     outs = [
-        ((n * ROWS, cols), F32, (ROWS, cols)),
-        ((n * ROWS, width + EXTRA), BF, (ROWS, width + EXTRA)),
-        ((n, own, HD, HD), BF, (1, own, HD, HD)),
+        ((n * ROWS, cols), F32, (TALL, cols)),
+        ((n * ROWS, width + EXTRA), BF, (TALL, width + EXTRA)),
+        ((n, own, HD, HD), BF, (SUB, own, HD, HD)),
     ]
-    return call(kernel, n, ins, outs, 2 * n * ROWS * cols * (width + 2 * ROWS))
+    return call(kernel, STEPS, ins, outs, 2 * n * ROWS * cols * (width + 2 * ROWS))
 
 
 def sglu_rows(n2, g, w_pair, w_third):
@@ -302,7 +304,7 @@
         ga_ref, gg_ref, mixed_ref, term_ref, leaving_ref,
     ):
         i = pl.program_id(0)
-        early = i < HALF
+        early = i < STEPS
         extra = jnp.where(early, gb_a[:, width:], gb_b[:, width:]).astype(F32)
         r = extra[:, 0:1] + extra[:, 1:2] + extra[:, 2:3]
         pull = extra[:, 3:4] + extra[:, 4:5] + extra[:, 5:6]
@@ -318,27 +320,29 @@
         def _():
             leaving_ref[...] = jnp.zeros_like(leaving_ref)
 
-        for j in range(own):
-            enter = jnp.where(sc_ref[0] == prev_ref[i], ramp_ref[:, j : j + 1], 0.0)
-            q = qkv_ref[:, j * HD : (j + 1) * HD].astype(F32)
-            term = dot((q * enter).astype(BF), ga[:, j * HD : (j + 1) * HD], TN)
-            term_ref[0, j] = term
-            leaving_ref[j] += reach_ref[j, i] * term
+        for s, j in ((s, j) for s in range(SUB) for j in range(own)):
+            b = i * SUB + s
+            block = slice(s * ROWS, (s + 1) * ROWS)
+            enter = jnp.where(sc_ref[s] == prev_ref[b], ramp_ref[:, j : j + 1], 0.0)
+            q = qkv_ref[block, j * HD : (j + 1) * HD].astype(F32)
+            term = dot((q * enter).astype(BF), ga[block, j * HD : (j + 1) * HD], TN)
+            term_ref[s, j] = term
+            leaving_ref[j] += reach_ref[j, b] * term
 
     n = 2 * HALF
-    ins = [(v, pair_spec((ROWS, v.shape[1]), late)) for late, v in enumerate(gb)]
+    ins = [(v, pair_spec((TALL, v.shape[1]), late)) for late, v in enumerate(gb)]
     ins += [(w_out, whole_spec(w_out))]
-    ins += [(v, pair_spec((ROWS, cols), late)) for late, v in enumerate(attn)]
+    ins += [(v, pair_spec((TALL, cols), late)) for late, v in enumerate(attn)]
     ins += [
-        (gate, block_spec((ROWS, cols))),
-        (qkv, block_spec((ROWS, 3 * cols))),
-        (at.cols, block_spec((1, ROWS, 1))),
+        (gate, block_spec((TALL, cols))),
+        (qkv, block_spec((TALL, 3 * cols))),
+        (at.cols, block_spec((SUB, ROWS, 1))),
         (at.ramps, whole_spec(at.ramps)),
     ] + [(v, scalar_spec()) for v in (at.prev, at.in_reach)]
-    outs = [((n * ROWS, cols), BF, (ROWS, cols))] * 3
-    outs += [((n, own, HD, HD), F32, (1, own, HD, HD))]
+    outs = [((n * ROWS, cols), BF, (TALL, cols))] * 3
+    outs += [((n, own, HD, HD), F32, (SUB, own, HD, HD))]
     outs += [((own, HD, HD), F32, pl.BlockSpec((own, HD, HD), lambda i: (0, 0, 0)))]
-    return call(kernel, n, ins, outs, 2 * n * ROWS * cols * width)
+    return call(kernel, 2 * STEPS, ins, outs, 2 * n * ROWS * cols * width)
 
 
 def project_back(h, qkv, raw, ga, gg, state, term, entering, w_in, width, at):
@@ -352,16 +356,17 @@
         w_refs = refs[7 : 7 + parts]
         sc_ref, sr_ref, fade_ref, ramp_ref = refs[7 + parts : 11 + parts]
         prev_ref, last_ref, inner_ref, reach_ref, gp_ref, back_ref = refs[11 + parts :]
-        i = pl.program_id(0) + h * HALF
-        for j in range(own):
+        for s, j in ((s, j) for s in range(SUB) for j in range(own)):
+            i = (pl.program_id(0) + h * STEPS) * SUB + s
+            block = slice(s * ROWS, (s + 1) * ROWS)
             head = slice(j * HD, (j + 1) * HD)
             kt = slice(cols + j * HD, cols + (j + 1) * HD)
             vt = slice(2 * cols + j * HD, 2 * cols + (j + 1) * HD)
-            q, k, v = qkv_ref[:, head], qkv_ref[:, kt], qkv_ref[:, vt]
-            g = ga_ref[:, head]
-            mask = mask_of(fade_ref[j], sc_ref[0], sr_ref[0])
-            enter = jnp.where(sc_ref[0] == prev_ref[i], ramp_ref[:, j : j + 1], 0.0)
-            leave = jnp.where(sc_ref[0] == last_ref[i], ramp_ref[:, own + j : own + j + 1], 0.0)
+            q, k, v = qkv_ref[block, head], qkv_ref[block, kt], qkv_ref[block, vt]
+            g = ga_ref[block, head]
+            mask = mask_of(fade_ref[j], sc_ref[s], sr_ref[s])
+            enter = jnp.where(sc_ref[s] == prev_ref[i], ramp_ref[:, j : j + 1], 0.0)
+            leave = jnp.where(sc_ref[s] == last_ref[i], ramp_ref[:, own + j : own + j + 1], 0.0)
             later = combine(
                 lambda c: inner_ref[j, c * 2 * HALF + i],
                 lambda c: term_ref[c, j],
@@ -370,14 +375,14 @@
             ).astype(BF)
             weights = (dot(q, k, NT) * mask).astype(BF)
             gs = (dot(g, v, NT) * mask).astype(BF)
-            gq = dot(gs, k) + enter * dot(g, state_ref[0, j], NT)
+            gq = dot(gs, k) + enter * dot(g, state_ref[s, j], NT)
             gk = dot(gs, q, TN) + leave * dot(v, later, NT)
             gv = dot(weights, g, TN) + leave * dot(k, later)
-            rq, rk = raw_ref[:, head], raw_ref[:, kt]
+            rq, rk = raw_ref[block, head], raw_ref[block, kt]
             sq, sk = jax.nn.sigmoid(rq), jax.nn.sigmoid(rk)
-            gp_ref[:, head] = (gq * (sq * (1.0 + rq * (1.0 - sq)))).astype(BF)
-            gp_ref[:, kt] = (gk * (sk * (1.0 + rk * (1.0 - sk)))).astype(BF)
-            gp_ref[:, vt] = gv.astype(BF)
+            gp_ref[block, head] = (gq * (sq * (1.0 + rq * (1.0 - sq)))).astype(BF)
+            gp_ref[block, kt] = (gk * (sk * (1.0 + rk * (1.0 - sk)))).astype(BF)
+            gp_ref[block, vt] = gv.astype(BF)
         gp_ref[:, 3 * cols :] = gg_ref[...]
         for k in range(parts):
             some = slice(k * deep, (k + 1) * deep)
@@ -386,26 +391,26 @@
     n = HALF
     some = pl.BlockSpec((deep, 4 * cols), lambda i: (0, 0), pipeline_mode=pl.Buffered(1))
     ins = [
-        (qkv, half_spec((ROWS, 3 * cols), h)),
-        (raw, half_spec((ROWS, 2 * cols), h)),
-        (ga, half_spec((ROWS, cols), h)),
-        (gg, half_spec((ROWS, cols), h)),
-        (state, block_spec((1, own, HD, HD))),
+        (qkv, half_spec((TALL, 3 * cols), h)),
+        (raw, half_spec((TALL, 2 * cols), h)),
+        (ga, half_spec((TALL, cols), h)),
+        (gg, half_spec((TALL, cols), h)),
+        (state, block_spec((SUB, own, HD, HD))),
         (term, whole_spec(term)),
         (entering, whole_spec(entering)),
     ] + [(w, some) for w in w_in]
     ins += [
-        (at.cols, half_spec((1, ROWS, 1), h)),
-        (at.rows, half_spec((1, 1, ROWS), h)),
+        (at.cols, half_spec((SUB, ROWS, 1), h)),
+        (at.rows, half_spec((SUB, 1, ROWS), h)),
         (at.fade, whole_spec(at.fade)),
         (at.ramps, whole_spec(at.ramps)),
     ]
     ins += [(v, scalar_spec()) for v in (at.prev, at.last, at.inner, at.out_reach)]
     outs = [
-        ((n * ROWS, 4 * cols), BF, (ROWS, 4 * cols)),
-        ((n * ROWS, width), BF, (ROWS, width)),
+        ((n * ROWS, 4 * cols), BF, (TALL, 4 * cols)),
+        ((n * ROWS, width), BF, (TALL, width)),
     ]
-    return call(kernel, n, ins, outs, 2 * n * ROWS * 4 * cols * width)
+    return call(kernel, STEPS, ins, outs, 2 * n * ROWS * 4 * cols * width)
 
 
 def one_by_one(count, shape):
@@ -964,19 +969,19 @@
     bdc = to_core(jnp.concatenate(bd))
     gb_a = pin(jnp.concatenate([gb, bx, by, *bd]))
     gb_b = pin(jnp.concatenate([bc, bxyc, bdc]))
-    end(third1, gb_a, gb_b, o_got)
+    a_pair = now(*pair2)
+    ready = [
+        (pin(plus(d_pair[1][m], a_pair[1][m])), pin(plus(d_pair[2][m], a_pair[0][m])))
+        for m in (0, 1)
+    ]
+    end(third1, gb_a, gb_b, o_got, *ready[0], *ready[1])
 
     third2 = gather2(now(d_third[2]), join(d_third[3], third1))
     ou, ov = first_step(*now(o_keep, o_got))
     ga, gg, mixed, d_term, d_leaving = attend_back_rows(
         (now(gb_a), gb_b), w_out, (attn_a, attn_b), gate, qkv, at
     )
-    a_pair = now(*pair2)
-    ready = [
-        (pin(plus(d_pair[1][m], a_pair[1][m])), pin(plus(d_pair[2][m], a_pair[0][m])))
-        for m in (0, 1)
-    ]
-    end(*third2, d_leaving, ou, ov, *ready[0], *ready[1])
+    end(*third2, d_leaving, ou, ov)
 
     first3 = gather3(*now(*ready[0]))
     d_out = grads_out(now(mixed), (gb_a, gb_b), width)
@@ -1024,9 +1029,10 @@
     three_got = to_y(now(to_three))
     grad_norm1 = total(keep[:rows], got[:rows], *now(sx, sy))
     input_grad = grad_mid + srms_back(xf, plan.turn(grad_norm1, dest))
-    end(*w2, three_got)
-
-    ready = join(d_w[1], w2[1]), join(d_w[2], w2[0])
+    summed = pin(plus(d_w[2], w2[0]))
+    end(*w2, three_got, summed)
+
+    ready = join(d_w[1], w2[1]), now(summed)
     w3 = gather3(*ready)
     to_2, to_4 = add_halves(after(o_keep, *ready), o_got, *now(ou, ov), width)
     ox, oy = to_x(to_2), to_y(to_4)

time: 732 us -> 722 us (0.986)
    unnamed x199 -> x197, local copies, waits for them, and re-layouts: 36.5 us -> 33.7 us
  transfers between devices with their start and end apart: 84 -> 84, of which waited for: 40 -> 42; matrix products, arithmetic and copies ran while one was open for 13% -> 14% of each run, Pallas kernels for 27% -> 27%
where the time goes in v5:
time: 722 us; the launch traced here: 712 us
  Pallas kernels  232 us (32%)
  waiting for transfers between devices  217 us (30%)
  starting transfers between devices  116 us (16%)
  other arithmetic  75 us (10%)
  local copies, waits for them, and re-layouts  54.6 us (8%)
  between operations  17 us (2%)
    pallas_call x26, Pallas kernels, call(): pl.pallas_call(kernel, grid=(steps,), in_specs=[s for _, s in ins], out_s...  232 us
    ppermute x80, waiting for transfers between devices, over(): return lambda v: pin(lax.ppermute(pin(v), axis, pairs))  208 us
    ppermute x80, starting transfers between devices, over(): return lambda v: pin(lax.ppermute(pin(v), axis, pairs))  101 us
    unnamed x197, local copies, waits for them, and re-layouts  33.7 us
  transfers between devices with their start and end apart: 84, of which 42 were waited for; matrix products, arithmetic and copies ran while one was open for 14% of the time, Pallas kernels for 27%

profile of v5, /device:TPU:0, one launch (start us, length us, event | category | flops | bytes accessed | tf_op | source)
XLA Modules:
  0.0 712.1 jit_solution(3258690955660186838)
XLA Ops:
  79.5 18.0 %collective-permute-done.5 = bf16[640,1024]{1,0:T(8,128)(2,1)S(1)} collective-permute-done((bf16[640,1024]{1,0:T(8,128)(2,1)}, bf16[640,1024]{1,0:T(8,128)(2,1)S(1)}, u32[]{:S(2)}, u32[]{:S(2)}) %collective-permute-start.5) | collective-permute-done | bytes 1310752 | tf_op jit(solution)/shard_map/ppermute | solution.py:770
  112.7 13.1 %collective-permute-done.11 = bf16[3,704,256]{2,1,0:T(8,128)(2,1)} collective-permute-done((bf16[3,704,256]{2,1,0:T(8,128)(2,1)}, bf16[3,704,256]{2,1,0:T(8,128)(2,1)}, u32[]{:S(2)}, u32[]{:S(2)}) %collective-permute-start.11) | collective-permute-done | bytes 1081376 | tf_op jit(solution)/shard_map/ppermute | solution.py:770
  138.9 17.4 %shard_map.290 = (f32[2048,512]{1,0:T(8,128)}, f32[2048,256]{1,0:T(8,128)}, bf16[2048,768]{1,0:T(8,128)(2,1)}, f32[8,2,128,128]{3,2,1,0:T(8,128)}, f32[2,128,128]{2,1,0:T(8,128)}) custom-call(bf16[1024,2048]{1,0:T(8,128)(2,1)} %constant_dynamic-update-slice_fusion.refs_0_, bf16[1024,2048]{1,0:T(8,128)(2,1)} %collective-permute-done.10.refs_1_, ...), custom_call_target="tpu_custom_call" | custom-call | flops 8589934592 | bytes 24387680 | tf_op jit(solution)/shard_map/pallas_call | solution.py:91
  214.3 6.6 collective-permute-done.22.u_ref
  233.7 25.0 %collective-permute-done.26.c = bf16[256,2176]{1,0:T(8,128)(2,1)S(1)} collective-permute-done((bf16[256,2176]{1,0:T(8,128)(2,1)}, bf16[256,2176]{1,0:T(8,128)(2,1)S(1)}, u32[]{:S(2)}, u32[]{:S(2)}) %collective-permute-start.26) | collective-permute-done | bytes 1114144 | tf_op jit(solution)/shard_map/ppermute | solution.py:770
  272.6 21.6 %collective-permute-done.31 = bf16[256,2048]{1,0:T(8,128)(2,1)S(1)} collective-permute-done((bf16[256,2048]{1,0:T(8,128)(2,1)}, bf16[256,2048]{1,0:T(8,128)(2,1)S(1)}, u32[]{:S(2)}, u32[]{:S(2)}) %collective-permute-start.31) | collective-permute-done | bytes 1048608 | tf_op jit(solution)/shard_map/ppermute | solution.py:770
  302.8 10.2 %collective-permute-done.36 = bf16[128,2048]{1,0:T(8,128)(2,1)S(1)} collective-permute-done((bf16[128,2048]{1,0:T(8,128)(2,1)S(1)}, bf16[128,2048]{1,0:T(8,128)(2,1)S(1)}, u32[]{:S(2)}, u32[]{:S(2)}) %collective-permute-start.36) | collective-permute-done | bytes 524320 | tf_op jit(solution)/shard_map/ppermute | solution.py:770
  321.9 23.7 %shard_map.296 = (bf16[1024,704]{1,0:T(8,128)(2,1)}, bf16[704,1024]{1,0:T(8,128)(2,1)}, bf16[704,1024]{1,0:T(8,128)(2,1)}, bf16[704,1024]{1,0:T(8,128)(2,1)}, bf16[1024,2048]{1,0:T(8,128)(2,1)}) custom-call(bf16[1024,2048]{1,0:T(8,128)(2,1)} %copy-done.76, bf16[1024,2048]{1,0:T(8,128)(2,1)} %collective-permute-done.30.refs_1_.refs_3_, ...), custom_call_target="tpu_custom_call" | custom-call | flops 14763950080 | bytes 27000832 | tf_op jit(solution)/shard_map/pallas_call | solution.py:91
  345.6 24.3 %shard_map.297 = (bf16[1024,704]{1,0:T(8,128)(2,1)}, bf16[704,1024]{1,0:T(8,128)(2,1)}, bf16[704,1024]{1,0:T(8,128)(2,1)}, bf16[704,1024]{1,0:T(8,128)(2,1)}, bf16[1024,2048]{1,0:T(8,128)(2,1)}) custom-call(bf16[1024,2048]{1,0:T(8,128)(2,1)} %copy-done.77, bf16[1024,2048]{1,0:T(8,128)(2,1)} %constant_dynamic-update-slice_fusion.5.refs_1_.refs_2_, ...), custom_call_target="tpu_custom_call" | custom-call | flops 14763950080 | bytes 27000832 | tf_op jit(solution)/shard_map/pallas_call | solution.py:91
  377.3 11.8 %shard_map.299 = (bf16[2,704,512]{2,1,0:T(8,128)(2,1)}, bf16[2,704,512]{2,1,0:T(8,128)(2,1)}) custom-call(bf16[704,1024]{1,0:T(8,128)(2,1)} %get-tuple-element.347.refs_0_, bf16[704,1024]{1,0:T(8,128)(2,1)} %get-tuple-element.329.refs_1_, bf16[704,1024]{1,0:T(8,128)(2,1)} %get-tuple-element.330.refs_2_, bf16[704,1024]{1,0:T(8,128)(2,1)} %get-tuple-element.331.refs_3_, ...), custom_call_target="tpu_custom_call" | custom-call | flops 11811160064 | bytes 17039360 | tf_op jit(solution)/shard_map/pallas_call | solution.py:91
  397.8 11.2 %shard_map.301 = (bf16[1,704,512]{2,1,0:T(8,128)(2,1)}, bf16[1,704,512]{2,1,0:T(8,128)(2,1)}, bf16[1,704,512]{2,1,0:T(8,128)(2,1)}, bf16[1,704,512]{2,1,0:T(8,128)(2,1)}) custom-call(bf16[704,1024]{1,0:T(8,128)(2,1)} %get-tuple-element.341.refs_0_, bf16[704,1024]{1,0:T(8,128)(2,1)} %get-tuple-element.342.refs_1_, ...), custom_call_target="tpu_custom_call" | custom-call | flops 5905580032 | bytes 14155776 | tf_op jit(solution)/shard_map/pallas_call | solution.py:91
  408.9 11.9 %shard_map.302 = (bf16[2,704,512]{2,1,0:T(8,128)(2,1)}, bf16[2,704,512]{2,1,0:T(8,128)(2,1)}) custom-call(bf16[704,1024]{1,0:T(8,128)(2,1)} %get-tuple-element.347.refs_0_, bf16[704,1024]{1,0:T(8,128)(2,1)} %get-tuple-element.329.refs_1_, bf16[704,1024]{1,0:T(8,128)(2,1)} %get-tuple-element.330.refs_2_, bf16[704,1024]{1,0:T(8,128)(2,1)} %get-tuple-element.331.refs_3_, ...), custom_call_target="tpu_custom_call" | custom-call | flops 11811160064 | bytes 17039360 | tf_op jit(solution)/shard_map/pallas_call | solution.py:91
  423.7 7.2 %collective-permute-start.49 = (bf16[2,704,512]{2,1,0:T(8,128)(2,1)S(1)}, bf16[2,704,512]{2,1,0:T(8,128)(2,1)}, u32[]{:S(2)}, u32[]{:S(2)}) collective-permute-start(bf16[2,704,512]{2,1,0:T(8,128)(2,1)S(1)} %copy-done.29), channel_id=1, source_target_pairs={{0,8},{24,16},{1,9},{25,17},{2,10},{26,18},{3,11},{27,19},{4,12},{... | collective-permute-start | bytes 4325384 | tf_op jit(solution)/shard_map/ppermute | solution.py:770
  438.4 6.9 shard_map.304
  445.3 6.9 shard_map.303.a_ref.a2.a4
  452.2 8.9 %collective-permute-done.46 = bf16[256,2176]{1,0:T(8,128)(2,1)S(1)} collective-permute-done((bf16[256,2176]{1,0:T(8,128)(2,1)}, bf16[256,2176]{1,0:T(8,128)(2,1)S(1)}, u32[]{:S(2)}, u32[]{:S(2)}) %collective-permute-start.46) | collective-permute-done | bytes 1114144 | tf_op jit(solution)/shard_map/ppermute | solution.py:770
  498.0 11.8 %shard_map.306 = (bf16[2048,256]{1,0:T(8,128)(2,1)}, bf16[2048,256]{1,0:T(8,128)(2,1)}, bf16[2048,256]{1,0:T(8,128)(2,1)}, f32[8,2,128,128]{3,2,1,0:T(8,128)}, f32[2,128,128]{2,1,0:T(8,128)}) custom-call(bf16[1024,2176]{1,0:T(8,128)(2,1)} %copy-done.9, bf16[1024,2176]{1,0:T(8,128)(2,1)} %copy-done.8, bf16[256,2048]{1,0:T(8,128)(2,1)} %maximum_maximum_fusion.w_ref, ...), custom_call_target="tpu_custom_call" | custom-call | flops 2147483648 | bytes 21766240 | tf_op jit(solution)/shard_map/pallas_call | solution.py:91
  524.1 13.0 %shard_map.309 = (bf16[1024,1024]{1,0:T(8,128)(2,1)}, bf16[1024,2048]{1,0:T(8,128)(2,1)}) custom-call(bf16[2048,768]{1,0:T(8,128)(2,1)} %get-tuple-element.398.qkv_ref.refs_0_, f32[2048,512]{1,0:T(8,128)} %get-tuple-element.390.refs_1_, bf16[2048,256]{1,0:T(8,128)(2,1)} %get-tuple-element.391.refs_2_, bf16[2048,256]{1,0:T(8,128)(2,1)} %get-tuple-element.392.refs_3_, ...), custom_call_target="tpu_custom_call" | custom-call | flops 4294967296 | bytes 23085696 | tf_op jit(solution)/shard_map/pallas_call | solution.py:91
  543.8 13.0 %shard_map.310 = (bf16[1024,1024]{1,0:T(8,128)(2,1)}, bf16[1024,2048]{1,0:T(8,128)(2,1)}) custom-call(bf16[2048,768]{1,0:T(8,128)(2,1)} %get-tuple-element.398.qkv_ref.refs_0_, f32[2048,512]{1,0:T(8,128)} %get-tuple-element.390.refs_1_, bf16[2048,256]{1,0:T(8,128)(2,1)} %get-tuple-element.391.refs_2_, bf16[2048,256]{1,0:T(8,128)(2,1)} %get-tuple-element.392.refs_3_, ...), custom_call_target="tpu_custom_call" | custom-call | flops 4294967296 | bytes 23085696 | tf_op jit(solution)/shard_map/pallas_call | solution.py:91
  568.5 15.8 %shard_map.311 = (bf16[640,1024]{1,0:T(8,128)(2,1)}, bf16[640,1024]{1,0:T(8,128)(2,1)}, bf16[640,1024]{1,0:T(8,128)(2,1)}, bf16[640,1024]{1,0:T(8,128)(2,1)}) custom-call(bf16[1024,2048]{1,0:T(8,128)(2,1)} %constant_dynamic-update-slice_fusion.refs_0_, bf16[1024,2048]{1,0:T(8,128)(2,1)} %collective-permute-done.10.refs_1_, ...), custom_call_target="tpu_custom_call" | custom-call | flops 8589934592 | bytes 18874400 | tf_op jit(solution)/shard_map/pallas_call | solution.py:91
  601.7 18.2 %collective-permute-done.73 = bf16[256,2048]{1,0:T(8,128)(2,1)S(1)} collective-permute-done((bf16[256,2048]{1,0:T(8,128)(2,1)}, bf16[256,2048]{1,0:T(8,128)(2,1)S(1)}, u32[]{:S(2)}, u32[]{:S(2)}) %collective-permute-start.73) | collective-permute-done | bytes 1048608 | tf_op jit(solution)/shard_map/ppermute | solution.py:770
  626.5 16.0 %collective-permute-done.76 = bf16[640,1024]{1,0:T(8,128)(2,1)S(1)} collective-permute-done((bf16[640,1024]{1,0:T(8,128)(2,1)}, bf16[640,1024]{1,0:T(8,128)(2,1)S(1)}, u32[]{:S(2)}, u32[]{:S(2)}) %collective-permute-start.76) | collective-permute-done | bytes 1310752 | tf_op jit(solution)/shard_map/ppermute | solution.py:770
  669.4 7.5 %multiply_add_fusion = (f32[2,256,1408]{2,1,0:T(8,128)}, f32[2,256,1408]{2,1,0:T(8,128)}, f32[2,256,1408]{2,1,0:T(8,128)}) fusion(f32[2,256,1408]{2,1,0:T(8,128)} %param.33, f32[2,256,1408]{2,1,0:T(8,128)S(1)} %copy-done.13, bf16[2,1408,256]{1,2,0:T(8,128)(2,1)} %copy.74, f32[2,256,1408]{2,1,0:T(8,128)} %param.29), kind=kLoop, calls=%fused_computation.9 | loop fusion | flops 7208960 | bytes 18743296 | tf_op jit(solution)/shard_map/add | solution.py:42
  696.3 8.2 %all-to-all-done.1.g_ref = bf16[8,64,1024]{2,1,0:T(8,128)(2,1)S(1)} async-done(((bf16[8,64,1024]{2,1,0:T(8,128)(2,1)}), bf16[8,64,1024]{2,1,0:T(8,128)(2,1)S(1)}, u32[]{:S(2)}, u32[]{:S(2)}) %all-to-all-start.1) | async-done | bytes 1048608 | tf_op jit(solution)/shard_map/all_to_all | solution.py:1046
  (500 shorter events, 366.9 us)
Async XLA Ops:
  28.4 31.2 %collective-permute-start.2 = (bf16[640,1024]{1,0:T(8,128)(2,1)S(1)}, bf16[640,1024]{1,0:T(8,128)(2,1)S(1)}, u32[]{:S(2)}, u32[]{:S(2)}) collective-permute-start(bf16[640,1024]{1,0:T(8,128)(2,1)S(1)} %pad_maximum_fusion.4.refs_2_.refs_7_), channel_id=1, source_target_pairs={{0,8},{8,0},{16,24},{24,16},{1,9},{9,1},{17,25},{25,17},{2,10},{10... | collective-permute-start | bytes 3932168 | tf_op jit(solution)/shard_map/ppermute | solution.py:770
  30.1 29.6 %collective-permute-start.3 = (bf16[640,1024]{1,0:T(8,128)(2,1)S(1)}, bf16[640,1024]{1,0:T(8,128)(2,1)}, u32[]{:S(2)}, u32[]{:S(2)}) collective-permute-start(bf16[640,1024]{1,0:T(8,128)(2,1)S(1)} %pad_maximum_fusion.4.refs_2_.refs_7_), channel_id=1, source_target_pairs={{8,16},{16,8},{9,17},{17,9},{10,18},{18,10},{11,19},{19,11},{12,20... | collective-permute-start | bytes 3932168 | tf_op jit(solution)/shard_map/ppermute | solution.py:770
  61.4 36.1 %collective-permute-start.5 = (bf16[640,1024]{1,0:T(8,128)(2,1)}, bf16[640,1024]{1,0:T(8,128)(2,1)S(1)}, u32[]{:S(2)}, u32[]{:S(2)}) collective-permute-start(bf16[640,1024]{1,0:T(8,128)(2,1)} %collective-permute-done.3), channel_id=1, source_target_pairs={{8,0},{16,24},{9,1},{17,25},{10,2},{18,26},{11,3},{19,27},{12,4},{... | collective-permute-start | bytes 3932168 | tf_op jit(solution)/shard_map/ppermute | solution.py:770
  99.2 34.4 %collective-permute-start.10 = (bf16[1024,2048]{1,0:T(8,128)(2,1)}, bf16[1024,2048]{1,0:T(8,128)(2,1)}, u32[]{:S(2)}, u32[]{:S(2)}) collective-permute-start(bf16[1024,2048]{1,0:T(8,128)(2,1)} %constant_dynamic-update-slice_fusion.refs_0_), channel_id=1, source_target_pairs={{0,1},{1,0},{2,3},{3,2},{4,5},{5,4},{6,7},{7,6},{8,9},{9,8},{10,11... | collective-permute-start | bytes 12582920 | tf_op jit(solution)/shard_map/ppermute | solution.py:770
  99.2 26.6 %collective-permute-start.11 = (bf16[3,704,256]{2,1,0:T(8,128)(2,1)}, bf16[3,704,256]{2,1,0:T(8,128)(2,1)}, u32[]{:S(2)}, u32[]{:S(2)}) collective-permute-start(bf16[3,704,256]{2,1,0:T(8,128)(2,1)} %get-tuple-element.254), channel_id=1, source_target_pairs={{0,4},{4,0},{1,5},{5,1},{2,6},{6,2},{3,7},{7,3},{8,12},{12,8},{9,1... | collective-permute-start | bytes 3244040 | tf_op jit(solution)/shard_map/ppermute | solution.py:770
  100.5 33.1 %collective-permute-start.8 = (bf16[640,1024]{1,0:T(8,128)(2,1)}, bf16[640,1024]{1,0:T(8,128)(2,1)}, u32[]{:S(2)}, u32[]{:S(2)}) collective-permute-start(bf16[640,1024]{1,0:T(8,128)(2,1)} %collective-permute-done.6), channel_id=1, source_target_pairs={{8,0},{16,24},{9,1},{17,25},{10,2},{18,26},{11,3},{19,27},{12,4},{... | collective-permute-start | bytes 3932168 | tf_op jit(solution)/shard_map/ppermute | solution.py:770
  133.6 33.0 %collective-permute-start.12 = (bf16[2,704,512]{2,1,0:T(8,128)(2,1)S(1)}, bf16[2,704,512]{2,1,0:T(8,128)(2,1)}, u32[]{:S(2)}, u32[]{:S(2)}) collective-permute-start(bf16[2,704,512]{2,1,0:T(8,128)(2,1)S(1)} %fusion.11.refs_2_), channel_id=1, source_target_pairs={{0,8},{8,0},{16,24},{24,16},{1,9},{9,1},{17,25},{25,17},{2,10},{10... | collective-permute-start | bytes 4325384 | tf_op jit(solution)/shard_map/ppermute | solution.py:770
  133.6 33.0 %collective-permute-start.13 = (bf16[2,704,512]{2,1,0:T(8,128)(2,1)S(1)}, bf16[2,704,512]{2,1,0:T(8,128)(2,1)S(1)}, u32[]{:S(2)}, u32[]{:S(2)}) collective-permute-start(bf16[2,704,512]{2,1,0:T(8,128)(2,1)S(1)} %fusion.11.refs_2_), channel_id=1, source_target_pairs={{8,16},{16,8},{9,17},{17,9},{10,18},{18,10},{11,19},{19,11},{12,20... | collective-permute-start | bytes 4325384 | tf_op jit(solution)/shard_map/ppermute | solution.py:770
  138.1 25.8 %collective-permute-start.14 = (bf16[256,2048]{1,0:T(8,128)(2,1)}, bf16[256,2048]{1,0:T(8,128)(2,1)S(1)}, u32[]{:S(2)}, u32[]{:S(2)}) collective-permute-start(bf16[256,2048]{1,0:T(8,128)(2,1)} %get-tuple-element.264), channel_id=1, source_target_pairs={{0,4},{4,0},{1,5},{5,1},{2,6},{6,2},{3,7},{7,3},{8,12},{12,8},{9,1... | collective-permute-start | bytes 3145736 | tf_op jit(solution)/shard_map/ppermute | solution.py:770
  224.1 39.5 %collective-permute-start.30 = (bf16[1024,2048]{1,0:T(8,128)(2,1)}, bf16[1024,2048]{1,0:T(8,128)(2,1)}, u32[]{:S(2)}, u32[]{:S(2)}) collective-permute-start(bf16[1024,2048]{1,0:T(8,128)(2,1)} %constant_dynamic-update-slice_fusion.5.refs_1_.refs_2_), channel_id=1, source_target_pairs={{0,1},{1,0},{2,3},{3,2},{4,5},{5,4},{6,7},{7,6},{8,9},{9,8},{10,11... | collective-permute-start | bytes 12582920 | tf_op jit(solution)/shard_map/ppermute | solution.py:770
  224.1 35.8 %collective-permute-start.29 = (bf16[2,704,512]{2,1,0:T(8,128)(2,1)}, bf16[2,704,512]{2,1,0:T(8,128)(2,1)S(1)}, u32[]{:S(2)}, u32[]{:S(2)}) collective-permute-start(bf16[2,704,512]{2,1,0:T(8,128)(2,1)} %collective-permute-done.12.refs_3_), channel_id=1, source_target_pairs={{8,16},{16,8},{9,17},{17,9},{10,18},{18,10},{11,19},{19,11},{12,20... | collective-permute-start | bytes 4325384 | tf_op jit(solution)/shard_map/ppermute | solution.py:770
  224.9 38.7 %collective-permute-start.28 = (bf16[2,704,512]{2,1,0:T(8,128)(2,1)S(1)}, bf16[2,704,512]{2,1,0:T(8,128)(2,1)S(1)}, u32[]{:S(2)}, u32[]{:S(2)}) collective-permute-start(bf16[2,704,512]{2,1,0:T(8,128)(2,1)S(1)} %copy-done.28), channel_id=1, source_target_pairs={{8,0},{16,24},{9,1},{17,25},{10,2},{18,26},{11,3},{19,27},{12,4},{... | collective-permute-start | bytes 4325384 | tf_op jit(solution)/shard_map/ppermute | solution.py:770
  231.6 27.2 %collective-permute-start.26 = (bf16[256,2176]{1,0:T(8,128)(2,1)}, bf16[256,2176]{1,0:T(8,128)(2,1)S(1)}, u32[]{:S(2)}, u32[]{:S(2)}) collective-permute-start(bf16[256,2176]{1,0:T(8,128)(2,1)} %get-tuple-element.290), channel_id=1, source_target_pairs={{0,2},{2,0},{1,3},{3,1},{4,6},{6,4},{5,7},{7,5},{8,10},{10,8},{9,1... | collective-permute-start | bytes 3342344 | tf_op jit(solution)/shard_map/ppermute | solution.py:770
  233.1 26.9 %collective-permute-start.27 = (bf16[256,2176]{1,0:T(8,128)(2,1)}, bf16[256,2176]{1,0:T(8,128)(2,1)S(1)}, u32[]{:S(2)}, u32[]{:S(2)}) collective-permute-start(bf16[256,2176]{1,0:T(8,128)(2,1)} %get-tuple-element.291), channel_id=1, source_target_pairs={{0,4},{4,0},{1,5},{5,1},{2,6},{6,2},{3,7},{7,3},{8,12},{12,8},{9,1... | collective-permute-start | bytes 3342344 | tf_op jit(solution)/shard_map/ppermute | solution.py:770
  263.6 34.3 %collective-permute-start.34 = (bf16[2,704,512]{2,1,0:T(8,128)(2,1)S(1)}, bf16[2,704,512]{2,1,0:T(8,128)(2,1)S(1)}, u32[]{:S(2)}, u32[]{:S(2)}) collective-permute-start(bf16[2,704,512]{2,1,0:T(8,128)(2,1)S(1)} %collective-permute-done.29), channel_id=1, source_target_pairs={{8,0},{16,24},{9,1},{17,25},{10,2},{18,26},{11,3},{19,27},{12,4},{... | collective-permute-start | bytes 4325384 | tf_op jit(solution)/shard_map/ppermute | solution.py:770
  390.1 32.3 %collective-permute-start.45 = (bf16[2,704,512]{2,1,0:T(8,128)(2,1)}, bf16[2,704,512]{2,1,0:T(8,128)(2,1)S(1)}, u32[]{:S(2)}, u32[]{:S(2)}) collective-permute-start(bf16[2,704,512]{2,1,0:T(8,128)(2,1)} %get-tuple-element.361), channel_id=1, source_target_pairs={{0,8},{24,16},{1,9},{25,17},{2,10},{26,18},{3,11},{27,19},{4,12},{... | collective-permute-start | bytes 4325384 | tf_op jit(solution)/shard_map/ppermute | solution.py:770
  422.8 38.7 %collective-permute-start.50 = (bf16[2,704,512]{2,1,0:T(8,128)(2,1)S(1)}, bf16[2,704,512]{2,1,0:T(8,128)(2,1)S(1)}, u32[]{:S(2)}, u32[]{:S(2)}) collective-permute-start(bf16[2,704,512]{2,1,0:T(8,128)(2,1)S(1)} %add_convert_fusion), channel_id=1, source_target_pairs={{8,16},{16,8},{9,17},{17,9},{10,18},{18,10},{11,19},{19,11},{12,20... | collective-permute-start | bytes 4325384 | tf_op jit(solution)/shard_map/ppermute | solution.py:770
  423.7 39.9 %collective-permute-start.49 = (bf16[2,704,512]{2,1,0:T(8,128)(2,1)S(1)}, bf16[2,704,512]{2,1,0:T(8,128)(2,1)}, u32[]{:S(2)}, u32[]{:S(2)}) collective-permute-start(bf16[2,704,512]{2,1,0:T(8,128)(2,1)S(1)} %copy-done.29), channel_id=1, source_target_pairs={{0,8},{24,16},{1,9},{25,17},{2,10},{26,18},{3,11},{27,19},{4,12},{... | collective-permute-start | bytes 4325384 | tf_op jit(solution)/shard_map/ppermute | solution.py:770
  511.2 25.9 %collective-permute-start.62 = (bf16[704,512]{1,0:T(8,128)(2,1)S(1)}, bf16[704,512]{1,0:T(8,128)(2,1)S(1)}, u32[]{:S(2)}, u32[]{:S(2)}) collective-permute-start(bf16[704,512]{1,0:T(8,128)(2,1)S(1)} %copy-done.64), channel_id=1, source_target_pairs={{8,16},{16,8},{9,17},{17,9},{10,18},{18,10},{11,19},{19,11},{12,20... | collective-permute-start | bytes 2162696 | tf_op jit(solution)/shard_map/ppermute | solution.py:770
  585.1 35.1 %collective-permute-start.72 = (bf16[640,1024]{1,0:T(8,128)(2,1)}, bf16[640,1024]{1,0:T(8,128)(2,1)S(1)}, u32[]{:S(2)}, u32[]{:S(2)}) collective-permute-start(bf16[640,1024]{1,0:T(8,128)(2,1)} %get-tuple-element.426), channel_id=1, source_target_pairs={{0,8},{24,16},{1,9},{25,17},{2,10},{26,18},{3,11},{27,19},{4,12},{... | collective-permute-start | bytes 3932168 | tf_op jit(solution)/shard_map/ppermute | solution.py:770
  590.4 52.1 %collective-permute-start.76 = (bf16[640,1024]{1,0:T(8,128)(2,1)}, bf16[640,1024]{1,0:T(8,128)(2,1)S(1)}, u32[]{:S(2)}, u32[]{:S(2)}) collective-permute-start(bf16[640,1024]{1,0:T(8,128)(2,1)} %get-tuple-element.441), channel_id=1, source_target_pairs={{0,8},{24,16},{1,9},{25,17},{2,10},{26,18},{3,11},{27,19},{4,12},{... | collective-permute-start | bytes 3932168 | tf_op jit(solution)/shard_map/ppermute | solution.py:770
  620.2 25.8 %collective-permute-start.77 = (bf16[3,704,256]{2,1,0:T(8,128)(2,1)S(1)}, bf16[3,704,256]{2,1,0:T(8,128)(2,1)S(1)}, u32[]{:S(2)}, u32[]{:S(2)}) collective-permute-start(bf16[3,704,256]{2,1,0:T(8,128)(2,1)S(1)} %get-tuple-element.442), channel_id=1, source_target_pairs={{0,4},{4,0},{1,5},{5,1},{2,6},{6,2},{3,7},{7,3},{8,12},{12,8},{9,1... | collective-permute-start | bytes 3244040 | tf_op jit(solution)/shard_map/ppermute | solution.py:770
  646.0 36.1 %collective-permute-start.80 = (bf16[640,1024]{1,0:T(8,128)(2,1)}, bf16[640,1024]{1,0:T(8,128)(2,1)}, u32[]{:S(2)}, u32[]{:S(2)}) collective-permute-start(bf16[640,1024]{1,0:T(8,128)(2,1)} %add_convert_fusion.2), channel_id=1, source_target_pairs={{8,16},{16,8},{9,17},{17,9},{10,18},{18,10},{11,19},{19,11},{12,20... | collective-permute-start | bytes 3932168 | tf_op jit(solution)/shard_map/ppermute | solution.py:770
  649.4 32.7 %collective-permute-start.79 = (bf16[640,1024]{1,0:T(8,128)(2,1)}, bf16[640,1024]{1,0:T(8,128)(2,1)}, u32[]{:S(2)}, u32[]{:S(2)}) collective-permute-start(bf16[640,1024]{1,0:T(8,128)(2,1)} %add_convert_fusion.1), channel_id=1, source_target_pairs={{0,8},{8,0},{16,24},{24,16},{1,9},{9,1},{17,25},{25,17},{2,10},{10... | collective-permute-start | bytes 3932168 | tf_op jit(solution)/shard_map/ppermute | solution.py:770
  (149 other events, 1886.8 us)

commit v6 on v5

--- a/solution.py
+++ b/solution.py
@@ -878,11 +878,11 @@
     attn_b, give, state_b = attend(1, qkv, gate, term, entering, w_out, at)
     end(give)
 
-    third1 = spread0(now(own_third))
+    third1 = spread0(after(own_third, entering))
     a_qkv, give = now(qkv, give)
     attn_a, keep, state_a = attend(0, a_qkv, gate, term, entering, w_out, at)
     got = to_core(give)
-    a_gx, a_gy = now(gx, gy)
+    a_gx, a_gy = after(gx, entering), after(gy, entering)
     gd = to_x(a_gy[:h2]), to_y(a_gx[h2:])
     end(*third1, got, keep, *gd)
 
@@ -1041,10 +1041,12 @@
     sum_third = sum_three[2].astype(F32)
     end(*w3, ox, oy)
 
-    sum_w = pin(total(d_w[0], *now(*w3)))
-    sum_in = pin(sum_w[:deep].astype(BF)).reshape(8, few, across)
+    w3 = now(*w3)
+    sum_in = total(*[v[:deep] for v in (d_w[0], *w3)])
+    sum_in = pin(sum_in.astype(BF)).reshape(8, few, across)
     sum_in = lax.all_to_all(sum_in, plan.tp, 0, 0, tiled=True)
-    sum_out = jnp.concatenate([sum_w[deep : deep + few], sum_w[deep + few :]], axis=1)
+    sum_out = pin(total(*[v[deep:] for v in (d_w[0], *w3)]))
+    sum_out = jnp.concatenate([sum_out[:few], sum_out[few:]], axis=1)
     output = mid + plan.turn(total(o_keep[:rows], o_got[:rows], *now(ox, oy)), dest)
     return output, input_grad, sum_in, sum_out, sum_pair, sum_third
 

time: 722 us -> 723 us (level)
  no operation moved by 1% of the time
where the time goes in v6:
time: 723 us; the launch traced here: 713 us
  Pallas kernels  232 us (32%)
  waiting for transfers between devices  217 us (30%)
  starting transfers between devices  116 us (16%)
  other arithmetic  76.8 us (11%)
  local copies, waits for them, and re-layouts  53.5 us (7%)
  between operations  17 us (2%)
    pallas_call x26, Pallas kernels, call(): pl.pallas_call(kernel, grid=(steps,), in_specs=[s for _, s in ins], out_s...  232 us
    ppermute x80, waiting for transfers between devices, over(): return lambda v: pin(lax.ppermute(pin(v), axis, pairs))  208 us
    ppermute x80, starting transfers between devices, over(): return lambda v: pin(lax.ppermute(pin(v), axis, pairs))  101 us
    unnamed x197, local copies, waits for them, and re-layouts  33.7 us
  transfers between devices with their start and end apart: 84, of which 42 were waited for; matrix products, arithmetic and copies ran while one was open for 14% of the time, Pallas kernels for 27%

profile of v6, /device:TPU:0, one launch (start us, length us, event | category | flops | bytes accessed | tf_op | source)
XLA Modules:
  0.0 712.8 jit_solution(6850751481036780027)
XLA Ops:
  79.5 18.0 %collective-permute-done.5 = bf16[640,1024]{1,0:T(8,128)(2,1)S(1)} collective-permute-done((bf16[640,1024]{1,0:T(8,128)(2,1)}, bf16[640,1024]{1,0:T(8,128)(2,1)S(1)}, u32[]{:S(2)}, u32[]{:S(2)}) %collective-permute-start.5) | collective-permute-done | bytes 1310752 | tf_op jit(solution)/shard_map/ppermute | solution.py:770
  112.7 13.1 %collective-permute-done.11 = bf16[3,704,256]{2,1,0:T(8,128)(2,1)} collective-permute-done((bf16[3,704,256]{2,1,0:T(8,128)(2,1)}, bf16[3,704,256]{2,1,0:T(8,128)(2,1)}, u32[]{:S(2)}, u32[]{:S(2)}) %collective-permute-start.11) | collective-permute-done | bytes 1081376 | tf_op jit(solution)/shard_map/ppermute | solution.py:770
  138.9 17.4 %shard_map.290 = (f32[2048,512]{1,0:T(8,128)}, f32[2048,256]{1,0:T(8,128)}, bf16[2048,768]{1,0:T(8,128)(2,1)}, f32[8,2,128,128]{3,2,1,0:T(8,128)}, f32[2,128,128]{2,1,0:T(8,128)}) custom-call(bf16[1024,2048]{1,0:T(8,128)(2,1)} %constant_dynamic-update-slice_fusion.refs_0_, bf16[1024,2048]{1,0:T(8,128)(2,1)} %collective-permute-done.10.refs_1_, ...), custom_call_target="tpu_custom_call" | custom-call | flops 8589934592 | bytes 24387680 | tf_op jit(solution)/shard_map/pallas_call | solution.py:91
  214.3 6.6 collective-permute-done.22.u_ref
  233.7 25.0 %collective-permute-done.26.c = bf16[256,2176]{1,0:T(8,128)(2,1)S(1)} collective-permute-done((bf16[256,2176]{1,0:T(8,128)(2,1)}, bf16[256,2176]{1,0:T(8,128)(2,1)S(1)}, u32[]{:S(2)}, u32[]{:S(2)}) %collective-permute-start.26) | collective-permute-done | bytes 1114144 | tf_op jit(solution)/shard_map/ppermute | solution.py:770
  272.6 21.6 %collective-permute-done.31 = bf16[256,2048]{1,0:T(8,128)(2,1)S(1)} collective-permute-done((bf16[256,2048]{1,0:T(8,128)(2,1)}, bf16[256,2048]{1,0:T(8,128)(2,1)S(1)}, u32[]{:S(2)}, u32[]{:S(2)}) %collective-permute-start.31) | collective-permute-done | bytes 1048608 | tf_op jit(solution)/shard_map/ppermute | solution.py:770
  302.8 10.2 %collective-permute-done.36 = bf16[128,2048]{1,0:T(8,128)(2,1)S(1)} collective-permute-done((bf16[128,2048]{1,0:T(8,128)(2,1)S(1)}, bf16[128,2048]{1,0:T(8,128)(2,1)S(1)}, u32[]{:S(2)}, u32[]{:S(2)}) %collective-permute-start.36) | collective-permute-done | bytes 524320 | tf_op jit(solution)/shard_map/ppermute | solution.py:770
  321.9 23.7 %shard_map.296 = (bf16[1024,704]{1,0:T(8,128)(2,1)}, bf16[704,1024]{1,0:T(8,128)(2,1)}, bf16[704,1024]{1,0:T(8,128)(2,1)}, bf16[704,1024]{1,0:T(8,128)(2,1)}, bf16[1024,2048]{1,0:T(8,128)(2,1)}) custom-call(bf16[1024,2048]{1,0:T(8,128)(2,1)} %copy-done.76, bf16[1024,2048]{1,0:T(8,128)(2,1)} %collective-permute-done.30.refs_1_.refs_3_, ...), custom_call_target="tpu_custom_call" | custom-call | flops 14763950080 | bytes 27000832 | tf_op jit(solution)/shard_map/pallas_call | solution.py:91
  345.6 24.3 %shard_map.297 = (bf16[1024,704]{1,0:T(8,128)(2,1)}, bf16[704,1024]{1,0:T(8,128)(2,1)}, bf16[704,1024]{1,0:T(8,128)(2,1)}, bf16[704,1024]{1,0:T(8,128)(2,1)}, bf16[1024,2048]{1,0:T(8,128)(2,1)}) custom-call(bf16[1024,2048]{1,0:T(8,128)(2,1)} %copy-done.77, bf16[1024,2048]{1,0:T(8,128)(2,1)} %constant_dynamic-update-slice_fusion.5.refs_1_.refs_2_, ...), custom_call_target="tpu_custom_call" | custom-call | flops 14763950080 | bytes 27000832 | tf_op jit(solution)/shard_map/pallas_call | solution.py:91
  377.3 11.8 %shard_map.299 = (bf16[2,704,512]{2,1,0:T(8,128)(2,1)}, bf16[2,704,512]{2,1,0:T(8,128)(2,1)}) custom-call(bf16[704,1024]{1,0:T(8,128)(2,1)} %get-tuple-element.347.refs_0_, bf16[704,1024]{1,0:T(8,128)(2,1)} %get-tuple-element.329.refs_1_, bf16[704,1024]{1,0:T(8,128)(2,1)} %get-tuple-element.330.refs_2_, bf16[704,1024]{1,0:T(8,128)(2,1)} %get-tuple-element.331.refs_3_, ...), custom_call_target="tpu_custom_call" | custom-call | flops 11811160064 | bytes 17039360 | tf_op jit(solution)/shard_map/pallas_call | solution.py:91
  397.8 11.2 %shard_map.301 = (bf16[1,704,512]{2,1,0:T(8,128)(2,1)}, bf16[1,704,512]{2,1,0:T(8,128)(2,1)}, bf16[1,704,512]{2,1,0:T(8,128)(2,1)}, bf16[1,704,512]{2,1,0:T(8,128)(2,1)}) custom-call(bf16[704,1024]{1,0:T(8,128)(2,1)} %get-tuple-element.341.refs_0_, bf16[704,1024]{1,0:T(8,128)(2,1)} %get-tuple-element.342.refs_1_, ...), custom_call_target="tpu_custom_call" | custom-call | flops 5905580032 | bytes 14155776 | tf_op jit(solution)/shard_map/pallas_call | solution.py:91
  408.9 11.9 %shard_map.302 = (bf16[2,704,512]{2,1,0:T(8,128)(2,1)}, bf16[2,704,512]{2,1,0:T(8,128)(2,1)}) custom-call(bf16[704,1024]{1,0:T(8,128)(2,1)} %get-tuple-element.347.refs_0_, bf16[704,1024]{1,0:T(8,128)(2,1)} %get-tuple-element.329.refs_1_, bf16[704,1024]{1,0:T(8,128)(2,1)} %get-tuple-element.330.refs_2_, bf16[704,1024]{1,0:T(8,128)(2,1)} %get-tuple-element.331.refs_3_, ...), custom_call_target="tpu_custom_call" | custom-call | flops 11811160064 | bytes 17039360 | tf_op jit(solution)/shard_map/pallas_call | solution.py:91
  423.7 7.2 %collective-permute-start.49 = (bf16[2,704,512]{2,1,0:T(8,128)(2,1)S(1)}, bf16[2,704,512]{2,1,0:T(8,128)(2,1)}, u32[]{:S(2)}, u32[]{:S(2)}) collective-permute-start(bf16[2,704,512]{2,1,0:T(8,128)(2,1)S(1)} %copy-done.29), channel_id=1, source_target_pairs={{0,8},{24,16},{1,9},{25,17},{2,10},{26,18},{3,11},{27,19},{4,12},{... | collective-permute-start | bytes 4325384 | tf_op jit(solution)/shard_map/ppermute | solution.py:770
  438.4 6.9 shard_map.304
  445.3 6.9 shard_map.303.a_ref.a2.a4
  452.2 8.9 %collective-permute-done.46 = bf16[256,2176]{1,0:T(8,128)(2,1)S(1)} collective-permute-done((bf16[256,2176]{1,0:T(8,128)(2,1)}, bf16[256,2176]{1,0:T(8,128)(2,1)S(1)}, u32[]{:S(2)}, u32[]{:S(2)}) %collective-permute-start.46) | collective-permute-done | bytes 1114144 | tf_op jit(solution)/shard_map/ppermute | solution.py:770
  498.0 11.8 %shard_map.306 = (bf16[2048,256]{1,0:T(8,128)(2,1)}, bf16[2048,256]{1,0:T(8,128)(2,1)}, bf16[2048,256]{1,0:T(8,128)(2,1)}, f32[8,2,128,128]{3,2,1,0:T(8,128)}, f32[2,128,128]{2,1,0:T(8,128)}) custom-call(bf16[1024,2176]{1,0:T(8,128)(2,1)} %copy-done.9, bf16[1024,2176]{1,0:T(8,128)(2,1)} %copy-done.8, bf16[256,2048]{1,0:T(8,128)(2,1)} %maximum_maximum_fusion.w_ref, ...), custom_call_target="tpu_custom_call" | custom-call | flops 2147483648 | bytes 21766240 | tf_op jit(solution)/shard_map/pallas_call | solution.py:91
  524.1 13.0 %shard_map.309 = (bf16[1024,1024]{1,0:T(8,128)(2,1)}, bf16[1024,2048]{1,0:T(8,128)(2,1)}) custom-call(bf16[2048,768]{1,0:T(8,128)(2,1)} %get-tuple-element.398.qkv_ref.refs_0_, f32[2048,512]{1,0:T(8,128)} %get-tuple-element.390.refs_1_, bf16[2048,256]{1,0:T(8,128)(2,1)} %get-tuple-element.391.refs_2_, bf16[2048,256]{1,0:T(8,128)(2,1)} %get-tuple-element.392.refs_3_, ...), custom_call_target="tpu_custom_call" | custom-call | flops 4294967296 | bytes 23085696 | tf_op jit(solution)/shard_map/pallas_call | solution.py:91
  543.8 13.0 %shard_map.310 = (bf16[1024,1024]{1,0:T(8,128)(2,1)}, bf16[1024,2048]{1,0:T(8,128)(2,1)}) custom-call(bf16[2048,768]{1,0:T(8,128)(2,1)} %get-tuple-element.398.qkv_ref.refs_0_, f32[2048,512]{1,0:T(8,128)} %get-tuple-element.390.refs_1_, bf16[2048,256]{1,0:T(8,128)(2,1)} %get-tuple-element.391.refs_2_, bf16[2048,256]{1,0:T(8,128)(2,1)} %get-tuple-element.392.refs_3_, ...), custom_call_target="tpu_custom_call" | custom-call | flops 4294967296 | bytes 23085696 | tf_op jit(solution)/shard_map/pallas_call | solution.py:91
  568.5 15.8 %shard_map.311 = (bf16[640,1024]{1,0:T(8,128)(2,1)}, bf16[640,1024]{1,0:T(8,128)(2,1)}, bf16[640,1024]{1,0:T(8,128)(2,1)}, bf16[640,1024]{1,0:T(8,128)(2,1)}) custom-call(bf16[1024,2048]{1,0:T(8,128)(2,1)} %constant_dynamic-update-slice_fusion.refs_0_, bf16[1024,2048]{1,0:T(8,128)(2,1)} %collective-permute-done.10.refs_1_, ...), custom_call_target="tpu_custom_call" | custom-call | flops 8589934592 | bytes 18874400 | tf_op jit(solution)/shard_map/pallas_call | solution.py:91
  601.7 18.2 %collective-permute-done.73 = bf16[256,2048]{1,0:T(8,128)(2,1)S(1)} collective-permute-done((bf16[256,2048]{1,0:T(8,128)(2,1)}, bf16[256,2048]{1,0:T(8,128)(2,1)S(1)}, u32[]{:S(2)}, u32[]{:S(2)}) %collective-permute-start.73) | collective-permute-done | bytes 1048608 | tf_op jit(solution)/shard_map/ppermute | solution.py:770
  626.5 16.0 %collective-permute-done.76 = bf16[640,1024]{1,0:T(8,128)(2,1)S(1)} collective-permute-done((bf16[640,1024]{1,0:T(8,128)(2,1)}, bf16[640,1024]{1,0:T(8,128)(2,1)S(1)}, u32[]{:S(2)}, u32[]{:S(2)}) %collective-permute-start.76) | collective-permute-done | bytes 1310752 | tf_op jit(solution)/shard_map/ppermute | solution.py:770
  669.4 7.5 %multiply_add_fusion = (f32[2,256,1408]{2,1,0:T(8,128)}, f32[2,256,1408]{2,1,0:T(8,128)}, f32[2,256,1408]{2,1,0:T(8,128)}) fusion(f32[2,256,1408]{2,1,0:T(8,128)} %param.33, f32[2,256,1408]{2,1,0:T(8,128)S(1)} %copy-done.13, bf16[2,1408,256]{1,2,0:T(8,128)(2,1)} %copy.74, f32[2,256,1408]{2,1,0:T(8,128)} %param.29), kind=kLoop, calls=%fused_computation.9 | loop fusion | flops 7208960 | bytes 18743296 | tf_op jit(solution)/shard_map/add | solution.py:42
  697.0 8.2 %all-to-all-done.1.g_ref = bf16[8,64,1024]{2,1,0:T(8,128)(2,1)S(1)} async-done(((bf16[8,64,1024]{2,1,0:T(8,128)(2,1)}), bf16[8,64,1024]{2,1,0:T(8,128)(2,1)S(1)}, u32[]{:S(2)}, u32[]{:S(2)}) %all-to-all-start.1) | async-done | bytes 1048608 | tf_op jit(solution)/shard_map/all_to_all | solution.py:1047
  (500 shorter events, 367.5 us)
Async XLA Ops:
  28.4 31.2 %collective-permute-start.2 = (bf16[640,1024]{1,0:T(8,128)(2,1)S(1)}, bf16[640,1024]{1,0:T(8,128)(2,1)S(1)}, u32[]{:S(2)}, u32[]{:S(2)}) collective-permute-start(bf16[640,1024]{1,0:T(8,128)(2,1)S(1)} %pad_maximum_fusion.4.refs_2_.refs_7_), channel_id=1, source_target_pairs={{0,8},{8,0},{16,24},{24,16},{1,9},{9,1},{17,25},{25,17},{2,10},{10... | collective-permute-start | bytes 3932168 | tf_op jit(solution)/shard_map/ppermute | solution.py:770
  30.1 29.6 %collective-permute-start.3 = (bf16[640,1024]{1,0:T(8,128)(2,1)S(1)}, bf16[640,1024]{1,0:T(8,128)(2,1)}, u32[]{:S(2)}, u32[]{:S(2)}) collective-permute-start(bf16[640,1024]{1,0:T(8,128)(2,1)S(1)} %pad_maximum_fusion.4.refs_2_.refs_7_), channel_id=1, source_target_pairs={{8,16},{16,8},{9,17},{17,9},{10,18},{18,10},{11,19},{19,11},{12,20... | collective-permute-start | bytes 3932168 | tf_op jit(solution)/shard_map/ppermute | solution.py:770
  61.4 36.1 %collective-permute-start.5 = (bf16[640,1024]{1,0:T(8,128)(2,1)}, bf16[640,1024]{1,0:T(8,128)(2,1)S(1)}, u32[]{:S(2)}, u32[]{:S(2)}) collective-permute-start(bf16[640,1024]{1,0:T(8,128)(2,1)} %collective-permute-done.3), channel_id=1, source_target_pairs={{8,0},{16,24},{9,1},{17,25},{10,2},{18,26},{11,3},{19,27},{12,4},{... | collective-permute-start | bytes 3932168 | tf_op jit(solution)/shard_map/ppermute | solution.py:770
  99.2 34.4 %collective-permute-start.10 = (bf16[1024,2048]{1,0:T(8,128)(2,1)}, bf16[1024,2048]{1,0:T(8,128)(2,1)}, u32[]{:S(2)}, u32[]{:S(2)}) collective-permute-start(bf16[1024,2048]{1,0:T(8,128)(2,1)} %constant_dynamic-update-slice_fusion.refs_0_), channel_id=1, source_target_pairs={{0,1},{1,0},{2,3},{3,2},{4,5},{5,4},{6,7},{7,6},{8,9},{9,8},{10,11... | collective-permute-start | bytes 12582920 | tf_op jit(solution)/shard_map/ppermute | solution.py:770
  99.2 26.6 %collective-permute-start.11 = (bf16[3,704,256]{2,1,0:T(8,128)(2,1)}, bf16[3,704,256]{2,1,0:T(8,128)(2,1)}, u32[]{:S(2)}, u32[]{:S(2)}) collective-permute-start(bf16[3,704,256]{2,1,0:T(8,128)(2,1)} %get-tuple-element.254), channel_id=1, source_target_pairs={{0,4},{4,0},{1,5},{5,1},{2,6},{6,2},{3,7},{7,3},{8,12},{12,8},{9,1... | collective-permute-start | bytes 3244040 | tf_op jit(solution)/shard_map/ppermute | solution.py:770
  100.5 33.1 %collective-permute-start.8 = (bf16[640,1024]{1,0:T(8,128)(2,1)}, bf16[640,1024]{1,0:T(8,128)(2,1)}, u32[]{:S(2)}, u32[]{:S(2)}) collective-permute-start(bf16[640,1024]{1,0:T(8,128)(2,1)} %collective-permute-done.6), channel_id=1, source_target_pairs={{8,0},{16,24},{9,1},{17,25},{10,2},{18,26},{11,3},{19,27},{12,4},{... | collective-permute-start | bytes 3932168 | tf_op jit(solution)/shard_map/ppermute | solution.py:770
  133.6 33.0 %collective-permute-start.12 = (bf16[2,704,512]{2,1,0:T(8,128)(2,1)S(1)}, bf16[2,704,512]{2,1,0:T(8,128)(2,1)}, u32[]{:S(2)}, u32[]{:S(2)}) collective-permute-start(bf16[2,704,512]{2,1,0:T(8,128)(2,1)S(1)} %fusion.11.refs_2_), channel_id=1, source_target_pairs={{0,8},{8,0},{16,24},{24,16},{1,9},{9,1},{17,25},{25,17},{2,10},{10... | collective-permute-start | bytes 4325384 | tf_op jit(solution)/shard_map/ppermute | solution.py:770
  133.6 33.0 %collective-permute-start.13 = (bf16[2,704,512]{2,1,0:T(8,128)(2,1)S(1)}, bf16[2,704,512]{2,1,0:T(8,128)(2,1)S(1)}, u32[]{:S(2)}, u32[]{:S(2)}) collective-permute-start(bf16[2,704,512]{2,1,0:T(8,128)(2,1)S(1)} %fusion.11.refs_2_), channel_id=1, source_target_pairs={{8,16},{16,8},{9,17},{17,9},{10,18},{18,10},{11,19},{19,11},{12,20... | collective-permute-start | bytes 4325384 | tf_op jit(solution)/shard_map/ppermute | solution.py:770
  138.1 25.8 %collective-permute-start.14 = (bf16[256,2048]{1,0:T(8,128)(2,1)}, bf16[256,2048]{1,0:T(8,128)(2,1)S(1)}, u32[]{:S(2)}, u32[]{:S(2)}) collective-permute-start(bf16[256,2048]{1,0:T(8,128)(2,1)} %get-tuple-element.264), channel_id=1, source_target_pairs={{0,4},{4,0},{1,5},{5,1},{2,6},{6,2},{3,7},{7,3},{8,12},{12,8},{9,1... | collective-permute-start | bytes 3145736 | tf_op jit(solution)/shard_map/ppermute | solution.py:770
  224.1 39.5 %collective-permute-start.30 = (bf16[1024,2048]{1,0:T(8,128)(2,1)}, bf16[1024,2048]{1,0:T(8,128)(2,1)}, u32[]{:S(2)}, u32[]{:S(2)}) collective-permute-start(bf16[1024,2048]{1,0:T(8,128)(2,1)} %constant_dynamic-update-slice_fusion.5.refs_1_.refs_2_), channel_id=1, source_target_pairs={{0,1},{1,0},{2,3},{3,2},{4,5},{5,4},{6,7},{7,6},{8,9},{9,8},{10,11... | collective-permute-start | bytes 12582920 | tf_op jit(solution)/shard_map/ppermute | solution.py:770
  224.1 35.8 %collective-permute-start.29 = (bf16[2,704,512]{2,1,0:T(8,128)(2,1)}, bf16[2,704,512]{2,1,0:T(8,128)(2,1)S(1)}, u32[]{:S(2)}, u32[]{:S(2)}) collective-permute-start(bf16[2,704,512]{2,1,0:T(8,128)(2,1)} %collective-permute-done.12.refs_3_), channel_id=1, source_target_pairs={{8,16},{16,8},{9,17},{17,9},{10,18},{18,10},{11,19},{19,11},{12,20... | collective-permute-start | bytes 4325384 | tf_op jit(solution)/shard_map/ppermute | solution.py:770
  224.9 38.7 %collective-permute-start.28 = (bf16[2,704,512]{2,1,0:T(8,128)(2,1)S(1)}, bf16[2,704,512]{2,1,0:T(8,128)(2,1)S(1)}, u32[]{:S(2)}, u32[]{:S(2)}) collective-permute-start(bf16[2,704,512]{2,1,0:T(8,128)(2,1)S(1)} %copy-done.28), channel_id=1, source_target_pairs={{8,0},{16,24},{9,1},{17,25},{10,2},{18,26},{11,3},{19,27},{12,4},{... | collective-permute-start | bytes 4325384 | tf_op jit(solution)/shard_map/ppermute | solution.py:770
  231.6 27.2 %collective-permute-start.26 = (bf16[256,2176]{1,0:T(8,128)(2,1)}, bf16[256,2176]{1,0:T(8,128)(2,1)S(1)}, u32[]{:S(2)}, u32[]{:S(2)}) collective-permute-start(bf16[256,2176]{1,0:T(8,128)(2,1)} %get-tuple-element.290), channel_id=1, source_target_pairs={{0,2},{2,0},{1,3},{3,1},{4,6},{6,4},{5,7},{7,5},{8,10},{10,8},{9,1... | collective-permute-start | bytes 3342344 | tf_op jit(solution)/shard_map/ppermute | solution.py:770
  233.1 26.9 %collective-permute-start.27 = (bf16[256,2176]{1,0:T(8,128)(2,1)}, bf16[256,2176]{1,0:T(8,128)(2,1)S(1)}, u32[]{:S(2)}, u32[]{:S(2)}) collective-permute-start(bf16[256,2176]{1,0:T(8,128)(2,1)} %get-tuple-element.291), channel_id=1, source_target_pairs={{0,4},{4,0},{1,5},{5,1},{2,6},{6,2},{3,7},{7,3},{8,12},{12,8},{9,1... | collective-permute-start | bytes 3342344 | tf_op jit(solution)/shard_map/ppermute | solution.py:770
  263.6 34.3 %collective-permute-start.34 = (bf16[2,704,512]{2,1,0:T(8,128)(2,1)S(1)}, bf16[2,704,512]{2,1,0:T(8,128)(2,1)S(1)}, u32[]{:S(2)}, u32[]{:S(2)}) collective-permute-start(bf16[2,704,512]{2,1,0:T(8,128)(2,1)S(1)} %collective-permute-done.29), channel_id=1, source_target_pairs={{8,0},{16,24},{9,1},{17,25},{10,2},{18,26},{11,3},{19,27},{12,4},{... | collective-permute-start | bytes 4325384 | tf_op jit(solution)/shard_map/ppermute | solution.py:770
  390.1 32.3 %collective-permute-start.45 = (bf16[2,704,512]{2,1,0:T(8,128)(2,1)}, bf16[2,704,512]{2,1,0:T(8,128)(2,1)S(1)}, u32[]{:S(2)}, u32[]{:S(2)}) collective-permute-start(bf16[2,704,512]{2,1,0:T(8,128)(2,1)} %get-tuple-element.361), channel_id=1, source_target_pairs={{0,8},{24,16},{1,9},{25,17},{2,10},{26,18},{3,11},{27,19},{4,12},{... | collective-permute-start | bytes 4325384 | tf_op jit(solution)/shard_map/ppermute | solution.py:770
  422.8 38.7 %collective-permute-start.50 = (bf16[2,704,512]{2,1,0:T(8,128)(2,1)S(1)}, bf16[2,704,512]{2,1,0:T(8,128)(2,1)S(1)}, u32[]{:S(2)}, u32[]{:S(2)}) collective-permute-start(bf16[2,704,512]{2,1,0:T(8,128)(2,1)S(1)} %add_convert_fusion), channel_id=1, source_target_pairs={{8,16},{16,8},{9,17},{17,9},{10,18},{18,10},{11,19},{19,11},{12,20... | collective-permute-start | bytes 4325384 | tf_op jit(solution)/shard_map/ppermute | solution.py:770
  423.7 39.9 %collective-permute-start.49 = (bf16[2,704,512]{2,1,0:T(8,128)(2,1)S(1)}, bf16[2,704,512]{2,1,0:T(8,128)(2,1)}, u32[]{:S(2)}, u32[]{:S(2)}) collective-permute-start(bf16[2,704,512]{2,1,0:T(8,128)(2,1)S(1)} %copy-done.29), channel_id=1, source_target_pairs={{0,8},{24,16},{1,9},{25,17},{2,10},{26,18},{3,11},{27,19},{4,12},{... | collective-permute-start | bytes 4325384 | tf_op jit(solution)/shard_map/ppermute | solution.py:770
  511.2 25.9 %collective-permute-start.62 = (bf16[704,512]{1,0:T(8,128)(2,1)S(1)}, bf16[704,512]{1,0:T(8,128)(2,1)S(1)}, u32[]{:S(2)}, u32[]{:S(2)}) collective-permute-start(bf16[704,512]{1,0:T(8,128)(2,1)S(1)} %copy-done.64), channel_id=1, source_target_pairs={{8,16},{16,8},{9,17},{17,9},{10,18},{18,10},{11,19},{19,11},{12,20... | collective-permute-start | bytes 2162696 | tf_op jit(solution)/shard_map/ppermute | solution.py:770
  585.1 35.1 %collective-permute-start.72 = (bf16[640,1024]{1,0:T(8,128)(2,1)}, bf16[640,1024]{1,0:T(8,128)(2,1)S(1)}, u32[]{:S(2)}, u32[]{:S(2)}) collective-permute-start(bf16[640,1024]{1,0:T(8,128)(2,1)} %get-tuple-element.426), channel_id=1, source_target_pairs={{0,8},{24,16},{1,9},{25,17},{2,10},{26,18},{3,11},{27,19},{4,12},{... | collective-permute-start | bytes 3932168 | tf_op jit(solution)/shard_map/ppermute | solution.py:770
  590.4 52.1 %collective-permute-start.76 = (bf16[640,1024]{1,0:T(8,128)(2,1)}, bf16[640,1024]{1,0:T(8,128)(2,1)S(1)}, u32[]{:S(2)}, u32[]{:S(2)}) collective-permute-start(bf16[640,1024]{1,0:T(8,128)(2,1)} %get-tuple-element.441), channel_id=1, source_target_pairs={{0,8},{24,16},{1,9},{25,17},{2,10},{26,18},{3,11},{27,19},{4,12},{... | collective-permute-start | bytes 3932168 | tf_op jit(solution)/shard_map/ppermute | solution.py:770
  620.2 25.8 %collective-permute-start.77 = (bf16[3,704,256]{2,1,0:T(8,128)(2,1)S(1)}, bf16[3,704,256]{2,1,0:T(8,128)(2,1)S(1)}, u32[]{:S(2)}, u32[]{:S(2)}) collective-permute-start(bf16[3,704,256]{2,1,0:T(8,128)(2,1)S(1)} %get-tuple-element.442), channel_id=1, source_target_pairs={{0,4},{4,0},{1,5},{5,1},{2,6},{6,2},{3,7},{7,3},{8,12},{12,8},{9,1... | collective-permute-start | bytes 3244040 | tf_op jit(solution)/shard_map/ppermute | solution.py:770
  646.0 36.1 %collective-permute-start.80 = (bf16[640,1024]{1,0:T(8,128)(2,1)}, bf16[640,1024]{1,0:T(8,128)(2,1)}, u32[]{:S(2)}, u32[]{:S(2)}) collective-permute-start(bf16[640,1024]{1,0:T(8,128)(2,1)} %add_convert_fusion.2), channel_id=1, source_target_pairs={{8,16},{16,8},{9,17},{17,9},{10,18},{18,10},{11,19},{19,11},{12,20... | collective-permute-start | bytes 3932168 | tf_op jit(solution)/shard_map/ppermute | solution.py:770
  649.4 32.7 %collective-permute-start.79 = (bf16[640,1024]{1,0:T(8,128)(2,1)}, bf16[640,1024]{1,0:T(8,128)(2,1)}, u32[]{:S(2)}, u32[]{:S(2)}) collective-permute-start(bf16[640,1024]{1,0:T(8,128)(2,1)} %add_convert_fusion.1), channel_id=1, source_target_pairs={{0,8},{8,0},{16,24},{24,16},{1,9},{9,1},{17,25},{25,17},{2,10},{10... | collective-permute-start | bytes 3932168 | tf_op jit(solution)/shard_map/ppermute | solution.py:770
  (149 other events, 1886.9 us)

commit v7 on v5

--- a/solution.py
+++ b/solution.py
@@ -612,7 +612,7 @@
 
 def renew_turned(grad, weight, moment, average, fan, tokens):
     few, total = weight.shape
-    block = 16
+    block = 32
 
     def kernel(g_ref, w_ref, m_ref, a_ref, m_new, w_new, a_new):
         for p in range(8):

time: 722 us -> 721 us (level)
  no operation moved by 1% of the time
where the time goes in v7:
time: 721 us; the launch traced here: 711 us
  Pallas kernels  231 us (32%)
  waiting for transfers between devices  217 us (30%)
  starting transfers between devices  116 us (16%)
  other arithmetic  75 us (10%)
  local copies, waits for them, and re-layouts  54.6 us (8%)
  between operations  17 us (2%)
    pallas_call x26, Pallas kernels, call(): pl.pallas_call(kernel, grid=(steps,), in_specs=[s for _, s in ins], out_s...  231 us
    ppermute x80, waiting for transfers between devices, over(): return lambda v: pin(lax.ppermute(pin(v), axis, pairs))  208 us
    ppermute x80, starting transfers between devices, over(): return lambda v: pin(lax.ppermute(pin(v), axis, pairs))  101 us
    unnamed x197, local copies, waits for them, and re-layouts  33.7 us
  transfers between devices with their start and end apart: 84, of which 42 were waited for; matrix products, arithmetic and copies ran while one was open for 14% of the time, Pallas kernels for 27%

profile of v7, /device:TPU:0, one launch (start us, length us, event | category | flops | bytes accessed | tf_op | source)
XLA Modules:
  0.0 711.3 jit_solution(10992915353650267989)
XLA Ops:
  79.5 18.0 %collective-permute-done.5 = bf16[640,1024]{1,0:T(8,128)(2,1)S(1)} collective-permute-done((bf16[640,1024]{1,0:T(8,128)(2,1)}, bf16[640,1024]{1,0:T(8,128)(2,1)S(1)}, u32[]{:S(2)}, u32[]{:S(2)}) %collective-permute-start.5) | collective-permute-done | bytes 1310752 | tf_op jit(solution)/shard_map/ppermute | solution.py:770
  112.7 13.1 %collective-permute-done.11 = bf16[3,704,256]{2,1,0:T(8,128)(2,1)} collective-permute-done((bf16[3,704,256]{2,1,0:T(8,128)(2,1)}, bf16[3,704,256]{2,1,0:T(8,128)(2,1)}, u32[]{:S(2)}, u32[]{:S(2)}) %collective-permute-start.11) | collective-permute-done | bytes 1081376 | tf_op jit(solution)/shard_map/ppermute | solution.py:770
  138.9 17.4 %shard_map.290 = (f32[2048,512]{1,0:T(8,128)}, f32[2048,256]{1,0:T(8,128)}, bf16[2048,768]{1,0:T(8,128)(2,1)}, f32[8,2,128,128]{3,2,1,0:T(8,128)}, f32[2,128,128]{2,1,0:T(8,128)}) custom-call(bf16[1024,2048]{1,0:T(8,128)(2,1)} %constant_dynamic-update-slice_fusion.refs_0_, bf16[1024,2048]{1,0:T(8,128)(2,1)} %collective-permute-done.10.refs_1_, ...), custom_call_target="tpu_custom_call" | custom-call | flops 8589934592 | bytes 24387680 | tf_op jit(solution)/shard_map/pallas_call | solution.py:91
  214.3 6.6 collective-permute-done.22.u_ref
  233.7 25.0 %collective-permute-done.26.c = bf16[256,2176]{1,0:T(8,128)(2,1)S(1)} collective-permute-done((bf16[256,2176]{1,0:T(8,128)(2,1)}, bf16[256,2176]{1,0:T(8,128)(2,1)S(1)}, u32[]{:S(2)}, u32[]{:S(2)}) %collective-permute-start.26) | collective-permute-done | bytes 1114144 | tf_op jit(solution)/shard_map/ppermute | solution.py:770
  272.6 21.6 %collective-permute-done.31 = bf16[256,2048]{1,0:T(8,128)(2,1)S(1)} collective-permute-done((bf16[256,2048]{1,0:T(8,128)(2,1)}, bf16[256,2048]{1,0:T(8,128)(2,1)S(1)}, u32[]{:S(2)}, u32[]{:S(2)}) %collective-permute-start.31) | collective-permute-done | bytes 1048608 | tf_op jit(solution)/shard_map/ppermute | solution.py:770
  302.8 10.2 %collective-permute-done.36 = bf16[128,2048]{1,0:T(8,128)(2,1)S(1)} collective-permute-done((bf16[128,2048]{1,0:T(8,128)(2,1)S(1)}, bf16[128,2048]{1,0:T(8,128)(2,1)S(1)}, u32[]{:S(2)}, u32[]{:S(2)}) %collective-permute-start.36) | collective-permute-done | bytes 524320 | tf_op jit(solution)/shard_map/ppermute | solution.py:770
  321.9 23.7 %shard_map.296 = (bf16[1024,704]{1,0:T(8,128)(2,1)}, bf16[704,1024]{1,0:T(8,128)(2,1)}, bf16[704,1024]{1,0:T(8,128)(2,1)}, bf16[704,1024]{1,0:T(8,128)(2,1)}, bf16[1024,2048]{1,0:T(8,128)(2,1)}) custom-call(bf16[1024,2048]{1,0:T(8,128)(2,1)} %copy-done.76, bf16[1024,2048]{1,0:T(8,128)(2,1)} %collective-permute-done.30.refs_1_.refs_3_, ...), custom_call_target="tpu_custom_call" | custom-call | flops 14763950080 | bytes 27000832 | tf_op jit(solution)/shard_map/pallas_call | solution.py:91
  345.6 24.3 %shard_map.297 = (bf16[1024,704]{1,0:T(8,128)(2,1)}, bf16[704,1024]{1,0:T(8,128)(2,1)}, bf16[704,1024]{1,0:T(8,128)(2,1)}, bf16[704,1024]{1,0:T(8,128)(2,1)}, bf16[1024,2048]{1,0:T(8,128)(2,1)}) custom-call(bf16[1024,2048]{1,0:T(8,128)(2,1)} %copy-done.77, bf16[1024,2048]{1,0:T(8,128)(2,1)} %constant_dynamic-update-slice_fusion.5.refs_1_.refs_2_, ...), custom_call_target="tpu_custom_call" | custom-call | flops 14763950080 | bytes 27000832 | tf_op jit(solution)/shard_map/pallas_call | solution.py:91
  377.3 11.8 %shard_map.299 = (bf16[2,704,512]{2,1,0:T(8,128)(2,1)}, bf16[2,704,512]{2,1,0:T(8,128)(2,1)}) custom-call(bf16[704,1024]{1,0:T(8,128)(2,1)} %get-tuple-element.347.refs_0_, bf16[704,1024]{1,0:T(8,128)(2,1)} %get-tuple-element.329.refs_1_, bf16[704,1024]{1,0:T(8,128)(2,1)} %get-tuple-element.330.refs_2_, bf16[704,1024]{1,0:T(8,128)(2,1)} %get-tuple-element.331.refs_3_, ...), custom_call_target="tpu_custom_call" | custom-call | flops 11811160064 | bytes 17039360 | tf_op jit(solution)/shard_map/pallas_call | solution.py:91
  397.8 11.2 %shard_map.301 = (bf16[1,704,512]{2,1,0:T(8,128)(2,1)}, bf16[1,704,512]{2,1,0:T(8,128)(2,1)}, bf16[1,704,512]{2,1,0:T(8,128)(2,1)}, bf16[1,704,512]{2,1,0:T(8,128)(2,1)}) custom-call(bf16[704,1024]{1,0:T(8,128)(2,1)} %get-tuple-element.341.refs_0_, bf16[704,1024]{1,0:T(8,128)(2,1)} %get-tuple-element.342.refs_1_, ...), custom_call_target="tpu_custom_call" | custom-call | flops 5905580032 | bytes 14155776 | tf_op jit(solution)/shard_map/pallas_call | solution.py:91
  408.9 11.9 %shard_map.302 = (bf16[2,704,512]{2,1,0:T(8,128)(2,1)}, bf16[2,704,512]{2,1,0:T(8,128)(2,1)}) custom-call(bf16[704,1024]{1,0:T(8,128)(2,1)} %get-tuple-element.347.refs_0_, bf16[704,1024]{1,0:T(8,128)(2,1)} %get-tuple-element.329.refs_1_, bf16[704,1024]{1,0:T(8,128)(2,1)} %get-tuple-element.330.refs_2_, bf16[704,1024]{1,0:T(8,128)(2,1)} %get-tuple-element.331.refs_3_, ...), custom_call_target="tpu_custom_call" | custom-call | flops 11811160064 | bytes 17039360 | tf_op jit(solution)/shard_map/pallas_call | solution.py:91
  423.7 7.2 %collective-permute-start.49 = (bf16[2,704,512]{2,1,0:T(8,128)(2,1)S(1)}, bf16[2,704,512]{2,1,0:T(8,128)(2,1)}, u32[]{:S(2)}, u32[]{:S(2)}) collective-permute-start(bf16[2,704,512]{2,1,0:T(8,128)(2,1)S(1)} %copy-done.29), channel_id=1, source_target_pairs={{0,8},{24,16},{1,9},{25,17},{2,10},{26,18},{3,11},{27,19},{4,12},{... | collective-permute-start | bytes 4325384 | tf_op jit(solution)/shard_map/ppermute | solution.py:770
  438.4 6.9 shard_map.304
  445.3 6.9 shard_map.303.a_ref.a2.a4
  452.2 8.9 %collective-permute-done.46 = bf16[256,2176]{1,0:T(8,128)(2,1)S(1)} collective-permute-done((bf16[256,2176]{1,0:T(8,128)(2,1)}, bf16[256,2176]{1,0:T(8,128)(2,1)S(1)}, u32[]{:S(2)}, u32[]{:S(2)}) %collective-permute-start.46) | collective-permute-done | bytes 1114144 | tf_op jit(solution)/shard_map/ppermute | solution.py:770
  498.0 11.8 %shard_map.306 = (bf16[2048,256]{1,0:T(8,128)(2,1)}, bf16[2048,256]{1,0:T(8,128)(2,1)}, bf16[2048,256]{1,0:T(8,128)(2,1)}, f32[8,2,128,128]{3,2,1,0:T(8,128)}, f32[2,128,128]{2,1,0:T(8,128)}) custom-call(bf16[1024,2176]{1,0:T(8,128)(2,1)} %copy-done.9, bf16[1024,2176]{1,0:T(8,128)(2,1)} %copy-done.8, bf16[256,2048]{1,0:T(8,128)(2,1)} %maximum_maximum_fusion.w_ref, ...), custom_call_target="tpu_custom_call" | custom-call | flops 2147483648 | bytes 21766240 | tf_op jit(solution)/shard_map/pallas_call | solution.py:91
  524.1 13.0 %shard_map.309 = (bf16[1024,1024]{1,0:T(8,128)(2,1)}, bf16[1024,2048]{1,0:T(8,128)(2,1)}) custom-call(bf16[2048,768]{1,0:T(8,128)(2,1)} %get-tuple-element.398.qkv_ref.refs_0_, f32[2048,512]{1,0:T(8,128)} %get-tuple-element.390.refs_1_, bf16[2048,256]{1,0:T(8,128)(2,1)} %get-tuple-element.391.refs_2_, bf16[2048,256]{1,0:T(8,128)(2,1)} %get-tuple-element.392.refs_3_, ...), custom_call_target="tpu_custom_call" | custom-call | flops 4294967296 | bytes 23085696 | tf_op jit(solution)/shard_map/pallas_call | solution.py:91
  543.8 13.0 %shard_map.310 = (bf16[1024,1024]{1,0:T(8,128)(2,1)}, bf16[1024,2048]{1,0:T(8,128)(2,1)}) custom-call(bf16[2048,768]{1,0:T(8,128)(2,1)} %get-tuple-element.398.qkv_ref.refs_0_, f32[2048,512]{1,0:T(8,128)} %get-tuple-element.390.refs_1_, bf16[2048,256]{1,0:T(8,128)(2,1)} %get-tuple-element.391.refs_2_, bf16[2048,256]{1,0:T(8,128)(2,1)} %get-tuple-element.392.refs_3_, ...), custom_call_target="tpu_custom_call" | custom-call | flops 4294967296 | bytes 23085696 | tf_op jit(solution)/shard_map/pallas_call | solution.py:91
  568.5 15.8 %shard_map.311 = (bf16[640,1024]{1,0:T(8,128)(2,1)}, bf16[640,1024]{1,0:T(8,128)(2,1)}, bf16[640,1024]{1,0:T(8,128)(2,1)}, bf16[640,1024]{1,0:T(8,128)(2,1)}) custom-call(bf16[1024,2048]{1,0:T(8,128)(2,1)} %constant_dynamic-update-slice_fusion.refs_0_, bf16[1024,2048]{1,0:T(8,128)(2,1)} %collective-permute-done.10.refs_1_, ...), custom_call_target="tpu_custom_call" | custom-call | flops 8589934592 | bytes 18874400 | tf_op jit(solution)/shard_map/pallas_call | solution.py:91
  601.7 18.2 %collective-permute-done.73 = bf16[256,2048]{1,0:T(8,128)(2,1)S(1)} collective-permute-done((bf16[256,2048]{1,0:T(8,128)(2,1)}, bf16[256,2048]{1,0:T(8,128)(2,1)S(1)}, u32[]{:S(2)}, u32[]{:S(2)}) %collective-permute-start.73) | collective-permute-done | bytes 1048608 | tf_op jit(solution)/shard_map/ppermute | solution.py:770
  626.5 16.0 %collective-permute-done.76 = bf16[640,1024]{1,0:T(8,128)(2,1)S(1)} collective-permute-done((bf16[640,1024]{1,0:T(8,128)(2,1)}, bf16[640,1024]{1,0:T(8,128)(2,1)S(1)}, u32[]{:S(2)}, u32[]{:S(2)}) %collective-permute-start.76) | collective-permute-done | bytes 1310752 | tf_op jit(solution)/shard_map/ppermute | solution.py:770
  669.4 7.5 %multiply_add_fusion = (f32[2,256,1408]{2,1,0:T(8,128)}, f32[2,256,1408]{2,1,0:T(8,128)}, f32[2,256,1408]{2,1,0:T(8,128)}) fusion(f32[2,256,1408]{2,1,0:T(8,128)} %param.33, f32[2,256,1408]{2,1,0:T(8,128)S(1)} %copy-done.13, bf16[2,1408,256]{1,2,0:T(8,128)(2,1)} %copy.74, f32[2,256,1408]{2,1,0:T(8,128)} %param.29), kind=kLoop, calls=%fused_computation.9 | loop fusion | flops 7208960 | bytes 18743296 | tf_op jit(solution)/shard_map/add | solution.py:42
  696.3 8.2 %all-to-all-done.1.g_ref = bf16[8,64,1024]{2,1,0:T(8,128)(2,1)S(1)} async-done(((bf16[8,64,1024]{2,1,0:T(8,128)(2,1)}), bf16[8,64,1024]{2,1,0:T(8,128)(2,1)S(1)}, u32[]{:S(2)}, u32[]{:S(2)}) %all-to-all-start.1) | async-done | bytes 1048608 | tf_op jit(solution)/shard_map/all_to_all | solution.py:1046
  (500 shorter events, 366.0 us)
Async XLA Ops:
  28.4 31.2 %collective-permute-start.2 = (bf16[640,1024]{1,0:T(8,128)(2,1)S(1)}, bf16[640,1024]{1,0:T(8,128)(2,1)S(1)}, u32[]{:S(2)}, u32[]{:S(2)}) collective-permute-start(bf16[640,1024]{1,0:T(8,128)(2,1)S(1)} %pad_maximum_fusion.4.refs_2_.refs_7_), channel_id=1, source_target_pairs={{0,8},{8,0},{16,24},{24,16},{1,9},{9,1},{17,25},{25,17},{2,10},{10... | collective-permute-start | bytes 3932168 | tf_op jit(solution)/shard_map/ppermute | solution.py:770
  30.1 29.6 %collective-permute-start.3 = (bf16[640,1024]{1,0:T(8,128)(2,1)S(1)}, bf16[640,1024]{1,0:T(8,128)(2,1)}, u32[]{:S(2)}, u32[]{:S(2)}) collective-permute-start(bf16[640,1024]{1,0:T(8,128)(2,1)S(1)} %pad_maximum_fusion.4.refs_2_.refs_7_), channel_id=1, source_target_pairs={{8,16},{16,8},{9,17},{17,9},{10,18},{18,10},{11,19},{19,11},{12,20... | collective-permute-start | bytes 3932168 | tf_op jit(solution)/shard_map/ppermute | solution.py:770
  61.4 36.1 %collective-permute-start.5 = (bf16[640,1024]{1,0:T(8,128)(2,1)}, bf16[640,1024]{1,0:T(8,128)(2,1)S(1)}, u32[]{:S(2)}, u32[]{:S(2)}) collective-permute-start(bf16[640,1024]{1,0:T(8,128)(2,1)} %collective-permute-done.3), channel_id=1, source_target_pairs={{8,0},{16,24},{9,1},{17,25},{10,2},{18,26},{11,3},{19,27},{12,4},{... | collective-permute-start | bytes 3932168 | tf_op jit(solution)/shard_map/ppermute | solution.py:770
  99.2 34.4 %collective-permute-start.10 = (bf16[1024,2048]{1,0:T(8,128)(2,1)}, bf16[1024,2048]{1,0:T(8,128)(2,1)}, u32[]{:S(2)}, u32[]{:S(2)}) collective-permute-start(bf16[1024,2048]{1,0:T(8,128)(2,1)} %constant_dynamic-update-slice_fusion.refs_0_), channel_id=1, source_target_pairs={{0,1},{1,0},{2,3},{3,2},{4,5},{5,4},{6,7},{7,6},{8,9},{9,8},{10,11... | collective-permute-start | bytes 12582920 | tf_op jit(solution)/shard_map/ppermute | solution.py:770
  99.2 26.6 %collective-permute-start.11 = (bf16[3,704,256]{2,1,0:T(8,128)(2,1)}, bf16[3,704,256]{2,1,0:T(8,128)(2,1)}, u32[]{:S(2)}, u32[]{:S(2)}) collective-permute-start(bf16[3,704,256]{2,1,0:T(8,128)(2,1)} %get-tuple-element.254), channel_id=1, source_target_pairs={{0,4},{4,0},{1,5},{5,1},{2,6},{6,2},{3,7},{7,3},{8,12},{12,8},{9,1... | collective-permute-start | bytes 3244040 | tf_op jit(solution)/shard_map/ppermute | solution.py:770
  100.5 33.1 %collective-permute-start.8 = (bf16[640,1024]{1,0:T(8,128)(2,1)}, bf16[640,1024]{1,0:T(8,128)(2,1)}, u32[]{:S(2)}, u32[]{:S(2)}) collective-permute-start(bf16[640,1024]{1,0:T(8,128)(2,1)} %collective-permute-done.6), channel_id=1, source_target_pairs={{8,0},{16,24},{9,1},{17,25},{10,2},{18,26},{11,3},{19,27},{12,4},{... | collective-permute-start | bytes 3932168 | tf_op jit(solution)/shard_map/ppermute | solution.py:770
  133.6 33.0 %collective-permute-start.12 = (bf16[2,704,512]{2,1,0:T(8,128)(2,1)S(1)}, bf16[2,704,512]{2,1,0:T(8,128)(2,1)}, u32[]{:S(2)}, u32[]{:S(2)}) collective-permute-start(bf16[2,704,512]{2,1,0:T(8,128)(2,1)S(1)} %fusion.11.refs_2_), channel_id=1, source_target_pairs={{0,8},{8,0},{16,24},{24,16},{1,9},{9,1},{17,25},{25,17},{2,10},{10... | collective-permute-start | bytes 4325384 | tf_op jit(solution)/shard_map/ppermute | solution.py:770
  133.6 33.0 %collective-permute-start.13 = (bf16[2,704,512]{2,1,0:T(8,128)(2,1)S(1)}, bf16[2,704,512]{2,1,0:T(8,128)(2,1)S(1)}, u32[]{:S(2)}, u32[]{:S(2)}) collective-permute-start(bf16[2,704,512]{2,1,0:T(8,128)(2,1)S(1)} %fusion.11.refs_2_), channel_id=1, source_target_pairs={{8,16},{16,8},{9,17},{17,9},{10,18},{18,10},{11,19},{19,11},{12,20... | collective-permute-start | bytes 4325384 | tf_op jit(solution)/shard_map/ppermute | solution.py:770
  138.1 25.8 %collective-permute-start.14 = (bf16[256,2048]{1,0:T(8,128)(2,1)}, bf16[256,2048]{1,0:T(8,128)(2,1)S(1)}, u32[]{:S(2)}, u32[]{:S(2)}) collective-permute-start(bf16[256,2048]{1,0:T(8,128)(2,1)} %get-tuple-element.264), channel_id=1, source_target_pairs={{0,4},{4,0},{1,5},{5,1},{2,6},{6,2},{3,7},{7,3},{8,12},{12,8},{9,1... | collective-permute-start | bytes 3145736 | tf_op jit(solution)/shard_map/ppermute | solution.py:770
  224.1 39.5 %collective-permute-start.30 = (bf16[1024,2048]{1,0:T(8,128)(2,1)}, bf16[1024,2048]{1,0:T(8,128)(2,1)}, u32[]{:S(2)}, u32[]{:S(2)}) collective-permute-start(bf16[1024,2048]{1,0:T(8,128)(2,1)} %constant_dynamic-update-slice_fusion.5.refs_1_.refs_2_), channel_id=1, source_target_pairs={{0,1},{1,0},{2,3},{3,2},{4,5},{5,4},{6,7},{7,6},{8,9},{9,8},{10,11... | collective-permute-start | bytes 12582920 | tf_op jit(solution)/shard_map/ppermute | solution.py:770
  224.1 35.8 %collective-permute-start.29 = (bf16[2,704,512]{2,1,0:T(8,128)(2,1)}, bf16[2,704,512]{2,1,0:T(8,128)(2,1)S(1)}, u32[]{:S(2)}, u32[]{:S(2)}) collective-permute-start(bf16[2,704,512]{2,1,0:T(8,128)(2,1)} %collective-permute-done.12.refs_3_), channel_id=1, source_target_pairs={{8,16},{16,8},{9,17},{17,9},{10,18},{18,10},{11,19},{19,11},{12,20... | collective-permute-start | bytes 4325384 | tf_op jit(solution)/shard_map/ppermute | solution.py:770
  224.9 38.7 %collective-permute-start.28 = (bf16[2,704,512]{2,1,0:T(8,128)(2,1)S(1)}, bf16[2,704,512]{2,1,0:T(8,128)(2,1)S(1)}, u32[]{:S(2)}, u32[]{:S(2)}) collective-permute-start(bf16[2,704,512]{2,1,0:T(8,128)(2,1)S(1)} %copy-done.28), channel_id=1, source_target_pairs={{8,0},{16,24},{9,1},{17,25},{10,2},{18,26},{11,3},{19,27},{12,4},{... | collective-permute-start | bytes 4325384 | tf_op jit(solution)/shard_map/ppermute | solution.py:770
  231.6 27.2 %collective-permute-start.26 = (bf16[256,2176]{1,0:T(8,128)(2,1)}, bf16[256,2176]{1,0:T(8,128)(2,1)S(1)}, u32[]{:S(2)}, u32[]{:S(2)}) collective-permute-start(bf16[256,2176]{1,0:T(8,128)(2,1)} %get-tuple-element.290), channel_id=1, source_target_pairs={{0,2},{2,0},{1,3},{3,1},{4,6},{6,4},{5,7},{7,5},{8,10},{10,8},{9,1... | collective-permute-start | bytes 3342344 | tf_op jit(solution)/shard_map/ppermute | solution.py:770
  233.1 26.9 %collective-permute-start.27 = (bf16[256,2176]{1,0:T(8,128)(2,1)}, bf16[256,2176]{1,0:T(8,128)(2,1)S(1)}, u32[]{:S(2)}, u32[]{:S(2)}) collective-permute-start(bf16[256,2176]{1,0:T(8,128)(2,1)} %get-tuple-element.291), channel_id=1, source_target_pairs={{0,4},{4,0},{1,5},{5,1},{2,6},{6,2},{3,7},{7,3},{8,12},{12,8},{9,1... | collective-permute-start | bytes 3342344 | tf_op jit(solution)/shard_map/ppermute | solution.py:770
  263.6 34.3 %collective-permute-start.34 = (bf16[2,704,512]{2,1,0:T(8,128)(2,1)S(1)}, bf16[2,704,512]{2,1,0:T(8,128)(2,1)S(1)}, u32[]{:S(2)}, u32[]{:S(2)}) collective-permute-start(bf16[2,704,512]{2,1,0:T(8,128)(2,1)S(1)} %collective-permute-done.29), channel_id=1, source_target_pairs={{8,0},{16,24},{9,1},{17,25},{10,2},{18,26},{11,3},{19,27},{12,4},{... | collective-permute-start | bytes 4325384 | tf_op jit(solution)/shard_map/ppermute | solution.py:770
  390.1 32.3 %collective-permute-start.45 = (bf16[2,704,512]{2,1,0:T(8,128)(2,1)}, bf16[2,704,512]{2,1,0:T(8,128)(2,1)S(1)}, u32[]{:S(2)}, u32[]{:S(2)}) collective-permute-start(bf16[2,704,512]{2,1,0:T(8,128)(2,1)} %get-tuple-element.361), channel_id=1, source_target_pairs={{0,8},{24,16},{1,9},{25,17},{2,10},{26,18},{3,11},{27,19},{4,12},{... | collective-permute-start | bytes 4325384 | tf_op jit(solution)/shard_map/ppermute | solution.py:770
  422.8 38.7 %collective-permute-start.50 = (bf16[2,704,512]{2,1,0:T(8,128)(2,1)S(1)}, bf16[2,704,512]{2,1,0:T(8,128)(2,1)S(1)}, u32[]{:S(2)}, u32[]{:S(2)}) collective-permute-start(bf16[2,704,512]{2,1,0:T(8,128)(2,1)S(1)} %add_convert_fusion), channel_id=1, source_target_pairs={{8,16},{16,8},{9,17},{17,9},{10,18},{18,10},{11,19},{19,11},{12,20... | collective-permute-start | bytes 4325384 | tf_op jit(solution)/shard_map/ppermute | solution.py:770
  423.7 39.9 %collective-permute-start.49 = (bf16[2,704,512]{2,1,0:T(8,128)(2,1)S(1)}, bf16[2,704,512]{2,1,0:T(8,128)(2,1)}, u32[]{:S(2)}, u32[]{:S(2)}) collective-permute-start(bf16[2,704,512]{2,1,0:T(8,128)(2,1)S(1)} %copy-done.29), channel_id=1, source_target_pairs={{0,8},{24,16},{1,9},{25,17},{2,10},{26,18},{3,11},{27,19},{4,12},{... | collective-permute-start | bytes 4325384 | tf_op jit(solution)/shard_map/ppermute | solution.py:770
  511.2 25.9 %collective-permute-start.62 = (bf16[704,512]{1,0:T(8,128)(2,1)S(1)}, bf16[704,512]{1,0:T(8,128)(2,1)S(1)}, u32[]{:S(2)}, u32[]{:S(2)}) collective-permute-start(bf16[704,512]{1,0:T(8,128)(2,1)S(1)} %copy-done.64), channel_id=1, source_target_pairs={{8,16},{16,8},{9,17},{17,9},{10,18},{18,10},{11,19},{19,11},{12,20... | collective-permute-start | bytes 2162696 | tf_op jit(solution)/shard_map/ppermute | solution.py:770
  585.1 35.1 %collective-permute-start.72 = (bf16[640,1024]{1,0:T(8,128)(2,1)}, bf16[640,1024]{1,0:T(8,128)(2,1)S(1)}, u32[]{:S(2)}, u32[]{:S(2)}) collective-permute-start(bf16[640,1024]{1,0:T(8,128)(2,1)} %get-tuple-element.426), channel_id=1, source_target_pairs={{0,8},{24,16},{1,9},{25,17},{2,10},{26,18},{3,11},{27,19},{4,12},{... | collective-permute-start | bytes 3932168 | tf_op jit(solution)/shard_map/ppermute | solution.py:770
  590.4 52.1 %collective-permute-start.76 = (bf16[640,1024]{1,0:T(8,128)(2,1)}, bf16[640,1024]{1,0:T(8,128)(2,1)S(1)}, u32[]{:S(2)}, u32[]{:S(2)}) collective-permute-start(bf16[640,1024]{1,0:T(8,128)(2,1)} %get-tuple-element.441), channel_id=1, source_target_pairs={{0,8},{24,16},{1,9},{25,17},{2,10},{26,18},{3,11},{27,19},{4,12},{... | collective-permute-start | bytes 3932168 | tf_op jit(solution)/shard_map/ppermute | solution.py:770
  620.2 25.8 %collective-permute-start.77 = (bf16[3,704,256]{2,1,0:T(8,128)(2,1)S(1)}, bf16[3,704,256]{2,1,0:T(8,128)(2,1)S(1)}, u32[]{:S(2)}, u32[]{:S(2)}) collective-permute-start(bf16[3,704,256]{2,1,0:T(8,128)(2,1)S(1)} %get-tuple-element.442), channel_id=1, source_target_pairs={{0,4},{4,0},{1,5},{5,1},{2,6},{6,2},{3,7},{7,3},{8,12},{12,8},{9,1... | collective-permute-start | bytes 3244040 | tf_op jit(solution)/shard_map/ppermute | solution.py:770
  646.0 36.1 %collective-permute-start.80 = (bf16[640,1024]{1,0:T(8,128)(2,1)}, bf16[640,1024]{1,0:T(8,128)(2,1)}, u32[]{:S(2)}, u32[]{:S(2)}) collective-permute-start(bf16[640,1024]{1,0:T(8,128)(2,1)} %add_convert_fusion.2), channel_id=1, source_target_pairs={{8,16},{16,8},{9,17},{17,9},{10,18},{18,10},{11,19},{19,11},{12,20... | collective-permute-start | bytes 3932168 | tf_op jit(solution)/shard_map/ppermute | solution.py:770
  649.4 32.7 %collective-permute-start.79 = (bf16[640,1024]{1,0:T(8,128)(2,1)}, bf16[640,1024]{1,0:T(8,128)(2,1)}, u32[]{:S(2)}, u32[]{:S(2)}) collective-permute-start(bf16[640,1024]{1,0:T(8,128)(2,1)} %add_convert_fusion.1), channel_id=1, source_target_pairs={{0,8},{8,0},{16,24},{24,16},{1,9},{9,1},{17,25},{25,17},{2,10},{10... | collective-permute-start | bytes 3932168 | tf_op jit(solution)/shard_map/ppermute | solution.py:770
  (149 other events, 1886.0 us)
